TPU v7x, 32 devices: a whole 2x2x4 slice. The times are simulated.
32 devices in a mesh: replica: 2 (over y), node: 8 (over z, x), shard: 2 (over core).
Axes of the slice: x: 2, y: 2, z: 4, core: 2. Of those that a mesh axis runs over, the one named last changes fastest.
Arguments:
- residual: bfloat16 [192, 6144], P(('replica', 'node'), 'shard'), parts along dimension 0, may hold values from -6 to 6
- queries: bfloat16 [192, 6144], P(('replica', 'node'), 'shard'), parts along dimension 0, may hold values from -110 to 110
- key_cache: bfloat16 [192, 128, 1024], P(('replica', 'node'), None, 'shard'), parts along dimension 0, may hold values from -4 to 4
- value_cache: bfloat16 [192, 128, 1024], P(('replica', 'node'), None, 'shard'), parts along dimension 0, may hold values from -6 to 6
- new_key: bfloat16 [192, 1024], P(('replica', 'node'), 'shard'), parts along dimension 0, may hold values from -4.1 to 4.1
- new_value: bfloat16 [192, 1024], P(('replica', 'node'), 'shard'), parts along dimension 0, may hold values from -6 to 6
- cache_lengths: int32 [192], P(('replica', 'node')), parts along dimension 0, may hold values from 1 to 128, 6144 in all
- norm_gain: float32 [6144], replicated, may hold values from 0.1 to 1.9
- router: bfloat16 [6144, 4], replicated, may hold values from -0.078125 to 0.078125
- routes: int32 [192, 2], P(('replica', 'node')), parts along dimension 0, may hold values from 0 to 3, all different within a row; in each aligned block of 12 rows (0 to 11, 12 to 23, ...) at most 9 rows name the same one
- gate_weight: bfloat16 [6144, 32768], P(None, ('node', 'shard')), may hold values from -0.078125 to 0.078125
- up_weight: bfloat16 [6144, 32768], P(None, ('node', 'shard')), may hold values from -0.078125 to 0.078125
- down_weight: bfloat16 [32768, 6144], P(('node', 'shard')), may hold values from -0.0625 to 0.0625
Outputs:
- mixed: bfloat16 [192, 6144], P(('replica', 'node'), 'shard'), parts along dimension 0
There are 2 independent parts, one for each index of `replica`. A program takes and returns all parts, laid end to end along the dimension named above; an argument that names none is the same for every part. Nothing has to cross between parts.
Inputs may be any that keep to these rules, and one draw needn't show every extreme that they name: `routes`: each row names two different experts; in the 12 rows of one index of node no expert is named more than 9 times, a bound that some block reaches. `cache_lengths`: one request fills all 128 positions.
All inputs are finite; a program needn't handle non-finite values. No bound on the sum of `cache_lengths` on one device may be relied on, other than what follows from the above.
Results may differ from a plain program's by a relative error of at most 0.0049.
Values may be sent and summed in bfloat16 or wider, within the bound.
No kernel may reach another device: no remote copies, remote signals or barrier semaphores. Data moves between devices by JAX's collectives and lax.ppermute only.
A program may use at most 192 MiB of HBM per device.

v0:
```python
import math

import jax
import jax.numpy as jnp
from jax import lax
from jax.sharding import PartitionSpec as P

QUERY_HEADS = 48
KV_HEADS = 8
HEAD_DIM = 128
EXPERTS = 4
CAP = 9


def attend_local(queries, key_cache, value_cache, new_key, new_value, cache_lengths):
    tok_count = queries.shape[0]
    cache_len = key_cache.shape[1]
    kv_local = key_cache.shape[2] // HEAD_DIM
    group_size = QUERY_HEADS // KV_HEADS
    query_rows = queries.reshape(tok_count, kv_local, group_size, HEAD_DIM)
    key_rows = key_cache.reshape(tok_count, cache_len, kv_local, HEAD_DIM)
    value_rows = value_cache.reshape(tok_count, cache_len, kv_local, HEAD_DIM)
    fresh_key = new_key.reshape(tok_count, kv_local, HEAD_DIM)
    fresh_value = new_value.reshape(tok_count, kv_local, HEAD_DIM)
    scaling = 1.0 / math.sqrt(HEAD_DIM)
    cache_scores = (
        jnp.einsum("tgjd,tpgd->tgjp", query_rows, key_rows, preferred_element_type=jnp.float32)
        * scaling
    )
    new_scores = (
        jnp.einsum("tgjd,tgd->tgj", query_rows, fresh_key, preferred_element_type=jnp.float32)
        * scaling
    )
    positions = lax.iota(jnp.int32, cache_len)
    valid = positions[None, :] < cache_lengths[:, None]
    cache_scores = jnp.where(valid[:, None, None, :], cache_scores, jnp.float32(-1e30))
    largest = jnp.maximum(jnp.max(cache_scores, axis=-1), new_scores)
    cache_terms = jnp.exp(cache_scores - largest[..., None])
    new_terms = jnp.exp(new_scores - largest)
    total = jnp.sum(cache_terms, axis=-1) + new_terms
    weighted = jnp.einsum(
        "tgjp,tpgd->tgjd",
        cache_terms.astype(jnp.bfloat16),
        value_rows,
        preferred_element_type=jnp.float32,
    )
    new_probs = lax.optimization_barrier(new_terms.astype(jnp.bfloat16)).astype(jnp.float32)
    weighted = weighted + new_probs[..., None] * fresh_value.astype(jnp.float32)[:, :, None, :]
    return (weighted / total[..., None]).reshape(tok_count, kv_local * group_size * HEAD_DIM)


def on_device(
    residual,
    queries,
    key_cache,
    value_cache,
    new_key,
    new_value,
    cache_lengths,
    norm_gain,
    router,
    routes,
    gate_weight,
    up_weight,
    down_weight,
):
    tok_count = residual.shape[0]
    attention = attend_local(queries, key_cache, value_cache, new_key, new_value, cache_lengths)
    carried_half = residual.astype(jnp.float32) + attention
    carried = lax.all_gather(carried_half, "shard", axis=1, tiled=True)
    mean_square = jnp.mean(carried * carried, axis=-1, keepdims=True)
    normed = (carried * lax.rsqrt(mean_square + 1e-05) * norm_gain).astype(jnp.bfloat16)
    logits = jnp.dot(normed, router, preferred_element_type=jnp.float32)
    pair_logits = jnp.take_along_axis(logits, routes, axis=1)
    first_share = jax.nn.sigmoid(pair_logits[:, 0] - pair_logits[:, 1])
    expert_ids = lax.iota(jnp.int32, EXPERTS)
    member = jnp.any(routes[:, :, None] == expert_ids[None, None, :], axis=1)
    slot_index = jnp.cumsum(member.astype(jnp.int32), axis=0) - 1
    slot_ids = lax.iota(jnp.int32, CAP)
    placed = jnp.logical_and(member[:, :, None], slot_index[:, :, None] == slot_ids[None, None, :])
    packed = jnp.einsum(
        "tec,td->ecd", placed.astype(jnp.bfloat16), normed, preferred_element_type=jnp.float32
    ).astype(jnp.bfloat16)
    group_nodes = lax.axis_size("node") // EXPERTS
    outgoing = jnp.repeat(packed, group_nodes, axis=0)
    incoming = lax.all_to_all(outgoing, "node", split_axis=0, concat_axis=0, tiled=True)
    sources, count, width = incoming.shape
    flat_rows = incoming.reshape(sources * count, width)
    gate_val = jnp.dot(flat_rows, gate_weight, preferred_element_type=jnp.float32)
    up_val = jnp.dot(flat_rows, up_weight, preferred_element_type=jnp.float32)
    hidden = (jax.nn.silu(gate_val) * up_val).astype(jnp.bfloat16)
    partial_out = jnp.dot(hidden, down_weight, preferred_element_type=jnp.float32).reshape(
        sources, count, width
    )
    returned = lax.all_to_all(partial_out, "node", split_axis=0, concat_axis=0, tiled=True)
    summed = returned.reshape(EXPERTS, group_nodes, CAP, returned.shape[2]).sum(axis=1)
    expert_out = lax.psum_scatter(summed, "shard", scatter_dimension=2, tiled=True)
    first_mask = (routes[:, 0, None] == expert_ids[None, :]).astype(jnp.float32)
    second_mask = (routes[:, 1, None] == expert_ids[None, :]).astype(jnp.float32)
    route_share = first_share[:, None] * first_mask + (1.0 - first_share)[:, None] * second_mask
    selection = (placed.astype(jnp.float32) * route_share[:, :, None]).reshape(
        tok_count, EXPERTS * CAP
    )
    moe_rows = jnp.dot(
        selection,
        expert_out.reshape(EXPERTS * CAP, expert_out.shape[2]),
        precision=lax.Precision.HIGHEST,
        preferred_element_type=jnp.float32,
    )
    return (carried_half + moe_rows).astype(jnp.bfloat16)


def solution(mesh):
    placed = (
        P(("replica", "node"), "shard"),
        P(("replica", "node"), "shard"),
        P(("replica", "node"), None, "shard"),
        P(("replica", "node"), None, "shard"),
        P(("replica", "node"), "shard"),
        P(("replica", "node"), "shard"),
        P(("replica", "node")),
        P(),
        P(),
        P(("replica", "node"), None),
        P(None, ("node", "shard")),
        P(None, ("node", "shard")),
        P(("node", "shard"), None),
    )
    return jax.shard_map(
        on_device,
        mesh=mesh,
        in_specs=placed,
        out_specs=P(("replica", "node"), "shard"),
        check_vma=False,
    )
```

profile of v0, /device:TPU:0, one launch (start us, length us, event | category | flops | bytes accessed | tf_op | source)
XLA Modules:
  0.0 187.3 jit_solution(7964782432552363386)
XLA Ops:
  6.5 0.0 copy-start
  6.5 0.0 reduce-scatter.2.cloned.1.call-start
  6.5 0.8 fusion.47
  7.4 0.2 reduce_window_sum.11
  7.6 0.7 iota_compare_fusion.1
  8.3 0.7 reshape.192
  9.1 0.7 reshape.175
  9.8 1.0 reshape.165
  10.8 0.2 fusion.54
  11.0 0.0 copy-done
  11.0 1.0 fusion.53
  12.0 0.3 fusion.29
  12.3 0.0 copy-done.7
  12.3 0.0 copy-start.4
  12.3 0.6 fusion.19
  13.0 0.2 copy-done.4
  13.2 2.2 %all_gather.3 = f32[12,6144]{1,0:T(8,128)S(1)} all-gather(f32[12,3072]{1,0:T(8,128)S(1)} %convert_add_fusion), channel_id=1, replica_groups=mesh['replica'=2,'node'=8,'shard'=2] {'shard'}, dimensions={1}, use_global_device_ids=true | all-gather | bytes 442368 | tf_op jit(solution)/shard_map/all_gather | solution.py:70
  15.4 0.2 multiply_reduce_fusion
  15.6 0.0 copy-done.5
  15.6 0.1 multiply_convert_fusion
  15.7 0.0 copy-start.2
  15.7 0.7 copy-done.2
  16.4 0.5 convolution_convert_fusion
  16.9 0.2 broadcast_in_dim.16
  17.0 44.2 %all_to_all.10 = bf16[8,9,6144]{2,1,0:T(8,128)(2,1)S(1)} all-to-all(bf16[8,9,6144]{2,1,0:T(8,128)(2,1)S(1)} %bitcast.57), channel_id=1, replica_groups=mesh['replica'=2,'node'=8,'shard'=2] {'node'}, dimensions={0} | all-to-all | bytes 1769472 | tf_op jit(solution)/shard_map/all_to_all | solution.py:86
  61.3 0.4 reshape.172
  61.7 10.5 %fusion.56 = f32[72,2048]{1,0:T(8,128)S(1)} fusion(bf16[72,6144]{1,0:T(8,128)(2,1)S(1)} %reshape.172, bf16[6144,2048]{1,0:T(8,128)(2,1)} %param.23), kind=kOutput, calls=%fused_computation.73 | convolution fusion | flops 1811939328 | bytes 26640384 | tf_op jit(solution)/shard_map/dot_general | solution.py:89
  72.2 19.9 %fusion.3 = f32[72,6144]{1,0:T(8,128)S(1)} fusion(bf16[2048,6144]{1,0:T(8,128)(2,1)} %param.25, bf16[72,6144]{1,0:T(8,128)(2,1)S(1)} %reshape.172, bf16[6144,2048]{1,0:T(8,128)(2,1)} %param.24, f32[72,2048]{1,0:T(8,128)S(1)} %fusion.56), kind=kOutput, calls=%fused_computation.8 | convolution fusion | flops 3624763392 | bytes 53575680 | tf_op jit(solution)/shard_map/dot_general | solution.py:92
  92.1 1.9 %reshape.173 = f32[8,9,6144]{2,1,0:T(8,128)} reshape(f32[72,6144]{1,0:T(8,128)S(1)} %fusion.3) | data formatting | bytes 3538944 | tf_op jit(solution)/shard_map/reshape | solution.py:92
  94.0 74.1 %all_to_all.11 = f32[8,9,6144]{2,1,0:T(8,128)S(1)} all-to-all(f32[8,9,6144]{2,1,0:T(8,128)} %reshape.173), channel_id=1, replica_groups=mesh['replica'=2,'node'=8,'shard'=2] {'node'}, dimensions={0} | all-to-all | bytes 3538944 | tf_op jit(solution)/shard_map/all_to_all | solution.py:95
  168.1 1.4 bitcast_reduce_fusion
  169.5 0.0 reduce-scatter.2.cloned.1.call-update
  169.6 0.6 copy-done.6
  170.2 0.1 copy.42
  170.3 0.1 copy.40
  170.4 0.1 copy.41
  170.5 0.1 copy.43
  170.6 0.1 copy.44
  170.7 0.1 reshape.176
  170.8 0.0 copy-done.3
  170.8 0.0 copy-done.8
  170.8 0.2 fusion.55
  171.0 0.9 gather_fusion
  171.9 0.1 reshape.179
  172.0 0.2 fusion.52
  172.2 5.5 %reduce-scatter.2.cloned.1.call-done = f32[4,9,3072]{2,1,0:T(8,128)} async-done(((f32[4,9,6144]{2,1,0:T(8,128)}), f32[4,9,3072]{2,1,0:T(8,128)}) %reduce-scatter.2.cloned.1.call-update) | async-done | bytes 442384 | tf_op jit(solution)/shard_map/reduce_scatter | solution.py:97
  177.7 2.8 %fusion.1 = bf16[12,3072]{1,0:T(8,128)(2,1)} fusion(f32[12,3072]{1,0:T(8,128)S(1)} %convert_add_fusion, f32[4,9,3072]{2,1,0:T(8,128)} %reduce-scatter.2.cloned.1.call-done, f32[12,4]{0,1:T(4,128)S(1)} %select_add_fusion, s32[12,4]{0,1:T(4,128)S(1)} %broadcast_add_fusion, pred[12,4]{0,1:T(4,128)(4,1)S(1)} %fusion.47), kind=kOutput, calls=%fused_computation.4 | convolution fusion | flops 16000272 | bytes 663984 | tf_op jit(solution)/shard_map/dot_general | solution.py:104
  180.5 0.0 copy-done.1
  (21 shorter events, 0.2 us)
Async XLA Ops:
  6.5 4.4 %copy-start = (bf16[12,128,512]{2,1,0:T(8,128)(2,1)S(1)}, bf16[12,128,512]{2,1,0:T(8,128)(2,1)}, u32[]{:S(2)}) copy-start(bf16[12,128,512]{2,1,0:T(8,128)(2,1)} %param.15) | copy-start | bytes 4718596
  6.5 5.8 %copy-start.7 = (bf16[12,128,512]{2,1,0:T(8,128)(2,1)S(1)}, bf16[12,128,512]{2,1,0:T(8,128)(2,1)}, u32[]{:S(2)}) copy-start(bf16[12,128,512]{2,1,0:T(8,128)(2,1)} %param.16) | copy-start | bytes 4718596
  6.5 171.1 %reduce-scatter.2.cloned.1.call-start = ((), (), s32[]{:S(2)}) async-start(), calls=%async_computation.3 | async-start | bytes 2359296 | tf_op jit(solution)/shard_map/reduce_scatter | solution.py:97
  12.3 0.9 copy-start.4
  12.9 2.7 %copy-start.5 = (f32[6144]{0:T(1024)S(1)}, f32[6144]{0:T(1024)}, u32[]{:S(2)}) copy-start(f32[6144]{0:T(1024)} %param.20) | copy-start | bytes 73732
  15.7 0.7 copy-start.2
  169.5 0.7 copy-start.6
  169.5 1.3 copy-start.3
  169.5 1.3 copy-start.8
  171.0 9.5 %copy-start.1 = (bf16[12,128,512]{2,1,0:T(8,128)(2,1)S(1)}, bf16[12,128,512]{2,1,0:T(8,128)(2,1)}, u32[]{:S(2)}) copy-start(bf16[12,128,512]{2,1,0:T(8,128)(2,1)} %param.15) | copy-start | bytes 4718596
Sparse Core Ops, SparseCore 0:
  169.7 7.9 reduce-scatter.1
where the time goes:
time: 188 us; the launch traced here: 187 us
  blocking collectives  121 us (64%)
  matrix products  35.6 us (19%)
  between operations  13.6 us (7%)
  local copies, waits for them, and re-layouts  8.16 us (4%)
  waiting for transfers between devices  5.49 us (3%)
  other arithmetic  4 us (2%)
    all_to_all x1, blocking collectives, on_device(): lax.all_to_all(partial_out, 'node', split_axis=0, concat_axis=0, tiled=True)  74.1 us
    all_to_all x1, blocking collectives, on_device(): lax.all_to_all(outgoing, 'node', split_axis=0, concat_axis=0, tiled=True)  44.2 us
    dot_general x1, matrix products, on_device(): jnp.dot(hidden, down_weight, preferred_element_type=jnp.float32)  19.9 us
    dot_general x1, matrix products, on_device(): jnp.dot(flat_rows, gate_weight, preferred_element_type=jnp.float32)  10.5 us
    reduce_scatter x1, waiting for transfers between devices, on_device(): lax.psum_scatter(summed, 'shard', scatter_dimension=2, tiled=True)  5.48 us
  transfers between devices with their start and end apart: 1, of which 1 were waited for; matrix products, arithmetic and copies ran while one was open for 1% of the time, Pallas kernels for 0%

commit v1 on v0

v1 whole, which is shorter than its diff:
```python
import functools
import math

import jax
import jax.numpy as jnp
from jax import lax
from jax.experimental import pallas as pl
from jax.experimental.pallas import tpu as pltpu
from jax.sharding import PartitionSpec as P

QUERY_HEADS = 48
KV_HEADS = 8
HEAD_DIM = 128
EXPERTS = 4
GROUP = QUERY_HEADS // KV_HEADS
LANES = 128
FOLD = 2
MIB = 1 << 20
F32 = jnp.float32
BF16 = jnp.bfloat16


def whole_spec(array):
    zeros = (0,) * len(array.shape)
    return pl.BlockSpec(array.shape, lambda *_: zeros)


def attend_kernel(
    place_ref, len_ref, q_ref, k_ref, v_ref, nk_ref, nv_ref, res_ref, gain_ref, rt_ref,
    carried_ref, pay_ref, stat_ref,
    q_scr, o_scr, nk_scr, nv_scr, pay_scr,
):
    tok, width = q_ref.shape
    cache_len, kv_width = k_ref.shape[1], k_ref.shape[2]
    heads = width // HEAD_DIM
    groups = kv_width // HEAD_DIM
    fold_width = width // FOLD
    scaling = 1.0 / math.sqrt(HEAD_DIM)
    half = place_ref[0]
    for h in range(heads):
        q_scr[h * tok:(h + 1) * tok, :] = q_ref[:, h * HEAD_DIM:(h + 1) * HEAD_DIM].astype(F32)
    nk_scr[...] = nk_ref[...].astype(F32)
    nv_scr[...] = nv_ref[...].astype(F32)
    row_group = lax.broadcasted_iota(jnp.int32, (heads, HEAD_DIM), 0) // GROUP
    position = lax.broadcasted_iota(jnp.int32, (heads, cache_len), 1)
    scores, fresh = [], []
    for t in range(tok):
        q_rows = q_scr[pl.ds(t, heads, stride=tok), :]
        q_wide = jnp.concatenate(
            [jnp.where(row_group == g, q_rows, 0.0) for g in range(groups)], axis=1
        )
        scores.append(
            lax.dot_general(
                q_wide.astype(BF16), k_ref[t], (((1,), (1,)), ((), ())),
                preferred_element_type=F32,
            ) * scaling
        )
        fresh.append(
            jnp.sum(q_wide * nk_scr[pl.ds(t, 1), :], axis=1, keepdims=True) * scaling
        )
    terms, fresh_terms, totals = [], [], []
    for t in range(tok):
        score = jnp.where(position < len_ref[t], scores[t], -1e30)
        largest = jnp.maximum(jnp.max(score, axis=1, keepdims=True), fresh[t])
        term = jnp.exp(score - largest)
        fresh_term = jnp.exp(fresh[t] - largest)
        totals.append(jnp.sum(term, axis=1, keepdims=True) + fresh_term)
        terms.append(term.astype(BF16))
        fresh_terms.append(fresh_term.astype(BF16).astype(F32))
    for t in range(tok):
        wide = jnp.dot(terms[t], v_ref[t], preferred_element_type=F32)
        wide = wide + fresh_terms[t] * nv_scr[pl.ds(t, 1), :]
        picked = wide[:, :HEAD_DIM]
        for g in range(1, groups):
            picked = jnp.where(
                row_group == g, wide[:, g * HEAD_DIM:(g + 1) * HEAD_DIM], picked
            )
        o_scr[pl.ds(t, heads, stride=tok), :] = picked / totals[t]
    for h in range(heads):
        cols = slice(h * HEAD_DIM, (h + 1) * HEAD_DIM)
        carried_ref[:, cols] = res_ref[:, cols].astype(F32) + o_scr[h * tok:(h + 1) * tok, :]
    carried = carried_ref[...]
    columns = pl.ds(pl.multiple_of(half * width, LANES), width)
    scaled = carried * gain_ref[:, columns]
    squares = jnp.sum(carried * carried, axis=1, keepdims=True)
    rounded = scaled.astype(BF16).astype(F32)
    router = rt_ref[:, columns].astype(F32)
    lane = lax.broadcasted_iota(jnp.int32, (tok, LANES), 1)
    stat = jnp.where(lane == EXPERTS, squares, 0.0)
    for e in range(EXPERTS):
        logit = jnp.sum(rounded * router[e:e + 1, :], axis=1, keepdims=True)
        stat = jnp.where(lane == e, logit, stat)
    stat_ref[...] = stat
    for f in range(FOLD):
        pay_scr[f * tok:(f + 1) * tok, :fold_width] = scaled[:, f * fold_width:(f + 1) * fold_width]
    first = squares.astype(BF16).astype(F32)
    second = (squares - first).astype(BF16).astype(F32)
    third = squares - first - second
    extra = jnp.where(lane == 0, first, jnp.where(lane == 1, second, jnp.where(lane == 2, third, 0.0)))
    for f in range(FOLD):
        pay_scr[f * tok:(f + 1) * tok, fold_width:] = extra
    pay_ref[...] = pay_scr[...].astype(BF16)


def attend(place, lengths, queries, key_cache, value_cache, new_key, new_value, residual, gain, router_t):
    tok, width = queries.shape
    kv_width = new_key.shape[1]
    heads = width // HEAD_DIM
    smem = pl.BlockSpec(memory_space=pltpu.SMEM)
    vmem = pl.BlockSpec(memory_space=pltpu.VMEM)
    return pl.pallas_call(
        attend_kernel,
        out_shape=(
            jax.ShapeDtypeStruct((tok, width), F32),
            jax.ShapeDtypeStruct((FOLD * tok, width // FOLD + LANES), BF16),
            jax.ShapeDtypeStruct((tok, LANES), F32),
        ),
        in_specs=[smem, smem] + [vmem] * 8,
        out_specs=(vmem, vmem, vmem),
        scratch_shapes=[
            pltpu.VMEM((heads * tok, HEAD_DIM), F32),
            pltpu.VMEM((heads * tok, HEAD_DIM), F32),
            pltpu.VMEM((tok, kv_width), F32),
            pltpu.VMEM((tok, kv_width), F32),
            pltpu.VMEM((FOLD * tok, width // FOLD + LANES), F32),
        ],
        compiler_params=pltpu.CompilerParams(vmem_limit_bytes=16 * MIB),
        cost_estimate=pl.CostEstimate(flops=10**8, bytes_accessed=4 * 10**6, transcendentals=10**5),
        name="attend",
    )(place, lengths, queries, key_cache, value_cache, new_key, new_value, residual, gain, router_t)


def unfold_rows(blocks, x_scr, f_scr, k_block):
    tok = blocks[0].shape[0] // FOLD
    fold_width = blocks[0].shape[1] - LANES
    per_fold = fold_width // k_block
    for f in range(FOLD):
        for i, block in enumerate(blocks):
            f_scr[i * tok:(i + 1) * tok, :] = block[:, :fold_width].astype(F32)[f * tok:(f + 1) * tok, :]
        for p in range(per_fold):
            x_scr[f * per_fold + p] = f_scr[:, p * k_block:(p + 1) * k_block].astype(BF16)


def expand_kernel(count, k_block, last, place_ref, *refs):
    blocks = refs[:count]
    step, steps = pl.program_id(0), pl.num_programs(0)
    if not last:
        gate_ref, up_ref, gate_acc, up_acc, x_scr, f_scr = refs[count:]
    else:
        stats = refs[count:2 * count]
        gate_in, up_in, gate_ref, up_ref, hidden_ref, gate_acc, up_acc, x_scr, f_scr = refs[2 * count:]

    @pl.when(step == 0)
    def _():
        unfold_rows(blocks, x_scr, f_scr, k_block)
        if last:
            gate_acc[...] = gate_in[...]
            up_acc[...] = up_in[...]
        else:
            gate_acc[...] = jnp.zeros_like(gate_acc)
            up_acc[...] = jnp.zeros_like(up_acc)

    rows = x_scr[step]
    gate_acc[...] += jnp.dot(rows, gate_ref[...], preferred_element_type=F32)
    up_acc[...] += jnp.dot(rows, up_ref[...], preferred_element_type=F32)
    if last:
        @pl.when(step == steps - 1)
        def _():
            tok = blocks[0].shape[0] // FOLD
            fold_width = blocks[0].shape[1] - LANES
            for i in range(count):
                both = stats[i][...].astype(F32) + 0.0
                mine = blocks[i][:, fold_width:].astype(F32)
                total = jnp.sum(both, axis=1, keepdims=True) + jnp.sum(mine, axis=1, keepdims=True)
                f_scr[i * tok:(i + 1) * tok, :LANES] = jnp.broadcast_to(total[:tok], (tok, LANES))
            features = 2 * FOLD * fold_width
            scale = lax.rsqrt(f_scr[:, 0:1] * (1.0 / features) + 1e-05)
            gate = gate_acc[...] * scale
            up = up_acc[...] * scale
            hidden_ref[...] = (gate / (1.0 + jnp.exp(-gate)) * up).astype(BF16)


def expand(place, blocks, gate_weight, up_weight, own=None, stat_blocks=()):
    last = own is not None
    count = len(blocks)
    tok = blocks[0].shape[0] // FOLD
    fold_width = blocks[0].shape[1] - LANES
    width = FOLD * fold_width
    hidden = gate_weight.shape[1]
    rows = count * tok
    k_block = math.gcd(512, fold_width)
    steps = width // k_block
    weight_spec = pl.BlockSpec(
        (k_block, hidden),
        (lambda k, place: ((1 - place[0]) * steps + k, 0)) if last
        else (lambda k, place: (place[0] * steps + k, 0)),
    )
    acc = jax.ShapeDtypeStruct((rows, hidden), F32)
    in_specs = [whole_spec(b) for b in blocks]
    operands = list(blocks)
    scratch = [pltpu.VMEM((steps, rows, k_block), BF16), pltpu.VMEM((rows, fold_width), F32)]
    if last:
        tail = fold_width // LANES
        in_specs += [pl.BlockSpec((FOLD * tok, LANES), lambda k, place: (0, tail))] * count
        operands += list(stat_blocks)
        in_specs += [whole_spec(acc)] * 2
        operands += list(own)
        out_shape = jax.ShapeDtypeStruct((rows, hidden), BF16)
        out_specs = whole_spec(out_shape)
        scratch = [pltpu.VMEM((rows, hidden), F32)] * 2 + scratch
    else:
        out_shape = (acc, acc)
        out_specs = (whole_spec(acc), whole_spec(acc))
    return pl.pallas_call(
        functools.partial(expand_kernel, count, k_block, last),
        out_shape=out_shape,
        grid_spec=pltpu.PrefetchScalarGridSpec(
            num_scalar_prefetch=1,
            grid=(steps,),
            in_specs=in_specs + [weight_spec, weight_spec],
            out_specs=out_specs,
            scratch_shapes=scratch,
        ),
        compiler_params=pltpu.CompilerParams(vmem_limit_bytes=40 * MIB),
        cost_estimate=pl.CostEstimate(
            flops=4 * rows * width * hidden, bytes_accessed=4 * width * hidden, transcendentals=0
        ),
        name="expand_last" if last else "expand_first",
    )(place, *operands, gate_weight, up_weight)


def contract_kernel(place_ref, hidden_ref, down_ref, out_ref):
    out_ref[...] = jnp.dot(
        hidden_ref[...], down_ref[...], preferred_element_type=F32
    ).astype(out_ref.dtype)


def contract(place, hidden, down_weight, other, out_type):
    rows, units = hidden.shape
    width = down_weight.shape[1] // 2
    n_block = 512
    steps = width // n_block

    def weight_at(n, place):
        side = 1 - place[0] if other else place[0]
        return (0, side * steps + n)

    return pl.pallas_call(
        contract_kernel,
        out_shape=jax.ShapeDtypeStruct((rows, width), out_type),
        grid_spec=pltpu.PrefetchScalarGridSpec(
            num_scalar_prefetch=1,
            grid=(steps,),
            in_specs=[whole_spec(hidden), pl.BlockSpec((units, n_block), weight_at)],
            out_specs=pl.BlockSpec((rows, n_block), lambda n, place: (0, n)),
        ),
        compiler_params=pltpu.CompilerParams(vmem_limit_bytes=40 * MIB),
        cost_estimate=pl.CostEstimate(
            flops=2 * rows * width * units, bytes_accessed=2 * width * units, transcendentals=0
        ),
        name="contract_other" if other else "contract_own",
    )(place, hidden, down_weight)


def split_kernel(own_ref, got_ref, keep_ref, *send_refs):
    size = keep_ref.shape[0]
    keep_ref[...] = own_ref[:size, :] + got_ref[:size, :].astype(F32)
    for u, send in enumerate(send_refs, 1):
        at = slice(u * size, (u + 1) * size)
        send[...] = (own_ref[at, :] + got_ref[at, :].astype(F32)).astype(BF16)


def split_rows(own, got, parts):
    rows, width = own.shape
    size = rows // parts
    vmem = pl.BlockSpec(memory_space=pltpu.VMEM)
    return pl.pallas_call(
        split_kernel,
        out_shape=(jax.ShapeDtypeStruct((size, width), F32),)
        + (jax.ShapeDtypeStruct((size, width), BF16),) * (parts - 1),
        in_specs=[vmem, vmem],
        out_specs=(vmem,) * parts,
        compiler_params=pltpu.CompilerParams(vmem_limit_bytes=40 * MIB),
        name="split_rows",
    )(own, got)


def planes_kernel(count, own_ref, *refs):
    got, keep_ref, sends, total, folded = (
        refs[:count], refs[count], refs[count + 1:-2], refs[-2], refs[-1]
    )
    value = own_ref[...]
    for ref in got:
        value = value + ref[...].astype(F32)
    total[...] = value
    tok = keep_ref.shape[0]
    fold_width = keep_ref.shape[1] // FOLD
    keep_ref[...] = total[:tok, :]
    for s, send in enumerate(sends, 1):
        for f in range(FOLD):
            folded[f * tok:(f + 1) * tok, :] = total[
                s * tok:(s + 1) * tok, f * fold_width:(f + 1) * fold_width
            ]
        send[...] = folded[...].astype(BF16)


def split_planes(own, got):
    rows, width = own.shape
    tok = rows // EXPERTS
    vmem = pl.BlockSpec(memory_space=pltpu.VMEM)
    return pl.pallas_call(
        functools.partial(planes_kernel, len(got)),
        out_shape=(jax.ShapeDtypeStruct((tok, width), F32),)
        + (jax.ShapeDtypeStruct((FOLD * tok, width // FOLD), BF16),) * (EXPERTS - 1),
        in_specs=[vmem] * (1 + len(got)),
        out_specs=(vmem,) * EXPERTS,
        scratch_shapes=[
            pltpu.VMEM((rows, width), F32),
            pltpu.VMEM((FOLD * tok, width // FOLD), F32),
        ],
        compiler_params=pltpu.CompilerParams(vmem_limit_bytes=40 * MIB),
        name="split_planes",
    )(own, *got)


def finish_kernel(place_ref, carried_ref, routes_ref, stat_ref, stat_got_ref, own_ref, *refs):
    got, out_ref, folded = refs[:-2], refs[-2], refs[-1]
    tok, width = carried_ref.shape
    fold_width = width // FOLD
    stat = stat_ref[...] + stat_got_ref[...]
    lane = lax.broadcasted_iota(jnp.int32, stat.shape, 1)
    scale = lax.rsqrt(stat[:, EXPERTS:EXPERTS + 1] * (1.0 / (2 * width)) + 1e-05)
    first, second = routes_ref[:, 0:1], routes_ref[:, 1:2]
    gap = (
        jnp.sum(jnp.where(lane == second, stat, 0.0), axis=1, keepdims=True)
        - jnp.sum(jnp.where(lane == first, stat, 0.0), axis=1, keepdims=True)
    ) * scale
    share = 1.0 / (1.0 + jnp.exp(gap))

    def weight(s):
        expert = lax.rem(place_ref[1] + s, EXPERTS)
        return jnp.where(first == expert, share, 0.0) + jnp.where(second == expert, 1.0 - share, 0.0)

    for f in range(FOLD):
        at = slice(f * fold_width, (f + 1) * fold_width)
        value = carried_ref[:, at] + weight(0) * own_ref[:, at]
        for s, ref in enumerate(got, 1):
            folded[...] = ref[...].astype(F32)
            value = value + weight(s) * folded[f * tok:(f + 1) * tok, :]
        out_ref[:, at] = value.astype(BF16)


def finish(place, carried, routes, stat, stat_got, own, got):
    tok, width = carried.shape
    smem = pl.BlockSpec(memory_space=pltpu.SMEM)
    vmem = pl.BlockSpec(memory_space=pltpu.VMEM)
    return pl.pallas_call(
        finish_kernel,
        out_shape=jax.ShapeDtypeStruct((tok, width), BF16),
        in_specs=[smem] + [vmem] * (5 + len(got)),
        out_specs=vmem,
        scratch_shapes=[pltpu.VMEM((FOLD * tok, width // FOLD), F32)],
        compiler_params=pltpu.CompilerParams(vmem_limit_bytes=16 * MIB),
        name="finish",
    )(place, carried, routes, stat, stat_got, own, *got)


def on_device(
    residual, queries, key_cache, value_cache, new_key, new_value, cache_lengths,
    norm_gain, router, routes, gate_weight, up_weight, down_weight,
):
    nodes = lax.axis_size("node")
    per_plane = nodes // EXPERTS
    place = jnp.stack(
        [lax.axis_index("shard"), lax.axis_index("node") // per_plane]
    ).astype(jnp.int32)

    def to_plane(array, s):
        perm = [
            (e * per_plane + j, (e + s) % EXPERTS * per_plane + j)
            for e in range(EXPERTS) for j in range(per_plane)
        ]
        return lax.ppermute(array, "node", perm)

    def to_column(array, u):
        perm = [
            (e * per_plane + j, e * per_plane + (j + u) % per_plane)
            for e in range(EXPERTS) for j in range(per_plane)
        ]
        return lax.ppermute(array, "node", perm)

    def to_core(array):
        return lax.ppermute(array, "shard", [(0, 1), (1, 0)])

    carried, payload, stat = attend(
        place, cache_lengths, queries, key_cache, value_cache, new_key, new_value,
        residual, norm_gain.reshape(1, -1), router.T,
    )
    in_column = [payload] + [to_plane(payload, s) for s in range(1, EXPERTS)]
    blocks = list(in_column)
    for u in range(1, per_plane):
        blocks += [to_column(block, u) for block in in_column]
    other_blocks = [to_core(block) for block in blocks]
    stat_got = to_core(stat)
    sums = expand(place, blocks, gate_weight, up_weight)
    hidden = expand(place, other_blocks, gate_weight, up_weight, sums, blocks)
    leaving = contract(place, hidden, down_weight, True, BF16)
    arrived = to_core(leaving)
    staying = contract(place, hidden, down_weight, False, F32)
    parts = split_rows(staying, arrived, per_plane)
    got = [to_column(parts[u], -u) for u in range(1, per_plane)]
    planes = split_planes(parts[0], got)
    returned = [to_plane(planes[s], -s) for s in range(1, EXPERTS)]
    return finish(place, carried, routes, stat, stat_got, planes[0], returned)


def solution(mesh):
    rows = ("replica", "node")
    in_specs = (
        P(rows, "shard"),
        P(rows, "shard"),
        P(rows, None, "shard"),
        P(rows, None, "shard"),
        P(rows, "shard"),
        P(rows, "shard"),
        P(rows),
        P(),
        P(),
        P(rows, None),
        P(None, ("node", "shard")),
        P(None, ("node", "shard")),
        P(("node", "shard"), None),
    )
    return jax.shard_map(
        on_device,
        mesh=mesh,
        in_specs=in_specs,
        out_specs=P(rows, "shard"),
        check_vma=False,
    )
```

time: 188 us -> 88.7 us (0.47)
  blocking collectives: 121 us -> 0 us
  Pallas kernels: 0 us -> 42.7 us
  matrix products: 35.6 us -> 0 us
  starting transfers between devices: 0.01 us -> 19.1 us
  between operations: 13.6 us -> 0.13 us
  waiting for transfers between devices: 5.49 us -> 17.8 us
  other arithmetic: 4 us -> 0.07 us
    all_to_all x2 -> x0, blocking collectives: 118 us -> none  [the longest x1 74.1 us: on_device(): lax.all_to_all(partial_out, 'node', split_axis=0, concat_axis=0, tiled=True)]
    pallas_call x0 -> x8, Pallas kernels: none -> 42.7 us  [the longest x2 23.7 us: expand(): pl.pallas_call(functools.partial(expand_kernel, count, k_block, last), ou...]
    dot_general x8 -> x0, matrix products: 35.6 us -> none  [the longest x1 19.9 us: on_device(): jnp.dot(hidden, down_weight, preferred_element_type=jnp.float32)]
    ppermute x0 -> x21, starting transfers between devices: none -> 19.1 us  [the longest x6 11.4 us: to_plane(): return lax.ppermute(array, 'node', perm)]
    ppermute x0 -> x21, waiting for transfers between devices: none -> 17.8 us  [the longest x5 11.3 us: to_column(): return lax.ppermute(array, 'node', perm)]
    unnamed x19 -> x21, local copies, waits for them, and re-layouts: 1.7 us -> 8.32 us
    reduce_scatter x1 -> x0, waiting for transfers between devices: 5.48 us -> none  [on_device(): lax.psum_scatter(summed, 'shard', scatter_dimension=2, tiled=True)]
    reshape x5 -> x0, local copies, waits for them, and re-layouts: 4.14 us -> none  [the longest x1 1.95 us: on_device(): jnp.dot(hidden, down_weight, preferred_element_type=jnp.float32)]
  transfers between devices with their start and end apart: 1 -> 21, of which waited for: 1 -> 7; matrix products, arithmetic and copies ran while one was open for 1% -> 0% of each run, Pallas kernels for 0% -> 22%
where the time goes in v1:
time: 88.7 us; the launch traced here: 88.2 us
  Pallas kernels  42.7 us (48%)
  starting transfers between devices  19.1 us (22%)
  waiting for transfers between devices  17.8 us (20%)
  local copies, waits for them, and re-layouts  8.32 us (9%)
    pallas_call x2, Pallas kernels, expand(): pl.pallas_call(functools.partial(expand_kernel, count, k_block, last), ou...  23.7 us
    pallas_call x2, Pallas kernels, contract(): pl.pallas_call(contract_kernel, out_shape=jax.ShapeDtypeStruct((rows, wid...  15.5 us
    ppermute x6, starting transfers between devices, to_plane(): return lax.ppermute(array, 'node', perm)  11.4 us
    ppermute x5, waiting for transfers between devices, to_column(): return lax.ppermute(array, 'node', perm)  11.3 us
    unnamed x21, local copies, waits for them, and re-layouts  8.32 us
    ppermute x5, starting transfers between devices, to_column(): return lax.ppermute(array, 'node', perm)  6.04 us
    ppermute x6, waiting for transfers between devices, to_plane(): return lax.ppermute(array, 'node', perm)  5.42 us
  transfers between devices with their start and end apart: 21, of which 7 were waited for; matrix products, arithmetic and copies ran while one was open for 0% of the time, Pallas kernels for 22%

profile of v1, /device:TPU:0, one launch (start us, length us, event | category | flops | bytes accessed | tf_op | source)
XLA Modules:
  0.0 88.2 jit_solution(7885879317205436904)
XLA Ops:
  0.0 0.1 pad_add_fusion.place_ref
  0.1 1.4 %copy-done = bf16[12,128,512]{2,1,0:T(8,128)(2,1)S(1)} copy-done((bf16[12,128,512]{2,1,0:T(8,128)(2,1)S(1)}, bf16[12,128,512]{2,1,0:T(8,128)(2,1)}, u32[]{:S(2)}) %copy-start) | copy-done | bytes 1572888
  1.5 1.4 %copy-done.1 = bf16[12,128,512]{2,1,0:T(8,128)(2,1)S(1)} copy-done((bf16[12,128,512]{2,1,0:T(8,128)(2,1)S(1)}, bf16[12,128,512]{2,1,0:T(8,128)(2,1)}, u32[]{:S(2)}) %copy-start.1) | copy-done | bytes 1572888
  2.9 0.9 %copy-done.2 = bf16[12,3072]{1,0:T(8,128)(2,1)S(1)} copy-done((bf16[12,3072]{1,0:T(8,128)(2,1)S(1)}, bf16[12,3072]{1,0:T(8,128)(2,1)}, u32[]{:S(2)}) %copy-start.2) | copy-done | bytes 73752
  3.8 0.9 %copy-done.3 = bf16[12,3072]{1,0:T(8,128)(2,1)S(1)} copy-done((bf16[12,3072]{1,0:T(8,128)(2,1)S(1)}, bf16[12,3072]{1,0:T(8,128)(2,1)}, u32[]{:S(2)}) %copy-start.3) | copy-done | bytes 73752
  4.7 0.8 copy-done.4
  5.5 0.7 copy-done.5
  6.2 0.7 copy-done.6
  6.9 0.7 copy-done.7
  7.7 0.7 copy-done.8
  8.3 1.6 %attend.1 = (f32[12,3072]{1,0:T(8,128)S(1)}, bf16[24,1664]{1,0:T(8,128)(2,1)S(1)}, f32[12,128]{1,0:T(8,128)S(1)}) custom-call(s32[2]{0:T(128)S(1)} %pad_add_fusion.place_ref, s32[12]{0:T(128)S(1)} %copy-done.8, bf16[12,3072]{1,0:T(8,128)(2,1)S(1)} %copy-done.2, bf16[12,128,512]{2,1,0:T(8,128)(2,1)S(1)} %copy-done, bf16[12,128,512]{2,1,0:T(8,128)(2,1)S(1)} %copy-done.1, ...), custom_call_target="tpu_custom_call" | custom-call | flops 100000000 | bytes 4000000 | tf_op jit(solution)/shard_map/attend/pallas_call | solution.py:111
  9.9 3.0 %collective-permute-start.2 = (bf16[24,1664]{1,0:T(8,128)(2,1)S(1)}, bf16[24,1664]{1,0:T(8,128)(2,1)S(1)}, u32[]{:S(2)}, u32[]{:S(2)}) collective-permute-start(bf16[24,1664]{1,0:T(8,128)(2,1)S(1)} %get-tuple-element.18.refs_0_.refs_8_), channel_id=1, source_target_pairs={{0,4},{2,6},{4,8},{6,10},{8,12},{10,14},{12,0},{14,2},{1,5},{3,7},... | collective-permute-start | bytes 239624 | tf_op jit(solution)/shard_map/ppermute | solution.py:383
  13.0 2.6 %collective-permute-start.4 = (bf16[24,1664]{1,0:T(8,128)(2,1)S(1)}, bf16[24,1664]{1,0:T(8,128)(2,1)S(1)}, u32[]{:S(2)}, u32[]{:S(2)}) collective-permute-start(bf16[24,1664]{1,0:T(8,128)(2,1)S(1)} %get-tuple-element.18.refs_0_.refs_8_), channel_id=1, source_target_pairs={{0,8},{2,10},{4,12},{6,14},{8,0},{10,2},{12,4},{14,6},{1,9},{3,11}... | collective-permute-start | bytes 239624 | tf_op jit(solution)/shard_map/ppermute | solution.py:383
  15.6 1.3 %collective-permute-start.6 = (bf16[24,1664]{1,0:T(8,128)(2,1)S(1)}, bf16[24,1664]{1,0:T(8,128)(2,1)S(1)}, u32[]{:S(2)}, u32[]{:S(2)}) collective-permute-start(bf16[24,1664]{1,0:T(8,128)(2,1)S(1)} %get-tuple-element.18.refs_0_.refs_8_), channel_id=1, source_target_pairs={{0,12},{2,14},{4,0},{6,2},{8,4},{10,6},{12,8},{14,10},{1,13},{3,15... | collective-permute-start | bytes 239624 | tf_op jit(solution)/shard_map/ppermute | solution.py:383
  16.9 1.5 %collective-permute-start.8 = (bf16[24,1664]{1,0:T(8,128)(2,1)S(1)}, bf16[24,1664]{1,0:T(8,128)(2,1)S(1)}, u32[]{:S(2)}, u32[]{:S(2)}) collective-permute-start(bf16[24,1664]{1,0:T(8,128)(2,1)S(1)} %get-tuple-element.18.refs_0_.refs_8_), channel_id=1, source_target_pairs={{0,2},{2,0},{4,6},{6,4},{8,10},{10,8},{12,14},{14,12},{1,3},{3,1},... | collective-permute-start | bytes 239624 | tf_op jit(solution)/shard_map/ppermute | solution.py:390
  18.4 1.3 %collective-permute-start.10 = (bf16[24,1664]{1,0:T(8,128)(2,1)S(1)}, bf16[24,1664]{1,0:T(8,128)(2,1)S(1)}, u32[]{:S(2)}, u32[]{:S(2)}) collective-permute-start(bf16[24,1664]{1,0:T(8,128)(2,1)S(1)} %collective-permute-done.2.refs_1_.refs_9_), channel_id=1, source_target_pairs={{0,2},{2,0},{4,6},{6,4},{8,10},{10,8},{12,14},{14,12},{1,3},{3,1},... | collective-permute-start | bytes 239624 | tf_op jit(solution)/shard_map/ppermute | solution.py:390
  19.7 1.2 %collective-permute-done.4.refs_2_.refs_10_ = bf16[24,1664]{1,0:T(8,128)(2,1)S(1)} collective-permute-done((bf16[24,1664]{1,0:T(8,128)(2,1)S(1)}, bf16[24,1664]{1,0:T(8,128)(2,1)S(1)}, u32[]{:S(2)}, u32[]{:S(2)}) %collective-permute-start.4) | collective-permute-done | bytes 79904 | tf_op jit(solution)/shard_map/ppermute | solution.py:383
  20.9 1.6 %collective-permute-start.12 = (bf16[24,1664]{1,0:T(8,128)(2,1)S(1)}, bf16[24,1664]{1,0:T(8,128)(2,1)S(1)}, u32[]{:S(2)}, u32[]{:S(2)}) collective-permute-start(bf16[24,1664]{1,0:T(8,128)(2,1)S(1)} %collective-permute-done.4.refs_2_.refs_10_), channel_id=1, source_target_pairs={{0,2},{2,0},{4,6},{6,4},{8,10},{10,8},{12,14},{14,12},{1,3},{3,1},... | collective-permute-start | bytes 239624 | tf_op jit(solution)/shard_map/ppermute | solution.py:390
  22.5 0.0 collective-permute-done.6.refs_3_.refs_11_
  22.5 0.4 collective-permute-start.14
  23.0 0.0 collective-permute-done.1.refs_0_
  23.0 0.5 collective-permute-start.5
  23.5 0.1 collective-permute-start.7
  23.5 2.6 %collective-permute-done.12.refs_6_.refs_14_ = bf16[24,1664]{1,0:T(8,128)(2,1)S(1)} collective-permute-done((bf16[24,1664]{1,0:T(8,128)(2,1)S(1)}, bf16[24,1664]{1,0:T(8,128)(2,1)S(1)}, u32[]{:S(2)}, u32[]{:S(2)}) %collective-permute-start.12) | collective-permute-done | bytes 79904 | tf_op jit(solution)/shard_map/ppermute | solution.py:390
  26.2 0.0 collective-permute-start.9
  26.2 0.9 %collective-permute-done.14.refs_7_.refs_15_ = bf16[24,1664]{1,0:T(8,128)(2,1)S(1)} collective-permute-done((bf16[24,1664]{1,0:T(8,128)(2,1)S(1)}, bf16[24,1664]{1,0:T(8,128)(2,1)S(1)}, u32[]{:S(2)}, u32[]{:S(2)}) %collective-permute-start.14) | collective-permute-done | bytes 79904 | tf_op jit(solution)/shard_map/ppermute | solution.py:390
  27.1 0.0 collective-permute-start.11
  27.1 0.0 collective-permute-done.3.refs_1_
  27.1 0.5 collective-permute-start.13
  27.6 0.0 collective-permute-done.5.refs_2_
  27.6 0.1 collective-permute-start.15
  27.6 11.6 %expand_first.1 = (f32[96,2048]{1,0:T(8,128)S(1)}, f32[96,2048]{1,0:T(8,128)S(1)}) custom-call(s32[2]{0:T(128)S(1)} %pad_add_fusion.place_ref, bf16[24,1664]{1,0:T(8,128)(2,1)S(1)} %get-tuple-element.18.refs_0_.refs_8_, bf16[24,1664]{1,0:T(8,128)(2,1)S(1)} %collective-permute-done.2.refs_1_.refs_9_, ...), custom_call_target="tpu_custom_call" | custom-call | flops 2415919104 | bytes 25165824 | tf_op jit(solution)/shard_map/expand_first/pallas_call | solution.py:214
  39.3 12.1 %expand_last.1.hidden_ref = bf16[96,2048]{1,0:T(8,128)(2,1)S(1)} custom-call(s32[2]{0:T(128)S(1)} %pad_add_fusion.place_ref, bf16[24,1664]{1,0:T(8,128)(2,1)S(1)} %collective-permute-done.1.refs_0_, bf16[24,1664]{1,0:T(8,128)(2,1)S(1)} %collective-permute-done.3.refs_1_, bf16[24,1664]{1,0:T(8,128)(2,1)S(1)} %collective-permute-done.5.refs_2_, ...), custom_call_target="tpu_custom_call" | custom-call | flops 2415919104 | bytes 25165824 | tf_op jit(solution)/shard_map/expand_last/pallas_call | solution.py:214
  51.4 0.0 copy-start.9
  51.4 7.7 %contract_other.1 = bf16[96,3072]{1,0:T(8,128)(2,1)S(1)} custom-call(s32[2]{0:T(128)S(1)} %pad_add_fusion.place_ref, bf16[96,2048]{1,0:T(8,128)(2,1)S(1)} %expand_last.1.hidden_ref, bf16[2048,6144]{1,0:T(8,128)(2,1)} %down_ref.3), custom_call_target="tpu_custom_call" | custom-call | flops 1207959552 | bytes 12582912 | tf_op jit(solution)/shard_map/contract_other/pallas_call | solution.py:248
  59.2 0.5 collective-permute-start.16
  59.7 7.7 %contract_own.1.own_ref = f32[96,3072]{1,0:T(8,128)S(1)} custom-call(s32[2]{0:T(128)S(1)} %pad_add_fusion.place_ref, bf16[96,2048]{1,0:T(8,128)(2,1)S(1)} %expand_last.1.hidden_ref, bf16[2048,6144]{1,0:T(8,128)(2,1)} %down_ref.3), custom_call_target="tpu_custom_call" | custom-call | flops 1207959552 | bytes 12582912 | tf_op jit(solution)/shard_map/contract_own/pallas_call | solution.py:248
  67.5 0.1 split_rows.1
  67.6 1.2 %collective-permute-start.17 = (bf16[48,3072]{1,0:T(8,128)(2,1)S(1)}, bf16[48,3072]{1,0:T(8,128)(2,1)S(1)}, u32[]{:S(2)}, u32[]{:S(2)}) collective-permute-start(bf16[48,3072]{1,0:T(8,128)(2,1)S(1)} %get-tuple-element.22), channel_id=1, source_target_pairs={{0,2},{2,0},{4,6},{6,4},{8,10},{10,8},{12,14},{14,12},{1,3},{3,1},... | collective-permute-start | bytes 884744 | tf_op jit(solution)/shard_map/ppermute | solution.py:390
  68.8 7.8 %collective-permute-done.17.refs_0_ = bf16[48,3072]{1,0:T(8,128)(2,1)S(1)} collective-permute-done((bf16[48,3072]{1,0:T(8,128)(2,1)S(1)}, bf16[48,3072]{1,0:T(8,128)(2,1)S(1)}, u32[]{:S(2)}, u32[]{:S(2)}) %collective-permute-start.17) | collective-permute-done | bytes 294944 | tf_op jit(solution)/shard_map/ppermute | solution.py:390
  76.6 0.1 split_planes.1
  76.8 3.3 %collective-permute-start.18 = (bf16[24,1536]{1,0:T(8,128)(2,1)S(1)}, bf16[24,1536]{1,0:T(8,128)(2,1)S(1)}, u32[]{:S(2)}, u32[]{:S(2)}) collective-permute-start(bf16[24,1536]{1,0:T(8,128)(2,1)S(1)} %get-tuple-element.24), channel_id=1, source_target_pairs={{0,12},{2,14},{4,0},{6,2},{8,4},{10,6},{12,8},{14,10},{1,13},{3,15... | collective-permute-start | bytes 221192 | tf_op jit(solution)/shard_map/ppermute | solution.py:383
  80.1 1.1 %collective-permute-start.20 = (bf16[24,1536]{1,0:T(8,128)(2,1)S(1)}, bf16[24,1536]{1,0:T(8,128)(2,1)S(1)}, u32[]{:S(2)}, u32[]{:S(2)}) collective-permute-start(bf16[24,1536]{1,0:T(8,128)(2,1)S(1)} %get-tuple-element.26), channel_id=1, source_target_pairs={{0,4},{2,6},{4,8},{6,10},{8,12},{10,14},{12,0},{14,2},{1,5},{3,7},... | collective-permute-start | bytes 221192 | tf_op jit(solution)/shard_map/ppermute | solution.py:383
  81.2 0.1 copy.14.routes_ref
  81.3 1.1 %collective-permute-done.stat_got_ref = f32[12,128]{1,0:T(8,128)S(1)} collective-permute-done((f32[12,128]{1,0:T(8,128)S(1)}, f32[12,128]{1,0:T(8,128)S(1)}, u32[]{:S(2)}, u32[]{:S(2)}) %collective-permute-start) | collective-permute-done | bytes 6176 | tf_op jit(solution)/shard_map/ppermute | solution.py:393
  82.4 0.2 collective-permute-done.18.refs_0_
  82.6 3.9 %collective-permute-done.19.refs_1_ = bf16[24,1536]{1,0:T(8,128)(2,1)S(1)} collective-permute-done((bf16[24,1536]{1,0:T(8,128)(2,1)S(1)}, bf16[24,1536]{1,0:T(8,128)(2,1)S(1)}, u32[]{:S(2)}, u32[]{:S(2)}) %collective-permute-start.19) | collective-permute-done | bytes 73760 | tf_op jit(solution)/shard_map/ppermute | solution.py:383
  86.6 1.6 %finish.1 = bf16[12,3072]{1,0:T(8,128)(2,1)} custom-call(s32[2]{0:T(128)S(1)} %pad_add_fusion.place_ref, f32[12,3072]{1,0:T(8,128)S(1)} %get-tuple-element.16.carried_ref, s32[12,2]{1,0:T(8,128)S(1)} %copy.14.routes_ref, f32[12,128]{1,0:T(8,128)S(1)} %get-tuple-element.17.stat_ref, f32[12,128]{1,0:T(8,128)S(1)} %collective-permute-done.stat_got_ref, ...), custom_call_target="tpu_custom_call" | custom-call | tf_op jit(solution)/shard_map/finish/pallas_call | solution.py:357
  (24 shorter events, 0.1 us)
Async XLA Ops:
  0.1 1.4 %copy-start = (bf16[12,128,512]{2,1,0:T(8,128)(2,1)S(1)}, bf16[12,128,512]{2,1,0:T(8,128)(2,1)}, u32[]{:S(2)}) copy-start(bf16[12,128,512]{2,1,0:T(8,128)(2,1)} %k_ref.1) | copy-start | bytes 4718596
  1.5 1.4 %copy-start.1 = (bf16[12,128,512]{2,1,0:T(8,128)(2,1)S(1)}, bf16[12,128,512]{2,1,0:T(8,128)(2,1)}, u32[]{:S(2)}) copy-start(bf16[12,128,512]{2,1,0:T(8,128)(2,1)} %v_ref.1) | copy-start | bytes 4718596
  2.9 0.9 %copy-start.2 = (bf16[12,3072]{1,0:T(8,128)(2,1)S(1)}, bf16[12,3072]{1,0:T(8,128)(2,1)}, u32[]{:S(2)}) copy-start(bf16[12,3072]{1,0:T(8,128)(2,1)} %q_ref.1) | copy-start | bytes 221188
  3.8 0.9 %copy-start.3 = (bf16[12,3072]{1,0:T(8,128)(2,1)S(1)}, bf16[12,3072]{1,0:T(8,128)(2,1)}, u32[]{:S(2)}) copy-start(bf16[12,3072]{1,0:T(8,128)(2,1)} %res_ref.1) | copy-start | bytes 221188
  4.7 0.8 copy-start.4
  5.5 0.7 copy-start.5
  6.2 0.7 copy-start.6
  6.9 0.7 copy-start.7
  7.7 0.7 copy-start.8
  9.9 8.5 %collective-permute-start.2 = (bf16[24,1664]{1,0:T(8,128)(2,1)S(1)}, bf16[24,1664]{1,0:T(8,128)(2,1)S(1)}, u32[]{:S(2)}, u32[]{:S(2)}) collective-permute-start(bf16[24,1664]{1,0:T(8,128)(2,1)S(1)} %get-tuple-element.18.refs_0_.refs_8_), channel_id=1, source_target_pairs={{0,4},{2,6},{4,8},{6,10},{8,12},{10,14},{12,0},{14,2},{1,5},{3,7},... | collective-permute-start | bytes 239624 | tf_op jit(solution)/shard_map/ppermute | solution.py:383
  13.0 7.9 %collective-permute-start.4 = (bf16[24,1664]{1,0:T(8,128)(2,1)S(1)}, bf16[24,1664]{1,0:T(8,128)(2,1)S(1)}, u32[]{:S(2)}, u32[]{:S(2)}) collective-permute-start(bf16[24,1664]{1,0:T(8,128)(2,1)S(1)} %get-tuple-element.18.refs_0_.refs_8_), channel_id=1, source_target_pairs={{0,8},{2,10},{4,12},{6,14},{8,0},{10,2},{12,4},{14,6},{1,9},{3,11}... | collective-permute-start | bytes 239624 | tf_op jit(solution)/shard_map/ppermute | solution.py:383
  15.6 7.0 %collective-permute-start.6 = (bf16[24,1664]{1,0:T(8,128)(2,1)S(1)}, bf16[24,1664]{1,0:T(8,128)(2,1)S(1)}, u32[]{:S(2)}, u32[]{:S(2)}) collective-permute-start(bf16[24,1664]{1,0:T(8,128)(2,1)S(1)} %get-tuple-element.18.refs_0_.refs_8_), channel_id=1, source_target_pairs={{0,12},{2,14},{4,0},{6,2},{8,4},{10,6},{12,8},{14,10},{1,13},{3,15... | collective-permute-start | bytes 239624 | tf_op jit(solution)/shard_map/ppermute | solution.py:383
  16.9 6.0 %collective-permute-start.8 = (bf16[24,1664]{1,0:T(8,128)(2,1)S(1)}, bf16[24,1664]{1,0:T(8,128)(2,1)S(1)}, u32[]{:S(2)}, u32[]{:S(2)}) collective-permute-start(bf16[24,1664]{1,0:T(8,128)(2,1)S(1)} %get-tuple-element.18.refs_0_.refs_8_), channel_id=1, source_target_pairs={{0,2},{2,0},{4,6},{6,4},{8,10},{10,8},{12,14},{14,12},{1,3},{3,1},... | collective-permute-start | bytes 239624 | tf_op jit(solution)/shard_map/ppermute | solution.py:390
  18.4 4.6 %collective-permute-start.1 = (bf16[24,1664]{1,0:T(8,128)(2,1)S(1)}, bf16[24,1664]{1,0:T(8,128)(2,1)S(1)}, u32[]{:S(2)}, u32[]{:S(2)}) collective-permute-start(bf16[24,1664]{1,0:T(8,128)(2,1)S(1)} %get-tuple-element.18.refs_0_.refs_8_), channel_id=1, source_target_pairs={{0,1},{1,0},{2,3},{3,2},{4,5},{5,4},{6,7},{7,6},{8,9},{9,8},{10,11... | collective-permute-start | bytes 239624 | tf_op jit(solution)/shard_map/ppermute | solution.py:393
  18.4 5.1 %collective-permute-start.10 = (bf16[24,1664]{1,0:T(8,128)(2,1)S(1)}, bf16[24,1664]{1,0:T(8,128)(2,1)S(1)}, u32[]{:S(2)}, u32[]{:S(2)}) collective-permute-start(bf16[24,1664]{1,0:T(8,128)(2,1)S(1)} %collective-permute-done.2.refs_1_.refs_9_), channel_id=1, source_target_pairs={{0,2},{2,0},{4,6},{6,4},{8,10},{10,8},{12,14},{14,12},{1,3},{3,1},... | collective-permute-start | bytes 239624 | tf_op jit(solution)/shard_map/ppermute | solution.py:390
  20.9 5.2 %collective-permute-start.12 = (bf16[24,1664]{1,0:T(8,128)(2,1)S(1)}, bf16[24,1664]{1,0:T(8,128)(2,1)S(1)}, u32[]{:S(2)}, u32[]{:S(2)}) collective-permute-start(bf16[24,1664]{1,0:T(8,128)(2,1)S(1)} %collective-permute-done.4.refs_2_.refs_10_), channel_id=1, source_target_pairs={{0,2},{2,0},{4,6},{6,4},{8,10},{10,8},{12,14},{14,12},{1,3},{3,1},... | collective-permute-start | bytes 239624 | tf_op jit(solution)/shard_map/ppermute | solution.py:390
  22.5 4.5 %collective-permute-start.14 = (bf16[24,1664]{1,0:T(8,128)(2,1)S(1)}, bf16[24,1664]{1,0:T(8,128)(2,1)S(1)}, u32[]{:S(2)}, u32[]{:S(2)}) collective-permute-start(bf16[24,1664]{1,0:T(8,128)(2,1)S(1)} %collective-permute-done.6.refs_3_.refs_11_), channel_id=1, source_target_pairs={{0,2},{2,0},{4,6},{6,4},{8,10},{10,8},{12,14},{14,12},{1,3},{3,1},... | collective-permute-start | bytes 239624 | tf_op jit(solution)/shard_map/ppermute | solution.py:390
  23.0 4.1 %collective-permute-start.3 = (bf16[24,1664]{1,0:T(8,128)(2,1)S(1)}, bf16[24,1664]{1,0:T(8,128)(2,1)S(1)}, u32[]{:S(2)}, u32[]{:S(2)}) collective-permute-start(bf16[24,1664]{1,0:T(8,128)(2,1)S(1)} %collective-permute-done.2.refs_1_.refs_9_), channel_id=1, source_target_pairs={{0,1},{1,0},{2,3},{3,2},{4,5},{5,4},{6,7},{7,6},{8,9},{9,8},{10,11... | collective-permute-start | bytes 239624 | tf_op jit(solution)/shard_map/ppermute | solution.py:393
  23.0 4.6 %collective-permute-start.5 = (bf16[24,1664]{1,0:T(8,128)(2,1)S(1)}, bf16[24,1664]{1,0:T(8,128)(2,1)S(1)}, u32[]{:S(2)}, u32[]{:S(2)}) collective-permute-start(bf16[24,1664]{1,0:T(8,128)(2,1)S(1)} %collective-permute-done.4.refs_2_.refs_10_), channel_id=1, source_target_pairs={{0,1},{1,0},{2,3},{3,2},{4,5},{5,4},{6,7},{7,6},{8,9},{9,8},{10,11... | collective-permute-start | bytes 239624 | tf_op jit(solution)/shard_map/ppermute | solution.py:393
  23.5 15.8 %collective-permute-start.7 = (bf16[24,1664]{1,0:T(8,128)(2,1)S(1)}, bf16[24,1664]{1,0:T(8,128)(2,1)S(1)}, u32[]{:S(2)}, u32[]{:S(2)}) collective-permute-start(bf16[24,1664]{1,0:T(8,128)(2,1)S(1)} %collective-permute-done.6.refs_3_.refs_11_), channel_id=1, source_target_pairs={{0,1},{1,0},{2,3},{3,2},{4,5},{5,4},{6,7},{7,6},{8,9},{9,8},{10,11... | collective-permute-start | bytes 239624 | tf_op jit(solution)/shard_map/ppermute | solution.py:393
  26.2 13.1 %collective-permute-start.9 = (bf16[24,1664]{1,0:T(8,128)(2,1)S(1)}, bf16[24,1664]{1,0:T(8,128)(2,1)S(1)}, u32[]{:S(2)}, u32[]{:S(2)}) collective-permute-start(bf16[24,1664]{1,0:T(8,128)(2,1)S(1)} %collective-permute-done.8.refs_4_.refs_12_), channel_id=1, source_target_pairs={{0,1},{1,0},{2,3},{3,2},{4,5},{5,4},{6,7},{7,6},{8,9},{9,8},{10,11... | collective-permute-start | bytes 239624 | tf_op jit(solution)/shard_map/ppermute | solution.py:393
  27.1 12.3 %collective-permute-start.11 = (bf16[24,1664]{1,0:T(8,128)(2,1)S(1)}, bf16[24,1664]{1,0:T(8,128)(2,1)S(1)}, u32[]{:S(2)}, u32[]{:S(2)}) collective-permute-start(bf16[24,1664]{1,0:T(8,128)(2,1)S(1)} %collective-permute-done.10.refs_5_.refs_13_), channel_id=1, source_target_pairs={{0,1},{1,0},{2,3},{3,2},{4,5},{5,4},{6,7},{7,6},{8,9},{9,8},{10,11... | collective-permute-start | bytes 239624 | tf_op jit(solution)/shard_map/ppermute | solution.py:393
  27.1 12.3 %collective-permute-start.13 = (bf16[24,1664]{1,0:T(8,128)(2,1)S(1)}, bf16[24,1664]{1,0:T(8,128)(2,1)S(1)}, u32[]{:S(2)}, u32[]{:S(2)}) collective-permute-start(bf16[24,1664]{1,0:T(8,128)(2,1)S(1)} %collective-permute-done.12.refs_6_.refs_14_), channel_id=1, source_target_pairs={{0,1},{1,0},{2,3},{3,2},{4,5},{5,4},{6,7},{7,6},{8,9},{9,8},{10,11... | collective-permute-start | bytes 239624 | tf_op jit(solution)/shard_map/ppermute | solution.py:393
  27.6 11.8 %collective-permute-start.15 = (bf16[24,1664]{1,0:T(8,128)(2,1)S(1)}, bf16[24,1664]{1,0:T(8,128)(2,1)S(1)}, u32[]{:S(2)}, u32[]{:S(2)}) collective-permute-start(bf16[24,1664]{1,0:T(8,128)(2,1)S(1)} %collective-permute-done.14.refs_7_.refs_15_), channel_id=1, source_target_pairs={{0,1},{1,0},{2,3},{3,2},{4,5},{5,4},{6,7},{7,6},{8,9},{9,8},{10,11... | collective-permute-start | bytes 239624 | tf_op jit(solution)/shard_map/ppermute | solution.py:393
  51.4 29.8 %copy-start.9 = (s32[12,2]{0,1:T(2,128)S(1)}, s32[12,2]{0,1:T(2,128)}, u32[]{:S(2)}) copy-start(s32[12,2]{0,1:T(2,128)} %param.22) | copy-start | bytes 292
  59.2 8.3 %collective-permute-start.16 = (bf16[96,3072]{1,0:T(8,128)(2,1)S(1)}, bf16[96,3072]{1,0:T(8,128)(2,1)S(1)}, u32[]{:S(2)}, u32[]{:S(2)}) collective-permute-start(bf16[96,3072]{1,0:T(8,128)(2,1)S(1)} %contract_other.1), channel_id=1, source_target_pairs={{0,1},{1,0},{2,3},{3,2},{4,5},{5,4},{6,7},{7,6},{8,9},{9,8},{10,11... | collective-permute-start | bytes 1769480 | tf_op jit(solution)/shard_map/ppermute | solution.py:393
  67.6 9.1 %collective-permute-start.17 = (bf16[48,3072]{1,0:T(8,128)(2,1)S(1)}, bf16[48,3072]{1,0:T(8,128)(2,1)S(1)}, u32[]{:S(2)}, u32[]{:S(2)}) collective-permute-start(bf16[48,3072]{1,0:T(8,128)(2,1)S(1)} %get-tuple-element.22), channel_id=1, source_target_pairs={{0,2},{2,0},{4,6},{6,4},{8,10},{10,8},{12,14},{14,12},{1,3},{3,1},... | collective-permute-start | bytes 884744 | tf_op jit(solution)/shard_map/ppermute | solution.py:390
  76.8 5.9 %collective-permute-start.18 = (bf16[24,1536]{1,0:T(8,128)(2,1)S(1)}, bf16[24,1536]{1,0:T(8,128)(2,1)S(1)}, u32[]{:S(2)}, u32[]{:S(2)}) collective-permute-start(bf16[24,1536]{1,0:T(8,128)(2,1)S(1)} %get-tuple-element.24), channel_id=1, source_target_pairs={{0,12},{2,14},{4,0},{6,2},{8,4},{10,6},{12,8},{14,10},{1,13},{3,15... | collective-permute-start | bytes 221192 | tf_op jit(solution)/shard_map/ppermute | solution.py:383
  80.1 6.5 %collective-permute-start.19 = (bf16[24,1536]{1,0:T(8,128)(2,1)S(1)}, bf16[24,1536]{1,0:T(8,128)(2,1)S(1)}, u32[]{:S(2)}, u32[]{:S(2)}) collective-permute-start(bf16[24,1536]{1,0:T(8,128)(2,1)S(1)} %get-tuple-element.25), channel_id=1, source_target_pairs={{0,8},{2,10},{4,12},{6,14},{8,0},{10,2},{12,4},{14,6},{1,9},{3,11}... | collective-permute-start | bytes 221192 | tf_op jit(solution)/shard_map/ppermute | solution.py:383
  80.1 6.5 %collective-permute-start.20 = (bf16[24,1536]{1,0:T(8,128)(2,1)S(1)}, bf16[24,1536]{1,0:T(8,128)(2,1)S(1)}, u32[]{:S(2)}, u32[]{:S(2)}) collective-permute-start(bf16[24,1536]{1,0:T(8,128)(2,1)S(1)} %get-tuple-element.26), channel_id=1, source_target_pairs={{0,4},{2,6},{4,8},{6,10},{8,12},{10,14},{12,0},{14,2},{1,5},{3,7},... | collective-permute-start | bytes 221192 | tf_op jit(solution)/shard_map/ppermute | solution.py:383
  81.2 1.2 %collective-permute-start = (f32[12,128]{1,0:T(8,128)S(1)}, f32[12,128]{1,0:T(8,128)S(1)}, u32[]{:S(2)}, u32[]{:S(2)}) collective-permute-start(f32[12,128]{1,0:T(8,128)S(1)} %get-tuple-element.17.stat_ref), channel_id=1, source_target_pairs={{0,1},{1,0},{2,3},{3,2},{4,5},{5,4},{6,7},{7,6},{8,9},{9,8},{10,11... | collective-permute-start | bytes 18440 | tf_op jit(solution)/shard_map/ppermute | solution.py:393

commit v2 on v0

v2 whole, which is shorter than its diff:
```python
import functools
import math

import jax
import jax.numpy as jnp
from jax import lax
from jax.experimental import pallas as pl
from jax.experimental.pallas import tpu as pltpu
from jax.sharding import PartitionSpec as P

QUERY_HEADS = 48
KV_HEADS = 8
HEAD_DIM = 128
EXPERTS = 4
GROUP = QUERY_HEADS // KV_HEADS
LANES = 128
FOLD = 2
MIB = 1 << 20
F32 = jnp.float32
BF16 = jnp.bfloat16


def whole_spec(array):
    zeros = (0,) * len(array.shape)
    return pl.BlockSpec(array.shape, lambda *_: zeros)


def in_vmem(*arrays):
    return [pltpu.with_memory_space_constraint(a, pltpu.VMEM) for a in arrays]


def in_hbm(*arrays):
    return [pltpu.with_memory_space_constraint(a, pltpu.HBM) for a in arrays]


VMEM_SPEC = pl.BlockSpec(memory_space=pltpu.VMEM)
SMEM_SPEC = pl.BlockSpec(memory_space=pltpu.SMEM)
HBM_SPEC = pl.BlockSpec(memory_space=pltpu.HBM)
ROUTE_LANE = 3 + 3 * EXPERTS
GATE_DEPTH = 2
DOWN_DEPTH = 4


def row_block(gate_weight):
    return math.gcd(512, gate_weight.shape[0] // 2)


def weight_copies(pairs, first, count, block, sems, split=2):
    part = block // split
    copies = []
    for i in range(count * split):
        for w, (source, target) in enumerate(pairs):
            copies.append(
                pltpu.make_async_copy(
                    source.at[pl.ds(first * block + i * part, part), :],
                    target.at[pl.ds(i * part, part), :], sems.at[w, i],
                )
            )
    return copies


def load_kernel(first, count, block, dep_ref, g_hbm, u_hbm, g_vmem, u_vmem, token_ref, sems):
    copies = weight_copies([(g_hbm, g_vmem), (u_hbm, u_vmem)], first, count, block, sems)
    for copy in copies:
        copy.start()
    token_ref[...] = jnp.zeros_like(token_ref)
    for copy in copies:
        copy.wait()


def load_blocks(first, count, after, gate_weight, up_weight):
    block = row_block(gate_weight)
    hidden = gate_weight.shape[1]
    piece = pltpu.VMEM((count * block, hidden), BF16)
    return pl.pallas_call(
        functools.partial(load_kernel, first, count, block),
        out_shape=(piece, piece, pltpu.VMEM((8, LANES), F32)),
        in_specs=[pl.BlockSpec(memory_space=pl.ANY), HBM_SPEC, HBM_SPEC],
        out_specs=(VMEM_SPEC,) * 3,
        scratch_shapes=[pltpu.SemaphoreType.DMA((2, 2 * count))],
        compiler_params=pltpu.CompilerParams(vmem_limit_bytes=MIB),
        cost_estimate=pl.CostEstimate(
            flops=0, bytes_accessed=4 * count * block * hidden, transcendentals=0
        ),
        name="load_weights",
    )(*in_vmem(after), *in_hbm(gate_weight, up_weight))


def join_kernel(a_ref, b_ref, token_ref, out_ref):
    out_ref[...] = jnp.concatenate(
        [a_ref[...].astype(F32), b_ref[...].astype(F32)], axis=0
    ).astype(BF16)


def join(a, b, token):
    return pl.pallas_call(
        join_kernel,
        out_shape=pltpu.VMEM((a.shape[0] + b.shape[0], a.shape[1]), BF16),
        in_specs=[VMEM_SPEC] * 3,
        out_specs=VMEM_SPEC,
        compiler_params=pltpu.CompilerParams(vmem_limit_bytes=2 * MIB),
        name="join",
    )(*in_vmem(a, b, token))


def relay_kernel(count, *refs):
    del refs


def relay(arrays, token):
    count = len(arrays)
    return list(pl.pallas_call(
        functools.partial(relay_kernel, count),
        out_shape=tuple(pltpu.VMEM(a.shape, a.dtype) for a in arrays),
        in_specs=[VMEM_SPEC] * (count + 1),
        out_specs=(VMEM_SPEC,) * count,
        input_output_aliases={i: i for i in range(count)},
        compiler_params=pltpu.CompilerParams(vmem_limit_bytes=MIB),
        name="relay",
    )(*in_vmem(*arrays, token)))


def split_three(value):
    first = value.astype(BF16).astype(F32)
    second = (value - first).astype(BF16).astype(F32)
    return first, second, value - first - second


def attend_kernel(
    ahead, block,
    place_ref, len_ref, routes_ref, q_hbm, k_hbm, v_hbm, nk_hbm, nv_hbm, res_hbm, gain_hbm, rt_hbm,
    g_hbm, u_hbm,
    carried_ref, pay_ref, g_vmem, u_vmem,
    q_ref, k_ref, v_ref, nk_ref, nv_ref, res_ref, gain_ref, rt_ref,
    q_scr, o_scr, nk_scr, nv_scr, pay_scr, sems, w_sems,
):
    tok, width = q_ref.shape
    cache_len, kv_width = k_ref.shape[1], k_ref.shape[2]
    heads = width // HEAD_DIM
    groups = kv_width // HEAD_DIM
    fold_width = width // FOLD
    scaling = 1.0 / math.sqrt(HEAD_DIM)
    columns = pl.ds(pl.multiple_of(place_ref[0] * width, LANES), width)
    half = tok // 2
    first, rest = pl.ds(0, half), pl.ds(half, tok - half)
    moves = [
        (q_hbm, q_ref), (nk_hbm, nk_ref),
        (k_hbm.at[first], k_ref.at[first]), (k_hbm.at[rest], k_ref.at[rest]),
        (v_hbm.at[first], v_ref.at[first]), (v_hbm.at[rest], v_ref.at[rest]),
        (nv_hbm, nv_ref), (res_hbm, res_ref),
        (gain_hbm.at[:, columns], gain_ref), (rt_hbm.at[:, columns], rt_ref),
    ]
    copies = [pltpu.make_async_copy(a, b, sems.at[i]) for i, (a, b) in enumerate(moves)]
    for copy in copies:
        copy.start()
    weights = weight_copies([(g_hbm, g_vmem), (u_hbm, u_vmem)], 0, ahead, block, w_sems)
    for copy in weights:
        copy.start()
    copies[0].wait()
    copies[1].wait()
    for h in range(heads):
        q_scr[h * tok:(h + 1) * tok, :] = q_ref[:, h * HEAD_DIM:(h + 1) * HEAD_DIM].astype(F32)
    nk_scr[...] = nk_ref[...].astype(F32)
    row_group = lax.broadcasted_iota(jnp.int32, (heads, HEAD_DIM), 0) // GROUP
    position = lax.broadcasted_iota(jnp.int32, (heads, cache_len), 1)
    scores, fresh = [], []
    for t in range(tok):
        if t == 0:
            copies[2].wait()
        if t == half:
            copies[3].wait()
        q_rows = q_scr[pl.ds(t, heads, stride=tok), :]
        q_wide = jnp.concatenate(
            [jnp.where(row_group == g, q_rows, 0.0) for g in range(groups)], axis=1
        )
        scores.append(
            lax.dot_general(
                q_wide.astype(BF16), k_ref[t], (((1,), (1,)), ((), ())),
                preferred_element_type=F32,
            ) * scaling
        )
        fresh.append(
            jnp.sum(q_wide * nk_scr[pl.ds(t, 1), :], axis=1, keepdims=True) * scaling
        )
    terms, fresh_terms, totals = [], [], []
    for t in range(tok):
        score = jnp.where(position < len_ref[t], scores[t], -1e30)
        largest = jnp.maximum(jnp.max(score, axis=1, keepdims=True), fresh[t])
        term = jnp.exp(score - largest)
        fresh_term = jnp.exp(fresh[t] - largest)
        totals.append(jnp.sum(term, axis=1, keepdims=True) + fresh_term)
        terms.append(term.astype(BF16))
        fresh_terms.append(fresh_term.astype(BF16).astype(F32))
    copies[6].wait()
    nv_scr[...] = nv_ref[...].astype(F32)
    for t in range(tok):
        if t == 0:
            copies[4].wait()
        if t == half:
            copies[5].wait()
        wide = jnp.dot(terms[t], v_ref[t], preferred_element_type=F32)
        wide = wide + fresh_terms[t] * nv_scr[pl.ds(t, 1), :]
        picked = wide[:, :HEAD_DIM]
        for g in range(1, groups):
            picked = jnp.where(
                row_group == g, wide[:, g * HEAD_DIM:(g + 1) * HEAD_DIM], picked
            )
        o_scr[pl.ds(t, heads, stride=tok), :] = picked / totals[t]
    for copy in copies[7:]:
        copy.wait()
    for h in range(heads):
        cols = slice(h * HEAD_DIM, (h + 1) * HEAD_DIM)
        carried_ref[:, cols] = res_ref[:, cols].astype(F32) + o_scr[h * tok:(h + 1) * tok, :]
    carried = carried_ref[...]
    scaled = carried * gain_ref[...]
    rounded = scaled.astype(BF16).astype(F32)
    router = rt_ref[...].astype(F32)
    for f in range(FOLD):
        pay_scr[f * tok:(f + 1) * tok, :fold_width] = scaled[:, f * fold_width:(f + 1) * fold_width]
    lane = lax.broadcasted_iota(jnp.int32, (tok, LANES), 1)
    row = lax.broadcasted_iota(jnp.int32, (tok, LANES), 0)
    sums = [jnp.sum(carried * carried, axis=1, keepdims=True)]
    for e in range(EXPERTS):
        sums.append(jnp.sum(rounded * router[e:e + 1, :], axis=1, keepdims=True))
    extra = jnp.zeros((tok, LANES), F32)
    for i, total in enumerate(sums):
        for j, term in enumerate(split_three(total)):
            extra = jnp.where(lane == 3 * i + j, term, extra)
    for t in range(tok):
        for i in range(2):
            extra = jnp.where(
                jnp.logical_and(row == t, lane == ROUTE_LANE + i),
                routes_ref[i, t].astype(F32), extra,
            )
    for f in range(FOLD):
        pay_scr[f * tok:(f + 1) * tok, fold_width:] = extra
    pay_ref[...] = pay_scr[...].astype(BF16)
    for copy in weights:
        copy.wait()


def attend(
    ahead, place, lengths, routes_t, queries, key_cache, value_cache, new_key, new_value,
    residual, gain, router_t, gate_weight, up_weight,
):
    tok, width = queries.shape
    kv_width = new_key.shape[1]
    heads = width // HEAD_DIM
    wide = width // FOLD + LANES
    piece = pltpu.VMEM((ahead * row_block(gate_weight), gate_weight.shape[1]), BF16)
    here = [
        pltpu.VMEM(a.shape, a.dtype)
        for a in (queries, key_cache, value_cache, new_key, new_value, residual)
    ]
    return pl.pallas_call(
        functools.partial(attend_kernel, ahead, row_block(gate_weight)),
        out_shape=(
            pltpu.VMEM((tok, width), F32),
            pltpu.VMEM((FOLD * tok, wide), BF16),
            piece,
            piece,
        ),
        in_specs=[SMEM_SPEC] * 3 + [HBM_SPEC] * 10,
        out_specs=(VMEM_SPEC,) * 4,
        scratch_shapes=here + [
            pltpu.VMEM((1, width), F32),
            pltpu.VMEM((EXPERTS, width), BF16),
            pltpu.VMEM((heads * tok, HEAD_DIM), F32),
            pltpu.VMEM((heads * tok, HEAD_DIM), F32),
            pltpu.VMEM((tok, kv_width), F32),
            pltpu.VMEM((tok, kv_width), F32),
            pltpu.VMEM((FOLD * tok, wide), F32),
            pltpu.SemaphoreType.DMA((10,)),
            pltpu.SemaphoreType.DMA((2, 2 * ahead)),
        ],
        compiler_params=pltpu.CompilerParams(vmem_limit_bytes=10 * MIB),
        cost_estimate=pl.CostEstimate(flops=10**8, bytes_accessed=8 * 10**6, transcendentals=10**5),
        name="attend",
    )(
        place,
        *in_hbm(
            lengths, routes_t, queries, key_cache, value_cache, new_key, new_value, residual, gain, router_t,
            gate_weight, up_weight,
        ),
    )


def down_copies(d_hbm, ring, sems, column, width, block, k):
    slot = lax.rem(k, ring.shape[0])
    return pltpu.make_async_copy(
        d_hbm.at[pl.ds(pl.multiple_of(k * block, block), block), pl.ds(column, width)],
        ring.at[slot], sems.at[slot],
    )


def down_pass(hidden, d_hbm, ring, sems, column, acc):
    steps, _, block = hidden.shape
    depth, _, width = ring.shape
    acc[...] = jnp.zeros_like(acc)

    def step(k, _):
        slot = lax.rem(k, depth)
        down_copies(d_hbm, ring, sems, column, width, block, k).wait()
        acc[...] += jnp.dot(hidden[k], ring[slot], preferred_element_type=F32)

        @pl.when(k + depth < steps)
        def _():
            down_copies(d_hbm, ring, sems, column, width, block, k + depth).start()

        return 0

    lax.fori_loop(0, steps, step, 0)


def experts_kernel(counts, block, per_plane, place_ref, *refs):
    mine, other = refs[:per_plane], refs[per_plane:2 * per_plane]
    refs = refs[2 * per_plane:]
    pieces = [refs[2 * i:2 * i + 2] for i in range(len(counts))]
    (g_hbm, u_hbm, d_hbm,
     hidden_ref, weight_ref, leaving_ref,
     x_scr, gate_acc, up_acc, gu_ring, ring, acc, g_sems, d_sems) = refs[2 * len(counts):]
    ready = sum(counts)
    rows, units = gate_acc.shape
    slots = EXPERTS
    tok = mine[0].shape[0] // (FOLD * slots)
    fold_width = mine[0].shape[1] - LANES
    width = FOLD * fold_width
    side = place_ref[0]
    steps = g_hbm.shape[0] // block
    per_fold = fold_width // block
    gu_depth = gu_ring.shape[0]

    def gu_copies(k):
        slot = lax.rem(k, gu_depth)
        at = pl.ds(pl.multiple_of(k * block, block), block)
        return [
            pltpu.make_async_copy(w.at[at, :], gu_ring.at[slot, i], g_sems.at[slot, i])
            for i, w in enumerate((g_hbm, u_hbm))
        ]

    for k in range(ready, min(ready + gu_depth, steps)):
        for copy in gu_copies(k):
            copy.start()
    d_steps, _, d_block = hidden_ref.shape
    column = pl.multiple_of((1 - side) * width, LANES)
    for k in range(min(ring.shape[0], d_steps)):
        down_copies(d_hbm, ring, d_sems, column, width, d_block, k).start()

    for arrays, base in ((mine, side * (width // block)), (other, (1 - side) * (width // block))):
        for f in range(FOLD):
            for u, array in enumerate(arrays):
                whole = array[:, :fold_width].astype(F32)
                for i in range(slots):
                    to = (u * slots + i) * tok
                    start = (i * FOLD + f) * tok
                    acc[to:to + tok, :fold_width] = whole[start:start + tok, :]
            for p in range(per_fold):
                x_scr[base + f * per_fold + p] = acc[:, p * block:(p + 1) * block].astype(BF16)

    gate_acc[...] = jnp.zeros_like(gate_acc)
    up_acc[...] = jnp.zeros_like(up_acc)

    first = 0
    for count, (g_ref, u_ref) in zip(counts, pieces):
        def held(k, _, first=first, g_ref=g_ref, u_ref=u_ref):
            at = pl.ds(pl.multiple_of(k * block, block), block)
            gate_acc[...] += jnp.dot(x_scr[first + k], g_ref[at, :], preferred_element_type=F32)
            up_acc[...] += jnp.dot(x_scr[first + k], u_ref[at, :], preferred_element_type=F32)
            return 0

        lax.fori_loop(0, count, held, 0)
        first += count

    def streamed(k, _):
        slot = lax.rem(k, gu_depth)
        for copy in gu_copies(k):
            copy.wait()
        gate_acc[...] += jnp.dot(x_scr[k], gu_ring[slot, 0], preferred_element_type=F32)
        up_acc[...] += jnp.dot(x_scr[k], gu_ring[slot, 1], preferred_element_type=F32)

        @pl.when(k + gu_depth < steps)
        def _():
            for copy in gu_copies(k + gu_depth):
                copy.start()

        return 0

    lax.fori_loop(ready, steps, streamed, 0)

    for u in range(per_plane):
        for i in range(slots):
            to = (u * slots + i) * tok
            start = i * FOLD * tok
            acc[to:to + tok, :LANES] = mine[u][:, fold_width:].astype(F32)[start:start + tok, :]
            acc[to:to + tok, LANES:2 * LANES] = other[u][:, fold_width:].astype(F32)[start:start + tok, :]
    own = acc[:, :LANES]
    both = own + acc[:, LANES:2 * LANES]
    lane = lax.broadcasted_iota(jnp.int32, (rows, LANES), 1)

    def pick(values, mask):
        return jnp.sum(jnp.where(mask, values, 0.0), axis=1, keepdims=True)

    scale = lax.rsqrt(pick(both, lane < 3) * (1.0 / (2 * width)) + 1e-05)
    first, second = pick(own, lane == ROUTE_LANE), pick(own, lane == ROUTE_LANE + 1)
    expert_of = (lane - 3) // 3
    logit_lane = jnp.logical_and(lane >= 3, lane < ROUTE_LANE)

    def logit_at(route):
        return pick(both, jnp.logical_and(logit_lane, expert_of == route.astype(jnp.int32))) * scale

    share = 1.0 / (1.0 + jnp.exp(logit_at(second) - logit_at(first)))
    here = place_ref[1].astype(F32)
    weight = jnp.where(first == here, share, 0.0) + jnp.where(second == here, 1.0 - share, 0.0)
    weight_ref[...] = jnp.broadcast_to(weight, weight_ref.shape)

    gate = gate_acc[...] * scale
    hidden = (gate / (1.0 + jnp.exp(-gate)) * (up_acc[...] * scale)).astype(BF16)
    for k in range(d_steps):
        hidden_ref[k] = hidden[:, k * d_block:(k + 1) * d_block]
    down_pass(hidden_ref, d_hbm, ring, d_sems, column, acc)
    leaving_ref[...] = (acc[...] * weight).astype(BF16)


def experts(place, mine, other, gate_weight, up_weight, down_weight, counts, pieces):
    slots = EXPERTS
    per_plane = len(mine)
    tok = mine[0].shape[0] // (FOLD * slots)
    rows = per_plane * slots * tok
    units = gate_weight.shape[1]
    width = down_weight.shape[1] // 2
    block = row_block(gate_weight)
    steps = gate_weight.shape[0] // block
    d_block = math.gcd(256, units)
    depth = min(DOWN_DEPTH, units // d_block)
    gu_depth = min(GATE_DEPTH, max(1, steps - sum(counts)))
    return pl.pallas_call(
        functools.partial(experts_kernel, counts, block, per_plane),
        out_shape=(
            pltpu.VMEM((units // d_block, rows, d_block), BF16),
            pltpu.VMEM((rows, LANES), F32),
            pltpu.VMEM((rows, width), BF16),
        ),
        in_specs=[SMEM_SPEC] + [VMEM_SPEC] * (2 * per_plane + 2 * len(counts)) + [HBM_SPEC] * 3,
        out_specs=(VMEM_SPEC,) * 3,
        scratch_shapes=[
            pltpu.VMEM((steps, rows, block), BF16),
            pltpu.VMEM((rows, units), F32),
            pltpu.VMEM((rows, units), F32),
            pltpu.VMEM((gu_depth, 2, block, units), BF16),
            pltpu.VMEM((depth, d_block, width), BF16),
            pltpu.VMEM((rows, width), F32),
            pltpu.SemaphoreType.DMA((gu_depth, 2)),
            pltpu.SemaphoreType.DMA((depth,)),
        ],
        compiler_params=pltpu.CompilerParams(vmem_limit_bytes=(25 if rows < 256 else 40) * MIB),
        cost_estimate=pl.CostEstimate(
            flops=6 * rows * 2 * width * units, bytes_accessed=3 * 4 * width * units, transcendentals=0
        ),
        name="experts",
    )(
        place, *in_vmem(*mine, *other, *[p for pair in pieces for p in pair]),
        *in_hbm(gate_weight, up_weight, down_weight),
    )


def own_kernel(place_ref, hidden_ref, weight_ref, d_hbm, out_ref, ring, sems):
    d_steps, _, d_block = hidden_ref.shape
    width = out_ref.shape[1]
    column = pl.multiple_of(place_ref[0] * width, LANES)
    for k in range(min(ring.shape[0], d_steps)):
        down_copies(d_hbm, ring, sems, column, width, d_block, k).start()
    down_pass(hidden_ref, d_hbm, ring, sems, column, out_ref)
    out_ref[...] = out_ref[...] * weight_ref[:, 0:1]


def own_half(place, hidden, weight, down_weight):
    d_steps, rows, d_block = hidden.shape
    width = down_weight.shape[1] // 2
    depth = min(8, d_steps)
    return pl.pallas_call(
        own_kernel,
        out_shape=pltpu.VMEM((rows, width), F32),
        in_specs=[SMEM_SPEC, VMEM_SPEC, VMEM_SPEC, HBM_SPEC],
        out_specs=VMEM_SPEC,
        scratch_shapes=[
            pltpu.VMEM((depth, d_block, width), BF16),
            pltpu.SemaphoreType.DMA((depth,)),
        ],
        compiler_params=pltpu.CompilerParams(vmem_limit_bytes=32 * MIB),
        cost_estimate=pl.CostEstimate(
            flops=2 * rows * width * d_steps * d_block,
            bytes_accessed=2 * width * d_steps * d_block, transcendentals=0,
        ),
        name="own_half",
    )(place, *in_vmem(hidden, weight), *in_hbm(down_weight))


def split_kernel(count, fold, own_ref, *refs):
    got, (keep_ref, *sends), total = refs[:count], refs[count:-1], refs[-1]
    value = own_ref[...]
    for ref in got:
        value = value + ref[...].astype(F32)
    total[...] = value
    size, width = keep_ref.shape
    keep_ref[...] = total[:size, :]
    for u, send in enumerate(sends, 1):
        part = total[u * size:(u + 1) * size, :]
        if fold:
            part = jnp.concatenate(
                [part[:, f * (width // FOLD):(f + 1) * (width // FOLD)] for f in range(FOLD)], axis=0
            )
        send[...] = part.astype(BF16)


def split_rows(own, got, parts, fold=False):
    rows, width = own.shape
    size = rows // parts
    sent = (FOLD * size, width // FOLD) if fold else (size, width)
    return pl.pallas_call(
        functools.partial(split_kernel, len(got), fold),
        out_shape=(pltpu.VMEM((size, width), F32),)
        + (pltpu.VMEM(sent, BF16),) * (parts - 1),
        in_specs=[VMEM_SPEC] * (1 + len(got)),
        out_specs=(VMEM_SPEC,) * parts,
        scratch_shapes=[pltpu.VMEM((rows, width), F32)],
        compiler_params=pltpu.CompilerParams(vmem_limit_bytes=32 * MIB),
        name="split_rows",
    )(*in_vmem(own, *got))


def finish_kernel(carried_ref, own_ref, got_ref, out_ref, folded):
    tok, width = carried_ref.shape
    fold_width = width // FOLD
    folded[...] = got_ref[...].astype(F32)
    for f in range(FOLD):
        at = slice(f * fold_width, (f + 1) * fold_width)
        value = carried_ref[:, at] + own_ref[:, at] + folded[f * tok:(f + 1) * tok, :]
        out_ref[:, at] = value.astype(BF16)


def finish(carried, own, got):
    tok, width = carried.shape
    return pl.pallas_call(
        finish_kernel,
        out_shape=jax.ShapeDtypeStruct((tok, width), BF16),
        in_specs=[VMEM_SPEC] * 3,
        out_specs=VMEM_SPEC,
        scratch_shapes=[pltpu.VMEM((FOLD * tok, width // FOLD), F32)],
        compiler_params=pltpu.CompilerParams(vmem_limit_bytes=8 * MIB),
        name="finish",
    )(*in_vmem(carried, own, got))


def on_device(
    residual, queries, key_cache, value_cache, new_key, new_value, cache_lengths,
    norm_gain, router, routes, gate_weight, up_weight, down_weight,
):
    nodes = lax.axis_size("node")
    per_plane = nodes // EXPERTS
    place = jnp.stack(
        [lax.axis_index("shard"), lax.axis_index("node") // per_plane]
    ).astype(jnp.int32)

    def to_plane(array, s):
        perm = [
            (e * per_plane + j, (e ^ s) * per_plane + j)
            for e in range(EXPERTS) for j in range(per_plane)
        ]
        return lax.ppermute(array, "node", perm)

    def to_column(array, u):
        perm = [
            (e * per_plane + j, e * per_plane + (j + u) % per_plane)
            for e in range(EXPERTS) for j in range(per_plane)
        ]
        return lax.ppermute(array, "node", perm)

    def to_core(array):
        return lax.ppermute(array, "shard", [(0, 1), (1, 0)])

    steps = gate_weight.shape[0] // row_block(gate_weight)
    counts = [n * steps // 12 for n in (1, 2, 2, 3)]

    def load(i, after):
        *piece, token = load_blocks(sum(counts[:i]), counts[i], after, gate_weight, up_weight)
        return piece, token

    carried, payload, *first = attend(
        counts[0], place, cache_lengths, routes.T, queries, key_cache, value_cache, new_key, new_value,
        residual, norm_gain.reshape(1, -1), router.T, gate_weight, up_weight,
    )
    far = to_plane(payload, 2)
    second, token = load(1, payload)
    pair = join(payload, far, token)
    near = to_plane(pair, 1)
    third, token = load(2, pair)
    column = join(pair, near, token)
    mine = [column] + [to_column(column, u) for u in range(1, per_plane)]
    fourth, token = load(3, column)
    mine = [column] + relay(mine[1:], token)
    other = [to_core(array) for array in mine]
    hidden, weight, leaving = experts(
        place, mine, other, gate_weight, up_weight, down_weight, counts,
        [first, second, third, fourth],
    )
    arrived = to_core(leaving)
    staying = own_half(place, hidden, weight, down_weight)
    keep, *sends = split_rows(staying, [arrived], per_plane)
    got = [to_column(sends[u - 1], -u) for u in range(1, per_plane)]
    keep, send = split_rows(keep, got, 2)
    keep, send = split_rows(keep, [to_plane(send, 1)], 2, fold=True)
    return finish(carried, keep, to_plane(send, 2))


def solution(mesh):
    rows = ("replica", "node")
    in_specs = (
        P(rows, "shard"),
        P(rows, "shard"),
        P(rows, None, "shard"),
        P(rows, None, "shard"),
        P(rows, "shard"),
        P(rows, "shard"),
        P(rows),
        P(),
        P(),
        P(rows, None),
        P(None, ("node", "shard")),
        P(None, ("node", "shard")),
        P(("node", "shard"), None),
    )
    return jax.shard_map(
        on_device,
        mesh=mesh,
        in_specs=in_specs,
        out_specs=P(rows, "shard"),
        check_vma=False,
    )
```

time: 188 us -> 72.4 us (0.39)
  blocking collectives: 121 us -> 0 us
  Pallas kernels: 0 us -> 39.5 us
  matrix products: 35.6 us -> 0 us
  starting transfers between devices: 0.01 us -> 14 us
  between operations: 13.6 us -> 0.09 us
  waiting for transfers between devices: 5.49 us -> 18.5 us
  local copies, waits for them, and re-layouts: 8.16 us -> 0.01 us
  other arithmetic: 4 us -> 0.07 us
    all_to_all x2 -> x0, blocking collectives: 118 us -> none  [the longest x1 74.1 us: on_device(): lax.all_to_all(partial_out, 'node', split_axis=0, concat_axis=0, tiled=True)]
    pallas_call x0 -> x13, Pallas kernels: none -> 39.5 us  [the longest x1 16.9 us: experts(): pl.pallas_call(functools.partial(experts_kernel, counts, block, per_plane...]
    dot_general x8 -> x0, matrix products: 35.6 us -> none  [the longest x1 19.9 us: on_device(): jnp.dot(hidden, down_weight, preferred_element_type=jnp.float32)]
    ppermute x0 -> x9, waiting for transfers between devices: none -> 18.5 us  [the longest x2 9.31 us: to_column(): return lax.ppermute(array, 'node', perm)]
    ppermute x0 -> x9, starting transfers between devices: none -> 14 us  [the longest x4 10.5 us: to_plane(): return lax.ppermute(array, 'node', perm)]
    reduce_scatter x1 -> x0, waiting for transfers between devices: 5.48 us -> none  [on_device(): lax.psum_scatter(summed, 'shard', scatter_dimension=2, tiled=True)]
    reshape x5 -> x0, local copies, waits for them, and re-layouts: 4.14 us -> none  [the longest x1 1.95 us: on_device(): jnp.dot(hidden, down_weight, preferred_element_type=jnp.float32)]
    all_gather x1 -> x0, blocking collectives: 2.17 us -> none  [on_device(): carried = lax.all_gather(carried_half, 'shard', axis=1, tiled=True)]
  transfers between devices with their start and end apart: 1 -> 9, of which waited for: 1 -> 7; matrix products, arithmetic and copies ran while one was open for 1% -> 0% of each run, Pallas kernels for 0% -> 24%
where the time goes in v2:
time: 72.4 us; the launch traced here: 72.2 us
  Pallas kernels  39.5 us (55%)
  waiting for transfers between devices  18.5 us (26%)
  starting transfers between devices  14 us (19%)
    pallas_call x1, Pallas kernels, experts(): pl.pallas_call(functools.partial(experts_kernel, counts, block, per_plane...  16.9 us
    pallas_call x3, Pallas kernels, load_blocks(): pl.pallas_call(functools.partial(load_kernel, first, count, block), out_s...  11.6 us
    ppermute x4, starting transfers between devices, to_plane(): return lax.ppermute(array, 'node', perm)  10.5 us
    ppermute x2, waiting for transfers between devices, to_column(): return lax.ppermute(array, 'node', perm)  9.31 us
    ppermute x4, waiting for transfers between devices, to_plane(): return lax.ppermute(array, 'node', perm)  7.63 us
    pallas_call x1, Pallas kernels, own_half(): pl.pallas_call(own_kernel, out_shape=pltpu.VMEM((rows, width), F32), in_s...  5.84 us
    pallas_call x1, Pallas kernels, attend(): pl.pallas_call(functools.partial(attend_kernel, ahead, row_block(gate_wei...  4.11 us
    ppermute x2, starting transfers between devices, to_column(): return lax.ppermute(array, 'node', perm)  3.34 us
  transfers between devices with their start and end apart: 9, of which 7 were waited for; matrix products, arithmetic and copies ran while one was open for 0% of the time, Pallas kernels for 24%

profile of v2, /device:TPU:0, one launch (start us, length us, event | category | flops | bytes accessed | tf_op | source)
XLA Modules:
  0.0 72.2 jit_solution(11103527851293997179)
XLA Ops:
  0.0 0.1 pad_add_fusion.place_ref
  0.1 0.0 copy-start
  0.1 4.1 %attend.1 = (f32[12,3072]{1,0:T(8,128)S(1)}, bf16[24,1664]{1,0:T(8,128)(2,1)S(1)}, bf16[512,2048]{1,0:T(8,128)(2,1)S(1)}, bf16[512,2048]{1,0:T(8,128)(2,1)S(1)}) custom-call(s32[2]{0:T(128)S(1)} %pad_add_fusion.place_ref, s32[12]{0:T(128)} %len_ref.1, s32[2,12]{1,0:T(2,128)} %bitcast.7, bf16[12,3072]{1,0:T(8,128)(2,1)} %q_hbm.1, ...), custom_call_target="tpu_custom_call" | custom-call | flops 100000000 | bytes 8000000 | tf_op jit(solution)/shard_map/attend/pallas_call | solution.py:255
  4.2 0.0 copy-done
  4.2 4.1 %collective-permute-start = (bf16[24,1664]{1,0:T(8,128)(2,1)S(1)}, bf16[24,1664]{1,0:T(8,128)(2,1)S(1)}, u32[]{:S(2)}, u32[]{:S(2)}) collective-permute-start(bf16[24,1664]{1,0:T(8,128)(2,1)S(1)} %get-tuple-element.28.dep_ref.a_ref), channel_id=1, source_target_pairs={{0,8},{2,10},{4,12},{6,14},{8,0},{10,2},{12,4},{14,6},{1,9},{3,11}... | collective-permute-start | bytes 239624 | tf_op jit(solution)/shard_map/ppermute | solution.py:569
  8.3 3.5 %load_weights.3 = (bf16[1024,2048]{1,0:T(8,128)(2,1)S(1)}, bf16[1024,2048]{1,0:T(8,128)(2,1)S(1)}, f32[8,128]{1,0:T(8,128)S(1)}) custom-call(bf16[24,1664]{1,0:T(8,128)(2,1)S(1)} %get-tuple-element.28.dep_ref.a_ref, bf16[6144,2048]{1,0:T(8,128)(2,1)} %refs_12_.1, bf16[6144,2048]{1,0:T(8,128)(2,1)} %refs_13_.1), custom_call_target="tpu_custom_call" | custom-call | bytes 8388608 | tf_op jit(solution)/shard_map/load_weights/pallas_call | solution.py:75
  11.8 0.6 collective-permute-done.b_ref
  12.4 1.0 %collective-permute-start.1 = (bf16[48,1664]{1,0:T(8,128)(2,1)S(1)}, bf16[48,1664]{1,0:T(8,128)(2,1)S(1)}, u32[]{:S(2)}, u32[]{:S(2)}) collective-permute-start(bf16[48,1664]{1,0:T(8,128)(2,1)S(1)} %join.2.dep_ref.a_ref), channel_id=1, source_target_pairs={{0,4},{2,6},{4,0},{6,2},{8,12},{10,14},{12,8},{14,10},{1,5},{3,7},... | collective-permute-start | bytes 479240 | tf_op jit(solution)/shard_map/ppermute | solution.py:569
  13.5 3.5 %load_weights.4 = (bf16[1024,2048]{1,0:T(8,128)(2,1)S(1)}, bf16[1024,2048]{1,0:T(8,128)(2,1)S(1)}, f32[8,128]{1,0:T(8,128)S(1)}) custom-call(bf16[48,1664]{1,0:T(8,128)(2,1)S(1)} %join.2.dep_ref.a_ref, bf16[6144,2048]{1,0:T(8,128)(2,1)} %refs_12_.1, bf16[6144,2048]{1,0:T(8,128)(2,1)} %refs_13_.1), custom_call_target="tpu_custom_call" | custom-call | bytes 8388608 | tf_op jit(solution)/shard_map/load_weights/pallas_call | solution.py:75
  16.9 0.8 %collective-permute-done.1.b_ref = bf16[48,1664]{1,0:T(8,128)(2,1)S(1)} collective-permute-done((bf16[48,1664]{1,0:T(8,128)(2,1)S(1)}, bf16[48,1664]{1,0:T(8,128)(2,1)S(1)}, u32[]{:S(2)}, u32[]{:S(2)}) %collective-permute-start.1) | collective-permute-done | bytes 159776 | tf_op jit(solution)/shard_map/ppermute | solution.py:569
  17.8 1.8 %collective-permute-start.2 = (bf16[96,1664]{1,0:T(8,128)(2,1)S(1)}, bf16[96,1664]{1,0:T(8,128)(2,1)S(1)}, u32[]{:S(2)}, u32[]{:S(2)}) collective-permute-start(bf16[96,1664]{1,0:T(8,128)(2,1)S(1)} %join.3.dep_ref.refs_0_), channel_id=1, source_target_pairs={{0,2},{2,0},{4,6},{6,4},{8,10},{10,8},{12,14},{14,12},{1,3},{3,1},... | collective-permute-start | bytes 958472 | tf_op jit(solution)/shard_map/ppermute | solution.py:576
  19.6 0.0 collective-permute-start.3
  19.6 4.7 %load_weights.5 = (bf16[1536,2048]{1,0:T(8,128)(2,1)S(1)}, bf16[1536,2048]{1,0:T(8,128)(2,1)S(1)}, f32[8,128]{1,0:T(8,128)S(1)}) custom-call(bf16[96,1664]{1,0:T(8,128)(2,1)S(1)} %join.3.dep_ref.refs_0_, bf16[6144,2048]{1,0:T(8,128)(2,1)} %refs_12_.1, bf16[6144,2048]{1,0:T(8,128)(2,1)} %refs_13_.1), custom_call_target="tpu_custom_call" | custom-call | bytes 12582912 | tf_op jit(solution)/shard_map/load_weights/pallas_call | solution.py:75
  24.3 1.5 %collective-permute-done.2.refs_0_ = bf16[96,1664]{1,0:T(8,128)(2,1)S(1)} collective-permute-done((bf16[96,1664]{1,0:T(8,128)(2,1)S(1)}, bf16[96,1664]{1,0:T(8,128)(2,1)S(1)}, u32[]{:S(2)}, u32[]{:S(2)}) %collective-permute-start.2) | collective-permute-done | bytes 319520 | tf_op jit(solution)/shard_map/ppermute | solution.py:576
  25.8 0.0 collective-permute-start.4
  25.8 0.0 collective-permute-done.3.refs_2_
  25.8 1.6 %collective-permute-done.4.refs_3_ = bf16[96,1664]{1,0:T(8,128)(2,1)S(1)} collective-permute-done((bf16[96,1664]{1,0:T(8,128)(2,1)S(1)}, bf16[96,1664]{1,0:T(8,128)(2,1)S(1)}, u32[]{:S(2)}, u32[]{:S(2)}) %collective-permute-start.4) | collective-permute-done | bytes 319520 | tf_op jit(solution)/shard_map/ppermute | solution.py:579
  27.4 0.0 copy-start.1
  27.4 16.9 %experts.1 = (bf16[8,96,256]{2,1,0:T(8,128)(2,1)S(1)}, f32[96,128]{1,0:T(8,128)S(1)}, bf16[96,3072]{1,0:T(8,128)(2,1)S(1)}) custom-call(s32[2]{0:T(128)} %copy-done, bf16[96,1664]{1,0:T(8,128)(2,1)S(1)} %join.3.dep_ref.refs_0_, bf16[96,1664]{1,0:T(8,128)(2,1)S(1)} %relay.1.refs_1_, bf16[96,1664]{1,0:T(8,128)(2,1)S(1)} %collective-permute-done.3.refs_2_, ...), custom_call_target="tpu_custom_call" | custom-call | flops 7247757312 | bytes 75497472 | tf_op jit(solution)/shard_map/experts/pallas_call | solution.py:436
  44.4 0.2 collective-permute-start.5
  44.6 0.0 copy-done.1
  44.6 5.8 %own_half.1.own_ref = f32[96,3072]{1,0:T(8,128)S(1)} custom-call(s32[2]{0:T(128)S(1)} %copy-done.1, bf16[8,96,256]{2,1,0:T(8,128)(2,1)S(1)} %get-tuple-element.40.hidden_ref, f32[96,128]{1,0:T(8,128)S(1)} %get-tuple-element.41.weight_ref, bf16[2048,6144]{1,0:T(8,128)(2,1)} %d_hbm.1), custom_call_target="tpu_custom_call" | custom-call | flops 1207959552 | bytes 12582912 | tf_op jit(solution)/shard_map/own_half/pallas_call | solution.py:480
  50.4 0.0 collective-permute-done.5.refs_0_
  50.4 0.1 split_rows.3
  50.6 1.6 %collective-permute-start.6 = (bf16[48,3072]{1,0:T(8,128)(2,1)S(1)}, bf16[48,3072]{1,0:T(8,128)(2,1)S(1)}, u32[]{:S(2)}, u32[]{:S(2)}) collective-permute-start(bf16[48,3072]{1,0:T(8,128)(2,1)S(1)} %get-tuple-element.44), channel_id=1, source_target_pairs={{0,2},{2,0},{4,6},{6,4},{8,10},{10,8},{12,14},{14,12},{1,3},{3,1},... | collective-permute-start | bytes 884744 | tf_op jit(solution)/shard_map/ppermute | solution.py:576
  52.1 7.8 %collective-permute-done.6.refs_0_ = bf16[48,3072]{1,0:T(8,128)(2,1)S(1)} collective-permute-done((bf16[48,3072]{1,0:T(8,128)(2,1)S(1)}, bf16[48,3072]{1,0:T(8,128)(2,1)S(1)}, u32[]{:S(2)}, u32[]{:S(2)}) %collective-permute-start.6) | collective-permute-done | bytes 294944 | tf_op jit(solution)/shard_map/ppermute | solution.py:576
  59.9 0.1 split_rows.4
  60.0 1.6 %collective-permute-start.7 = (bf16[24,3072]{1,0:T(8,128)(2,1)S(1)}, bf16[24,3072]{1,0:T(8,128)(2,1)S(1)}, u32[]{:S(2)}, u32[]{:S(2)}) collective-permute-start(bf16[24,3072]{1,0:T(8,128)(2,1)S(1)} %get-tuple-element.46), channel_id=1, source_target_pairs={{0,4},{2,6},{4,0},{6,2},{8,12},{10,14},{12,8},{14,10},{1,5},{3,7},... | collective-permute-start | bytes 442376 | tf_op jit(solution)/shard_map/ppermute | solution.py:569
  61.5 3.8 %collective-permute-done.7.refs_0_ = bf16[24,3072]{1,0:T(8,128)(2,1)S(1)} collective-permute-done((bf16[24,3072]{1,0:T(8,128)(2,1)S(1)}, bf16[24,3072]{1,0:T(8,128)(2,1)S(1)}, u32[]{:S(2)}, u32[]{:S(2)}) %collective-permute-start.7) | collective-permute-done | bytes 147488 | tf_op jit(solution)/shard_map/ppermute | solution.py:569
  65.4 3.8 %collective-permute-start.8 = (bf16[24,1536]{1,0:T(8,128)(2,1)S(1)}, bf16[24,1536]{1,0:T(8,128)(2,1)S(1)}, u32[]{:S(2)}, u32[]{:S(2)}) collective-permute-start(bf16[24,1536]{1,0:T(8,128)(2,1)S(1)} %get-tuple-element.48), channel_id=1, source_target_pairs={{0,8},{2,10},{4,12},{6,14},{8,0},{10,2},{12,4},{14,6},{1,9},{3,11}... | collective-permute-start | bytes 221192 | tf_op jit(solution)/shard_map/ppermute | solution.py:569
  69.2 2.3 %collective-permute-done.8.got_ref = bf16[24,1536]{1,0:T(8,128)(2,1)S(1)} collective-permute-done((bf16[24,1536]{1,0:T(8,128)(2,1)S(1)}, bf16[24,1536]{1,0:T(8,128)(2,1)S(1)}, u32[]{:S(2)}, u32[]{:S(2)}) %collective-permute-start.8) | collective-permute-done | bytes 73760 | tf_op jit(solution)/shard_map/ppermute | solution.py:569
  71.5 0.7 finish.1
  (4 shorter events, 0.1 us)
Async XLA Ops:
  0.1 4.1 %copy-start = (s32[2]{0:T(128)}, s32[2]{0:T(128)S(1)}, u32[]{:S(2)}) copy-start(s32[2]{0:T(128)S(1)} %pad_add_fusion.place_ref) | copy-start | bytes 28
  4.2 8.2 %collective-permute-start = (bf16[24,1664]{1,0:T(8,128)(2,1)S(1)}, bf16[24,1664]{1,0:T(8,128)(2,1)S(1)}, u32[]{:S(2)}, u32[]{:S(2)}) collective-permute-start(bf16[24,1664]{1,0:T(8,128)(2,1)S(1)} %get-tuple-element.28.dep_ref.a_ref), channel_id=1, source_target_pairs={{0,8},{2,10},{4,12},{6,14},{8,0},{10,2},{12,4},{14,6},{1,9},{3,11}... | collective-permute-start | bytes 239624 | tf_op jit(solution)/shard_map/ppermute | solution.py:569
  12.4 5.3 %collective-permute-start.1 = (bf16[48,1664]{1,0:T(8,128)(2,1)S(1)}, bf16[48,1664]{1,0:T(8,128)(2,1)S(1)}, u32[]{:S(2)}, u32[]{:S(2)}) collective-permute-start(bf16[48,1664]{1,0:T(8,128)(2,1)S(1)} %join.2.dep_ref.a_ref), channel_id=1, source_target_pairs={{0,4},{2,6},{4,0},{6,2},{8,12},{10,14},{12,8},{14,10},{1,5},{3,7},... | collective-permute-start | bytes 479240 | tf_op jit(solution)/shard_map/ppermute | solution.py:569
  17.8 8.0 %collective-permute-start.2 = (bf16[96,1664]{1,0:T(8,128)(2,1)S(1)}, bf16[96,1664]{1,0:T(8,128)(2,1)S(1)}, u32[]{:S(2)}, u32[]{:S(2)}) collective-permute-start(bf16[96,1664]{1,0:T(8,128)(2,1)S(1)} %join.3.dep_ref.refs_0_), channel_id=1, source_target_pairs={{0,2},{2,0},{4,6},{6,4},{8,10},{10,8},{12,14},{14,12},{1,3},{3,1},... | collective-permute-start | bytes 958472 | tf_op jit(solution)/shard_map/ppermute | solution.py:576
  19.6 6.2 %collective-permute-start.3 = (bf16[96,1664]{1,0:T(8,128)(2,1)S(1)}, bf16[96,1664]{1,0:T(8,128)(2,1)S(1)}, u32[]{:S(2)}, u32[]{:S(2)}) collective-permute-start(bf16[96,1664]{1,0:T(8,128)(2,1)S(1)} %join.3.dep_ref.refs_0_), channel_id=1, source_target_pairs={{0,1},{1,0},{2,3},{3,2},{4,5},{5,4},{6,7},{7,6},{8,9},{9,8},{10,11... | collective-permute-start | bytes 958472 | tf_op jit(solution)/shard_map/ppermute | solution.py:579
  25.8 1.6 %collective-permute-start.4 = (bf16[96,1664]{1,0:T(8,128)(2,1)S(1)}, bf16[96,1664]{1,0:T(8,128)(2,1)S(1)}, u32[]{:S(2)}, u32[]{:S(2)}) collective-permute-start(bf16[96,1664]{1,0:T(8,128)(2,1)S(1)} %relay.1.refs_1_), channel_id=1, source_target_pairs={{0,1},{1,0},{2,3},{3,2},{4,5},{5,4},{6,7},{7,6},{8,9},{9,8},{10,11... | collective-permute-start | bytes 958472 | tf_op jit(solution)/shard_map/ppermute | solution.py:579
  27.4 17.1 %copy-start.1 = (s32[2]{0:T(128)S(1)}, s32[2]{0:T(128)}, u32[]{:S(2)}) copy-start(s32[2]{0:T(128)} %copy-done) | copy-start | bytes 28
  44.4 6.0 %collective-permute-start.5 = (bf16[96,3072]{1,0:T(8,128)(2,1)S(1)}, bf16[96,3072]{1,0:T(8,128)(2,1)S(1)}, u32[]{:S(2)}, u32[]{:S(2)}) collective-permute-start(bf16[96,3072]{1,0:T(8,128)(2,1)S(1)} %get-tuple-element.42), channel_id=1, source_target_pairs={{0,1},{1,0},{2,3},{3,2},{4,5},{5,4},{6,7},{7,6},{8,9},{9,8},{10,11... | collective-permute-start | bytes 1769480 | tf_op jit(solution)/shard_map/ppermute | solution.py:579
  50.6 9.4 %collective-permute-start.6 = (bf16[48,3072]{1,0:T(8,128)(2,1)S(1)}, bf16[48,3072]{1,0:T(8,128)(2,1)S(1)}, u32[]{:S(2)}, u32[]{:S(2)}) collective-permute-start(bf16[48,3072]{1,0:T(8,128)(2,1)S(1)} %get-tuple-element.44), channel_id=1, source_target_pairs={{0,2},{2,0},{4,6},{6,4},{8,10},{10,8},{12,14},{14,12},{1,3},{3,1},... | collective-permute-start | bytes 884744 | tf_op jit(solution)/shard_map/ppermute | solution.py:576
  60.0 5.4 %collective-permute-start.7 = (bf16[24,3072]{1,0:T(8,128)(2,1)S(1)}, bf16[24,3072]{1,0:T(8,128)(2,1)S(1)}, u32[]{:S(2)}, u32[]{:S(2)}) collective-permute-start(bf16[24,3072]{1,0:T(8,128)(2,1)S(1)} %get-tuple-element.46), channel_id=1, source_target_pairs={{0,4},{2,6},{4,0},{6,2},{8,12},{10,14},{12,8},{14,10},{1,5},{3,7},... | collective-permute-start | bytes 442376 | tf_op jit(solution)/shard_map/ppermute | solution.py:569
  65.4 6.1 %collective-permute-start.8 = (bf16[24,1536]{1,0:T(8,128)(2,1)S(1)}, bf16[24,1536]{1,0:T(8,128)(2,1)S(1)}, u32[]{:S(2)}, u32[]{:S(2)}) collective-permute-start(bf16[24,1536]{1,0:T(8,128)(2,1)S(1)} %get-tuple-element.48), channel_id=1, source_target_pairs={{0,8},{2,10},{4,12},{6,14},{8,0},{10,2},{12,4},{14,6},{1,9},{3,11}... | collective-permute-start | bytes 221192 | tf_op jit(solution)/shard_map/ppermute | solution.py:569

commit v3 on v2

v3 whole, which is shorter than its diff:
```python
import functools
import math

import jax
import jax.numpy as jnp
from jax import lax
from jax.experimental import pallas as pl
from jax.experimental.pallas import tpu as pltpu
from jax.sharding import PartitionSpec as P

QUERY_HEADS = 48
KV_HEADS = 8
HEAD_DIM = 128
EXPERTS = 4
GROUP = QUERY_HEADS // KV_HEADS
LANES = 128
FOLD = 2
MIB = 1 << 20
F32 = jnp.float32
BF16 = jnp.bfloat16


def whole_spec(array):
    zeros = (0,) * len(array.shape)
    return pl.BlockSpec(array.shape, lambda *_: zeros)


def small(shape, dtype):
    return math.prod(shape) * jnp.dtype(dtype).itemsize <= 17 * MIB // 4


def vmem_array(shape, dtype):
    return pltpu.VMEM(shape, dtype) if small(shape, dtype) else jax.ShapeDtypeStruct(shape, dtype)


def in_vmem(*arrays):
    return [
        pltpu.with_memory_space_constraint(a, pltpu.VMEM) if small(a.shape, a.dtype) else a
        for a in arrays
    ]


def in_hbm(*arrays):
    return [pltpu.with_memory_space_constraint(a, pltpu.HBM) for a in arrays]


VMEM_SPEC = pl.BlockSpec(memory_space=pltpu.VMEM)
SMEM_SPEC = pl.BlockSpec(memory_space=pltpu.SMEM)
HBM_SPEC = pl.BlockSpec(memory_space=pltpu.HBM)
ROUTE_LANE = 3 + 3 * EXPERTS
DOWN_DEPTH = 4


def row_unit(gate_weight):
    return gate_weight.shape[0] // 12


def weight_copies(pairs, first, rows, sems):
    parts = sems.shape[1]
    part = rows // parts
    copies = []
    for i in range(parts):
        for w, (source, target) in enumerate(pairs):
            copies.append(
                pltpu.make_async_copy(
                    source.at[pl.ds(pl.multiple_of(first + i * part, 16), part), :],
                    target.at[pl.ds(i * part, part), :], sems.at[w, i],
                )
            )
    return copies


def load_kernel(first, rows, place_ref, dep_ref, g_hbm, u_hbm, g_vmem, u_vmem, token_ref, sems):
    base = place_ref[0] * (g_hbm.shape[0] // 2) + first
    copies = weight_copies([(g_hbm, g_vmem), (u_hbm, u_vmem)], base, rows, sems)
    for copy in copies:
        copy.start()
    token_ref[...] = jnp.zeros_like(token_ref)
    for copy in copies:
        copy.wait()


def load_rows(first, rows, place, after, gate_weight, up_weight):
    hidden = gate_weight.shape[1]
    piece = pltpu.VMEM((rows, hidden), BF16)
    return pl.pallas_call(
        functools.partial(load_kernel, first, rows),
        out_shape=(piece, piece, pltpu.VMEM((8, LANES), F32)),
        in_specs=[SMEM_SPEC, pl.BlockSpec(memory_space=pl.ANY), HBM_SPEC, HBM_SPEC],
        out_specs=(VMEM_SPEC,) * 3,
        scratch_shapes=[pltpu.SemaphoreType.DMA((2, 4))],
        compiler_params=pltpu.CompilerParams(vmem_limit_bytes=MIB),
        cost_estimate=pl.CostEstimate(flops=0, bytes_accessed=4 * rows * hidden, transcendentals=0),
        name="load_weights",
    )(place, *in_vmem(after), *in_hbm(gate_weight, up_weight))


def join_kernel(a_ref, b_ref, token_ref, out_ref):
    out_ref[...] = jnp.concatenate(
        [a_ref[...].astype(F32), b_ref[...].astype(F32)], axis=0
    ).astype(BF16)


def join(a, b, token):
    return pl.pallas_call(
        join_kernel,
        out_shape=vmem_array((a.shape[0] + b.shape[0], a.shape[1]), BF16),
        in_specs=[VMEM_SPEC] * 3,
        out_specs=VMEM_SPEC,
        compiler_params=pltpu.CompilerParams(vmem_limit_bytes=(2 if a.shape[0] < 256 else 24) * MIB),
        name="join",
    )(*in_vmem(a, b, token))


def relay_kernel(count, *refs):
    del refs


def relay(arrays, token):
    count = len(arrays)
    return list(pl.pallas_call(
        functools.partial(relay_kernel, count),
        out_shape=tuple(pltpu.VMEM(a.shape, a.dtype) for a in arrays),
        in_specs=[VMEM_SPEC] * (count + 1),
        out_specs=(VMEM_SPEC,) * count,
        input_output_aliases={i: i for i in range(count)},
        compiler_params=pltpu.CompilerParams(vmem_limit_bytes=MIB),
        name="relay",
    )(*in_vmem(*arrays, token)))


def split_three(value):
    first = value.astype(BF16).astype(F32)
    second = (value - first).astype(BF16).astype(F32)
    return first, second, value - first - second


def attend_kernel(
    ahead,
    place_ref, len_ref, routes_ref, q_hbm, k_hbm, v_hbm, nk_hbm, nv_hbm, res_hbm, gain_hbm, rt_hbm,
    g_hbm, u_hbm,
    carried_ref, pay_ref, g_vmem, u_vmem,
    q_ref, k_ref, v_ref, nk_ref, nv_ref, res_ref, gain_ref, rt_ref,
    q_scr, o_scr, nk_scr, nv_scr, pay_scr, sems, w_sems,
):
    tok, width = q_ref.shape
    cache_len, kv_width = k_ref.shape[1], k_ref.shape[2]
    heads = width // HEAD_DIM
    groups = kv_width // HEAD_DIM
    fold_width = width // FOLD
    scaling = 1.0 / math.sqrt(HEAD_DIM)
    columns = pl.ds(pl.multiple_of(place_ref[0] * width, LANES), width)
    half = tok // 2
    first, rest = pl.ds(0, half), pl.ds(half, tok - half)
    moves = [
        (q_hbm, q_ref), (nk_hbm, nk_ref),
        (k_hbm.at[first], k_ref.at[first]), (k_hbm.at[rest], k_ref.at[rest]),
        (v_hbm.at[first], v_ref.at[first]), (v_hbm.at[rest], v_ref.at[rest]),
        (nv_hbm, nv_ref), (res_hbm, res_ref),
        (gain_hbm.at[:, columns], gain_ref), (rt_hbm.at[:, columns], rt_ref),
    ]
    copies = [pltpu.make_async_copy(a, b, sems.at[i]) for i, (a, b) in enumerate(moves)]
    for copy in copies:
        copy.start()
    weights = weight_copies(
        [(g_hbm, g_vmem), (u_hbm, u_vmem)], place_ref[0] * (g_hbm.shape[0] // 2), ahead, w_sems
    )
    for copy in weights:
        copy.start()
    copies[0].wait()
    copies[1].wait()
    for h in range(heads):
        q_scr[h * tok:(h + 1) * tok, :] = q_ref[:, h * HEAD_DIM:(h + 1) * HEAD_DIM].astype(F32)
    nk_scr[...] = nk_ref[...].astype(F32)
    row_group = lax.broadcasted_iota(jnp.int32, (heads, HEAD_DIM), 0) // GROUP
    position = lax.broadcasted_iota(jnp.int32, (heads, cache_len), 1)
    scores, fresh = [], []
    for t in range(tok):
        if t == 0:
            copies[2].wait()
        if t == half:
            copies[3].wait()
        q_rows = q_scr[pl.ds(t, heads, stride=tok), :]
        q_wide = jnp.concatenate(
            [jnp.where(row_group == g, q_rows, 0.0) for g in range(groups)], axis=1
        )
        scores.append(
            lax.dot_general(
                q_wide.astype(BF16), k_ref[t], (((1,), (1,)), ((), ())),
                preferred_element_type=F32,
            ) * scaling
        )
        fresh.append(
            jnp.sum(q_wide * nk_scr[pl.ds(t, 1), :], axis=1, keepdims=True) * scaling
        )
    terms, fresh_terms, totals = [], [], []
    for t in range(tok):
        score = jnp.where(position < len_ref[t], scores[t], -1e30)
        largest = jnp.maximum(jnp.max(score, axis=1, keepdims=True), fresh[t])
        term = jnp.exp(score - largest)
        fresh_term = jnp.exp(fresh[t] - largest)
        totals.append(jnp.sum(term, axis=1, keepdims=True) + fresh_term)
        terms.append(term.astype(BF16))
        fresh_terms.append(fresh_term.astype(BF16).astype(F32))
    copies[6].wait()
    nv_scr[...] = nv_ref[...].astype(F32)
    for t in range(tok):
        if t == 0:
            copies[4].wait()
        if t == half:
            copies[5].wait()
        wide = jnp.dot(terms[t], v_ref[t], preferred_element_type=F32)
        wide = wide + fresh_terms[t] * nv_scr[pl.ds(t, 1), :]
        picked = wide[:, :HEAD_DIM]
        for g in range(1, groups):
            picked = jnp.where(
                row_group == g, wide[:, g * HEAD_DIM:(g + 1) * HEAD_DIM], picked
            )
        o_scr[pl.ds(t, heads, stride=tok), :] = picked / totals[t]
    for copy in copies[7:]:
        copy.wait()
    for h in range(heads):
        cols = slice(h * HEAD_DIM, (h + 1) * HEAD_DIM)
        carried_ref[:, cols] = res_ref[:, cols].astype(F32) + o_scr[h * tok:(h + 1) * tok, :]
    carried = carried_ref[...]
    scaled = carried * gain_ref[...]
    rounded = scaled.astype(BF16).astype(F32)
    router = rt_ref[...].astype(F32)
    for f in range(FOLD):
        pay_scr[f * tok:(f + 1) * tok, :fold_width] = scaled[:, f * fold_width:(f + 1) * fold_width]
    lane = lax.broadcasted_iota(jnp.int32, (tok, LANES), 1)
    row = lax.broadcasted_iota(jnp.int32, (tok, LANES), 0)
    sums = [jnp.sum(carried * carried, axis=1, keepdims=True)]
    for e in range(EXPERTS):
        sums.append(jnp.sum(rounded * router[e:e + 1, :], axis=1, keepdims=True))
    extra = jnp.zeros((tok, LANES), F32)
    for i, total in enumerate(sums):
        for j, term in enumerate(split_three(total)):
            extra = jnp.where(lane == 3 * i + j, term, extra)
    for t in range(tok):
        for i in range(2):
            extra = jnp.where(
                jnp.logical_and(row == t, lane == ROUTE_LANE + i),
                routes_ref[i, t].astype(F32), extra,
            )
    for f in range(FOLD):
        pay_scr[f * tok:(f + 1) * tok, fold_width:] = extra
    pay_ref[...] = pay_scr[...].astype(BF16)
    for copy in weights:
        copy.wait()


def attend(
    ahead, place, lengths, routes_t, queries, key_cache, value_cache, new_key, new_value,
    residual, gain, router_t, gate_weight, up_weight,
):
    tok, width = queries.shape
    kv_width = new_key.shape[1]
    heads = width // HEAD_DIM
    wide = width // FOLD + LANES
    piece = pltpu.VMEM((ahead, gate_weight.shape[1]), BF16)
    here = [
        pltpu.VMEM(a.shape, a.dtype)
        for a in (queries, key_cache, value_cache, new_key, new_value, residual)
    ]
    return pl.pallas_call(
        functools.partial(attend_kernel, ahead),
        out_shape=(
            pltpu.VMEM((tok, width), F32),
            pltpu.VMEM((FOLD * tok, wide), BF16),
            piece,
            piece,
        ),
        in_specs=[SMEM_SPEC] * 3 + [HBM_SPEC] * 10,
        out_specs=(VMEM_SPEC,) * 4,
        scratch_shapes=here + [
            pltpu.VMEM((1, width), F32),
            pltpu.VMEM((EXPERTS, width), BF16),
            pltpu.VMEM((heads * tok, HEAD_DIM), F32),
            pltpu.VMEM((heads * tok, HEAD_DIM), F32),
            pltpu.VMEM((tok, kv_width), F32),
            pltpu.VMEM((tok, kv_width), F32),
            pltpu.VMEM((FOLD * tok, wide), F32),
            pltpu.SemaphoreType.DMA((10,)),
            pltpu.SemaphoreType.DMA((2, 2)),
        ],
        compiler_params=pltpu.CompilerParams(vmem_limit_bytes=10 * MIB),
        cost_estimate=pl.CostEstimate(flops=10**8, bytes_accessed=8 * 10**6, transcendentals=10**5),
        name="attend",
    )(
        place,
        *in_hbm(
            lengths, routes_t, queries, key_cache, value_cache, new_key, new_value, residual, gain, router_t,
            gate_weight, up_weight,
        ),
    )


def block_rows(arrays, swap, tok):
    per_array = arrays[0].shape[0] // (FOLD * tok)
    places = [(array, i * FOLD * tok) for array in arrays for i in range(per_array)]
    if swap:
        quarter = len(places) // 4
        places = (
            places[:quarter] + places[2 * quarter:3 * quarter]
            + places[quarter:2 * quarter] + places[3 * quarter:]
        )
    return places


def unfold(arrays, swap, tok, x_scr, f_scr):
    fold_width = f_scr.shape[1]
    for f in range(FOLD):
        for i, (array, start) in enumerate(block_rows(arrays, swap, tok)):
            block = array[start:start + FOLD * tok, :fold_width].astype(F32)
            f_scr[i * tok:(i + 1) * tok, :] = block[f * tok:(f + 1) * tok, :]
        x_scr[:, f * fold_width:(f + 1) * fold_width] = f_scr[...].astype(BF16)


def first_half_kernel(
    heights, tok, place_ref, a_ref, b_ref, *refs
):
    pieces = [refs[2 * i:2 * i + 2] for i in range(len(heights))]
    g_hbm, u_hbm, gate_ref, up_ref, *later, x_scr, f_scr, sems = refs[2 * len(heights):]
    half = g_hbm.shape[0] // 2
    copies = []
    for i in range(len(later) // 2):
        height = later[2 * i].shape[0]
        copies += weight_copies(
            [(g_hbm, later[2 * i]), (u_hbm, later[2 * i + 1])],
            (1 - place_ref[0]) * half + i * height, height, sems.at[i],
        )
    for copy in copies:
        copy.start()
    unfold([a_ref, b_ref], False, tok, x_scr, f_scr)
    first = 0
    for i, (height, (g_ref, u_ref)) in enumerate(zip(heights, pieces)):
        rows = x_scr[:, first:first + height]
        for weight, out in ((g_ref, gate_ref), (u_ref, up_ref)):
            part = jnp.dot(rows, weight[...], preferred_element_type=F32)
            out[...] = part if i == 0 else out[...] + part
        first += height
    for copy in copies:
        copy.wait()


def first_half(tok, place, mine, pieces, gate_weight, up_weight):
    heights = tuple(p[0].shape[0] for p in pieces)
    rows = sum(a.shape[0] for a in mine) // FOLD
    width, units = gate_weight.shape
    fold_width = mine[0].shape[1] - LANES
    acc, later = pltpu.VMEM((rows, units), F32), pltpu.VMEM((2 * row_unit(gate_weight), units), BF16)
    return pl.pallas_call(
        functools.partial(first_half_kernel, heights, tok),
        out_shape=(acc, acc, later, later),
        in_specs=[SMEM_SPEC] + [VMEM_SPEC] * (2 + 2 * len(heights)) + [HBM_SPEC] * 2,
        out_specs=(VMEM_SPEC,) * 4,
        scratch_shapes=[
            pltpu.VMEM((rows, width // 2), BF16),
            pltpu.VMEM((rows, fold_width), F32),
            pltpu.SemaphoreType.DMA((1, 2, 4)),
        ],
        compiler_params=pltpu.CompilerParams(vmem_limit_bytes=(6 if rows < 256 else 32) * MIB),
        cost_estimate=pl.CostEstimate(
            flops=2 * rows * width * units, bytes_accessed=width * units, transcendentals=0
        ),
        name="first_half",
    )(
        place, *in_vmem(*mine, *[p for pair in pieces for p in pair]),
        *in_hbm(gate_weight, up_weight),
    )


def second_half_kernel(
    tok, place_ref, a_ref, b_ref, oa_ref, ob_ref, gate_in, up_in, *refs
):
    (g_ref, u_ref, g_hbm, u_hbm, d_hbm, staying_ref, leaving_ref,
     x_scr, f_scr, gate_acc, up_acc, h_scr, gu_scr, ring, gu_sems, sems) = refs
    rows, units = gate_acc.shape
    width = staying_ref.shape[1]
    fold_width = f_scr.shape[1]
    side = place_ref[0]
    depth, d_block, d_wide = ring.shape
    k_steps, n_steps = units // d_block, width // d_wide
    total = 2 * n_steps * k_steps

    def down_copy(i):
        n, k = i // k_steps, i % k_steps
        half = jnp.where(n < n_steps, 1 - side, side)
        column = half * width + lax.rem(n, n_steps) * d_wide
        slot = lax.rem(i, depth)
        return pltpu.make_async_copy(
            d_hbm.at[
                pl.ds(pl.multiple_of(k * d_block, d_block), d_block),
                pl.ds(pl.multiple_of(column, LANES), d_wide),
            ],
            ring.at[slot], sems.at[slot],
        )

    height = g_ref.shape[0]
    blocks = gu_scr.shape[0]
    copies = [
        weight_copies(
            [(g_hbm, gu_scr.at[i, 0]), (u_hbm, gu_scr.at[i, 1])],
            (1 - side) * width + (i + 1) * height, height, gu_sems.at[i],
        )
        for i in range(blocks)
    ]
    for group in copies:
        for copy in group:
            copy.start()
    for i in range(min(depth, total)):
        down_copy(jnp.int32(i)).start()
    unfold([oa_ref, ob_ref], True, tok, x_scr, f_scr)
    part = x_scr[:, :height]
    gate_acc[...] = gate_in[...] + jnp.dot(part, g_ref[...], preferred_element_type=F32)
    up_acc[...] = up_in[...] + jnp.dot(part, u_ref[...], preferred_element_type=F32)
    for i in range(blocks):
        for copy in copies[i]:
            copy.wait()
        part = x_scr[:, (i + 1) * height:(i + 2) * height]
        gate_acc[...] += jnp.dot(part, gu_scr[i, 0], preferred_element_type=F32)
        up_acc[...] += jnp.dot(part, gu_scr[i, 1], preferred_element_type=F32)

    for at, arrays, swap in ((0, [a_ref, b_ref], False), (LANES, [oa_ref, ob_ref], True)):
        for i, (array, start) in enumerate(block_rows(arrays, swap, tok)):
            extra = array[start:start + FOLD * tok, fold_width:].astype(F32)
            f_scr[i * tok:(i + 1) * tok, at:at + LANES] = extra[:tok, :]
    own = f_scr[:, :LANES]
    both = own + f_scr[:, LANES:2 * LANES]
    lane = lax.broadcasted_iota(jnp.int32, (rows, LANES), 1)

    def pick(values, mask):
        return jnp.sum(jnp.where(mask, values, 0.0), axis=1, keepdims=True)

    scale = lax.rsqrt(pick(both, lane < 3) * (1.0 / (2 * width)) + 1e-05)
    first, second = pick(own, lane == ROUTE_LANE), pick(own, lane == ROUTE_LANE + 1)
    expert_of = (lane - 3) // 3
    logit_lane = jnp.logical_and(lane >= 3, lane < ROUTE_LANE)

    def logit_at(route):
        return pick(both, jnp.logical_and(logit_lane, expert_of == route.astype(jnp.int32))) * scale

    share = 1.0 / (1.0 + jnp.exp(logit_at(second) - logit_at(first)))
    here = place_ref[1].astype(F32)
    weight = jnp.where(first == here, share, 0.0) + jnp.where(second == here, 1.0 - share, 0.0)

    gate = gate_acc[...] * scale
    h_scr[...] = (gate / (1.0 + jnp.exp(-gate)) * (up_acc[...] * scale)).astype(BF16)

    def columns(n):
        value = None
        for k in range(k_steps):
            i = n * k_steps + k
            slot = lax.rem(i, depth)
            down_copy(i).wait()
            part = jnp.dot(
                h_scr[:, k * d_block:(k + 1) * d_block], ring[slot], preferred_element_type=F32
            )
            value = part if value is None else value + part

            @pl.when(i + depth < total)
            def _():
                down_copy(i + depth).start()

        return value * weight

    def leave(n, _):
        value = columns(n)
        quarter = rows // 4
        value = jnp.concatenate(
            [value[q * quarter:(q + 1) * quarter, :] for q in (0, 2, 1, 3)], axis=0
        )
        leaving_ref[:, pl.ds(pl.multiple_of(n * d_wide, LANES), d_wide)] = value.astype(BF16)
        return 0

    def stay(n, _):
        staying_ref[:, pl.ds(pl.multiple_of(n * d_wide, LANES), d_wide)] = columns(n + n_steps)
        return 0

    lax.fori_loop(0, n_steps, leave, 0)
    lax.fori_loop(0, n_steps, stay, 0)


def second_half(tok, place, mine, other, sums, weights, gate_weight, up_weight, down_weight):
    rows, units = sums[0].shape
    width = down_weight.shape[1] // 2
    fold_width = mine[0].shape[1] - LANES
    d_block, d_wide = math.gcd(1024, units), math.gcd(1536, width)
    total = 2 * (width // d_wide) * (units // d_block)
    depth = min(DOWN_DEPTH, total)
    height = weights[0].shape[0]
    blocks = width // height - 1
    return pl.pallas_call(
        functools.partial(second_half_kernel, tok),
        out_shape=(vmem_array((rows, width), F32), vmem_array((rows, width), BF16)),
        in_specs=[SMEM_SPEC] + [VMEM_SPEC] * 8 + [HBM_SPEC] * 3,
        out_specs=(VMEM_SPEC,) * 2,
        scratch_shapes=[
            pltpu.VMEM((rows, width), BF16),
            pltpu.VMEM((rows, fold_width), F32),
            pltpu.VMEM((rows, units), F32),
            pltpu.VMEM((rows, units), F32),
            pltpu.VMEM((rows, units), BF16),
            pltpu.VMEM((blocks, 2, height, units), BF16),
            pltpu.VMEM((depth, d_block, d_wide), BF16),
            pltpu.SemaphoreType.DMA((blocks, 2, 4)),
            pltpu.SemaphoreType.DMA((depth,)),
        ],
        compiler_params=pltpu.CompilerParams(vmem_limit_bytes=(38 if rows < 256 else 48) * MIB),
        cost_estimate=pl.CostEstimate(
            flops=6 * rows * width * units, bytes_accessed=4 * width * units, transcendentals=0
        ),
        name="second_half",
    )(
        place, *in_vmem(*mine, *other, *sums, *weights),
        *in_hbm(gate_weight, up_weight, down_weight),
    )


def split_kernel(fold, own_ref, got_ref, keep_ref, send_ref, total):
    total[...] = own_ref[...] + got_ref[...].astype(F32)
    size, width = keep_ref.shape
    keep_ref[...] = total[:size, :]
    part = total[size:, :]
    if fold:
        part = jnp.concatenate(
            [part[:, f * (width // FOLD):(f + 1) * (width // FOLD)] for f in range(FOLD)], axis=0
        )
    send_ref[...] = part.astype(BF16)


def split_rows(own, got, fold=False):
    rows, width = own.shape
    size = rows // 2
    sent = (FOLD * size, width // FOLD) if fold else (size, width)
    return pl.pallas_call(
        functools.partial(split_kernel, fold),
        out_shape=(vmem_array((size, width), F32), vmem_array(sent, BF16)),
        in_specs=[VMEM_SPEC] * 2,
        out_specs=(VMEM_SPEC,) * 2,
        scratch_shapes=[pltpu.VMEM((rows, width), F32)],
        compiler_params=pltpu.CompilerParams(vmem_limit_bytes=(8 if rows < 256 else 32) * MIB),
        name="split_rows",
    )(*in_vmem(own, got))


def finish_kernel(carried_ref, own_ref, got_ref, out_ref, folded):
    tok, width = carried_ref.shape
    fold_width = width // FOLD
    folded[...] = got_ref[...].astype(F32)
    for f in range(FOLD):
        at = slice(f * fold_width, (f + 1) * fold_width)
        value = carried_ref[:, at] + own_ref[:, at] + folded[f * tok:(f + 1) * tok, :]
        out_ref[:, at] = value.astype(BF16)


def finish(carried, own, got):
    tok, width = carried.shape
    return pl.pallas_call(
        finish_kernel,
        out_shape=jax.ShapeDtypeStruct((tok, width), BF16),
        in_specs=[VMEM_SPEC] * 3,
        out_specs=VMEM_SPEC,
        scratch_shapes=[pltpu.VMEM((FOLD * tok, width // FOLD), F32)],
        compiler_params=pltpu.CompilerParams(vmem_limit_bytes=8 * MIB),
        name="finish",
    )(*in_vmem(carried, own, got))


def on_device(
    residual, queries, key_cache, value_cache, new_key, new_value, cache_lengths,
    norm_gain, router, routes, gate_weight, up_weight, down_weight,
):
    nodes = lax.axis_size("node")
    per_plane = nodes // EXPERTS
    place = jnp.stack(
        [lax.axis_index("shard"), lax.axis_index("node") // per_plane]
    ).astype(jnp.int32)

    stages = nodes.bit_length() - 1
    masks = [nodes >> (s + 1) for s in range(stages)]
    routes_of = (masks, masks[:-2] + masks[:-3:-1])

    def exchange(array, stage):
        perm = [
            (2 * n + c, 2 * (n ^ routes_of[c][stage]) + c) for n in range(nodes) for c in range(2)
        ]
        return lax.ppermute(array, ("node", "shard"), perm)

    def to_core(array):
        return lax.ppermute(array, "shard", [(0, 1), (1, 0)])

    unit = row_unit(gate_weight)
    tok = residual.shape[0]
    heights = [unit, 2 * unit, unit, 2 * unit]
    held, payload, *piece = attend(
        heights[0], place, cache_lengths, routes.T, queries, key_cache, value_cache, new_key, new_value,
        residual, norm_gain.reshape(1, -1), router.T, gate_weight, up_weight,
    )
    carried, pieces, first, token = held, [piece], heights[0], None
    for stage in range(stages):
        got = exchange(payload, stage)
        if len(pieces) < len(heights):
            height = heights[len(pieces)]
            *piece, token = load_rows(first, height, place, payload, gate_weight, up_weight)
            pieces.append(piece)
            first += height
        if stage < stages - 1:
            payload = join(payload, got, token)
    mine = [payload, *relay([got], token)]
    other = [to_core(array) for array in mine]
    gate, up, *weights = first_half(tok, place, mine, pieces, gate_weight, up_weight)
    staying, leaving = second_half(
        tok, place, mine, other, (gate, up), weights, gate_weight, up_weight, down_weight
    )
    keep, send = split_rows(staying, to_core(leaving))
    for stage in range(stages - 1, 0, -1):
        keep, send = split_rows(keep, exchange(send, stage), fold=stage == 1)
    return finish(carried, keep, exchange(send, 0))


def solution(mesh):
    rows = ("replica", "node")
    in_specs = (
        P(rows, "shard"),
        P(rows, "shard"),
        P(rows, None, "shard"),
        P(rows, None, "shard"),
        P(rows, "shard"),
        P(rows, "shard"),
        P(rows),
        P(),
        P(),
        P(rows, None),
        P(None, ("node", "shard")),
        P(None, ("node", "shard")),
        P(("node", "shard"), None),
    )
    return jax.shard_map(
        on_device,
        mesh=mesh,
        in_specs=in_specs,
        out_specs=P(rows, "shard"),
        check_vma=False,
    )
```

time: 72.4 us -> 70.3 us (0.971)
  waiting for transfers between devices: 18.5 us -> 15.7 us
  Pallas kernels: 39.5 us -> 40.6 us
    ppermute x6, waiting for transfers between devices: 16.9 us -> 14.1 us  [exchange(): return lax.ppermute(array, ('node', 'shard'), perm)]
    pallas_call x11, Pallas kernels: 38.8 us -> 39.9 us  [the longest x1 16.8 us: second_half(): pl.pallas_call(functools.partial(second_half_kernel, tok), out_shape=(vme...]
    ppermute x6, starting transfers between devices: 13.8 us -> 13 us  [exchange(): return lax.ppermute(array, ('node', 'shard'), perm)]
  transfers between devices with their start and end apart: 9 -> 9, of which waited for: 7 -> 7; matrix products, arithmetic and copies ran while one was open for 0% -> 0% of each run, Pallas kernels for 24% -> 27%
where the time goes in v3:
time: 70.3 us; the launch traced here: 70.2 us
  Pallas kernels  40.6 us (58%)
  waiting for transfers between devices  15.7 us (22%)
  starting transfers between devices  13.7 us (19%)
    pallas_call x1, Pallas kernels, second_half(): pl.pallas_call(functools.partial(second_half_kernel, tok), out_shape=(vme...  16.8 us
    ppermute x6, waiting for transfers between devices, exchange(): return lax.ppermute(array, ('node', 'shard'), perm)  14.1 us
    ppermute x6, starting transfers between devices, exchange(): return lax.ppermute(array, ('node', 'shard'), perm)  13 us
    pallas_call x3, Pallas kernels, load_rows(): pl.pallas_call(functools.partial(load_kernel, first, rows), out_shape=(pi...  10.8 us
    pallas_call x1, Pallas kernels, first_half(): pl.pallas_call(functools.partial(first_half_kernel, heights, tok), out_sh...  8 us
    pallas_call x1, Pallas kernels, attend(): pl.pallas_call(functools.partial(attend_kernel, ahead), out_shape=(pltpu....  4.06 us
    ppermute x3, waiting for transfers between devices, to_core(): return lax.ppermute(array, 'shard', [(0, 1), (1, 0)])  1.64 us
  transfers between devices with their start and end apart: 9, of which 7 were waited for; matrix products, arithmetic and copies ran while one was open for 0% of the time, Pallas kernels for 27%

profile of v3, /device:TPU:0, one launch (start us, length us, event | category | flops | bytes accessed | tf_op | source)
XLA Modules:
  0.0 70.2 jit_solution(8611572286989071939)
XLA Ops:
  0.0 0.1 pad_add_fusion.place_ref
  0.1 4.1 %attend.1 = (f32[12,3072]{1,0:T(8,128)S(1)}, bf16[24,1664]{1,0:T(8,128)(2,1)S(1)}, bf16[512,2048]{1,0:T(8,128)(2,1)S(1)}, bf16[512,2048]{1,0:T(8,128)(2,1)S(1)}) custom-call(s32[2]{0:T(128)S(1)} %pad_add_fusion.place_ref, s32[12]{0:T(128)} %len_ref.1, s32[2,12]{1,0:T(2,128)} %bitcast.7, bf16[12,3072]{1,0:T(8,128)(2,1)} %q_hbm.1, ...), custom_call_target="tpu_custom_call" | custom-call | flops 100000000 | bytes 8000000 | tf_op jit(solution)/shard_map/attend/pallas_call | solution.py:266
  4.1 4.1 %collective-permute-start = (bf16[24,1664]{1,0:T(8,128)(2,1)S(1)}, bf16[24,1664]{1,0:T(8,128)(2,1)S(1)}, u32[]{:S(2)}, u32[]{:S(2)}) collective-permute-start(bf16[24,1664]{1,0:T(8,128)(2,1)S(1)} %get-tuple-element.31.dep_ref.a_ref), channel_id=1, source_target_pairs={{0,8},{1,9},{2,10},{3,11},{4,12},{5,13},{6,14},{7,15},{8,0},{9,1},... | collective-permute-start | bytes 239624 | tf_op jit(solution)/shard_map/ppermute | solution.py:589
  8.2 4.0 %load_weights.3 = (bf16[1024,2048]{1,0:T(8,128)(2,1)S(1)}, bf16[1024,2048]{1,0:T(8,128)(2,1)S(1)}, f32[8,128]{1,0:T(8,128)S(1)}) custom-call(s32[2]{0:T(128)S(1)} %pad_add_fusion.place_ref, bf16[24,1664]{1,0:T(8,128)(2,1)S(1)} %get-tuple-element.31.dep_ref.a_ref, bf16[6144,2048]{1,0:T(8,128)(2,1)} %refs_2_.1, bf16[6144,2048]{1,0:T(8,128)(2,1)} %refs_3_.1), custom_call_target="tpu_custom_call" | custom-call | bytes 8388608 | tf_op jit(solution)/shard_map/load_weights/pallas_call | solution.py:86
  12.3 0.1 collective-permute-done.b_ref
  12.4 1.6 %collective-permute-start.1 = (bf16[48,1664]{1,0:T(8,128)(2,1)S(1)}, bf16[48,1664]{1,0:T(8,128)(2,1)S(1)}, u32[]{:S(2)}, u32[]{:S(2)}) collective-permute-start(bf16[48,1664]{1,0:T(8,128)(2,1)S(1)} %join.2.dep_ref.a_ref), channel_id=1, source_target_pairs={{0,4},{1,3},{2,6},{3,1},{4,0},{5,7},{6,2},{7,5},{8,12},{9,11},{10,... | collective-permute-start | bytes 479240 | tf_op jit(solution)/shard_map/ppermute | solution.py:589
  13.9 2.8 %load_weights.4 = (bf16[512,2048]{1,0:T(8,128)(2,1)S(1)}, bf16[512,2048]{1,0:T(8,128)(2,1)S(1)}, f32[8,128]{1,0:T(8,128)S(1)}) custom-call(s32[2]{0:T(128)S(1)} %pad_add_fusion.place_ref, bf16[48,1664]{1,0:T(8,128)(2,1)S(1)} %join.2.dep_ref.a_ref, bf16[6144,2048]{1,0:T(8,128)(2,1)} %refs_2_.1, bf16[6144,2048]{1,0:T(8,128)(2,1)} %refs_3_.1), custom_call_target="tpu_custom_call" | custom-call | bytes 4194304 | tf_op jit(solution)/shard_map/load_weights/pallas_call | solution.py:86
  16.7 1.0 %collective-permute-done.1.b_ref = bf16[48,1664]{1,0:T(8,128)(2,1)S(1)} collective-permute-done((bf16[48,1664]{1,0:T(8,128)(2,1)S(1)}, bf16[48,1664]{1,0:T(8,128)(2,1)S(1)}, u32[]{:S(2)}, u32[]{:S(2)}) %collective-permute-start.1) | collective-permute-done | bytes 159776 | tf_op jit(solution)/shard_map/ppermute | solution.py:589
  17.7 1.8 %collective-permute-start.2 = (bf16[96,1664]{1,0:T(8,128)(2,1)S(1)}, bf16[96,1664]{1,0:T(8,128)(2,1)S(1)}, u32[]{:S(2)}, u32[]{:S(2)}) collective-permute-start(bf16[96,1664]{1,0:T(8,128)(2,1)S(1)} %join.3.dep_ref.a_ref), channel_id=1, source_target_pairs={{0,2},{1,5},{2,0},{3,7},{4,6},{5,1},{6,4},{7,3},{8,10},{9,13},{10,... | collective-permute-start | bytes 958472 | tf_op jit(solution)/shard_map/ppermute | solution.py:589
  19.5 4.0 %load_weights.5 = (bf16[1024,2048]{1,0:T(8,128)(2,1)S(1)}, bf16[1024,2048]{1,0:T(8,128)(2,1)S(1)}, f32[8,128]{1,0:T(8,128)S(1)}) custom-call(s32[2]{0:T(128)S(1)} %pad_add_fusion.place_ref, bf16[96,1664]{1,0:T(8,128)(2,1)S(1)} %join.3.dep_ref.a_ref, bf16[6144,2048]{1,0:T(8,128)(2,1)} %refs_2_.1, bf16[6144,2048]{1,0:T(8,128)(2,1)} %refs_3_.1), custom_call_target="tpu_custom_call" | custom-call | bytes 8388608 | tf_op jit(solution)/shard_map/load_weights/pallas_call | solution.py:86
  23.5 0.1 collective-permute-start.3
  23.6 1.2 %collective-permute-done.2.refs_0_ = bf16[96,1664]{1,0:T(8,128)(2,1)S(1)} collective-permute-done((bf16[96,1664]{1,0:T(8,128)(2,1)S(1)}, bf16[96,1664]{1,0:T(8,128)(2,1)S(1)}, u32[]{:S(2)}, u32[]{:S(2)}) %collective-permute-start.2) | collective-permute-done | bytes 319520 | tf_op jit(solution)/shard_map/ppermute | solution.py:589
  24.8 0.0 collective-permute-start.4
  24.8 8.0 %first_half.1 = (f32[96,2048]{1,0:T(8,128)S(1)}, f32[96,2048]{1,0:T(8,128)S(1)}, bf16[1024,2048]{1,0:T(8,128)(2,1)S(1)}, bf16[1024,2048]{1,0:T(8,128)(2,1)S(1)}) custom-call(s32[2]{0:T(128)S(1)} %pad_add_fusion.place_ref, bf16[96,1664]{1,0:T(8,128)(2,1)S(1)} %join.3.dep_ref.a_ref, bf16[96,1664]{1,0:T(8,128)(2,1)S(1)} %relay.1.b_ref, ...), custom_call_target="tpu_custom_call" | custom-call | flops 2415919104 | bytes 12582912 | tf_op jit(solution)/shard_map/first_half/pallas_call | solution.py:353
  32.8 0.0 collective-permute-done.3.oa_ref
  32.8 0.0 collective-permute-done.4.ob_ref
  32.8 16.8 %second_half.1 = (f32[96,3072]{1,0:T(8,128)S(1)}, bf16[96,3072]{1,0:T(8,128)(2,1)S(1)}) custom-call(s32[2]{0:T(128)S(1)} %pad_add_fusion.place_ref, bf16[96,1664]{1,0:T(8,128)(2,1)S(1)} %join.3.dep_ref.a_ref, bf16[96,1664]{1,0:T(8,128)(2,1)S(1)} %relay.1.b_ref, bf16[96,1664]{1,0:T(8,128)(2,1)S(1)} %collective-permute-done.3.oa_ref, ...), custom_call_target="tpu_custom_call" | custom-call | flops 3623878656 | bytes 25165824 | tf_op jit(solution)/shard_map/second_half/pallas_call | solution.py:494
  49.7 0.6 collective-permute-start.5
  50.3 1.6 %collective-permute-done.5.got_ref = bf16[96,3072]{1,0:T(8,128)(2,1)S(1)} collective-permute-done((bf16[96,3072]{1,0:T(8,128)(2,1)S(1)}, bf16[96,3072]{1,0:T(8,128)(2,1)S(1)}, u32[]{:S(2)}, u32[]{:S(2)}) %collective-permute-start.5) | collective-permute-done | bytes 589856 | tf_op jit(solution)/shard_map/ppermute | solution.py:592
  51.9 0.1 split_rows.3
  52.1 1.8 %collective-permute-start.6 = (bf16[48,3072]{1,0:T(8,128)(2,1)S(1)}, bf16[48,3072]{1,0:T(8,128)(2,1)S(1)}, u32[]{:S(2)}, u32[]{:S(2)}) collective-permute-start(bf16[48,3072]{1,0:T(8,128)(2,1)S(1)} %get-tuple-element.50), channel_id=1, source_target_pairs={{0,2},{1,5},{2,0},{3,7},{4,6},{5,1},{6,4},{7,3},{8,10},{9,13},{10,... | collective-permute-start | bytes 884744 | tf_op jit(solution)/shard_map/ppermute | solution.py:589
  53.8 5.0 %collective-permute-done.6.got_ref = bf16[48,3072]{1,0:T(8,128)(2,1)S(1)} collective-permute-done((bf16[48,3072]{1,0:T(8,128)(2,1)S(1)}, bf16[48,3072]{1,0:T(8,128)(2,1)S(1)}, u32[]{:S(2)}, u32[]{:S(2)}) %collective-permute-start.6) | collective-permute-done | bytes 294944 | tf_op jit(solution)/shard_map/ppermute | solution.py:589
  58.8 0.1 split_rows.4
  58.9 1.6 %collective-permute-start.7 = (bf16[24,3072]{1,0:T(8,128)(2,1)S(1)}, bf16[24,3072]{1,0:T(8,128)(2,1)S(1)}, u32[]{:S(2)}, u32[]{:S(2)}) collective-permute-start(bf16[24,3072]{1,0:T(8,128)(2,1)S(1)} %get-tuple-element.52), channel_id=1, source_target_pairs={{0,4},{1,3},{2,6},{3,1},{4,0},{5,7},{6,2},{7,5},{8,12},{9,11},{10,... | collective-permute-start | bytes 442376 | tf_op jit(solution)/shard_map/ppermute | solution.py:589
  60.5 3.6 %collective-permute-done.7.got_ref = bf16[24,3072]{1,0:T(8,128)(2,1)S(1)} collective-permute-done((bf16[24,3072]{1,0:T(8,128)(2,1)S(1)}, bf16[24,3072]{1,0:T(8,128)(2,1)S(1)}, u32[]{:S(2)}, u32[]{:S(2)}) %collective-permute-start.7) | collective-permute-done | bytes 147488 | tf_op jit(solution)/shard_map/ppermute | solution.py:589
  64.2 2.2 %collective-permute-start.8 = (bf16[24,1536]{1,0:T(8,128)(2,1)S(1)}, bf16[24,1536]{1,0:T(8,128)(2,1)S(1)}, u32[]{:S(2)}, u32[]{:S(2)}) collective-permute-start(bf16[24,1536]{1,0:T(8,128)(2,1)S(1)} %get-tuple-element.54), channel_id=1, source_target_pairs={{0,8},{1,9},{2,10},{3,11},{4,12},{5,13},{6,14},{7,15},{8,0},{9,1},... | collective-permute-start | bytes 221192 | tf_op jit(solution)/shard_map/ppermute | solution.py:589
  66.3 3.2 %collective-permute-done.8.got_ref = bf16[24,1536]{1,0:T(8,128)(2,1)S(1)} collective-permute-done((bf16[24,1536]{1,0:T(8,128)(2,1)S(1)}, bf16[24,1536]{1,0:T(8,128)(2,1)S(1)}, u32[]{:S(2)}, u32[]{:S(2)}) %collective-permute-start.8) | collective-permute-done | bytes 73760 | tf_op jit(solution)/shard_map/ppermute | solution.py:589
  69.5 0.7 finish.1
  (4 shorter events, 0.1 us)
Async XLA Ops:
  4.1 8.2 %collective-permute-start = (bf16[24,1664]{1,0:T(8,128)(2,1)S(1)}, bf16[24,1664]{1,0:T(8,128)(2,1)S(1)}, u32[]{:S(2)}, u32[]{:S(2)}) collective-permute-start(bf16[24,1664]{1,0:T(8,128)(2,1)S(1)} %get-tuple-element.31.dep_ref.a_ref), channel_id=1, source_target_pairs={{0,8},{1,9},{2,10},{3,11},{4,12},{5,13},{6,14},{7,15},{8,0},{9,1},... | collective-permute-start | bytes 239624 | tf_op jit(solution)/shard_map/ppermute | solution.py:589
  12.4 5.3 %collective-permute-start.1 = (bf16[48,1664]{1,0:T(8,128)(2,1)S(1)}, bf16[48,1664]{1,0:T(8,128)(2,1)S(1)}, u32[]{:S(2)}, u32[]{:S(2)}) collective-permute-start(bf16[48,1664]{1,0:T(8,128)(2,1)S(1)} %join.2.dep_ref.a_ref), channel_id=1, source_target_pairs={{0,4},{1,3},{2,6},{3,1},{4,0},{5,7},{6,2},{7,5},{8,12},{9,11},{10,... | collective-permute-start | bytes 479240 | tf_op jit(solution)/shard_map/ppermute | solution.py:589
  17.7 7.1 %collective-permute-start.2 = (bf16[96,1664]{1,0:T(8,128)(2,1)S(1)}, bf16[96,1664]{1,0:T(8,128)(2,1)S(1)}, u32[]{:S(2)}, u32[]{:S(2)}) collective-permute-start(bf16[96,1664]{1,0:T(8,128)(2,1)S(1)} %join.3.dep_ref.a_ref), channel_id=1, source_target_pairs={{0,2},{1,5},{2,0},{3,7},{4,6},{5,1},{6,4},{7,3},{8,10},{9,13},{10,... | collective-permute-start | bytes 958472 | tf_op jit(solution)/shard_map/ppermute | solution.py:589
  23.5 9.3 %collective-permute-start.3 = (bf16[96,1664]{1,0:T(8,128)(2,1)S(1)}, bf16[96,1664]{1,0:T(8,128)(2,1)S(1)}, u32[]{:S(2)}, u32[]{:S(2)}) collective-permute-start(bf16[96,1664]{1,0:T(8,128)(2,1)S(1)} %join.3.dep_ref.a_ref), channel_id=1, source_target_pairs={{0,1},{1,0},{2,3},{3,2},{4,5},{5,4},{6,7},{7,6},{8,9},{9,8},{10,11... | collective-permute-start | bytes 958472 | tf_op jit(solution)/shard_map/ppermute | solution.py:592
  24.8 8.0 %collective-permute-start.4 = (bf16[96,1664]{1,0:T(8,128)(2,1)S(1)}, bf16[96,1664]{1,0:T(8,128)(2,1)S(1)}, u32[]{:S(2)}, u32[]{:S(2)}) collective-permute-start(bf16[96,1664]{1,0:T(8,128)(2,1)S(1)} %relay.1.b_ref), channel_id=1, source_target_pairs={{0,1},{1,0},{2,3},{3,2},{4,5},{5,4},{6,7},{7,6},{8,9},{9,8},{10,11... | collective-permute-start | bytes 958472 | tf_op jit(solution)/shard_map/ppermute | solution.py:592
  49.7 2.3 %collective-permute-start.5 = (bf16[96,3072]{1,0:T(8,128)(2,1)S(1)}, bf16[96,3072]{1,0:T(8,128)(2,1)S(1)}, u32[]{:S(2)}, u32[]{:S(2)}) collective-permute-start(bf16[96,3072]{1,0:T(8,128)(2,1)S(1)} %get-tuple-element.48), channel_id=1, source_target_pairs={{0,1},{1,0},{2,3},{3,2},{4,5},{5,4},{6,7},{7,6},{8,9},{9,8},{10,11... | collective-permute-start | bytes 1769480 | tf_op jit(solution)/shard_map/ppermute | solution.py:592
  52.1 6.8 %collective-permute-start.6 = (bf16[48,3072]{1,0:T(8,128)(2,1)S(1)}, bf16[48,3072]{1,0:T(8,128)(2,1)S(1)}, u32[]{:S(2)}, u32[]{:S(2)}) collective-permute-start(bf16[48,3072]{1,0:T(8,128)(2,1)S(1)} %get-tuple-element.50), channel_id=1, source_target_pairs={{0,2},{1,5},{2,0},{3,7},{4,6},{5,1},{6,4},{7,3},{8,10},{9,13},{10,... | collective-permute-start | bytes 884744 | tf_op jit(solution)/shard_map/ppermute | solution.py:589
  58.9 5.2 %collective-permute-start.7 = (bf16[24,3072]{1,0:T(8,128)(2,1)S(1)}, bf16[24,3072]{1,0:T(8,128)(2,1)S(1)}, u32[]{:S(2)}, u32[]{:S(2)}) collective-permute-start(bf16[24,3072]{1,0:T(8,128)(2,1)S(1)} %get-tuple-element.52), channel_id=1, source_target_pairs={{0,4},{1,3},{2,6},{3,1},{4,0},{5,7},{6,2},{7,5},{8,12},{9,11},{10,... | collective-permute-start | bytes 442376 | tf_op jit(solution)/shard_map/ppermute | solution.py:589
  64.2 5.3 %collective-permute-start.8 = (bf16[24,1536]{1,0:T(8,128)(2,1)S(1)}, bf16[24,1536]{1,0:T(8,128)(2,1)S(1)}, u32[]{:S(2)}, u32[]{:S(2)}) collective-permute-start(bf16[24,1536]{1,0:T(8,128)(2,1)S(1)} %get-tuple-element.54), channel_id=1, source_target_pairs={{0,8},{1,9},{2,10},{3,11},{4,12},{5,13},{6,14},{7,15},{8,0},{9,1},... | collective-permute-start | bytes 221192 | tf_op jit(solution)/shard_map/ppermute | solution.py:589

commit v4 on v3

v4 whole, which is shorter than its diff:
```python
import functools
import math

import jax
import jax.numpy as jnp
from jax import lax
from jax.experimental import pallas as pl
from jax.experimental.pallas import tpu as pltpu
from jax.sharding import PartitionSpec as P

QUERY_HEADS = 48
KV_HEADS = 8
HEAD_DIM = 128
EXPERTS = 4
GROUP = QUERY_HEADS // KV_HEADS
LANES = 128
FOLD = 2
MIB = 1 << 20
F32 = jnp.float32
BF16 = jnp.bfloat16


def whole_spec(array):
    zeros = (0,) * len(array.shape)
    return pl.BlockSpec(array.shape, lambda *_: zeros)


def small(shape, dtype):
    return math.prod(shape) * jnp.dtype(dtype).itemsize <= 17 * MIB // 4


def vmem_array(shape, dtype):
    return pltpu.VMEM(shape, dtype) if small(shape, dtype) else jax.ShapeDtypeStruct(shape, dtype)


def in_vmem(*arrays):
    return [
        pltpu.with_memory_space_constraint(a, pltpu.VMEM) if small(a.shape, a.dtype) else a
        for a in arrays
    ]


def in_hbm(*arrays):
    return [pltpu.with_memory_space_constraint(a, pltpu.HBM) for a in arrays]


VMEM_SPEC = pl.BlockSpec(memory_space=pltpu.VMEM)
SMEM_SPEC = pl.BlockSpec(memory_space=pltpu.SMEM)
HBM_SPEC = pl.BlockSpec(memory_space=pltpu.HBM)
ROUTE_LANE = 3 + 3 * EXPERTS
GATE_DEPTH = 4
DOWN_DEPTH = 4


def row_unit(gate_weight):
    return gate_weight.shape[0] // 12


def pair_copies(sources, targets, first, rows, sems):
    at = pl.ds(pl.multiple_of(first, 16), rows)
    return [
        pltpu.make_async_copy(source.at[at, :], target, sems.at[i])
        for i, (source, target) in enumerate(zip(sources, targets))
    ]


def split_three(value):
    first = value.astype(BF16).astype(F32)
    second = (value - first).astype(BF16).astype(F32)
    return first, second, value - first - second


def attend_kernel(
    place_ref, len_ref, routes_ref, q_hbm, k_hbm, v_hbm, nk_hbm, nv_hbm, res_hbm, gain_hbm, rt_hbm,
    carried_ref, pay_ref,
    q_ref, k_ref, v_ref, nk_ref, nv_ref, res_ref, gain_ref, rt_ref,
    q_scr, o_scr, nk_scr, nv_scr, pay_scr, sems,
):
    tok, width = q_ref.shape
    cache_len, kv_width = k_ref.shape[1], k_ref.shape[2]
    heads = width // HEAD_DIM
    groups = kv_width // HEAD_DIM
    fold_width = width // FOLD
    scaling = 1.0 / math.sqrt(HEAD_DIM)
    columns = pl.ds(pl.multiple_of(place_ref[0] * width, LANES), width)
    half = tok // 2
    first, rest = pl.ds(0, half), pl.ds(half, tok - half)
    moves = [
        (q_hbm, q_ref), (nk_hbm, nk_ref),
        (k_hbm.at[first], k_ref.at[first]), (k_hbm.at[rest], k_ref.at[rest]),
        (v_hbm.at[first], v_ref.at[first]), (v_hbm.at[rest], v_ref.at[rest]),
        (nv_hbm, nv_ref), (res_hbm, res_ref),
        (gain_hbm.at[:, columns], gain_ref), (rt_hbm.at[:, columns], rt_ref),
    ]
    copies = [pltpu.make_async_copy(a, b, sems.at[i]) for i, (a, b) in enumerate(moves)]
    for copy in copies:
        copy.start()
    copies[0].wait()
    copies[1].wait()
    for h in range(heads):
        q_scr[h * tok:(h + 1) * tok, :] = q_ref[:, h * HEAD_DIM:(h + 1) * HEAD_DIM].astype(F32)
    nk_scr[...] = nk_ref[...].astype(F32)
    row_group = lax.broadcasted_iota(jnp.int32, (heads, HEAD_DIM), 0) // GROUP
    position = lax.broadcasted_iota(jnp.int32, (heads, cache_len), 1)
    scores, fresh = [], []
    for t in range(tok):
        if t == 0:
            copies[2].wait()
        if t == half:
            copies[3].wait()
        q_rows = q_scr[pl.ds(t, heads, stride=tok), :]
        q_wide = jnp.concatenate(
            [jnp.where(row_group == g, q_rows, 0.0) for g in range(groups)], axis=1
        )
        scores.append(
            lax.dot_general(
                q_wide.astype(BF16), k_ref[t], (((1,), (1,)), ((), ())),
                preferred_element_type=F32,
            ) * scaling
        )
        fresh.append(
            jnp.sum(q_wide * nk_scr[pl.ds(t, 1), :], axis=1, keepdims=True) * scaling
        )
    terms, fresh_terms, totals = [], [], []
    for t in range(tok):
        score = jnp.where(position < len_ref[t], scores[t], -1e30)
        largest = jnp.maximum(jnp.max(score, axis=1, keepdims=True), fresh[t])
        term = jnp.exp(score - largest)
        fresh_term = jnp.exp(fresh[t] - largest)
        totals.append(jnp.sum(term, axis=1, keepdims=True) + fresh_term)
        terms.append(term.astype(BF16))
        fresh_terms.append(fresh_term.astype(BF16).astype(F32))
    copies[6].wait()
    nv_scr[...] = nv_ref[...].astype(F32)
    for t in range(tok):
        if t == 0:
            copies[4].wait()
        if t == half:
            copies[5].wait()
        wide = jnp.dot(terms[t], v_ref[t], preferred_element_type=F32)
        wide = wide + fresh_terms[t] * nv_scr[pl.ds(t, 1), :]
        picked = wide[:, :HEAD_DIM]
        for g in range(1, groups):
            picked = jnp.where(
                row_group == g, wide[:, g * HEAD_DIM:(g + 1) * HEAD_DIM], picked
            )
        o_scr[pl.ds(t, heads, stride=tok), :] = picked / totals[t]
    for copy in copies[7:]:
        copy.wait()
    for h in range(heads):
        cols = slice(h * HEAD_DIM, (h + 1) * HEAD_DIM)
        carried_ref[:, cols] = res_ref[:, cols].astype(F32) + o_scr[h * tok:(h + 1) * tok, :]
    carried = carried_ref[...]
    scaled = carried * gain_ref[...]
    rounded = scaled.astype(BF16).astype(F32)
    router = rt_ref[...].astype(F32)
    for f in range(FOLD):
        pay_scr[f * tok:(f + 1) * tok, :fold_width] = scaled[:, f * fold_width:(f + 1) * fold_width]
    lane = lax.broadcasted_iota(jnp.int32, (tok, LANES), 1)
    row = lax.broadcasted_iota(jnp.int32, (tok, LANES), 0)
    sums = [jnp.sum(carried * carried, axis=1, keepdims=True)]
    for e in range(EXPERTS):
        sums.append(jnp.sum(rounded * router[e:e + 1, :], axis=1, keepdims=True))
    extra = jnp.zeros((tok, LANES), F32)
    for i, total in enumerate(sums):
        for j, term in enumerate(split_three(total)):
            extra = jnp.where(lane == 3 * i + j, term, extra)
    for t in range(tok):
        for i in range(2):
            extra = jnp.where(
                jnp.logical_and(row == t, lane == ROUTE_LANE + i),
                routes_ref[i, t].astype(F32), extra,
            )
    for f in range(FOLD):
        pay_scr[f * tok:(f + 1) * tok, fold_width:] = extra
    pay_ref[...] = pay_scr[...].astype(BF16)


def attend(
    place, lengths, routes_t, queries, key_cache, value_cache, new_key, new_value,
    residual, gain, router_t,
):
    tok, width = queries.shape
    kv_width = new_key.shape[1]
    heads = width // HEAD_DIM
    wide = width // FOLD + LANES
    here = [
        pltpu.VMEM(a.shape, a.dtype)
        for a in (queries, key_cache, value_cache, new_key, new_value, residual)
    ]
    return pl.pallas_call(
        attend_kernel,
        out_shape=(
            pltpu.VMEM((tok, width), F32),
            pltpu.VMEM((FOLD * tok, wide), BF16),
        ),
        in_specs=[SMEM_SPEC] * 3 + [HBM_SPEC] * 8,
        out_specs=(VMEM_SPEC,) * 2,
        scratch_shapes=here + [
            pltpu.VMEM((1, width), F32),
            pltpu.VMEM((EXPERTS, width), BF16),
            pltpu.VMEM((heads * tok, HEAD_DIM), F32),
            pltpu.VMEM((heads * tok, HEAD_DIM), F32),
            pltpu.VMEM((tok, kv_width), F32),
            pltpu.VMEM((tok, kv_width), F32),
            pltpu.VMEM((FOLD * tok, wide), F32),
            pltpu.SemaphoreType.DMA((10,)),
        ],
        compiler_params=pltpu.CompilerParams(vmem_limit_bytes=10 * MIB),
        cost_estimate=pl.CostEstimate(flops=10**8, bytes_accessed=8 * 10**6, transcendentals=10**5),
        name="attend",
    )(
        place,
        *in_hbm(
            lengths, routes_t, queries, key_cache, value_cache, new_key, new_value, residual, gain, router_t,
        ),
    )


def sources_of(place_ref, count):
    out = []
    for r in range(count):
        left, right = ((sum(m for t, m in enumerate(side) if r >> t & 1)) for side in stage_masks(count))
        out.append(lax.bitwise_xor(place_ref[2], jnp.where(place_ref[0] == 0, left, right)))
    return out


def unfold(place_ref, array, x_scr, f_scr):
    count = array.shape[0]
    tok = array.shape[1] // FOLD
    fold_width = f_scr.shape[1]
    block = x_scr.shape[2]
    per_fold = fold_width // block
    sources = sources_of(place_ref, count)
    for f in range(FOLD):
        for i, source in enumerate(sources):
            rows = array[source][:, :fold_width].astype(F32)
            f_scr[i * tok:(i + 1) * tok, :] = rows[f * tok:(f + 1) * tok, :]
        for p in range(per_fold):
            x_scr[f * per_fold + p] = f_scr[:, p * block:(p + 1) * block].astype(BF16)


def first_half_kernel(
    place_ref, mine_ref, g_hbm, u_hbm, gate_ref, up_ref, g_next, u_next, x_scr, f_scr, ring, sems, next_sems
):
    width = g_hbm.shape[0] // 2
    depth, _, block, _ = ring.shape
    steps = width // block
    base = place_ref[0] * width

    def copies(k):
        slot = lax.rem(k, depth)
        return pair_copies(
            (g_hbm, u_hbm), (ring.at[slot, 0], ring.at[slot, 1]), base + k * block, block, sems.at[slot]
        )

    for k in range(min(depth, steps)):
        for copy in copies(jnp.int32(k)):
            copy.start()
    following = pair_copies(
        (g_hbm, u_hbm), (g_next, u_next), (1 - place_ref[0]) * width, block, next_sems
    )
    unfold(place_ref, mine_ref, x_scr, f_scr)
    gate_ref[...] = jnp.zeros_like(gate_ref)
    up_ref[...] = jnp.zeros_like(up_ref)

    def step(k, _):
        slot = lax.rem(k, depth)
        for copy in copies(k):
            copy.wait()
        gate_ref[...] += jnp.dot(x_scr[k], ring[slot, 0], preferred_element_type=F32)
        up_ref[...] += jnp.dot(x_scr[k], ring[slot, 1], preferred_element_type=F32)

        @pl.when(k + depth < steps)
        def _():
            for copy in copies(k + depth):
                copy.start()

        @pl.when(k + depth == max(steps, depth))
        def _():
            for copy in following:
                copy.start()

        return 0

    lax.fori_loop(0, steps, step, 0)
    for copy in following:
        copy.wait()


def first_half(place, mine, gate_weight, up_weight):
    count, folded, wide = mine.shape
    rows, fold_width = count * folded // FOLD, wide - LANES
    width, units = gate_weight.shape
    block = math.gcd(512, fold_width)
    steps = width // 2 // block
    depth = min(GATE_DEPTH, steps)
    acc, later = pltpu.VMEM((rows, units), F32), pltpu.VMEM((block, units), BF16)
    return pl.pallas_call(
        first_half_kernel,
        out_shape=(acc, acc, later, later),
        in_specs=[SMEM_SPEC, VMEM_SPEC] + [HBM_SPEC] * 2,
        out_specs=(VMEM_SPEC,) * 4,
        scratch_shapes=[
            pltpu.VMEM((steps, rows, block), BF16),
            pltpu.VMEM((rows, fold_width), F32),
            pltpu.VMEM((depth, 2, block, units), BF16),
            pltpu.SemaphoreType.DMA((depth, 2)),
            pltpu.SemaphoreType.DMA((2,)),
        ],
        compiler_params=pltpu.CompilerParams(vmem_limit_bytes=(24 if rows < 256 else 40) * MIB),
        cost_estimate=pl.CostEstimate(
            flops=2 * rows * width * units, bytes_accessed=2 * width * units, transcendentals=0
        ),
        name="first_half",
    )(place, *in_vmem(mine), *in_hbm(gate_weight, up_weight))


def second_half_kernel(
    place_ref, mine_ref, other_ref, gate_in, up_in, g_ref, u_ref, g_hbm, u_hbm, d_hbm,
    staying_ref, leaving_ref,
    x_scr, f_scr, gate_acc, up_acc, h_scr, gu_ring, ring, gu_sems, sems,
):
    rows, units = gate_acc.shape
    width = staying_ref.shape[1]
    count = mine_ref.shape[0]
    tok = rows // count
    fold_width = f_scr.shape[1]
    side = place_ref[0]
    depth, _, d_wide = ring.shape
    per_side = width // d_wide
    total = 2 * per_side
    gu_depth, _, block, _ = gu_ring.shape
    steps = width // block
    base = (1 - side) * width

    def gu_copies(k):
        slot = lax.rem(k - 1, gu_depth)
        return pair_copies(
            (g_hbm, u_hbm), (gu_ring.at[slot, 0], gu_ring.at[slot, 1]), base + k * block, block,
            gu_sems.at[slot],
        )

    def down_copy(n):
        half = jnp.where(n < per_side, 1 - side, side)
        column = half * width + lax.rem(n, per_side) * d_wide
        slot = lax.rem(n, depth)
        return pltpu.make_async_copy(
            d_hbm.at[:, pl.ds(pl.multiple_of(column, LANES), d_wide)], ring.at[slot], sems.at[slot]
        )

    for k in range(1, 1 + min(gu_depth, steps - 1)):
        for copy in gu_copies(jnp.int32(k)):
            copy.start()
    unfold(place_ref, other_ref, x_scr, f_scr)
    gate_acc[...] = gate_in[...] + jnp.dot(x_scr[0], g_ref[...], preferred_element_type=F32)
    up_acc[...] = up_in[...] + jnp.dot(x_scr[0], u_ref[...], preferred_element_type=F32)

    def step(k, _):
        slot = lax.rem(k - 1, gu_depth)
        for copy in gu_copies(k):
            copy.wait()
        gate_acc[...] += jnp.dot(x_scr[k], gu_ring[slot, 0], preferred_element_type=F32)
        up_acc[...] += jnp.dot(x_scr[k], gu_ring[slot, 1], preferred_element_type=F32)

        @pl.when(k + gu_depth < steps)
        def _():
            for copy in gu_copies(k + gu_depth):
                copy.start()

        ahead = k + gu_depth - steps

        @pl.when(jnp.logical_and(ahead >= 0, ahead < depth))
        def _():
            down_copy(ahead).start()

        return 0

    lax.fori_loop(1, steps, step, 0)
    for n in range(max(0, min(gu_depth, steps - 1)), depth):
        down_copy(jnp.int32(n)).start()

    for i, source in enumerate(sources_of(place_ref, count)):
        for at, array in ((0, mine_ref), (LANES, other_ref)):
            extra = array[source][:, fold_width:].astype(F32)
            f_scr[i * tok:(i + 1) * tok, at:at + LANES] = extra[:tok, :]
    own = f_scr[:, :LANES]
    both = own + f_scr[:, LANES:2 * LANES]
    lane = lax.broadcasted_iota(jnp.int32, (rows, LANES), 1)

    def pick(values, mask):
        return jnp.sum(jnp.where(mask, values, 0.0), axis=1, keepdims=True)

    scale = lax.rsqrt(pick(both, lane < 3) * (1.0 / (2 * width)) + 1e-05)
    first, second = pick(own, lane == ROUTE_LANE), pick(own, lane == ROUTE_LANE + 1)
    expert_of = (lane - 3) // 3
    logit_lane = jnp.logical_and(lane >= 3, lane < ROUTE_LANE)

    def logit_at(route):
        return pick(both, jnp.logical_and(logit_lane, expert_of == route.astype(jnp.int32))) * scale

    share = 1.0 / (1.0 + jnp.exp(logit_at(second) - logit_at(first)))
    here = place_ref[1].astype(F32)
    weight = jnp.where(first == here, share, 0.0) + jnp.where(second == here, 1.0 - share, 0.0)

    gate = gate_acc[...] * scale
    h_scr[...] = (gate / (1.0 + jnp.exp(-gate)) * (up_acc[...] * scale)).astype(BF16)

    def columns(n, _):
        slot = lax.rem(n, depth)
        down_copy(n).wait()
        value = jnp.dot(h_scr[...], ring[slot], preferred_element_type=F32) * weight
        to = pl.ds(pl.multiple_of(lax.rem(n, per_side) * d_wide, LANES), d_wide)

        @pl.when(n + depth < total)
        def _():
            down_copy(n + depth).start()

        @pl.when(n < per_side)
        def _():
            quarter = rows // 4
            leaving_ref[:, to] = jnp.concatenate(
                [value[q * quarter:(q + 1) * quarter, :] for q in (0, 2, 1, 3)], axis=0
            ).astype(BF16)

        @pl.when(n >= per_side)
        def _():
            staying_ref[:, to] = value

        return 0

    lax.fori_loop(0, total, columns, 0)


def second_half(place, mine, other, sums, weights, gate_weight, up_weight, down_weight):
    rows, units = sums[0].shape
    width = down_weight.shape[1] // 2
    fold_width = mine.shape[2] - LANES
    d_wide = math.gcd(768, width)
    depth = min(DOWN_DEPTH, 2 * (width // d_wide))
    block = weights[0].shape[0]
    steps = width // block
    gu_depth = min(GATE_DEPTH, steps - 1)
    return pl.pallas_call(
        second_half_kernel,
        out_shape=(vmem_array((rows, width), F32), vmem_array((rows, width), BF16)),
        in_specs=[SMEM_SPEC] + [VMEM_SPEC] * 6 + [HBM_SPEC] * 3,
        out_specs=(VMEM_SPEC,) * 2,
        scratch_shapes=[
            pltpu.VMEM((steps, rows, block), BF16),
            pltpu.VMEM((rows, fold_width), F32),
            pltpu.VMEM((rows, units), F32),
            pltpu.VMEM((rows, units), F32),
            pltpu.VMEM((rows, units), BF16),
            pltpu.VMEM((gu_depth, 2, block, units), BF16),
            pltpu.VMEM((depth, units, d_wide), BF16),
            pltpu.SemaphoreType.DMA((gu_depth, 2)),
            pltpu.SemaphoreType.DMA((depth,)),
        ],
        compiler_params=pltpu.CompilerParams(vmem_limit_bytes=(38 if rows < 256 else 48) * MIB),
        cost_estimate=pl.CostEstimate(
            flops=6 * rows * width * units, bytes_accessed=4 * width * units, transcendentals=0
        ),
        name="second_half",
    )(
        place, *in_vmem(mine, other, *sums, *weights),
        *in_hbm(gate_weight, up_weight, down_weight),
    )


def split_kernel(fold, own_ref, got_ref, keep_ref, send_ref, total):
    total[...] = own_ref[...] + got_ref[...].astype(F32)
    size, width = keep_ref.shape
    keep_ref[...] = total[:size, :]
    part = total[size:, :]
    if fold:
        part = jnp.concatenate(
            [part[:, f * (width // FOLD):(f + 1) * (width // FOLD)] for f in range(FOLD)], axis=0
        )
    send_ref[...] = part.astype(BF16)


def split_rows(own, got, fold=False):
    rows, width = own.shape
    size = rows // 2
    sent = (FOLD * size, width // FOLD) if fold else (size, width)
    return pl.pallas_call(
        functools.partial(split_kernel, fold),
        out_shape=(vmem_array((size, width), F32), vmem_array(sent, BF16)),
        in_specs=[VMEM_SPEC] * 2,
        out_specs=(VMEM_SPEC,) * 2,
        scratch_shapes=[pltpu.VMEM((rows, width), F32)],
        compiler_params=pltpu.CompilerParams(vmem_limit_bytes=(8 if rows < 256 else 32) * MIB),
        name="split_rows",
    )(*in_vmem(own, got))


def finish_kernel(carried_ref, own_ref, got_ref, out_ref, folded):
    tok, width = carried_ref.shape
    fold_width = width // FOLD
    folded[...] = got_ref[...].astype(F32)
    for f in range(FOLD):
        at = slice(f * fold_width, (f + 1) * fold_width)
        value = carried_ref[:, at] + own_ref[:, at] + folded[f * tok:(f + 1) * tok, :]
        out_ref[:, at] = value.astype(BF16)


def finish(carried, own, got):
    tok, width = carried.shape
    return pl.pallas_call(
        finish_kernel,
        out_shape=jax.ShapeDtypeStruct((tok, width), BF16),
        in_specs=[VMEM_SPEC] * 3,
        out_specs=VMEM_SPEC,
        scratch_shapes=[pltpu.VMEM((FOLD * tok, width // FOLD), F32)],
        compiler_params=pltpu.CompilerParams(vmem_limit_bytes=8 * MIB),
        name="finish",
    )(*in_vmem(carried, own, got))


def stage_masks(nodes):
    masks = [nodes >> (s + 1) for s in range(nodes.bit_length() - 1)]
    return masks, masks[:-2] + masks[:-3:-1]


def on_device(
    residual, queries, key_cache, value_cache, new_key, new_value, cache_lengths,
    norm_gain, router, routes, gate_weight, up_weight, down_weight,
):
    nodes = lax.axis_size("node")
    per_plane = nodes // EXPERTS
    place = jnp.stack(
        [lax.axis_index("shard"), lax.axis_index("node") // per_plane, lax.axis_index("node")]
    ).astype(jnp.int32)

    stages = nodes.bit_length() - 1
    routes_of = stage_masks(nodes)

    def exchange(array, stage):
        perm = [
            (2 * n + c, 2 * (n ^ routes_of[c][stage]) + c) for n in range(nodes) for c in range(2)
        ]
        return lax.ppermute(array, ("node", "shard"), perm)

    def to_core(array):
        return lax.ppermute(array, "shard", [(0, 1), (1, 0)])

    carried, payload = attend(
        place, cache_lengths, routes.T, queries, key_cache, value_cache, new_key, new_value,
        residual, norm_gain.reshape(1, -1), router.T,
    )
    mine = lax.all_gather(payload, "node")
    other = to_core(mine)
    gate, up, *weights = first_half(place, mine, gate_weight, up_weight)
    staying, leaving = second_half(
        place, mine, other, (gate, up), weights, gate_weight, up_weight, down_weight
    )
    keep, send = split_rows(staying, to_core(leaving))
    for stage in range(stages - 1, 0, -1):
        keep, send = split_rows(keep, exchange(send, stage), fold=stage == 1)
    return finish(carried, keep, exchange(send, 0))


def solution(mesh):
    rows = ("replica", "node")
    in_specs = (
        P(rows, "shard"),
        P(rows, "shard"),
        P(rows, None, "shard"),
        P(rows, None, "shard"),
        P(rows, "shard"),
        P(rows, "shard"),
        P(rows),
        P(),
        P(),
        P(rows, None),
        P(None, ("node", "shard")),
        P(None, ("node", "shard")),
        P(("node", "shard"), None),
    )
    return jax.shard_map(
        on_device,
        mesh=mesh,
        in_specs=in_specs,
        out_specs=P(rows, "shard"),
        check_vma=False,
    )
```

time: 70.3 us -> 85.2 us (1.21)
  blocking collectives: 0 us -> 33.4 us
  starting transfers between devices: 13.7 us -> 3.91 us
  Pallas kernels: 40.6 us -> 31.3 us
    all_gather x0 -> x1, blocking collectives: none -> 33.4 us  [on_device(): mine = lax.all_gather(payload, 'node')]
    ppermute x6 -> x3, starting transfers between devices: 13 us -> 3.33 us  [exchange(): return lax.ppermute(array, ('node', 'shard'), perm)]
    pallas_call x9 -> x3, Pallas kernels: 39.7 us -> 30.4 us  [the longest x1 16.4 us: second_half(): pl.pallas_call(second_half_kernel, out_shape=(vmem_array((rows, width), F...]
    ppermute x6 -> x3, waiting for transfers between devices: 14.1 us -> 14.8 us  [exchange(): return lax.ppermute(array, ('node', 'shard'), perm)]
  transfers between devices with their start and end apart: 9 -> 5, of which waited for: 7 -> 4; matrix products, arithmetic and copies ran while one was open for 0% -> 0% of each run, Pallas kernels for 27% -> 12%
where the time goes in v4:
time: 85.2 us; the launch traced here: 85 us
  blocking collectives  33.4 us (39%)
  Pallas kernels  31.3 us (37%)
  waiting for transfers between devices  16.4 us (19%)
  starting transfers between devices  3.91 us (5%)
    all_gather x1, blocking collectives, on_device(): mine = lax.all_gather(payload, 'node')  33.4 us
    pallas_call x1, Pallas kernels, second_half(): pl.pallas_call(second_half_kernel, out_shape=(vmem_array((rows, width), F...  16.4 us
    ppermute x3, waiting for transfers between devices, exchange(): return lax.ppermute(array, ('node', 'shard'), perm)  14.8 us
    pallas_call x1, Pallas kernels, first_half(): pl.pallas_call(first_half_kernel, out_shape=(acc, acc, later, later), in_...  10.2 us
    pallas_call x1, Pallas kernels, attend(): pl.pallas_call(attend_kernel, out_shape=(pltpu.VMEM((tok, width), F32), p...  3.66 us
    ppermute x3, starting transfers between devices, exchange(): return lax.ppermute(array, ('node', 'shard'), perm)  3.33 us
  transfers between devices with their start and end apart: 5, of which 4 were waited for; matrix products, arithmetic and copies ran while one was open for 0% of the time, Pallas kernels for 12%

profile of v4, /device:TPU:0, one launch (start us, length us, event | category | flops | bytes accessed | tf_op | source)
XLA Modules:
  0.0 85.0 jit_solution(15789404096777018025)
XLA Ops:
  0.0 0.1 pad_add_fusion.place_ref
  0.1 3.7 %attend.1 = (f32[12,3072]{1,0:T(8,128)S(1)}, bf16[24,1664]{1,0:T(8,128)(2,1)S(1)}) custom-call(s32[3]{0:T(128)S(1)} %pad_add_fusion.place_ref, s32[12]{0:T(128)} %len_ref.1, s32[2,12]{1,0:T(2,128)} %bitcast.12, bf16[12,3072]{1,0:T(8,128)(2,1)} %q_hbm.1, bf16[12,128,512]{2,1,0:T(8,128)(2,1)} %k_hbm.1, bf16[12,128,512]{2,1,0:T(8,128)(2,1)} %v_hbm.1, ...), custom_call_target="tpu_custom_call" | custom-call | flops 100000000 | bytes 8000000 | tf_op jit(solution)/shard_map/attend/pallas_call | solution.py:191
  3.7 33.4 %all-gather = bf16[192,1664]{1,0:T(8,128)(2,1)S(1)} all-gather(bf16[24,1664]{1,0:T(8,128)(2,1)S(1)} %get-tuple-element.20), channel_id=2, replica_groups=mesh['replica'=2,'node'=8,'shard'=2] {'node'}, dimensions={0}, use_global_device_ids=true | all-gather | bytes 718848 | tf_op jit(solution)/shard_map/all_gather | solution.py:552
  37.1 0.0 collective-permute-start
  37.1 10.2 %first_half.1 = (f32[96,2048]{1,0:T(8,128)S(1)}, f32[96,2048]{1,0:T(8,128)S(1)}, bf16[512,2048]{1,0:T(8,128)(2,1)S(1)}, bf16[512,2048]{1,0:T(8,128)(2,1)S(1)}) custom-call(s32[3]{0:T(128)S(1)} %pad_add_fusion.place_ref, bf16[8,24,1664]{2,1,0:T(8,128)(2,1)S(1)} %bitcast.8, bf16[6144,2048]{1,0:T(8,128)(2,1)} %g_hbm.3, bf16[6144,2048]{1,0:T(8,128)(2,1)} %u_hbm.3), custom_call_target="tpu_custom_call" | custom-call | flops 2415919104 | bytes 25165824 | tf_op jit(solution)/shard_map/first_half/pallas_call | solution.py:299
  47.4 0.0 collective-permute-done.other_ref
  47.4 16.4 %second_half.1 = (f32[96,3072]{1,0:T(8,128)S(1)}, bf16[96,3072]{1,0:T(8,128)(2,1)S(1)}) custom-call(s32[3]{0:T(128)S(1)} %pad_add_fusion.place_ref, bf16[8,24,1664]{2,1,0:T(8,128)(2,1)S(1)} %bitcast.9, bf16[8,24,1664]{2,1,0:T(8,128)(2,1)S(1)} %collective-permute-done.other_ref, f32[96,2048]{1,0:T(8,128)S(1)} %get-tuple-element.21.gate_in, ...), custom_call_target="tpu_custom_call" | custom-call | flops 3623878656 | bytes 25165824 | tf_op jit(solution)/shard_map/second_half/pallas_call | solution.py:444
  63.8 0.6 collective-permute-start.1
  64.4 1.6 %collective-permute-done.1.got_ref = bf16[96,3072]{1,0:T(8,128)(2,1)S(1)} collective-permute-done((bf16[96,3072]{1,0:T(8,128)(2,1)S(1)}, bf16[96,3072]{1,0:T(8,128)(2,1)S(1)}, u32[]{:S(2)}, u32[]{:S(2)}) %collective-permute-start.1) | collective-permute-done | bytes 589856 | tf_op jit(solution)/shard_map/ppermute | solution.py:546
  66.0 0.1 split_rows.3
  66.2 1.7 %collective-permute-start.2 = (bf16[48,3072]{1,0:T(8,128)(2,1)S(1)}, bf16[48,3072]{1,0:T(8,128)(2,1)S(1)}, u32[]{:S(2)}, u32[]{:S(2)}) collective-permute-start(bf16[48,3072]{1,0:T(8,128)(2,1)S(1)} %get-tuple-element.28), channel_id=1, source_target_pairs={{0,2},{1,5},{2,0},{3,7},{4,6},{5,1},{6,4},{7,3},{8,10},{9,13},{10,... | collective-permute-start | bytes 884744 | tf_op jit(solution)/shard_map/ppermute | solution.py:543
  67.9 5.0 %collective-permute-done.2.got_ref = bf16[48,3072]{1,0:T(8,128)(2,1)S(1)} collective-permute-done((bf16[48,3072]{1,0:T(8,128)(2,1)S(1)}, bf16[48,3072]{1,0:T(8,128)(2,1)S(1)}, u32[]{:S(2)}, u32[]{:S(2)}) %collective-permute-start.2) | collective-permute-done | bytes 294944 | tf_op jit(solution)/shard_map/ppermute | solution.py:543
  72.9 0.1 split_rows.4
  73.0 0.1 collective-permute-start.3
  73.1 5.1 %collective-permute-done.3.got_ref = bf16[24,3072]{1,0:T(8,128)(2,1)S(1)} collective-permute-done((bf16[24,3072]{1,0:T(8,128)(2,1)S(1)}, bf16[24,3072]{1,0:T(8,128)(2,1)S(1)}, u32[]{:S(2)}, u32[]{:S(2)}) %collective-permute-start.3) | collective-permute-done | bytes 147488 | tf_op jit(solution)/shard_map/ppermute | solution.py:543
  78.3 1.5 %collective-permute-start.4 = (bf16[24,1536]{1,0:T(8,128)(2,1)S(1)}, bf16[24,1536]{1,0:T(8,128)(2,1)S(1)}, u32[]{:S(2)}, u32[]{:S(2)}) collective-permute-start(bf16[24,1536]{1,0:T(8,128)(2,1)S(1)} %get-tuple-element.32), channel_id=1, source_target_pairs={{0,8},{1,9},{2,10},{3,11},{4,12},{5,13},{6,14},{7,15},{8,0},{9,1},... | collective-permute-start | bytes 221192 | tf_op jit(solution)/shard_map/ppermute | solution.py:543
  79.8 4.6 %collective-permute-done.4.got_ref = bf16[24,1536]{1,0:T(8,128)(2,1)S(1)} collective-permute-done((bf16[24,1536]{1,0:T(8,128)(2,1)S(1)}, bf16[24,1536]{1,0:T(8,128)(2,1)S(1)}, u32[]{:S(2)}, u32[]{:S(2)}) %collective-permute-start.4) | collective-permute-done | bytes 73760 | tf_op jit(solution)/shard_map/ppermute | solution.py:543
  84.4 0.7 finish.1
  (1 shorter events, 0.0 us)
Async XLA Ops:
  37.1 10.3 %collective-permute-start = (bf16[8,24,1664]{2,1,0:T(8,128)(2,1)S(1)}, bf16[8,24,1664]{2,1,0:T(8,128)(2,1)S(1)}, u32[]{:S(2)}, u32[]{:S(2)}) collective-permute-start(bf16[8,24,1664]{2,1,0:T(8,128)(2,1)S(1)} %bitcast.7), channel_id=1, source_target_pairs={{0,1},{1,0},{2,3},{3,2},{4,5},{5,4},{6,7},{7,6},{8,9},{9,8},{10,11... | collective-permute-start | bytes 1916936 | tf_op jit(solution)/shard_map/ppermute | solution.py:546
  63.8 2.2 %collective-permute-start.1 = (bf16[96,3072]{1,0:T(8,128)(2,1)S(1)}, bf16[96,3072]{1,0:T(8,128)(2,1)S(1)}, u32[]{:S(2)}, u32[]{:S(2)}) collective-permute-start(bf16[96,3072]{1,0:T(8,128)(2,1)S(1)} %get-tuple-element.26), channel_id=1, source_target_pairs={{0,1},{1,0},{2,3},{3,2},{4,5},{5,4},{6,7},{7,6},{8,9},{9,8},{10,11... | collective-permute-start | bytes 1769480 | tf_op jit(solution)/shard_map/ppermute | solution.py:546
  66.2 6.8 %collective-permute-start.2 = (bf16[48,3072]{1,0:T(8,128)(2,1)S(1)}, bf16[48,3072]{1,0:T(8,128)(2,1)S(1)}, u32[]{:S(2)}, u32[]{:S(2)}) collective-permute-start(bf16[48,3072]{1,0:T(8,128)(2,1)S(1)} %get-tuple-element.28), channel_id=1, source_target_pairs={{0,2},{1,5},{2,0},{3,7},{4,6},{5,1},{6,4},{7,3},{8,10},{9,13},{10,... | collective-permute-start | bytes 884744 | tf_op jit(solution)/shard_map/ppermute | solution.py:543
  73.0 5.2 %collective-permute-start.3 = (bf16[24,3072]{1,0:T(8,128)(2,1)S(1)}, bf16[24,3072]{1,0:T(8,128)(2,1)S(1)}, u32[]{:S(2)}, u32[]{:S(2)}) collective-permute-start(bf16[24,3072]{1,0:T(8,128)(2,1)S(1)} %get-tuple-element.30), channel_id=1, source_target_pairs={{0,4},{1,3},{2,6},{3,1},{4,0},{5,7},{6,2},{7,5},{8,12},{9,11},{10,... | collective-permute-start | bytes 442376 | tf_op jit(solution)/shard_map/ppermute | solution.py:543
  78.3 6.1 %collective-permute-start.4 = (bf16[24,1536]{1,0:T(8,128)(2,1)S(1)}, bf16[24,1536]{1,0:T(8,128)(2,1)S(1)}, u32[]{:S(2)}, u32[]{:S(2)}) collective-permute-start(bf16[24,1536]{1,0:T(8,128)(2,1)S(1)} %get-tuple-element.32), channel_id=1, source_target_pairs={{0,8},{1,9},{2,10},{3,11},{4,12},{5,13},{6,14},{7,15},{8,0},{9,1},... | collective-permute-start | bytes 221192 | tf_op jit(solution)/shard_map/ppermute | solution.py:543

commit v5 on v3

--- a/solution.py
+++ b/solution.py
@@ -40,6 +40,10 @@
     ]
 
 
+def in_vmem_always(arrays):
+    return [pltpu.with_memory_space_constraint(a, pltpu.VMEM) for a in arrays]
+
+
 def in_hbm(*arrays):
     return [pltpu.with_memory_space_constraint(a, pltpu.HBM) for a in arrays]
 
@@ -48,6 +52,7 @@
 SMEM_SPEC = pl.BlockSpec(memory_space=pltpu.SMEM)
 HBM_SPEC = pl.BlockSpec(memory_space=pltpu.HBM)
 ROUTE_LANE = 3 + 3 * EXPERTS
+READY = 4
 DOWN_DEPTH = 4
 
 
@@ -55,24 +60,29 @@
     return gate_weight.shape[0] // 12
 
 
-def weight_copies(pairs, first, rows, sems):
+def own_side():
+    return lax.axis_index("shard")
+
+
+def pair_copies(sources, first, targets, to, rows, sems):
     parts = sems.shape[1]
     part = rows // parts
-    copies = []
-    for i in range(parts):
-        for w, (source, target) in enumerate(pairs):
-            copies.append(
-                pltpu.make_async_copy(
-                    source.at[pl.ds(pl.multiple_of(first + i * part, 16), part), :],
-                    target.at[pl.ds(i * part, part), :], sems.at[w, i],
-                )
-            )
-    return copies
-
-
-def load_kernel(first, rows, place_ref, dep_ref, g_hbm, u_hbm, g_vmem, u_vmem, token_ref, sems):
-    base = place_ref[0] * (g_hbm.shape[0] // 2) + first
-    copies = weight_copies([(g_hbm, g_vmem), (u_hbm, u_vmem)], base, rows, sems)
+    return [
+        pltpu.make_async_copy(
+            source.at[pl.ds(pl.multiple_of(first + p * part, 16), part), :],
+            target.at[pl.ds(to + p * part, part), :], sems.at[i, p],
+        )
+        for p in range(parts) for i, (source, target) in enumerate(zip(sources, targets))
+    ]
+
+
+def load_kernel(first, rows, dep_ref, *refs):
+    g_hbm, u_hbm, g_in, u_in, g_vmem, u_vmem, token_ref, sems = refs
+    del dep_ref, g_in, u_in
+    half = g_hbm.shape[0] // 2
+    copies = pair_copies(
+        (g_hbm, u_hbm), own_side() * half + first, (g_vmem, u_vmem), first, rows, sems
+    )
     for copy in copies:
         copy.start()
     token_ref[...] = jnp.zeros_like(token_ref)
@@ -80,19 +90,19 @@
         copy.wait()
 
 
-def load_rows(first, rows, place, after, gate_weight, up_weight):
+def load_rows(first, rows, after, gate_weight, up_weight, held):
     hidden = gate_weight.shape[1]
-    piece = pltpu.VMEM((rows, hidden), BF16)
     return pl.pallas_call(
-        functools.partial(load_kernel, first, rows),
-        out_shape=(piece, piece, pltpu.VMEM((8, LANES), F32)),
-        in_specs=[SMEM_SPEC, pl.BlockSpec(memory_space=pl.ANY), HBM_SPEC, HBM_SPEC],
+        lambda *refs: load_kernel(first, rows, *refs),
+        out_shape=tuple(pltpu.VMEM(h.shape, BF16) for h in held) + (pltpu.VMEM((8, LANES), F32),),
+        in_specs=[pl.BlockSpec(memory_space=pl.ANY), HBM_SPEC, HBM_SPEC, VMEM_SPEC, VMEM_SPEC],
         out_specs=(VMEM_SPEC,) * 3,
         scratch_shapes=[pltpu.SemaphoreType.DMA((2, 4))],
+        input_output_aliases={3: 0, 4: 1},
         compiler_params=pltpu.CompilerParams(vmem_limit_bytes=MIB),
         cost_estimate=pl.CostEstimate(flops=0, bytes_accessed=4 * rows * hidden, transcendentals=0),
         name="load_weights",
-    )(place, *in_vmem(after), *in_hbm(gate_weight, up_weight))
+    )(*in_vmem(after), *in_hbm(gate_weight, up_weight), *in_vmem_always(held))
 
 
 def join_kernel(a_ref, b_ref, token_ref, out_ref):
@@ -137,11 +147,11 @@
 
 def attend_kernel(
     ahead,
-    place_ref, len_ref, routes_ref, q_hbm, k_hbm, v_hbm, nk_hbm, nv_hbm, res_hbm, gain_hbm, rt_hbm,
+    len_hbm, routes_hbm, q_hbm, k_hbm, v_hbm, nk_hbm, nv_hbm, res_hbm, gain_hbm, rt_hbm,
     g_hbm, u_hbm,
     carried_ref, pay_ref, g_vmem, u_vmem,
     q_ref, k_ref, v_ref, nk_ref, nv_ref, res_ref, gain_ref, rt_ref,
-    q_scr, o_scr, nk_scr, nv_scr, pay_scr, sems, w_sems,
+    q_scr, o_scr, nk_scr, nv_scr, pay_scr, len_ref, routes_ref, sems, w_sems,
 ):
     tok, width = q_ref.shape
     cache_len, kv_width = k_ref.shape[1], k_ref.shape[2]
@@ -149,7 +159,7 @@
     groups = kv_width // HEAD_DIM
     fold_width = width // FOLD
     scaling = 1.0 / math.sqrt(HEAD_DIM)
-    columns = pl.ds(pl.multiple_of(place_ref[0] * width, LANES), width)
+    columns = pl.ds(pl.multiple_of(own_side() * width, LANES), width)
     half = tok // 2
     first, rest = pl.ds(0, half), pl.ds(half, tok - half)
     moves = [
@@ -158,12 +168,13 @@
         (v_hbm.at[first], v_ref.at[first]), (v_hbm.at[rest], v_ref.at[rest]),
         (nv_hbm, nv_ref), (res_hbm, res_ref),
         (gain_hbm.at[:, columns], gain_ref), (rt_hbm.at[:, columns], rt_ref),
+        (len_hbm, len_ref), (routes_hbm, routes_ref),
     ]
     copies = [pltpu.make_async_copy(a, b, sems.at[i]) for i, (a, b) in enumerate(moves)]
     for copy in copies:
         copy.start()
-    weights = weight_copies(
-        [(g_hbm, g_vmem), (u_hbm, u_vmem)], place_ref[0] * (g_hbm.shape[0] // 2), ahead, w_sems
+    weights = pair_copies(
+        (g_hbm, u_hbm), own_side() * (g_hbm.shape[0] // 2), (g_vmem, u_vmem), 0, ahead, w_sems
     )
     for copy in weights:
         copy.start()
@@ -193,6 +204,7 @@
         fresh.append(
             jnp.sum(q_wide * nk_scr[pl.ds(t, 1), :], axis=1, keepdims=True) * scaling
         )
+    copies[10].wait()
     terms, fresh_terms, totals = [], [], []
     for t in range(tok):
         score = jnp.where(position < len_ref[t], scores[t], -1e30)
@@ -217,7 +229,7 @@
                 row_group == g, wide[:, g * HEAD_DIM:(g + 1) * HEAD_DIM], picked
             )
         o_scr[pl.ds(t, heads, stride=tok), :] = picked / totals[t]
-    for copy in copies[7:]:
+    for copy in copies[7:10] + copies[11:]:
         copy.wait()
     for h in range(heads):
         cols = slice(h * HEAD_DIM, (h + 1) * HEAD_DIM)
@@ -251,14 +263,14 @@
 
 
 def attend(
-    ahead, place, lengths, routes_t, queries, key_cache, value_cache, new_key, new_value,
+    ahead, lengths, routes_t, queries, key_cache, value_cache, new_key, new_value,
     residual, gain, router_t, gate_weight, up_weight,
 ):
     tok, width = queries.shape
     kv_width = new_key.shape[1]
     heads = width // HEAD_DIM
     wide = width // FOLD + LANES
-    piece = pltpu.VMEM((ahead, gate_weight.shape[1]), BF16)
+    piece = pltpu.VMEM((gate_weight.shape[0] // 2, gate_weight.shape[1]), BF16)
     here = [
         pltpu.VMEM(a.shape, a.dtype)
         for a in (queries, key_cache, value_cache, new_key, new_value, residual)
@@ -271,7 +283,7 @@
             piece,
             piece,
         ),
-        in_specs=[SMEM_SPEC] * 3 + [HBM_SPEC] * 10,
+        in_specs=[HBM_SPEC] * 12,
         out_specs=(VMEM_SPEC,) * 4,
         scratch_shapes=here + [
             pltpu.VMEM((1, width), F32),
@@ -281,14 +293,15 @@
             pltpu.VMEM((tok, kv_width), F32),
             pltpu.VMEM((tok, kv_width), F32),
             pltpu.VMEM((FOLD * tok, wide), F32),
-            pltpu.SemaphoreType.DMA((10,)),
+            pltpu.SMEM(lengths.shape, jnp.int32),
+            pltpu.SMEM(routes_t.shape, jnp.int32),
+            pltpu.SemaphoreType.DMA((12,)),
             pltpu.SemaphoreType.DMA((2, 2)),
         ],
         compiler_params=pltpu.CompilerParams(vmem_limit_bytes=10 * MIB),
         cost_estimate=pl.CostEstimate(flops=10**8, bytes_accessed=8 * 10**6, transcendentals=10**5),
         name="attend",
     )(
-        place,
         *in_hbm(
             lengths, routes_t, queries, key_cache, value_cache, new_key, new_value, residual, gain, router_t,
             gate_weight, up_weight,
@@ -310,117 +323,130 @@
 
 def unfold(arrays, swap, tok, x_scr, f_scr):
     fold_width = f_scr.shape[1]
+    block = x_scr.shape[2]
+    per_fold = fold_width // block
     for f in range(FOLD):
         for i, (array, start) in enumerate(block_rows(arrays, swap, tok)):
-            block = array[start:start + FOLD * tok, :fold_width].astype(F32)
-            f_scr[i * tok:(i + 1) * tok, :] = block[f * tok:(f + 1) * tok, :]
-        x_scr[:, f * fold_width:(f + 1) * fold_width] = f_scr[...].astype(BF16)
+            rows = array[start:start + FOLD * tok, :fold_width].astype(F32)
+            f_scr[i * tok:(i + 1) * tok, :] = rows[f * tok:(f + 1) * tok, :]
+        for p in range(per_fold):
+            x_scr[f * per_fold + p] = f_scr[:, p * block:(p + 1) * block].astype(BF16)
+
+
+def add_block(x_scr, k, g_ref, u_ref, at, gate_acc, up_acc):
+    gate_acc[...] += jnp.dot(x_scr[k], g_ref[at, :], preferred_element_type=F32)
+    up_acc[...] += jnp.dot(x_scr[k], u_ref[at, :], preferred_element_type=F32)
+
+
+def other_copies(sources, targets, k, block, sems):
+    width = targets[0].shape[0]
+    at = pl.ds(pl.multiple_of(k * block, block), block)
+    first = pl.multiple_of((1 - own_side()) * width + k * block, block)
+    return [
+        pltpu.make_async_copy(source.at[pl.ds(first, block), :], target.at[at, :], sems.at[i, k])
+        for i, (source, target) in enumerate(zip(sources, targets))
+    ]
 
 
 def first_half_kernel(
-    heights, tok, place_ref, a_ref, b_ref, *refs
+    tok, ready, a_ref, b_ref, g_hbm, u_hbm, g_in, u_in,
+    gate_ref, up_ref, g_ref, u_ref, x_scr, f_scr, sems,
 ):
-    pieces = [refs[2 * i:2 * i + 2] for i in range(len(heights))]
-    g_hbm, u_hbm, gate_ref, up_ref, *later, x_scr, f_scr, sems = refs[2 * len(heights):]
-    half = g_hbm.shape[0] // 2
-    copies = []
-    for i in range(len(later) // 2):
-        height = later[2 * i].shape[0]
-        copies += weight_copies(
-            [(g_hbm, later[2 * i]), (u_hbm, later[2 * i + 1])],
-            (1 - place_ref[0]) * half + i * height, height, sems.at[i],
-        )
-    for copy in copies:
-        copy.start()
+    del g_in, u_in
+    steps, _, block = x_scr.shape
     unfold([a_ref, b_ref], False, tok, x_scr, f_scr)
-    first = 0
-    for i, (height, (g_ref, u_ref)) in enumerate(zip(heights, pieces)):
-        rows = x_scr[:, first:first + height]
-        for weight, out in ((g_ref, gate_ref), (u_ref, up_ref)):
-            part = jnp.dot(rows, weight[...], preferred_element_type=F32)
-            out[...] = part if i == 0 else out[...] + part
-        first += height
-    for copy in copies:
-        copy.wait()
-
-
-def first_half(tok, place, mine, pieces, gate_weight, up_weight):
-    heights = tuple(p[0].shape[0] for p in pieces)
+    gate_ref[...] = jnp.zeros_like(gate_ref)
+    up_ref[...] = jnp.zeros_like(up_ref)
+
+    def step(k, _):
+        at = pl.ds(pl.multiple_of(k * block, block), block)
+        add_block(x_scr, k, g_ref, u_ref, at, gate_ref, up_ref)
+
+        @pl.when(k < ready)
+        def _():
+            for copy in other_copies((g_hbm, u_hbm), (g_ref, u_ref), k, block, sems):
+                copy.start()
+
+        return 0
+
+    lax.fori_loop(0, steps, step, 0)
+    for k in range(ready):
+        for copy in other_copies((g_hbm, u_hbm), (g_ref, u_ref), k, block, sems):
+            copy.wait()
+
+
+def first_half(tok, mine, held, gate_weight, up_weight):
     rows = sum(a.shape[0] for a in mine) // FOLD
     width, units = gate_weight.shape
     fold_width = mine[0].shape[1] - LANES
-    acc, later = pltpu.VMEM((rows, units), F32), pltpu.VMEM((2 * row_unit(gate_weight), units), BF16)
+    block = math.gcd(512, fold_width)
+    steps = width // 2 // block
+    acc = pltpu.VMEM((rows, units), F32)
     return pl.pallas_call(
-        functools.partial(first_half_kernel, heights, tok),
-        out_shape=(acc, acc, later, later),
-        in_specs=[SMEM_SPEC] + [VMEM_SPEC] * (2 + 2 * len(heights)) + [HBM_SPEC] * 2,
+        functools.partial(first_half_kernel, tok, READY),
+        out_shape=(acc, acc) + tuple(pltpu.VMEM(h.shape, BF16) for h in held),
+        in_specs=[VMEM_SPEC] * 2 + [HBM_SPEC] * 2 + [VMEM_SPEC] * 2,
         out_specs=(VMEM_SPEC,) * 4,
         scratch_shapes=[
-            pltpu.VMEM((rows, width // 2), BF16),
+            pltpu.VMEM((steps, rows, block), BF16),
             pltpu.VMEM((rows, fold_width), F32),
-            pltpu.SemaphoreType.DMA((1, 2, 4)),
+            pltpu.SemaphoreType.DMA((2, steps)),
         ],
-        compiler_params=pltpu.CompilerParams(vmem_limit_bytes=(6 if rows < 256 else 32) * MIB),
+        input_output_aliases={4: 2, 5: 3},
+        compiler_params=pltpu.CompilerParams(vmem_limit_bytes=(5 if rows < 256 else 24) * MIB),
         cost_estimate=pl.CostEstimate(
             flops=2 * rows * width * units, bytes_accessed=width * units, transcendentals=0
         ),
         name="first_half",
-    )(
-        place, *in_vmem(*mine, *[p for pair in pieces for p in pair]),
-        *in_hbm(gate_weight, up_weight),
-    )
+    )(*in_vmem(*mine), *in_hbm(gate_weight, up_weight), *in_vmem_always(held))
 
 
 def second_half_kernel(
-    tok, place_ref, a_ref, b_ref, oa_ref, ob_ref, gate_in, up_in, *refs
+    tok, per_plane, ready, a_ref, b_ref, oa_ref, ob_ref, gate_in, up_in, g_hbm, u_hbm, d_hbm, g_in, u_in,
+    staying_ref, leaving_ref, g_ref, u_ref,
+    x_scr, f_scr, gate_acc, up_acc, h_scr, ring, gu_sems, sems,
 ):
-    (g_ref, u_ref, g_hbm, u_hbm, d_hbm, staying_ref, leaving_ref,
-     x_scr, f_scr, gate_acc, up_acc, h_scr, gu_scr, ring, gu_sems, sems) = refs
+    del g_in, u_in
     rows, units = gate_acc.shape
     width = staying_ref.shape[1]
     fold_width = f_scr.shape[1]
-    side = place_ref[0]
-    depth, d_block, d_wide = ring.shape
-    k_steps, n_steps = units // d_block, width // d_wide
-    total = 2 * n_steps * k_steps
-
-    def down_copy(i):
-        n, k = i // k_steps, i % k_steps
-        half = jnp.where(n < n_steps, 1 - side, side)
-        column = half * width + lax.rem(n, n_steps) * d_wide
-        slot = lax.rem(i, depth)
+    side = own_side()
+    depth, _, d_wide = ring.shape
+    per_side = width // d_wide
+    total = 2 * per_side
+    steps, _, block = x_scr.shape
+
+    def down_copy(n):
+        half = jnp.where(n < per_side, 1 - side, side)
+        column = half * width + lax.rem(n, per_side) * d_wide
+        slot = lax.rem(n, depth)
         return pltpu.make_async_copy(
-            d_hbm.at[
-                pl.ds(pl.multiple_of(k * d_block, d_block), d_block),
-                pl.ds(pl.multiple_of(column, LANES), d_wide),
-            ],
-            ring.at[slot], sems.at[slot],
+            d_hbm.at[:, pl.ds(pl.multiple_of(column, LANES), d_wide)], ring.at[slot], sems.at[slot]
         )
 
-    height = g_ref.shape[0]
-    blocks = gu_scr.shape[0]
-    copies = [
-        weight_copies(
-            [(g_hbm, gu_scr.at[i, 0]), (u_hbm, gu_scr.at[i, 1])],
-            (1 - side) * width + (i + 1) * height, height, gu_sems.at[i],
-        )
-        for i in range(blocks)
-    ]
-    for group in copies:
-        for copy in group:
+    for k in range(ready, steps):
+        for copy in other_copies((g_hbm, u_hbm), (g_ref, u_ref), k, block, gu_sems):
             copy.start()
-    for i in range(min(depth, total)):
-        down_copy(jnp.int32(i)).start()
     unfold([oa_ref, ob_ref], True, tok, x_scr, f_scr)
-    part = x_scr[:, :height]
-    gate_acc[...] = gate_in[...] + jnp.dot(part, g_ref[...], preferred_element_type=F32)
-    up_acc[...] = up_in[...] + jnp.dot(part, u_ref[...], preferred_element_type=F32)
-    for i in range(blocks):
-        for copy in copies[i]:
-            copy.wait()
-        part = x_scr[:, (i + 1) * height:(i + 2) * height]
-        gate_acc[...] += jnp.dot(part, gu_scr[i, 0], preferred_element_type=F32)
-        up_acc[...] += jnp.dot(part, gu_scr[i, 1], preferred_element_type=F32)
+    gate_acc[...] = gate_in[...]
+    up_acc[...] = up_in[...]
+
+    def step(k, _):
+        @pl.when(k >= ready)
+        def _():
+            for copy in other_copies((g_hbm, u_hbm), (g_ref, u_ref), k, block, gu_sems):
+                copy.wait()
+
+        at = pl.ds(pl.multiple_of(k * block, block), block)
+        add_block(x_scr, k, g_ref, u_ref, at, gate_acc, up_acc)
+
+        @pl.when(k < depth)
+        def _():
+            down_copy(k).start()
+
+        return 0
+
+    lax.fori_loop(0, steps, step, 0)
 
     for at, arrays, swap in ((0, [a_ref, b_ref], False), (LANES, [oa_ref, ob_ref], True)):
         for i, (array, start) in enumerate(block_rows(arrays, swap, tok)):
@@ -442,80 +468,72 @@
         return pick(both, jnp.logical_and(logit_lane, expert_of == route.astype(jnp.int32))) * scale
 
     share = 1.0 / (1.0 + jnp.exp(logit_at(second) - logit_at(first)))
-    here = place_ref[1].astype(F32)
+    here = (lax.axis_index("node") // per_plane).astype(F32)
     weight = jnp.where(first == here, share, 0.0) + jnp.where(second == here, 1.0 - share, 0.0)
 
     gate = gate_acc[...] * scale
     h_scr[...] = (gate / (1.0 + jnp.exp(-gate)) * (up_acc[...] * scale)).astype(BF16)
 
-    def columns(n):
-        value = None
-        for k in range(k_steps):
-            i = n * k_steps + k
-            slot = lax.rem(i, depth)
-            down_copy(i).wait()
-            part = jnp.dot(
-                h_scr[:, k * d_block:(k + 1) * d_block], ring[slot], preferred_element_type=F32
-            )
-            value = part if value is None else value + part
-
-            @pl.when(i + depth < total)
-            def _():
-                down_copy(i + depth).start()
-
-        return value * weight
-
-    def leave(n, _):
-        value = columns(n)
-        quarter = rows // 4
-        value = jnp.concatenate(
-            [value[q * quarter:(q + 1) * quarter, :] for q in (0, 2, 1, 3)], axis=0
-        )
-        leaving_ref[:, pl.ds(pl.multiple_of(n * d_wide, LANES), d_wide)] = value.astype(BF16)
+    def columns(n, _):
+        slot = lax.rem(n, depth)
+        down_copy(n).wait()
+        value = jnp.dot(h_scr[...], ring[slot], preferred_element_type=F32) * weight
+        to = pl.ds(pl.multiple_of(lax.rem(n, per_side) * d_wide, LANES), d_wide)
+
+        @pl.when(n + depth < total)
+        def _():
+            down_copy(n + depth).start()
+
+        @pl.when(n < per_side)
+        def _():
+            quarter = rows // 4
+            leaving_ref[:, to] = jnp.concatenate(
+                [value[q * quarter:(q + 1) * quarter, :] for q in (0, 2, 1, 3)], axis=0
+            ).astype(BF16)
+
+        @pl.when(n >= per_side)
+        def _():
+            staying_ref[:, to] = value
+
         return 0
 
-    def stay(n, _):
-        staying_ref[:, pl.ds(pl.multiple_of(n * d_wide, LANES), d_wide)] = columns(n + n_steps)
-        return 0
-
-    lax.fori_loop(0, n_steps, leave, 0)
-    lax.fori_loop(0, n_steps, stay, 0)
-
-
-def second_half(tok, place, mine, other, sums, weights, gate_weight, up_weight, down_weight):
+    lax.fori_loop(0, total, columns, 0)
+
+
+def second_half(tok, per_plane, mine, other, sums, held, gate_weight, up_weight, down_weight):
     rows, units = sums[0].shape
     width = down_weight.shape[1] // 2
     fold_width = mine[0].shape[1] - LANES
-    d_block, d_wide = math.gcd(1024, units), math.gcd(1536, width)
-    total = 2 * (width // d_wide) * (units // d_block)
-    depth = min(DOWN_DEPTH, total)
-    height = weights[0].shape[0]
-    blocks = width // height - 1
+    d_wide = math.gcd(768, width)
+    block = math.gcd(512, fold_width)
+    steps = width // block
+    depth = min(DOWN_DEPTH, 2 * (width // d_wide), steps)
     return pl.pallas_call(
-        functools.partial(second_half_kernel, tok),
-        out_shape=(vmem_array((rows, width), F32), vmem_array((rows, width), BF16)),
-        in_specs=[SMEM_SPEC] + [VMEM_SPEC] * 8 + [HBM_SPEC] * 3,
-        out_specs=(VMEM_SPEC,) * 2,
+        functools.partial(second_half_kernel, tok, per_plane, READY),
+        out_shape=(vmem_array((rows, width), F32), vmem_array((rows, width), BF16))
+        + tuple(pltpu.VMEM(h.shape, BF16) for h in held),
+        in_specs=[VMEM_SPEC] * 6 + [HBM_SPEC] * 3 + [VMEM_SPEC] * 2,
+        out_specs=(VMEM_SPEC,) * 4,
         scratch_shapes=[
-            pltpu.VMEM((rows, width), BF16),
+            pltpu.VMEM((steps, rows, block), BF16),
             pltpu.VMEM((rows, fold_width), F32),
             pltpu.VMEM((rows, units), F32),
             pltpu.VMEM((rows, units), F32),
             pltpu.VMEM((rows, units), BF16),
-            pltpu.VMEM((blocks, 2, height, units), BF16),
-            pltpu.VMEM((depth, d_block, d_wide), BF16),
-            pltpu.SemaphoreType.DMA((blocks, 2, 4)),
+            pltpu.VMEM((depth, units, d_wide), BF16),
+            pltpu.SemaphoreType.DMA((2, steps)),
             pltpu.SemaphoreType.DMA((depth,)),
         ],
-        compiler_params=pltpu.CompilerParams(vmem_limit_bytes=(38 if rows < 256 else 48) * MIB),
+        input_output_aliases={9: 2, 10: 3},
+        compiler_params=pltpu.CompilerParams(vmem_limit_bytes=(22 if rows < 256 else 40) * MIB),
         cost_estimate=pl.CostEstimate(
             flops=6 * rows * width * units, bytes_accessed=4 * width * units, transcendentals=0
         ),
         name="second_half",
     )(
-        place, *in_vmem(*mine, *other, *sums, *weights),
-        *in_hbm(gate_weight, up_weight, down_weight),
-    )
+        *in_vmem(*mine, *other, *sums), *in_hbm(gate_weight, up_weight, down_weight),
+        *in_vmem_always(held),
+    )[:2]
 
 
 def split_kernel(fold, own_ref, got_ref, keep_ref, send_ref, total):
@@ -574,10 +592,6 @@
 ):
     nodes = lax.axis_size("node")
     per_plane = nodes // EXPERTS
-    place = jnp.stack(
-        [lax.axis_index("shard"), lax.axis_index("node") // per_plane]
-    ).astype(jnp.int32)
-
     stages = nodes.bit_length() - 1
     masks = [nodes >> (s + 1) for s in range(stages)]
     routes_of = (masks, masks[:-2] + masks[:-3:-1])
@@ -593,26 +607,24 @@
 
     unit = row_unit(gate_weight)
     tok = residual.shape[0]
-    heights = [unit, 2 * unit, unit, 2 * unit]
-    held, payload, *piece = attend(
-        heights[0], place, cache_lengths, routes.T, queries, key_cache, value_cache, new_key, new_value,
+    heights = [unit, 2 * unit, 2 * unit, unit]
+    carried, payload, *held = attend(
+        heights[0], cache_lengths, routes.T, queries, key_cache, value_cache, new_key, new_value,
         residual, norm_gain.reshape(1, -1), router.T, gate_weight, up_weight,
     )
-    carried, pieces, first, token = held, [piece], heights[0], None
+    first = heights[0]
     for stage in range(stages):
         got = exchange(payload, stage)
-        if len(pieces) < len(heights):
-            height = heights[len(pieces)]
-            *piece, token = load_rows(first, height, place, payload, gate_weight, up_weight)
-            pieces.append(piece)
-            first += height
+        if stage + 1 < len(heights):
+            *held, token = load_rows(first, heights[stage + 1], payload, gate_weight, up_weight, held)
+            first += heights[stage + 1]
         if stage < stages - 1:
             payload = join(payload, got, token)
     mine = [payload, *relay([got], token)]
     other = [to_core(array) for array in mine]
-    gate, up, *weights = first_half(tok, place, mine, pieces, gate_weight, up_weight)
+    gate, up, *held = first_half(tok, mine, held, gate_weight, up_weight)
     staying, leaving = second_half(
-        tok, place, mine, other, (gate, up), weights, gate_weight, up_weight, down_weight
+        tok, per_plane, mine, other, (gate, up), held, gate_weight, up_weight, down_weight
     )
     keep, send = split_rows(staying, to_core(leaving))
     for stage in range(stages - 1, 0, -1):

time: 70.3 us -> 64.3 us (0.915)
  Pallas kernels: 40.6 us -> 32.3 us
  waiting for transfers between devices: 15.7 us -> 19.1 us
  starting transfers between devices: 13.7 us -> 12.6 us
    pallas_call x5, Pallas kernels: 35.6 us -> 28 us  [the longest x1 11.8 us: second_half(): pl.pallas_call(functools.partial(second_half_kernel, tok, per_plane, READ...]
    ppermute x6, waiting for transfers between devices: 14.1 us -> 17.5 us  [exchange(): return lax.ppermute(array, ('node', 'shard'), perm)]
    ppermute x6, starting transfers between devices: 13 us -> 12.1 us  [exchange(): return lax.ppermute(array, ('node', 'shard'), perm)]
  transfers between devices with their start and end apart: 9 -> 9, of which waited for: 7 -> 7; matrix products, arithmetic and copies ran while one was open for 0% -> 0% of each run, Pallas kernels for 27% -> 25%
where the time goes in v5:
time: 64.3 us; the launch traced here: 64.1 us
  Pallas kernels  32.3 us (50%)
  waiting for transfers between devices  19.1 us (30%)
  starting transfers between devices  12.6 us (20%)
    ppermute x6, waiting for transfers between devices, exchange(): return lax.ppermute(array, ('node', 'shard'), perm)  17.5 us
    ppermute x6, starting transfers between devices, exchange(): return lax.ppermute(array, ('node', 'shard'), perm)  12.1 us
    pallas_call x1, Pallas kernels, second_half(): pl.pallas_call(functools.partial(second_half_kernel, tok, per_plane, READ...  11.8 us
    pallas_call x3, Pallas kernels, load_rows(): pl.pallas_call(lambda *refs: load_kernel(first, rows, *refs), out_shape=t...  9.16 us
    pallas_call x1, Pallas kernels, first_half(): pl.pallas_call(functools.partial(first_half_kernel, tok, READY), out_shap...  7.07 us
    pallas_call x1, Pallas kernels, attend(): pl.pallas_call(functools.partial(attend_kernel, ahead), out_shape=(pltpu....  3.37 us
    ppermute x3, waiting for transfers between devices, to_core(): return lax.ppermute(array, 'shard', [(0, 1), (1, 0)])  1.64 us
  transfers between devices with their start and end apart: 9, of which 7 were waited for; matrix products, arithmetic and copies ran while one was open for 0% of the time, Pallas kernels for 25%

profile of v5, /device:TPU:0, one launch (start us, length us, event | category | flops | bytes accessed | tf_op | source)
XLA Modules:
  0.0 64.1 jit_solution(12556883345448432979)
XLA Ops:
  0.0 3.4 %attend.1 = (f32[12,3072]{1,0:T(8,128)S(1)}, bf16[24,1664]{1,0:T(8,128)(2,1)S(1)}, bf16[3072,2048]{1,0:T(8,128)(2,1)S(1)}, bf16[3072,2048]{1,0:T(8,128)(2,1)S(1)}) custom-call(s32[12]{0:T(128)} %len_hbm.1, s32[2,12]{1,0:T(2,128)} %bitcast.5, bf16[12,3072]{1,0:T(8,128)(2,1)} %q_hbm.1, bf16[12,128,512]{2,1,0:T(8,128)(2,1)} %k_hbm.1, ...), custom_call_target="tpu_custom_call" | custom-call | flops 100000000 | bytes 8000000 | tf_op jit(solution)/shard_map/attend/pallas_call | solution.py:278
  3.4 4.1 %collective-permute-start = (bf16[24,1664]{1,0:T(8,128)(2,1)S(1)}, bf16[24,1664]{1,0:T(8,128)(2,1)S(1)}, u32[]{:S(2)}, u32[]{:S(2)}) collective-permute-start(bf16[24,1664]{1,0:T(8,128)(2,1)S(1)} %get-tuple-element.31.refs_0_.a_ref), channel_id=1, source_target_pairs={{0,8},{1,9},{2,10},{3,11},{4,12},{5,13},{6,14},{7,15},{8,0},{9,1},... | collective-permute-start | bytes 239624 | tf_op jit(solution)/shard_map/ppermute | solution.py:603
  7.5 3.5 %load_weights.3 = (bf16[3072,2048]{1,0:T(8,128)(2,1)S(1)}, bf16[3072,2048]{1,0:T(8,128)(2,1)S(1)}, f32[8,128]{1,0:T(8,128)S(1)}) custom-call(bf16[24,1664]{1,0:T(8,128)(2,1)S(1)} %get-tuple-element.31.refs_0_.a_ref, bf16[6144,2048]{1,0:T(8,128)(2,1)} %g_hbm.5, bf16[6144,2048]{1,0:T(8,128)(2,1)} %u_hbm.5, ...), custom_call_target="tpu_custom_call", output_to_operand_aliasing={{0}: (3, {}), {1}: (4, {})} | custom-call | bytes 8388608 | tf_op jit(solution)/shard_map/load_weights/pallas_call | solution.py:95
  11.0 0.6 collective-permute-done.b_ref
  11.6 1.0 %collective-permute-start.1 = (bf16[48,1664]{1,0:T(8,128)(2,1)S(1)}, bf16[48,1664]{1,0:T(8,128)(2,1)S(1)}, u32[]{:S(2)}, u32[]{:S(2)}) collective-permute-start(bf16[48,1664]{1,0:T(8,128)(2,1)S(1)} %join.2.refs_0_.a_ref), channel_id=1, source_target_pairs={{0,4},{1,3},{2,6},{3,1},{4,0},{5,7},{6,2},{7,5},{8,12},{9,11},{10,... | collective-permute-start | bytes 479240 | tf_op jit(solution)/shard_map/ppermute | solution.py:603
  12.6 3.5 %load_weights.4 = (bf16[3072,2048]{1,0:T(8,128)(2,1)S(1)}, bf16[3072,2048]{1,0:T(8,128)(2,1)S(1)}, f32[8,128]{1,0:T(8,128)S(1)}) custom-call(bf16[48,1664]{1,0:T(8,128)(2,1)S(1)} %join.2.refs_0_.a_ref, bf16[6144,2048]{1,0:T(8,128)(2,1)} %g_hbm.5, bf16[6144,2048]{1,0:T(8,128)(2,1)} %u_hbm.5, ...), custom_call_target="tpu_custom_call", output_to_operand_aliasing={{0}: (3, {}), {1}: (4, {})} | custom-call | bytes 8388608 | tf_op jit(solution)/shard_map/load_weights/pallas_call | solution.py:95
  16.1 0.8 %collective-permute-done.1.b_ref = bf16[48,1664]{1,0:T(8,128)(2,1)S(1)} collective-permute-done((bf16[48,1664]{1,0:T(8,128)(2,1)S(1)}, bf16[48,1664]{1,0:T(8,128)(2,1)S(1)}, u32[]{:S(2)}, u32[]{:S(2)}) %collective-permute-start.1) | collective-permute-done | bytes 159776 | tf_op jit(solution)/shard_map/ppermute | solution.py:603
  17.0 1.8 %collective-permute-start.2 = (bf16[96,1664]{1,0:T(8,128)(2,1)S(1)}, bf16[96,1664]{1,0:T(8,128)(2,1)S(1)}, u32[]{:S(2)}, u32[]{:S(2)}) collective-permute-start(bf16[96,1664]{1,0:T(8,128)(2,1)S(1)} %join.3.refs_0_.a_ref), channel_id=1, source_target_pairs={{0,2},{1,5},{2,0},{3,7},{4,6},{5,1},{6,4},{7,3},{8,10},{9,13},{10,... | collective-permute-start | bytes 958472 | tf_op jit(solution)/shard_map/ppermute | solution.py:603
  18.7 0.0 collective-permute-start.3
  18.7 2.2 %load_weights.5 = (bf16[3072,2048]{1,0:T(8,128)(2,1)S(1)}, bf16[3072,2048]{1,0:T(8,128)(2,1)S(1)}, f32[8,128]{1,0:T(8,128)S(1)}) custom-call(bf16[96,1664]{1,0:T(8,128)(2,1)S(1)} %join.3.refs_0_.a_ref, bf16[6144,2048]{1,0:T(8,128)(2,1)} %g_hbm.5, bf16[6144,2048]{1,0:T(8,128)(2,1)} %u_hbm.5, ...), custom_call_target="tpu_custom_call", output_to_operand_aliasing={{0}: (3, {}), {1}: (4, {})} | custom-call | bytes 4194304 | tf_op jit(solution)/shard_map/load_weights/pallas_call | solution.py:95
  21.0 3.1 %collective-permute-done.2.refs_0_ = bf16[96,1664]{1,0:T(8,128)(2,1)S(1)} collective-permute-done((bf16[96,1664]{1,0:T(8,128)(2,1)S(1)}, bf16[96,1664]{1,0:T(8,128)(2,1)S(1)}, u32[]{:S(2)}, u32[]{:S(2)}) %collective-permute-start.2) | collective-permute-done | bytes 319520 | tf_op jit(solution)/shard_map/ppermute | solution.py:603
  24.0 0.0 collective-permute-start.4
  24.0 7.1 %first_half.1 = (f32[96,2048]{1,0:T(8,128)S(1)}, f32[96,2048]{1,0:T(8,128)S(1)}, bf16[3072,2048]{1,0:T(8,128)(2,1)S(1)}, bf16[3072,2048]{1,0:T(8,128)(2,1)S(1)}) custom-call(bf16[96,1664]{1,0:T(8,128)(2,1)S(1)} %join.3.refs_0_.a_ref, bf16[96,1664]{1,0:T(8,128)(2,1)S(1)} %relay.1.b_ref, ...), custom_call_target="tpu_custom_call", output_to_operand_aliasing={{2}: (4, {}), {3}: (5, {})} | custom-call | flops 2415919104 | bytes 12582912 | tf_op jit(solution)/shard_map/first_half/pallas_call | solution.py:385
  31.1 0.0 collective-permute-done.3.oa_ref
  31.1 0.0 collective-permute-done.4.ob_ref
  31.1 11.8 %second_half.1 = (f32[96,3072]{1,0:T(8,128)S(1)}, bf16[96,3072]{1,0:T(8,128)(2,1)S(1)}, bf16[3072,2048]{1,0:T(8,128)(2,1)S(1)}, bf16[3072,2048]{1,0:T(8,128)(2,1)S(1)}) custom-call(bf16[96,1664]{1,0:T(8,128)(2,1)S(1)} %join.3.refs_0_.a_ref, bf16[96,1664]{1,0:T(8,128)(2,1)S(1)} %relay.1.b_ref, ...), custom_call_target="tpu_custom_call", output_to_operand_aliasing={{2}: (9, {}), {3}: (10, {})} | custom-call | flops 3623878656 | bytes 25165824 | tf_op jit(solution)/shard_map/second_half/pallas_call | solution.py:511
  42.9 0.6 collective-permute-start.5
  43.5 1.6 %collective-permute-done.5.got_ref = bf16[96,3072]{1,0:T(8,128)(2,1)S(1)} collective-permute-done((bf16[96,3072]{1,0:T(8,128)(2,1)S(1)}, bf16[96,3072]{1,0:T(8,128)(2,1)S(1)}, u32[]{:S(2)}, u32[]{:S(2)}) %collective-permute-start.5) | collective-permute-done | bytes 589856 | tf_op jit(solution)/shard_map/ppermute | solution.py:606
  45.1 0.1 split_rows.3
  45.2 1.8 %collective-permute-start.6 = (bf16[48,3072]{1,0:T(8,128)(2,1)S(1)}, bf16[48,3072]{1,0:T(8,128)(2,1)S(1)}, u32[]{:S(2)}, u32[]{:S(2)}) collective-permute-start(bf16[48,3072]{1,0:T(8,128)(2,1)S(1)} %get-tuple-element.50), channel_id=1, source_target_pairs={{0,2},{1,5},{2,0},{3,7},{4,6},{5,1},{6,4},{7,3},{8,10},{9,13},{10,... | collective-permute-start | bytes 884744 | tf_op jit(solution)/shard_map/ppermute | solution.py:603
  47.0 5.0 %collective-permute-done.6.got_ref = bf16[48,3072]{1,0:T(8,128)(2,1)S(1)} collective-permute-done((bf16[48,3072]{1,0:T(8,128)(2,1)S(1)}, bf16[48,3072]{1,0:T(8,128)(2,1)S(1)}, u32[]{:S(2)}, u32[]{:S(2)}) %collective-permute-start.6) | collective-permute-done | bytes 294944 | tf_op jit(solution)/shard_map/ppermute | solution.py:603
  52.0 0.1 split_rows.4
  52.1 1.0 %collective-permute-start.7 = (bf16[24,3072]{1,0:T(8,128)(2,1)S(1)}, bf16[24,3072]{1,0:T(8,128)(2,1)S(1)}, u32[]{:S(2)}, u32[]{:S(2)}) collective-permute-start(bf16[24,3072]{1,0:T(8,128)(2,1)S(1)} %get-tuple-element.52), channel_id=1, source_target_pairs={{0,4},{1,3},{2,6},{3,1},{4,0},{5,7},{6,2},{7,5},{8,12},{9,11},{10,... | collective-permute-start | bytes 442376 | tf_op jit(solution)/shard_map/ppermute | solution.py:603
  53.1 4.2 %collective-permute-done.7.got_ref = bf16[24,3072]{1,0:T(8,128)(2,1)S(1)} collective-permute-done((bf16[24,3072]{1,0:T(8,128)(2,1)S(1)}, bf16[24,3072]{1,0:T(8,128)(2,1)S(1)}, u32[]{:S(2)}, u32[]{:S(2)}) %collective-permute-start.7) | collective-permute-done | bytes 147488 | tf_op jit(solution)/shard_map/ppermute | solution.py:603
  57.3 2.4 %collective-permute-start.8 = (bf16[24,1536]{1,0:T(8,128)(2,1)S(1)}, bf16[24,1536]{1,0:T(8,128)(2,1)S(1)}, u32[]{:S(2)}, u32[]{:S(2)}) collective-permute-start(bf16[24,1536]{1,0:T(8,128)(2,1)S(1)} %get-tuple-element.54), channel_id=1, source_target_pairs={{0,8},{1,9},{2,10},{3,11},{4,12},{5,13},{6,14},{7,15},{8,0},{9,1},... | collective-permute-start | bytes 221192 | tf_op jit(solution)/shard_map/ppermute | solution.py:603
  59.7 3.7 %collective-permute-done.8.got_ref = bf16[24,1536]{1,0:T(8,128)(2,1)S(1)} collective-permute-done((bf16[24,1536]{1,0:T(8,128)(2,1)S(1)}, bf16[24,1536]{1,0:T(8,128)(2,1)S(1)}, u32[]{:S(2)}, u32[]{:S(2)}) %collective-permute-start.8) | collective-permute-done | bytes 73760 | tf_op jit(solution)/shard_map/ppermute | solution.py:603
  63.5 0.7 %finish.1 = bf16[12,3072]{1,0:T(8,128)(2,1)} custom-call(f32[12,3072]{1,0:T(8,128)S(1)} %get-tuple-element.30.carried_ref, f32[12,3072]{1,0:T(8,128)S(1)} %get-tuple-element.53.own_ref, bf16[24,1536]{1,0:T(8,128)(2,1)S(1)} %collective-permute-done.8.got_ref), custom_call_target="tpu_custom_call" | custom-call | tf_op jit(solution)/shard_map/finish/pallas_call | solution.py:578
  (4 shorter events, 0.1 us)
Async XLA Ops:
  3.4 8.2 %collective-permute-start = (bf16[24,1664]{1,0:T(8,128)(2,1)S(1)}, bf16[24,1664]{1,0:T(8,128)(2,1)S(1)}, u32[]{:S(2)}, u32[]{:S(2)}) collective-permute-start(bf16[24,1664]{1,0:T(8,128)(2,1)S(1)} %get-tuple-element.31.refs_0_.a_ref), channel_id=1, source_target_pairs={{0,8},{1,9},{2,10},{3,11},{4,12},{5,13},{6,14},{7,15},{8,0},{9,1},... | collective-permute-start | bytes 239624 | tf_op jit(solution)/shard_map/ppermute | solution.py:603
  11.6 5.3 %collective-permute-start.1 = (bf16[48,1664]{1,0:T(8,128)(2,1)S(1)}, bf16[48,1664]{1,0:T(8,128)(2,1)S(1)}, u32[]{:S(2)}, u32[]{:S(2)}) collective-permute-start(bf16[48,1664]{1,0:T(8,128)(2,1)S(1)} %join.2.refs_0_.a_ref), channel_id=1, source_target_pairs={{0,4},{1,3},{2,6},{3,1},{4,0},{5,7},{6,2},{7,5},{8,12},{9,11},{10,... | collective-permute-start | bytes 479240 | tf_op jit(solution)/shard_map/ppermute | solution.py:603
  17.0 7.1 %collective-permute-start.2 = (bf16[96,1664]{1,0:T(8,128)(2,1)S(1)}, bf16[96,1664]{1,0:T(8,128)(2,1)S(1)}, u32[]{:S(2)}, u32[]{:S(2)}) collective-permute-start(bf16[96,1664]{1,0:T(8,128)(2,1)S(1)} %join.3.refs_0_.a_ref), channel_id=1, source_target_pairs={{0,2},{1,5},{2,0},{3,7},{4,6},{5,1},{6,4},{7,3},{8,10},{9,13},{10,... | collective-permute-start | bytes 958472 | tf_op jit(solution)/shard_map/ppermute | solution.py:603
  18.7 12.4 %collective-permute-start.3 = (bf16[96,1664]{1,0:T(8,128)(2,1)S(1)}, bf16[96,1664]{1,0:T(8,128)(2,1)S(1)}, u32[]{:S(2)}, u32[]{:S(2)}) collective-permute-start(bf16[96,1664]{1,0:T(8,128)(2,1)S(1)} %join.3.refs_0_.a_ref), channel_id=1, source_target_pairs={{0,1},{1,0},{2,3},{3,2},{4,5},{5,4},{6,7},{7,6},{8,9},{9,8},{10,11... | collective-permute-start | bytes 958472 | tf_op jit(solution)/shard_map/ppermute | solution.py:606
  24.0 7.1 %collective-permute-start.4 = (bf16[96,1664]{1,0:T(8,128)(2,1)S(1)}, bf16[96,1664]{1,0:T(8,128)(2,1)S(1)}, u32[]{:S(2)}, u32[]{:S(2)}) collective-permute-start(bf16[96,1664]{1,0:T(8,128)(2,1)S(1)} %relay.1.b_ref), channel_id=1, source_target_pairs={{0,1},{1,0},{2,3},{3,2},{4,5},{5,4},{6,7},{7,6},{8,9},{9,8},{10,11... | collective-permute-start | bytes 958472 | tf_op jit(solution)/shard_map/ppermute | solution.py:606
  42.9 2.2 %collective-permute-start.5 = (bf16[96,3072]{1,0:T(8,128)(2,1)S(1)}, bf16[96,3072]{1,0:T(8,128)(2,1)S(1)}, u32[]{:S(2)}, u32[]{:S(2)}) collective-permute-start(bf16[96,3072]{1,0:T(8,128)(2,1)S(1)} %get-tuple-element.48), channel_id=1, source_target_pairs={{0,1},{1,0},{2,3},{3,2},{4,5},{5,4},{6,7},{7,6},{8,9},{9,8},{10,11... | collective-permute-start | bytes 1769480 | tf_op jit(solution)/shard_map/ppermute | solution.py:606
  45.2 6.8 %collective-permute-start.6 = (bf16[48,3072]{1,0:T(8,128)(2,1)S(1)}, bf16[48,3072]{1,0:T(8,128)(2,1)S(1)}, u32[]{:S(2)}, u32[]{:S(2)}) collective-permute-start(bf16[48,3072]{1,0:T(8,128)(2,1)S(1)} %get-tuple-element.50), channel_id=1, source_target_pairs={{0,2},{1,5},{2,0},{3,7},{4,6},{5,1},{6,4},{7,3},{8,10},{9,13},{10,... | collective-permute-start | bytes 884744 | tf_op jit(solution)/shard_map/ppermute | solution.py:603
  52.1 5.2 %collective-permute-start.7 = (bf16[24,3072]{1,0:T(8,128)(2,1)S(1)}, bf16[24,3072]{1,0:T(8,128)(2,1)S(1)}, u32[]{:S(2)}, u32[]{:S(2)}) collective-permute-start(bf16[24,3072]{1,0:T(8,128)(2,1)S(1)} %get-tuple-element.52), channel_id=1, source_target_pairs={{0,4},{1,3},{2,6},{3,1},{4,0},{5,7},{6,2},{7,5},{8,12},{9,11},{10,... | collective-permute-start | bytes 442376 | tf_op jit(solution)/shard_map/ppermute | solution.py:603
  57.3 6.1 %collective-permute-start.8 = (bf16[24,1536]{1,0:T(8,128)(2,1)S(1)}, bf16[24,1536]{1,0:T(8,128)(2,1)S(1)}, u32[]{:S(2)}, u32[]{:S(2)}) collective-permute-start(bf16[24,1536]{1,0:T(8,128)(2,1)S(1)} %get-tuple-element.54), channel_id=1, source_target_pairs={{0,8},{1,9},{2,10},{3,11},{4,12},{5,13},{6,14},{7,15},{8,0},{9,1},... | collective-permute-start | bytes 221192 | tf_op jit(solution)/shard_map/ppermute | solution.py:603

commit v6 on v5

--- a/solution.py
+++ b/solution.py
@@ -20,11 +20,6 @@
 BF16 = jnp.bfloat16
 
 
-def whole_spec(array):
-    zeros = (0,) * len(array.shape)
-    return pl.BlockSpec(array.shape, lambda *_: zeros)
-
-
 def small(shape, dtype):
     return math.prod(shape) * jnp.dtype(dtype).itemsize <= 17 * MIB // 4
 
@@ -54,10 +49,6 @@
 ROUTE_LANE = 3 + 3 * EXPERTS
 READY = 4
 DOWN_DEPTH = 4
-
-
-def row_unit(gate_weight):
-    return gate_weight.shape[0] // 12
 
 
 def own_side():
@@ -76,9 +67,8 @@
     ]
 
 
-def load_kernel(first, rows, dep_ref, *refs):
-    g_hbm, u_hbm, g_in, u_in, g_vmem, u_vmem, token_ref, sems = refs
-    del dep_ref, g_in, u_in
+def load_kernel(first, rows, dep_ref, g_hbm, u_hbm, *refs):
+    g_vmem, u_vmem, token_ref, sems = refs[-4:]
     half = g_hbm.shape[0] // 2
     copies = pair_copies(
         (g_hbm, u_hbm), own_side() * half + first, (g_vmem, u_vmem), first, rows, sems
@@ -91,14 +81,14 @@
 
 
 def load_rows(first, rows, after, gate_weight, up_weight, held):
-    hidden = gate_weight.shape[1]
-    return pl.pallas_call(
-        lambda *refs: load_kernel(first, rows, *refs),
-        out_shape=tuple(pltpu.VMEM(h.shape, BF16) for h in held) + (pltpu.VMEM((8, LANES), F32),),
-        in_specs=[pl.BlockSpec(memory_space=pl.ANY), HBM_SPEC, HBM_SPEC, VMEM_SPEC, VMEM_SPEC],
+    width, hidden = gate_weight.shape
+    return pl.pallas_call(
+        functools.partial(load_kernel, first, rows),
+        out_shape=(pltpu.VMEM((width // 2, hidden), BF16),) * 2 + (pltpu.VMEM((8, LANES), F32),),
+        in_specs=[pl.BlockSpec(memory_space=pl.ANY), HBM_SPEC, HBM_SPEC] + [VMEM_SPEC] * len(held),
         out_specs=(VMEM_SPEC,) * 3,
         scratch_shapes=[pltpu.SemaphoreType.DMA((2, 4))],
-        input_output_aliases={3: 0, 4: 1},
+        input_output_aliases={3 + i: i for i in range(len(held))},
         compiler_params=pltpu.CompilerParams(vmem_limit_bytes=MIB),
         cost_estimate=pl.CostEstimate(flops=0, bytes_accessed=4 * rows * hidden, transcendentals=0),
         name="load_weights",
@@ -122,21 +112,39 @@
     )(*in_vmem(a, b, token))
 
 
-def relay_kernel(count, *refs):
-    del refs
-
-
-def relay(arrays, token):
-    count = len(arrays)
-    return list(pl.pallas_call(
-        functools.partial(relay_kernel, count),
-        out_shape=tuple(pltpu.VMEM(a.shape, a.dtype) for a in arrays),
-        in_specs=[VMEM_SPEC] * (count + 1),
-        out_specs=(VMEM_SPEC,) * count,
-        input_output_aliases={i: i for i in range(count)},
-        compiler_params=pltpu.CompilerParams(vmem_limit_bytes=MIB),
-        name="relay",
-    )(*in_vmem(*arrays, token)))
+def spread_kernel(part, tok, array_ref, *refs):
+    x_ref, f_scr = refs[-2:]
+    blocks, rows, block = x_ref.shape
+    fold_width = f_scr.shape[1] - LANES
+    per_fold = fold_width // block
+    size = rows // 2
+    to = slice(part * size, (part + 1) * size)
+    whole = array_ref[...].astype(F32)
+    for f in range(FOLD):
+        for i in range(size // tok):
+            start = (i * FOLD + f) * tok
+            f_scr[i * tok:(i + 1) * tok, :] = whole[start:start + tok, :]
+        for p in range(per_fold):
+            x_ref[f * per_fold + p, to, :] = f_scr[:, p * block:(p + 1) * block].astype(BF16)
+        if f == 0:
+            x_ref[blocks - 1, to, :LANES] = f_scr[:, fold_width:].astype(BF16)
+
+
+def spread(part, tok, array, held, token):
+    folded, wide = array.shape
+    fold_width = wide - LANES
+    block = math.gcd(512, fold_width)
+    shape = (FOLD * fold_width // block + 1, 2 * folded // FOLD, block)
+    return pl.pallas_call(
+        functools.partial(spread_kernel, part, tok),
+        out_shape=pltpu.VMEM(shape, BF16),
+        in_specs=[VMEM_SPEC] * (2 + len(held)),
+        out_specs=VMEM_SPEC,
+        scratch_shapes=[pltpu.VMEM((folded // FOLD, wide), F32)],
+        input_output_aliases={1: 0} if held else {},
+        compiler_params=pltpu.CompilerParams(vmem_limit_bytes=(3 if folded < 256 else 24) * MIB),
+        name="spread",
+    )(*in_vmem(array), *in_vmem_always(held), *in_vmem(token))
 
 
 def split_three(value):
@@ -146,12 +154,10 @@
 
 
 def attend_kernel(
-    ahead,
     len_hbm, routes_hbm, q_hbm, k_hbm, v_hbm, nk_hbm, nv_hbm, res_hbm, gain_hbm, rt_hbm,
-    g_hbm, u_hbm,
-    carried_ref, pay_ref, g_vmem, u_vmem,
+    carried_ref, pay_ref,
     q_ref, k_ref, v_ref, nk_ref, nv_ref, res_ref, gain_ref, rt_ref,
-    q_scr, o_scr, nk_scr, nv_scr, pay_scr, len_ref, routes_ref, sems, w_sems,
+    q_scr, o_scr, nk_scr, nv_scr, pay_scr, len_ref, routes_ref, sems,
 ):
     tok, width = q_ref.shape
     cache_len, kv_width = k_ref.shape[1], k_ref.shape[2]
@@ -172,11 +178,6 @@
     ]
     copies = [pltpu.make_async_copy(a, b, sems.at[i]) for i, (a, b) in enumerate(moves)]
     for copy in copies:
-        copy.start()
-    weights = pair_copies(
-        (g_hbm, u_hbm), own_side() * (g_hbm.shape[0] // 2), (g_vmem, u_vmem), 0, ahead, w_sems
-    )
-    for copy in weights:
         copy.start()
     copies[0].wait()
     copies[1].wait()
@@ -258,33 +259,28 @@
     for f in range(FOLD):
         pay_scr[f * tok:(f + 1) * tok, fold_width:] = extra
     pay_ref[...] = pay_scr[...].astype(BF16)
-    for copy in weights:
-        copy.wait()
 
 
 def attend(
-    ahead, lengths, routes_t, queries, key_cache, value_cache, new_key, new_value,
-    residual, gain, router_t, gate_weight, up_weight,
+    lengths, routes_t, queries, key_cache, value_cache, new_key, new_value,
+    residual, gain, router_t,
 ):
     tok, width = queries.shape
     kv_width = new_key.shape[1]
     heads = width // HEAD_DIM
     wide = width // FOLD + LANES
-    piece = pltpu.VMEM((gate_weight.shape[0] // 2, gate_weight.shape[1]), BF16)
     here = [
         pltpu.VMEM(a.shape, a.dtype)
         for a in (queries, key_cache, value_cache, new_key, new_value, residual)
     ]
     return pl.pallas_call(
-        functools.partial(attend_kernel, ahead),
+        attend_kernel,
         out_shape=(
             pltpu.VMEM((tok, width), F32),
             pltpu.VMEM((FOLD * tok, wide), BF16),
-            piece,
-            piece,
         ),
-        in_specs=[HBM_SPEC] * 12,
-        out_specs=(VMEM_SPEC,) * 4,
+        in_specs=[HBM_SPEC] * 10,
+        out_specs=(VMEM_SPEC,) * 2,
         scratch_shapes=here + [
             pltpu.VMEM((1, width), F32),
             pltpu.VMEM((EXPERTS, width), BF16),
@@ -296,7 +292,6 @@
             pltpu.SMEM(lengths.shape, jnp.int32),
             pltpu.SMEM(routes_t.shape, jnp.int32),
             pltpu.SemaphoreType.DMA((12,)),
-            pltpu.SemaphoreType.DMA((2, 2)),
         ],
         compiler_params=pltpu.CompilerParams(vmem_limit_bytes=10 * MIB),
         cost_estimate=pl.CostEstimate(flops=10**8, bytes_accessed=8 * 10**6, transcendentals=10**5),
@@ -304,33 +299,8 @@
     )(
         *in_hbm(
             lengths, routes_t, queries, key_cache, value_cache, new_key, new_value, residual, gain, router_t,
-            gate_weight, up_weight,
         ),
     )
-
-
-def block_rows(arrays, swap, tok):
-    per_array = arrays[0].shape[0] // (FOLD * tok)
-    places = [(array, i * FOLD * tok) for array in arrays for i in range(per_array)]
-    if swap:
-        quarter = len(places) // 4
-        places = (
-            places[:quarter] + places[2 * quarter:3 * quarter]
-            + places[quarter:2 * quarter] + places[3 * quarter:]
-        )
-    return places
-
-
-def unfold(arrays, swap, tok, x_scr, f_scr):
-    fold_width = f_scr.shape[1]
-    block = x_scr.shape[2]
-    per_fold = fold_width // block
-    for f in range(FOLD):
-        for i, (array, start) in enumerate(block_rows(arrays, swap, tok)):
-            rows = array[start:start + FOLD * tok, :fold_width].astype(F32)
-            f_scr[i * tok:(i + 1) * tok, :] = rows[f * tok:(f + 1) * tok, :]
-        for p in range(per_fold):
-            x_scr[f * per_fold + p] = f_scr[:, p * block:(p + 1) * block].astype(BF16)
 
 
 def add_block(x_scr, k, g_ref, u_ref, at, gate_acc, up_acc):
@@ -349,18 +319,17 @@
 
 
 def first_half_kernel(
-    tok, ready, a_ref, b_ref, g_hbm, u_hbm, g_in, u_in,
-    gate_ref, up_ref, g_ref, u_ref, x_scr, f_scr, sems,
+    ready, x_ref, g_hbm, u_hbm, g_in, u_in, gate_ref, up_ref, g_ref, u_ref, sems
 ):
     del g_in, u_in
-    steps, _, block = x_scr.shape
-    unfold([a_ref, b_ref], False, tok, x_scr, f_scr)
+    _, _, block = x_ref.shape
+    steps = g_ref.shape[0] // block
     gate_ref[...] = jnp.zeros_like(gate_ref)
     up_ref[...] = jnp.zeros_like(up_ref)
 
     def step(k, _):
         at = pl.ds(pl.multiple_of(k * block, block), block)
-        add_block(x_scr, k, g_ref, u_ref, at, gate_ref, up_ref)
+        add_block(x_ref, k, g_ref, u_ref, at, gate_ref, up_ref)
 
         @pl.when(k < ready)
         def _():
@@ -375,59 +344,68 @@
             copy.wait()
 
 
-def first_half(tok, mine, held, gate_weight, up_weight):
-    rows = sum(a.shape[0] for a in mine) // FOLD
+def first_half(rows_in, held, gate_weight, up_weight):
+    _, rows, block = rows_in.shape
     width, units = gate_weight.shape
-    fold_width = mine[0].shape[1] - LANES
-    block = math.gcd(512, fold_width)
     steps = width // 2 // block
     acc = pltpu.VMEM((rows, units), F32)
     return pl.pallas_call(
-        functools.partial(first_half_kernel, tok, READY),
+        functools.partial(first_half_kernel, READY),
         out_shape=(acc, acc) + tuple(pltpu.VMEM(h.shape, BF16) for h in held),
-        in_specs=[VMEM_SPEC] * 2 + [HBM_SPEC] * 2 + [VMEM_SPEC] * 2,
+        in_specs=[VMEM_SPEC] + [HBM_SPEC] * 2 + [VMEM_SPEC] * 2,
         out_specs=(VMEM_SPEC,) * 4,
-        scratch_shapes=[
-            pltpu.VMEM((steps, rows, block), BF16),
-            pltpu.VMEM((rows, fold_width), F32),
-            pltpu.SemaphoreType.DMA((2, steps)),
-        ],
-        input_output_aliases={4: 2, 5: 3},
-        compiler_params=pltpu.CompilerParams(vmem_limit_bytes=(5 if rows < 256 else 24) * MIB),
+        scratch_shapes=[pltpu.SemaphoreType.DMA((2, steps))],
+        input_output_aliases={3: 2, 4: 3},
+        compiler_params=pltpu.CompilerParams(vmem_limit_bytes=(4 if rows < 256 else 16) * MIB),
         cost_estimate=pl.CostEstimate(
             flops=2 * rows * width * units, bytes_accessed=width * units, transcendentals=0
         ),
         name="first_half",
-    )(*in_vmem(*mine), *in_hbm(gate_weight, up_weight), *in_vmem_always(held))
+    )(*in_vmem_always([rows_in]), *in_hbm(gate_weight, up_weight), *in_vmem_always(held))
 
 
 def second_half_kernel(
-    tok, per_plane, ready, a_ref, b_ref, oa_ref, ob_ref, gate_in, up_in, g_hbm, u_hbm, d_hbm, g_in, u_in,
+    per_plane, ready, x_ref, ox_ref, gate_in, up_in, g_hbm, u_hbm, d_hbm, g_in, u_in,
     staying_ref, leaving_ref, g_ref, u_ref,
-    x_scr, f_scr, gate_acc, up_acc, h_scr, ring, gu_sems, sems,
+    x_scr, gate_acc, up_acc, h_scr, ring, gu_sems, sems,
 ):
     del g_in, u_in
     rows, units = gate_acc.shape
     width = staying_ref.shape[1]
-    fold_width = f_scr.shape[1]
     side = own_side()
     depth, _, d_wide = ring.shape
     per_side = width // d_wide
     total = 2 * per_side
     steps, _, block = x_scr.shape
-
-    def down_copy(n):
-        half = jnp.where(n < per_side, 1 - side, side)
-        column = half * width + lax.rem(n, per_side) * d_wide
-        slot = lax.rem(n, depth)
+    free = -(-units // block)
+    spare = units // d_wide
+    ends = [0, depth, depth + spare, depth + 2 * spare]
+
+    def place(part, n):
+        if part == 0:
+            return ring.at[n]
+        column = (n - ends[part]) * d_wide
+        if not isinstance(n, int):
+            column = pl.multiple_of(column, LANES)
+        return (g_ref, u_ref)[part - 1].at[pl.ds(0, units), pl.ds(column, d_wide)]
+
+    def down_copy(part, n):
+        column = jnp.where(n < per_side, 1 - side, side) * width + lax.rem(n, per_side) * d_wide
         return pltpu.make_async_copy(
-            d_hbm.at[:, pl.ds(pl.multiple_of(column, LANES), d_wide)], ring.at[slot], sems.at[slot]
+            d_hbm.at[:, pl.ds(pl.multiple_of(column, LANES), d_wide)], place(part, n), sems.at[n]
+        )
+
+    def in_order(values):
+        quarter = rows // 4
+        return jnp.concatenate(
+            [values[q * quarter:(q + 1) * quarter, :] for q in (0, 2, 1, 3)], axis=0
         )
 
     for k in range(ready, steps):
         for copy in other_copies((g_hbm, u_hbm), (g_ref, u_ref), k, block, gu_sems):
             copy.start()
-    unfold([oa_ref, ob_ref], True, tok, x_scr, f_scr)
+    for k in range(steps):
+        x_scr[k] = in_order(ox_ref[k].astype(F32)).astype(BF16)
     gate_acc[...] = gate_in[...]
     up_acc[...] = up_in[...]
 
@@ -440,20 +418,17 @@
         at = pl.ds(pl.multiple_of(k * block, block), block)
         add_block(x_scr, k, g_ref, u_ref, at, gate_acc, up_acc)
 
-        @pl.when(k < depth)
-        def _():
-            down_copy(k).start()
+        for n in range(total):
+            @pl.when(k == (min(n + 1, steps - 2) if n < depth else max(free - 1, steps - 2)))
+            def _(n=n):
+                down_copy(sum(n >= end for end in ends[1:]), n).start()
 
         return 0
 
     lax.fori_loop(0, steps, step, 0)
 
-    for at, arrays, swap in ((0, [a_ref, b_ref], False), (LANES, [oa_ref, ob_ref], True)):
-        for i, (array, start) in enumerate(block_rows(arrays, swap, tok)):
-            extra = array[start:start + FOLD * tok, fold_width:].astype(F32)
-            f_scr[i * tok:(i + 1) * tok, at:at + LANES] = extra[:tok, :]
-    own = f_scr[:, :LANES]
-    both = own + f_scr[:, LANES:2 * LANES]
+    own = x_ref[steps, :, :LANES].astype(F32)
+    both = own + in_order(ox_ref[steps, :, :LANES].astype(F32))
     lane = lax.broadcasted_iota(jnp.int32, (rows, LANES), 1)
 
     def pick(values, mask):
@@ -474,22 +449,14 @@
     gate = gate_acc[...] * scale
     h_scr[...] = (gate / (1.0 + jnp.exp(-gate)) * (up_acc[...] * scale)).astype(BF16)
 
-    def columns(n, _):
-        slot = lax.rem(n, depth)
-        down_copy(n).wait()
-        value = jnp.dot(h_scr[...], ring[slot], preferred_element_type=F32) * weight
+    def columns(part, n, _):
+        down_copy(part, n).wait()
+        value = jnp.dot(h_scr[...], place(part, n)[...], preferred_element_type=F32) * weight
         to = pl.ds(pl.multiple_of(lax.rem(n, per_side) * d_wide, LANES), d_wide)
-
-        @pl.when(n + depth < total)
-        def _():
-            down_copy(n + depth).start()
 
         @pl.when(n < per_side)
         def _():
-            quarter = rows // 4
-            leaving_ref[:, to] = jnp.concatenate(
-                [value[q * quarter:(q + 1) * quarter, :] for q in (0, 2, 1, 3)], axis=0
-            ).astype(BF16)
+            leaving_ref[:, to] = in_order(value).astype(BF16)
 
         @pl.when(n >= per_side)
         def _():
@@ -497,42 +464,44 @@
 
         return 0
 
-    lax.fori_loop(0, total, columns, 0)
-
-
-def second_half(tok, per_plane, mine, other, sums, held, gate_weight, up_weight, down_weight):
+    for part in range(3):
+        low, high = min(ends[part], total), min(ends[part + 1], total)
+        if low < high:
+            lax.fori_loop(low, high, functools.partial(columns, part), 0)
+
+
+def second_half(per_plane, mine, other, sums, held, gate_weight, up_weight, down_weight):
     rows, units = sums[0].shape
     width = down_weight.shape[1] // 2
-    fold_width = mine[0].shape[1] - LANES
+    block = mine.shape[2]
+    steps = width // block
     d_wide = math.gcd(768, width)
-    block = math.gcd(512, fold_width)
-    steps = width // block
-    depth = min(DOWN_DEPTH, 2 * (width // d_wide), steps)
-    return pl.pallas_call(
-        functools.partial(second_half_kernel, tok, per_plane, READY),
+    total = 2 * (width // d_wide)
+    depth = max(DOWN_DEPTH, total - 2 * (units // d_wide))
+    return pl.pallas_call(
+        functools.partial(second_half_kernel, per_plane, READY),
         out_shape=(vmem_array((rows, width), F32), vmem_array((rows, width), BF16))
         + tuple(pltpu.VMEM(h.shape, BF16) for h in held),
-        in_specs=[VMEM_SPEC] * 6 + [HBM_SPEC] * 3 + [VMEM_SPEC] * 2,
+        in_specs=[VMEM_SPEC] * 4 + [HBM_SPEC] * 3 + [VMEM_SPEC] * 2,
         out_specs=(VMEM_SPEC,) * 4,
         scratch_shapes=[
             pltpu.VMEM((steps, rows, block), BF16),
-            pltpu.VMEM((rows, fold_width), F32),
             pltpu.VMEM((rows, units), F32),
             pltpu.VMEM((rows, units), F32),
             pltpu.VMEM((rows, units), BF16),
             pltpu.VMEM((depth, units, d_wide), BF16),
             pltpu.SemaphoreType.DMA((2, steps)),
-            pltpu.SemaphoreType.DMA((depth,)),
+            pltpu.SemaphoreType.DMA((total,)),
         ],
-        input_output_aliases={9: 2, 10: 3},
+        input_output_aliases={7: 2, 8: 3},
         compiler_params=pltpu.CompilerParams(vmem_limit_bytes=(22 if rows < 256 else 40) * MIB),
         cost_estimate=pl.CostEstimate(
             flops=6 * rows * width * units, bytes_accessed=4 * width * units, transcendentals=0
         ),
         name="second_half",
     )(
-        *in_vmem(*mine, *other, *sums), *in_hbm(gate_weight, up_weight, down_weight),
-        *in_vmem_always(held),
+        *in_vmem_always([mine, other]), *in_vmem(*sums),
+        *in_hbm(gate_weight, up_weight, down_weight), *in_vmem_always(held),
     )[:2]
 
 
@@ -605,26 +574,27 @@
     def to_core(array):
         return lax.ppermute(array, "shard", [(0, 1), (1, 0)])
 
-    unit = row_unit(gate_weight)
     tok = residual.shape[0]
-    heights = [unit, 2 * unit, 2 * unit, unit]
-    carried, payload, *held = attend(
-        heights[0], cache_lengths, routes.T, queries, key_cache, value_cache, new_key, new_value,
-        residual, norm_gain.reshape(1, -1), router.T, gate_weight, up_weight,
+    half = gate_weight.shape[0] // 2
+    heights = [half // 2, half // 4, half // 4]
+    carried, payload = attend(
+        cache_lengths, routes.T, queries, key_cache, value_cache, new_key, new_value,
+        residual, norm_gain.reshape(1, -1), router.T,
     )
-    first = heights[0]
+    first, held = 0, []
     for stage in range(stages):
         got = exchange(payload, stage)
-        if stage + 1 < len(heights):
-            *held, token = load_rows(first, heights[stage + 1], payload, gate_weight, up_weight, held)
-            first += heights[stage + 1]
+        if stage < len(heights):
+            *held, token = load_rows(first, heights[stage], payload, gate_weight, up_weight, held)
+            first += heights[stage]
         if stage < stages - 1:
             payload = join(payload, got, token)
-    mine = [payload, *relay([got], token)]
-    other = [to_core(array) for array in mine]
-    gate, up, *held = first_half(tok, mine, held, gate_weight, up_weight)
+    mine = spread(0, tok, payload, [], token)
+    mine = spread(1, tok, got, [mine], token)
+    other = to_core(mine)
+    gate, up, *held = first_half(mine, held, gate_weight, up_weight)
     staying, leaving = second_half(
-        tok, per_plane, mine, other, (gate, up), held, gate_weight, up_weight, down_weight
+        per_plane, mine, other, (gate, up), held, gate_weight, up_weight, down_weight
     )
     keep, send = split_rows(staying, to_core(leaving))
     for stage in range(stages - 1, 0, -1):

time: 64.3 us -> 63.5 us (0.988)
  waiting for transfers between devices: 19.1 us -> 17.6 us
  Pallas kernels: 32.3 us -> 33 us
    ppermute x6, waiting for transfers between devices: 17.5 us -> 16 us  [exchange(): return lax.ppermute(array, ('node', 'shard'), perm)]
    pallas_call x7 -> x8, Pallas kernels: 31.4 us -> 32.1 us  [the longest x1 11.9 us: second_half(): pl.pallas_call(functools.partial(second_half_kernel, per_plane, READY), o...]
    ppermute x3 -> x2, waiting for transfers between devices: 1.64 us -> 1.63 us  [to_core(): return lax.ppermute(array, 'shard', [(0, 1), (1, 0)])]
  transfers between devices with their start and end apart: 9 -> 8, of which waited for: 7 -> 6; matrix products, arithmetic and copies ran while one was open for 0% -> 0% of each run, Pallas kernels for 25% -> 27%
where the time goes in v6:
time: 63.5 us; the launch traced here: 63.4 us
  Pallas kernels  33 us (52%)
  waiting for transfers between devices  17.6 us (28%)
  starting transfers between devices  12.7 us (20%)
    ppermute x6, waiting for transfers between devices, exchange(): return lax.ppermute(array, ('node', 'shard'), perm)  16 us
    ppermute x6, starting transfers between devices, exchange(): return lax.ppermute(array, ('node', 'shard'), perm)  12 us
    pallas_call x1, Pallas kernels, second_half(): pl.pallas_call(functools.partial(second_half_kernel, per_plane, READY), o...  11.9 us
    pallas_call x3, Pallas kernels, load_rows(): pl.pallas_call(functools.partial(load_kernel, first, rows), out_shape=(pl...  10.4 us
    pallas_call x1, Pallas kernels, first_half(): pl.pallas_call(functools.partial(first_half_kernel, READY), out_shape=(ac...  6.62 us
    pallas_call x1, Pallas kernels, attend(): pl.pallas_call(attend_kernel, out_shape=(pltpu.VMEM((tok, width), F32), p...  3.04 us
    ppermute x2, waiting for transfers between devices, to_core(): return lax.ppermute(array, 'shard', [(0, 1), (1, 0)])  1.63 us
  transfers between devices with their start and end apart: 8, of which 6 were waited for; matrix products, arithmetic and copies ran while one was open for 0% of the time, Pallas kernels for 27%

profile of v6, /device:TPU:0, one launch (start us, length us, event | category | flops | bytes accessed | tf_op | source)
XLA Modules:
  0.0 63.4 jit_solution(9697261092079539052)
XLA Ops:
  0.0 3.0 %attend.1 = (f32[12,3072]{1,0:T(8,128)S(1)}, bf16[24,1664]{1,0:T(8,128)(2,1)S(1)}) custom-call(s32[12]{0:T(128)} %len_hbm.1, s32[2,12]{1,0:T(2,128)} %bitcast.5, bf16[12,3072]{1,0:T(8,128)(2,1)} %q_hbm.1, bf16[12,128,512]{2,1,0:T(8,128)(2,1)} %k_hbm.1, bf16[12,128,512]{2,1,0:T(8,128)(2,1)} %v_hbm.1, bf16[12,512]{1,0:T(8,128)(2,1)} %nk_hbm.1, ...), custom_call_target="tpu_custom_call" | custom-call | flops 100000000 | bytes 8000000 | tf_op jit(solution)/shard_map/attend/pallas_call | solution.py:276
  3.0 4.1 %collective-permute-start = (bf16[24,1664]{1,0:T(8,128)(2,1)S(1)}, bf16[24,1664]{1,0:T(8,128)(2,1)S(1)}, u32[]{:S(2)}, u32[]{:S(2)}) collective-permute-start(bf16[24,1664]{1,0:T(8,128)(2,1)S(1)} %get-tuple-element.29.dep_ref.a_ref), channel_id=1, source_target_pairs={{0,8},{1,9},{2,10},{3,11},{4,12},{5,13},{6,14},{7,15},{8,0},{9,1},... | collective-permute-start | bytes 239624 | tf_op jit(solution)/shard_map/ppermute | solution.py:572
  7.2 4.7 %load_weights.3 = (bf16[3072,2048]{1,0:T(8,128)(2,1)S(1)}, bf16[3072,2048]{1,0:T(8,128)(2,1)S(1)}, f32[8,128]{1,0:T(8,128)S(1)}) custom-call(bf16[24,1664]{1,0:T(8,128)(2,1)S(1)} %get-tuple-element.29.dep_ref.a_ref, bf16[6144,2048]{1,0:T(8,128)(2,1)} %g_hbm.9, bf16[6144,2048]{1,0:T(8,128)(2,1)} %u_hbm.9), custom_call_target="tpu_custom_call" | custom-call | bytes 12582912 | tf_op jit(solution)/shard_map/load_weights/pallas_call | solution.py:85
  11.9 0.0 collective-permute-done.b_ref
  11.9 1.6 %collective-permute-start.1 = (bf16[48,1664]{1,0:T(8,128)(2,1)S(1)}, bf16[48,1664]{1,0:T(8,128)(2,1)S(1)}, u32[]{:S(2)}, u32[]{:S(2)}) collective-permute-start(bf16[48,1664]{1,0:T(8,128)(2,1)S(1)} %join.2.dep_ref.a_ref), channel_id=1, source_target_pairs={{0,4},{1,3},{2,6},{3,1},{4,0},{5,7},{6,2},{7,5},{8,12},{9,11},{10,... | collective-permute-start | bytes 479240 | tf_op jit(solution)/shard_map/ppermute | solution.py:572
  13.5 2.9 %load_weights.4 = (bf16[3072,2048]{1,0:T(8,128)(2,1)S(1)}, bf16[3072,2048]{1,0:T(8,128)(2,1)S(1)}, f32[8,128]{1,0:T(8,128)S(1)}) custom-call(bf16[48,1664]{1,0:T(8,128)(2,1)S(1)} %join.2.dep_ref.a_ref, bf16[6144,2048]{1,0:T(8,128)(2,1)} %g_hbm.9, bf16[6144,2048]{1,0:T(8,128)(2,1)} %u_hbm.9, ...), custom_call_target="tpu_custom_call", output_to_operand_aliasing={{0}: (3, {}), {1}: (4, {})} | custom-call | bytes 6291456 | tf_op jit(solution)/shard_map/load_weights/pallas_call | solution.py:85
  16.4 0.8 %collective-permute-done.1.b_ref = bf16[48,1664]{1,0:T(8,128)(2,1)S(1)} collective-permute-done((bf16[48,1664]{1,0:T(8,128)(2,1)S(1)}, bf16[48,1664]{1,0:T(8,128)(2,1)S(1)}, u32[]{:S(2)}, u32[]{:S(2)}) %collective-permute-start.1) | collective-permute-done | bytes 159776 | tf_op jit(solution)/shard_map/ppermute | solution.py:572
  17.3 1.6 %collective-permute-start.2 = (bf16[96,1664]{1,0:T(8,128)(2,1)S(1)}, bf16[96,1664]{1,0:T(8,128)(2,1)S(1)}, u32[]{:S(2)}, u32[]{:S(2)}) collective-permute-start(bf16[96,1664]{1,0:T(8,128)(2,1)S(1)} %join.3.dep_ref.array_ref), channel_id=1, source_target_pairs={{0,2},{1,5},{2,0},{3,7},{4,6},{5,1},{6,4},{7,3},{8,10},{9,13},{10,... | collective-permute-start | bytes 958472 | tf_op jit(solution)/shard_map/ppermute | solution.py:572
  18.8 2.9 %load_weights.5 = (bf16[3072,2048]{1,0:T(8,128)(2,1)S(1)}, bf16[3072,2048]{1,0:T(8,128)(2,1)S(1)}, f32[8,128]{1,0:T(8,128)S(1)}) custom-call(bf16[96,1664]{1,0:T(8,128)(2,1)S(1)} %join.3.dep_ref.array_ref, bf16[6144,2048]{1,0:T(8,128)(2,1)} %g_hbm.9, bf16[6144,2048]{1,0:T(8,128)(2,1)} %u_hbm.9, ...), custom_call_target="tpu_custom_call", output_to_operand_aliasing={{0}: (3, {}), {1}: (4, {})} | custom-call | bytes 6291456 | tf_op jit(solution)/shard_map/load_weights/pallas_call | solution.py:85
  21.7 0.1 spread.2.refs_0_
  21.8 2.6 %collective-permute-done.2.array_ref = bf16[96,1664]{1,0:T(8,128)(2,1)S(1)} collective-permute-done((bf16[96,1664]{1,0:T(8,128)(2,1)S(1)}, bf16[96,1664]{1,0:T(8,128)(2,1)S(1)}, u32[]{:S(2)}, u32[]{:S(2)}) %collective-permute-start.2) | collective-permute-done | bytes 319520 | tf_op jit(solution)/shard_map/ppermute | solution.py:572
  24.3 0.1 spread.3.x_ref
  24.4 0.1 collective-permute-start.3
  24.5 6.6 %first_half.1 = (f32[96,2048]{1,0:T(8,128)S(1)}, f32[96,2048]{1,0:T(8,128)S(1)}, bf16[3072,2048]{1,0:T(8,128)(2,1)S(1)}, bf16[3072,2048]{1,0:T(8,128)(2,1)S(1)}) custom-call(bf16[7,96,512]{2,1,0:T(8,128)(2,1)S(1)} %spread.3.x_ref, bf16[6144,2048]{1,0:T(8,128)(2,1)} %g_hbm.9, bf16[6144,2048]{1,0:T(8,128)(2,1)} %u_hbm.9, ...), custom_call_target="tpu_custom_call", output_to_operand_aliasing={{2}: (3, {}), {3}: (4, {})} | custom-call | flops 2415919104 | bytes 12582912 | tf_op jit(solution)/shard_map/first_half/pallas_call | solution.py:352
  31.1 0.0 collective-permute-done.3.ox_ref
  31.1 11.9 %second_half.1 = (f32[96,3072]{1,0:T(8,128)S(1)}, bf16[96,3072]{1,0:T(8,128)(2,1)S(1)}, bf16[3072,2048]{1,0:T(8,128)(2,1)S(1)}, bf16[3072,2048]{1,0:T(8,128)(2,1)S(1)}) custom-call(bf16[7,96,512]{2,1,0:T(8,128)(2,1)S(1)} %spread.3.x_ref, bf16[7,96,512]{2,1,0:T(8,128)(2,1)S(1)} %collective-permute-done.3.ox_ref, ...), custom_call_target="tpu_custom_call", output_to_operand_aliasing={{2}: (7, {}), {3}: (8, {})} | custom-call | flops 3623878656 | bytes 25165824 | tf_op jit(solution)/shard_map/second_half/pallas_call | solution.py:481
  43.0 0.6 collective-permute-start.4
  43.5 1.6 %collective-permute-done.4.got_ref = bf16[96,3072]{1,0:T(8,128)(2,1)S(1)} collective-permute-done((bf16[96,3072]{1,0:T(8,128)(2,1)S(1)}, bf16[96,3072]{1,0:T(8,128)(2,1)S(1)}, u32[]{:S(2)}, u32[]{:S(2)}) %collective-permute-start.4) | collective-permute-done | bytes 589856 | tf_op jit(solution)/shard_map/ppermute | solution.py:575
  45.2 0.1 split_rows.3
  45.3 1.6 %collective-permute-start.5 = (bf16[48,3072]{1,0:T(8,128)(2,1)S(1)}, bf16[48,3072]{1,0:T(8,128)(2,1)S(1)}, u32[]{:S(2)}, u32[]{:S(2)}) collective-permute-start(bf16[48,3072]{1,0:T(8,128)(2,1)S(1)} %get-tuple-element.46), channel_id=1, source_target_pairs={{0,2},{1,5},{2,0},{3,7},{4,6},{5,1},{6,4},{7,3},{8,10},{9,13},{10,... | collective-permute-start | bytes 884744 | tf_op jit(solution)/shard_map/ppermute | solution.py:572
  46.8 5.2 %collective-permute-done.5.got_ref = bf16[48,3072]{1,0:T(8,128)(2,1)S(1)} collective-permute-done((bf16[48,3072]{1,0:T(8,128)(2,1)S(1)}, bf16[48,3072]{1,0:T(8,128)(2,1)S(1)}, u32[]{:S(2)}, u32[]{:S(2)}) %collective-permute-start.5) | collective-permute-done | bytes 294944 | tf_op jit(solution)/shard_map/ppermute | solution.py:572
  52.0 0.1 split_rows.4
  52.1 1.6 %collective-permute-start.6 = (bf16[24,3072]{1,0:T(8,128)(2,1)S(1)}, bf16[24,3072]{1,0:T(8,128)(2,1)S(1)}, u32[]{:S(2)}, u32[]{:S(2)}) collective-permute-start(bf16[24,3072]{1,0:T(8,128)(2,1)S(1)} %get-tuple-element.48), channel_id=1, source_target_pairs={{0,4},{1,3},{2,6},{3,1},{4,0},{5,7},{6,2},{7,5},{8,12},{9,11},{10,... | collective-permute-start | bytes 442376 | tf_op jit(solution)/shard_map/ppermute | solution.py:572
  53.7 3.6 %collective-permute-done.6.got_ref = bf16[24,3072]{1,0:T(8,128)(2,1)S(1)} collective-permute-done((bf16[24,3072]{1,0:T(8,128)(2,1)S(1)}, bf16[24,3072]{1,0:T(8,128)(2,1)S(1)}, u32[]{:S(2)}, u32[]{:S(2)}) %collective-permute-start.6) | collective-permute-done | bytes 147488 | tf_op jit(solution)/shard_map/ppermute | solution.py:572
  57.4 1.5 %collective-permute-start.7 = (bf16[24,1536]{1,0:T(8,128)(2,1)S(1)}, bf16[24,1536]{1,0:T(8,128)(2,1)S(1)}, u32[]{:S(2)}, u32[]{:S(2)}) collective-permute-start(bf16[24,1536]{1,0:T(8,128)(2,1)S(1)} %get-tuple-element.50), channel_id=1, source_target_pairs={{0,8},{1,9},{2,10},{3,11},{4,12},{5,13},{6,14},{7,15},{8,0},{9,1},... | collective-permute-start | bytes 221192 | tf_op jit(solution)/shard_map/ppermute | solution.py:572
  58.9 3.8 %collective-permute-done.7.got_ref = bf16[24,1536]{1,0:T(8,128)(2,1)S(1)} collective-permute-done((bf16[24,1536]{1,0:T(8,128)(2,1)S(1)}, bf16[24,1536]{1,0:T(8,128)(2,1)S(1)}, u32[]{:S(2)}, u32[]{:S(2)}) %collective-permute-start.7) | collective-permute-done | bytes 73760 | tf_op jit(solution)/shard_map/ppermute | solution.py:572
  62.7 0.7 %finish.1 = bf16[12,3072]{1,0:T(8,128)(2,1)} custom-call(f32[12,3072]{1,0:T(8,128)S(1)} %get-tuple-element.28.carried_ref, f32[12,3072]{1,0:T(8,128)S(1)} %get-tuple-element.49.own_ref, bf16[24,1536]{1,0:T(8,128)(2,1)S(1)} %collective-permute-done.7.got_ref), custom_call_target="tpu_custom_call" | custom-call | tf_op jit(solution)/shard_map/finish/pallas_call | solution.py:547
  (3 shorter events, 0.1 us)
Async XLA Ops:
  3.0 8.8 %collective-permute-start = (bf16[24,1664]{1,0:T(8,128)(2,1)S(1)}, bf16[24,1664]{1,0:T(8,128)(2,1)S(1)}, u32[]{:S(2)}, u32[]{:S(2)}) collective-permute-start(bf16[24,1664]{1,0:T(8,128)(2,1)S(1)} %get-tuple-element.29.dep_ref.a_ref), channel_id=1, source_target_pairs={{0,8},{1,9},{2,10},{3,11},{4,12},{5,13},{6,14},{7,15},{8,0},{9,1},... | collective-permute-start | bytes 239624 | tf_op jit(solution)/shard_map/ppermute | solution.py:572
  11.9 5.3 %collective-permute-start.1 = (bf16[48,1664]{1,0:T(8,128)(2,1)S(1)}, bf16[48,1664]{1,0:T(8,128)(2,1)S(1)}, u32[]{:S(2)}, u32[]{:S(2)}) collective-permute-start(bf16[48,1664]{1,0:T(8,128)(2,1)S(1)} %join.2.dep_ref.a_ref), channel_id=1, source_target_pairs={{0,4},{1,3},{2,6},{3,1},{4,0},{5,7},{6,2},{7,5},{8,12},{9,11},{10,... | collective-permute-start | bytes 479240 | tf_op jit(solution)/shard_map/ppermute | solution.py:572
  17.3 7.1 %collective-permute-start.2 = (bf16[96,1664]{1,0:T(8,128)(2,1)S(1)}, bf16[96,1664]{1,0:T(8,128)(2,1)S(1)}, u32[]{:S(2)}, u32[]{:S(2)}) collective-permute-start(bf16[96,1664]{1,0:T(8,128)(2,1)S(1)} %join.3.dep_ref.array_ref), channel_id=1, source_target_pairs={{0,2},{1,5},{2,0},{3,7},{4,6},{5,1},{6,4},{7,3},{8,10},{9,13},{10,... | collective-permute-start | bytes 958472 | tf_op jit(solution)/shard_map/ppermute | solution.py:572
  24.4 6.7 %collective-permute-start.3 = (bf16[7,96,512]{2,1,0:T(8,128)(2,1)S(1)}, bf16[7,96,512]{2,1,0:T(8,128)(2,1)S(1)}, u32[]{:S(2)}, u32[]{:S(2)}) collective-permute-start(bf16[7,96,512]{2,1,0:T(8,128)(2,1)S(1)} %spread.3.x_ref), channel_id=1, source_target_pairs={{0,1},{1,0},{2,3},{3,2},{4,5},{5,4},{6,7},{7,6},{8,9},{9,8},{10,11... | collective-permute-start | bytes 2064392 | tf_op jit(solution)/shard_map/ppermute | solution.py:575
  43.0 2.2 %collective-permute-start.4 = (bf16[96,3072]{1,0:T(8,128)(2,1)S(1)}, bf16[96,3072]{1,0:T(8,128)(2,1)S(1)}, u32[]{:S(2)}, u32[]{:S(2)}) collective-permute-start(bf16[96,3072]{1,0:T(8,128)(2,1)S(1)} %get-tuple-element.44), channel_id=1, source_target_pairs={{0,1},{1,0},{2,3},{3,2},{4,5},{5,4},{6,7},{7,6},{8,9},{9,8},{10,11... | collective-permute-start | bytes 1769480 | tf_op jit(solution)/shard_map/ppermute | solution.py:575
  45.3 6.8 %collective-permute-start.5 = (bf16[48,3072]{1,0:T(8,128)(2,1)S(1)}, bf16[48,3072]{1,0:T(8,128)(2,1)S(1)}, u32[]{:S(2)}, u32[]{:S(2)}) collective-permute-start(bf16[48,3072]{1,0:T(8,128)(2,1)S(1)} %get-tuple-element.46), channel_id=1, source_target_pairs={{0,2},{1,5},{2,0},{3,7},{4,6},{5,1},{6,4},{7,3},{8,10},{9,13},{10,... | collective-permute-start | bytes 884744 | tf_op jit(solution)/shard_map/ppermute | solution.py:572
  52.1 5.2 %collective-permute-start.6 = (bf16[24,3072]{1,0:T(8,128)(2,1)S(1)}, bf16[24,3072]{1,0:T(8,128)(2,1)S(1)}, u32[]{:S(2)}, u32[]{:S(2)}) collective-permute-start(bf16[24,3072]{1,0:T(8,128)(2,1)S(1)} %get-tuple-element.48), channel_id=1, source_target_pairs={{0,4},{1,3},{2,6},{3,1},{4,0},{5,7},{6,2},{7,5},{8,12},{9,11},{10,... | collective-permute-start | bytes 442376 | tf_op jit(solution)/shard_map/ppermute | solution.py:572
  57.4 5.3 %collective-permute-start.7 = (bf16[24,1536]{1,0:T(8,128)(2,1)S(1)}, bf16[24,1536]{1,0:T(8,128)(2,1)S(1)}, u32[]{:S(2)}, u32[]{:S(2)}) collective-permute-start(bf16[24,1536]{1,0:T(8,128)(2,1)S(1)} %get-tuple-element.50), channel_id=1, source_target_pairs={{0,8},{1,9},{2,10},{3,11},{4,12},{5,13},{6,14},{7,15},{8,0},{9,1},... | collective-permute-start | bytes 221192 | tf_op jit(solution)/shard_map/ppermute | solution.py:572

commit v7 on v6

--- a/solution.py
+++ b/solution.py
@@ -8,6 +8,7 @@
 from jax.experimental.pallas import tpu as pltpu
 from jax.sharding import PartitionSpec as P
 
+MIB = 1 << 20
 QUERY_HEADS = 48
 KV_HEADS = 8
 HEAD_DIM = 128
@@ -15,7 +16,6 @@
 GROUP = QUERY_HEADS // KV_HEADS
 LANES = 128
 FOLD = 2
-MIB = 1 << 20
 F32 = jnp.float32
 BF16 = jnp.bfloat16
 
@@ -48,6 +48,7 @@
 HBM_SPEC = pl.BlockSpec(memory_space=pltpu.HBM)
 ROUTE_LANE = 3 + 3 * EXPERTS
 READY = 4
+HELD_BELOW = 22 * MIB
 DOWN_DEPTH = 4
 
 
@@ -89,16 +90,41 @@
         out_specs=(VMEM_SPEC,) * 3,
         scratch_shapes=[pltpu.SemaphoreType.DMA((2, 4))],
         input_output_aliases={3 + i: i for i in range(len(held))},
-        compiler_params=pltpu.CompilerParams(vmem_limit_bytes=MIB),
+        compiler_params=pltpu.CompilerParams(vmem_limit_bytes=HELD_BELOW),
         cost_estimate=pl.CostEstimate(flops=0, bytes_accessed=4 * rows * hidden, transcendentals=0),
         name="load_weights",
     )(*in_vmem(after), *in_hbm(gate_weight, up_weight), *in_vmem_always(held))
 
 
+def unfold_kernel(tok, *refs):
+    *arrays, _, out_ref, scr = refs
+    fold_width = arrays[0].shape[1] - LANES
+    for i, array in enumerate(arrays):
+        rows = array[...].astype(F32)
+        to = slice(i * tok, (i + 1) * tok)
+        for f in range(FOLD):
+            scr[to, f * fold_width:(f + 1) * fold_width] = rows[f * tok:(f + 1) * tok, :fold_width]
+        scr[to, FOLD * fold_width:] = rows[:tok, fold_width:]
+    out_ref[...] = scr[...].astype(BF16)
+
+
+def unfold(tok, arrays, token):
+    shape = (len(arrays) * tok, FOLD * (arrays[0].shape[1] - LANES) + LANES)
+    return pl.pallas_call(
+        functools.partial(unfold_kernel, tok),
+        out_shape=pltpu.VMEM(shape, BF16),
+        in_specs=[VMEM_SPEC] * (len(arrays) + 1),
+        out_specs=VMEM_SPEC,
+        scratch_shapes=[pltpu.VMEM(shape, F32)],
+        compiler_params=pltpu.CompilerParams(vmem_limit_bytes=3 * MIB),
+        name="unfold",
+    )(*in_vmem_always([*arrays, token]))
+
+
 def join_kernel(a_ref, b_ref, token_ref, out_ref):
-    out_ref[...] = jnp.concatenate(
-        [a_ref[...].astype(F32), b_ref[...].astype(F32)], axis=0
-    ).astype(BF16)
+    rows = a_ref.shape[0]
+    out_ref[:rows, :] = a_ref[...]
+    out_ref[rows:, :] = b_ref[...]
 
 
 def join(a, b, token):
@@ -107,42 +133,31 @@
         out_shape=vmem_array((a.shape[0] + b.shape[0], a.shape[1]), BF16),
         in_specs=[VMEM_SPEC] * 3,
         out_specs=VMEM_SPEC,
-        compiler_params=pltpu.CompilerParams(vmem_limit_bytes=(2 if a.shape[0] < 256 else 24) * MIB),
+        compiler_params=pltpu.CompilerParams(vmem_limit_bytes=16 * MIB),
         name="join",
     )(*in_vmem(a, b, token))
 
 
-def spread_kernel(part, tok, array_ref, *refs):
-    x_ref, f_scr = refs[-2:]
+def spread_kernel(part, array_ref, *refs):
+    x_ref = refs[-1]
     blocks, rows, block = x_ref.shape
-    fold_width = f_scr.shape[1] - LANES
-    per_fold = fold_width // block
     size = rows // 2
     to = slice(part * size, (part + 1) * size)
-    whole = array_ref[...].astype(F32)
-    for f in range(FOLD):
-        for i in range(size // tok):
-            start = (i * FOLD + f) * tok
-            f_scr[i * tok:(i + 1) * tok, :] = whole[start:start + tok, :]
-        for p in range(per_fold):
-            x_ref[f * per_fold + p, to, :] = f_scr[:, p * block:(p + 1) * block].astype(BF16)
-        if f == 0:
-            x_ref[blocks - 1, to, :LANES] = f_scr[:, fold_width:].astype(BF16)
-
-
-def spread(part, tok, array, held, token):
-    folded, wide = array.shape
-    fold_width = wide - LANES
-    block = math.gcd(512, fold_width)
-    shape = (FOLD * fold_width // block + 1, 2 * folded // FOLD, block)
-    return pl.pallas_call(
-        functools.partial(spread_kernel, part, tok),
-        out_shape=pltpu.VMEM(shape, BF16),
+    for k in range(blocks - 1):
+        x_ref[k, to, :] = array_ref[:, k * block:(k + 1) * block]
+    x_ref[blocks - 1, to, :LANES] = array_ref[:, (blocks - 1) * block:]
+
+
+def spread(part, array, held, token):
+    size, wide = array.shape
+    block = math.gcd(512, wide - LANES)
+    return pl.pallas_call(
+        functools.partial(spread_kernel, part),
+        out_shape=pltpu.VMEM(((wide - LANES) // block + 1, 2 * size, block), BF16),
         in_specs=[VMEM_SPEC] * (2 + len(held)),
         out_specs=VMEM_SPEC,
-        scratch_shapes=[pltpu.VMEM((folded // FOLD, wide), F32)],
         input_output_aliases={1: 0} if held else {},
-        compiler_params=pltpu.CompilerParams(vmem_limit_bytes=(3 if folded < 256 else 24) * MIB),
+        compiler_params=pltpu.CompilerParams(vmem_limit_bytes=(MIB if size < 128 else 16 * MIB)),
         name="spread",
     )(*in_vmem(array), *in_vmem_always(held), *in_vmem(token))
 
@@ -166,15 +181,17 @@
     fold_width = width // FOLD
     scaling = 1.0 / math.sqrt(HEAD_DIM)
     columns = pl.ds(pl.multiple_of(own_side() * width, LANES), width)
-    half = tok // 2
-    first, rest = pl.ds(0, half), pl.ds(half, tok - half)
-    moves = [
-        (q_hbm, q_ref), (nk_hbm, nk_ref),
-        (k_hbm.at[first], k_ref.at[first]), (k_hbm.at[rest], k_ref.at[rest]),
-        (v_hbm.at[first], v_ref.at[first]), (v_hbm.at[rest], v_ref.at[rest]),
+    parts = math.gcd(4, tok)
+    each = tok // parts
+    moves = [(q_hbm, q_ref), (nk_hbm, nk_ref), (len_hbm, len_ref)]
+    for source, target in ((k_hbm, k_ref), (v_hbm, v_ref)):
+        moves += [
+            (source.at[pl.ds(p * each, each)], target.at[pl.ds(p * each, each)]) for p in range(parts)
+        ]
+    moves += [
         (nv_hbm, nv_ref), (res_hbm, res_ref),
         (gain_hbm.at[:, columns], gain_ref), (rt_hbm.at[:, columns], rt_ref),
-        (len_hbm, len_ref), (routes_hbm, routes_ref),
+        (routes_hbm, routes_ref),
     ]
     copies = [pltpu.make_async_copy(a, b, sems.at[i]) for i, (a, b) in enumerate(moves)]
     for copy in copies:
@@ -188,10 +205,8 @@
     position = lax.broadcasted_iota(jnp.int32, (heads, cache_len), 1)
     scores, fresh = [], []
     for t in range(tok):
-        if t == 0:
-            copies[2].wait()
-        if t == half:
-            copies[3].wait()
+        if t % each == 0:
+            copies[3 + t // each].wait()
         q_rows = q_scr[pl.ds(t, heads, stride=tok), :]
         q_wide = jnp.concatenate(
             [jnp.where(row_group == g, q_rows, 0.0) for g in range(groups)], axis=1
@@ -205,7 +220,7 @@
         fresh.append(
             jnp.sum(q_wide * nk_scr[pl.ds(t, 1), :], axis=1, keepdims=True) * scaling
         )
-    copies[10].wait()
+    copies[2].wait()
     terms, fresh_terms, totals = [], [], []
     for t in range(tok):
         score = jnp.where(position < len_ref[t], scores[t], -1e30)
@@ -215,13 +230,11 @@
         totals.append(jnp.sum(term, axis=1, keepdims=True) + fresh_term)
         terms.append(term.astype(BF16))
         fresh_terms.append(fresh_term.astype(BF16).astype(F32))
-    copies[6].wait()
+    copies[3 + 2 * parts].wait()
     nv_scr[...] = nv_ref[...].astype(F32)
     for t in range(tok):
-        if t == 0:
-            copies[4].wait()
-        if t == half:
-            copies[5].wait()
+        if t % each == 0:
+            copies[3 + parts + t // each].wait()
         wide = jnp.dot(terms[t], v_ref[t], preferred_element_type=F32)
         wide = wide + fresh_terms[t] * nv_scr[pl.ds(t, 1), :]
         picked = wide[:, :HEAD_DIM]
@@ -230,7 +243,7 @@
                 row_group == g, wide[:, g * HEAD_DIM:(g + 1) * HEAD_DIM], picked
             )
         o_scr[pl.ds(t, heads, stride=tok), :] = picked / totals[t]
-    for copy in copies[7:10] + copies[11:]:
+    for copy in copies[4 + 2 * parts:]:
         copy.wait()
     for h in range(heads):
         cols = slice(h * HEAD_DIM, (h + 1) * HEAD_DIM)
@@ -291,7 +304,7 @@
             pltpu.VMEM((FOLD * tok, wide), F32),
             pltpu.SMEM(lengths.shape, jnp.int32),
             pltpu.SMEM(routes_t.shape, jnp.int32),
-            pltpu.SemaphoreType.DMA((12,)),
+            pltpu.SemaphoreType.DMA((8 + 2 * math.gcd(4, tok),)),
         ],
         compiler_params=pltpu.CompilerParams(vmem_limit_bytes=10 * MIB),
         cost_estimate=pl.CostEstimate(flops=10**8, bytes_accessed=8 * 10**6, transcendentals=10**5),
@@ -356,7 +369,7 @@
         out_specs=(VMEM_SPEC,) * 4,
         scratch_shapes=[pltpu.SemaphoreType.DMA((2, steps))],
         input_output_aliases={3: 2, 4: 3},
-        compiler_params=pltpu.CompilerParams(vmem_limit_bytes=(4 if rows < 256 else 16) * MIB),
+        compiler_params=pltpu.CompilerParams(vmem_limit_bytes=HELD_BELOW),
         cost_estimate=pl.CostEstimate(
             flops=2 * rows * width * units, bytes_accessed=width * units, transcendentals=0
         ),
@@ -494,7 +507,7 @@
             pltpu.SemaphoreType.DMA((total,)),
         ],
         input_output_aliases={7: 2, 8: 3},
-        compiler_params=pltpu.CompilerParams(vmem_limit_bytes=(22 if rows < 256 else 40) * MIB),
+        compiler_params=pltpu.CompilerParams(vmem_limit_bytes=HELD_BELOW if rows < 256 else 40 * MIB),
         cost_estimate=pl.CostEstimate(
             flops=6 * rows * width * units, bytes_accessed=4 * width * units, transcendentals=0
         ),
@@ -505,37 +518,61 @@
     )[:2]
 
 
-def split_kernel(fold, own_ref, got_ref, keep_ref, send_ref, total):
-    total[...] = own_ref[...] + got_ref[...].astype(F32)
-    size, width = keep_ref.shape
-    keep_ref[...] = total[:size, :]
-    part = total[size:, :]
-    if fold:
-        part = jnp.concatenate(
-            [part[:, f * (width // FOLD):(f + 1) * (width // FOLD)] for f in range(FOLD)], axis=0
-        )
-    send_ref[...] = part.astype(BF16)
-
-
-def split_rows(own, got, fold=False):
+def split_kernel(own_ref, got_ref, keep_ref, send_ref):
+    size = keep_ref.shape[0]
+    keep_ref[...] = own_ref[:size, :] + got_ref[:size, :].astype(F32)
+    send_ref[...] = (own_ref[size:, :] + got_ref[size:, :].astype(F32)).astype(BF16)
+
+
+def split_rows(own, got):
     rows, width = own.shape
     size = rows // 2
-    sent = (FOLD * size, width // FOLD) if fold else (size, width)
-    return pl.pallas_call(
-        functools.partial(split_kernel, fold),
-        out_shape=(vmem_array((size, width), F32), vmem_array(sent, BF16)),
+    return pl.pallas_call(
+        split_kernel,
+        out_shape=(vmem_array((size, width), F32), vmem_array((size, width), BF16)),
         in_specs=[VMEM_SPEC] * 2,
         out_specs=(VMEM_SPEC,) * 2,
-        scratch_shapes=[pltpu.VMEM((rows, width), F32)],
         compiler_params=pltpu.CompilerParams(vmem_limit_bytes=(8 if rows < 256 else 32) * MIB),
         name="split_rows",
     )(*in_vmem(own, got))
 
 
-def finish_kernel(carried_ref, own_ref, got_ref, out_ref, folded):
+def split_last_kernel(own_ref, got_ref, keep_ref, *refs):
+    *sends, total = refs
+    total[...] = own_ref[...] + got_ref[...].astype(F32)
+    tok, width = keep_ref.shape
+    fold_width = width // FOLD
+    keep_ref[...] = total[:tok, :]
+    for i, send in enumerate(sends, 1):
+        rows = total[i * tok:(i + 1) * tok, :]
+        send[...] = jnp.concatenate(
+            [rows[:, f * fold_width:(f + 1) * fold_width] for f in range(FOLD)], axis=0
+        ).astype(BF16)
+
+
+def split_last(own, got, parts):
+    rows, width = own.shape
+    tok = rows // parts
+    return pl.pallas_call(
+        split_last_kernel,
+        out_shape=(pltpu.VMEM((tok, width), F32),)
+        + (pltpu.VMEM((FOLD * tok, width // FOLD), BF16),) * (parts - 1),
+        in_specs=[VMEM_SPEC] * 2,
+        out_specs=(VMEM_SPEC,) * parts,
+        scratch_shapes=[pltpu.VMEM((rows, width), F32)],
+        compiler_params=pltpu.CompilerParams(vmem_limit_bytes=4 * MIB),
+        name="split_last",
+    )(*in_vmem(own, got))
+
+
+def finish_kernel(carried_ref, own_ref, *refs):
+    *got, out_ref, folded = refs
     tok, width = carried_ref.shape
     fold_width = width // FOLD
-    folded[...] = got_ref[...].astype(F32)
+    total = got[0][...].astype(F32)
+    for ref in got[1:]:
+        total = total + ref[...].astype(F32)
+    folded[...] = total
     for f in range(FOLD):
         at = slice(f * fold_width, (f + 1) * fold_width)
         value = carried_ref[:, at] + own_ref[:, at] + folded[f * tok:(f + 1) * tok, :]
@@ -547,12 +584,12 @@
     return pl.pallas_call(
         finish_kernel,
         out_shape=jax.ShapeDtypeStruct((tok, width), BF16),
-        in_specs=[VMEM_SPEC] * 3,
+        in_specs=[VMEM_SPEC] * (2 + len(got)),
         out_specs=VMEM_SPEC,
         scratch_shapes=[pltpu.VMEM((FOLD * tok, width // FOLD), F32)],
         compiler_params=pltpu.CompilerParams(vmem_limit_bytes=8 * MIB),
         name="finish",
-    )(*in_vmem(carried, own, got))
+    )(*in_vmem(carried, own, *got))
 
 
 def on_device(
@@ -565,10 +602,9 @@
     masks = [nodes >> (s + 1) for s in range(stages)]
     routes_of = (masks, masks[:-2] + masks[:-3:-1])
 
-    def exchange(array, stage):
-        perm = [
-            (2 * n + c, 2 * (n ^ routes_of[c][stage]) + c) for n in range(nodes) for c in range(2)
-        ]
+    def exchange(array, *flips):
+        masks = [sum(side[s] for s in flips) for side in routes_of]
+        perm = [(2 * n + c, 2 * (n ^ masks[c]) + c) for n in range(nodes) for c in range(2)]
         return lax.ppermute(array, ("node", "shard"), perm)
 
     def to_core(array):
@@ -576,30 +612,33 @@
 
     tok = residual.shape[0]
     half = gate_weight.shape[0] // 2
-    heights = [half // 2, half // 4, half // 4]
     carried, payload = attend(
         cache_lengths, routes.T, queries, key_cache, value_cache, new_key, new_value,
         residual, norm_gain.reshape(1, -1), router.T,
     )
-    first, held = 0, []
-    for stage in range(stages):
+    near = ((0,), (1,), (0, 1))
+    got = [exchange(payload, *flips) for flips in near]
+    *held, token = load_rows(0, half // 2, payload, gate_weight, up_weight, [])
+    payload = unfold(tok, [payload, *got], token)
+    for stage in range(2, stages):
         got = exchange(payload, stage)
-        if stage < len(heights):
-            *held, token = load_rows(first, heights[stage], payload, gate_weight, up_weight, held)
-            first += heights[stage]
+        if stage == 2:
+            *held, token = load_rows(half // 2, half - half // 2, payload, gate_weight, up_weight, held)
         if stage < stages - 1:
             payload = join(payload, got, token)
-    mine = spread(0, tok, payload, [], token)
-    mine = spread(1, tok, got, [mine], token)
+    mine = spread(0, payload, [], token)
+    mine = spread(1, got, [mine], token)
     other = to_core(mine)
     gate, up, *held = first_half(mine, held, gate_weight, up_weight)
     staying, leaving = second_half(
         per_plane, mine, other, (gate, up), held, gate_weight, up_weight, down_weight
     )
-    keep, send = split_rows(staying, to_core(leaving))
-    for stage in range(stages - 1, 0, -1):
-        keep, send = split_rows(keep, exchange(send, stage), fold=stage == 1)
-    return finish(carried, keep, exchange(send, 0))
+    keep, got = staying, to_core(leaving)
+    for stage in range(stages - 1, 1, -1):
+        keep, send = split_rows(keep, got)
+        got = exchange(send, stage)
+    keep, *sends = split_last(keep, got, 1 + len(near))
+    return finish(carried, keep, [exchange(send, *flips) for send, flips in zip(sends, near)])
 
 
 def solution(mesh):

time: 63.5 us -> 60.6 us (0.954)
  starting transfers between devices: 12.7 us -> 11 us
  waiting for transfers between devices: 17.6 us -> 16.9 us
    ppermute x6 -> x8, starting transfers between devices: 12 us -> 10.4 us  [exchange(): return lax.ppermute(array, ('node', 'shard'), perm)]
    pallas_call x3 -> x2, Pallas kernels: 10.4 us -> 9.41 us  [load_rows(): pl.pallas_call(functools.partial(load_kernel, first, rows), out_shape=(pl...]
    ppermute x6 -> x8, waiting for transfers between devices: 16 us -> 15.3 us  [exchange(): return lax.ppermute(array, ('node', 'shard'), perm)]
  transfers between devices with their start and end apart: 8 -> 10, of which waited for: 6 -> 7; matrix products, arithmetic and copies ran while one was open for 0% -> 0% of each run, Pallas kernels for 27% -> 27%
where the time goes in v7:
time: 60.6 us; the launch traced here: 60.5 us
  Pallas kernels  32.5 us (54%)
  waiting for transfers between devices  16.9 us (28%)
  starting transfers between devices  11 us (18%)
    ppermute x8, waiting for transfers between devices, exchange(): return lax.ppermute(array, ('node', 'shard'), perm)  15.3 us
    pallas_call x1, Pallas kernels, second_half(): pl.pallas_call(functools.partial(second_half_kernel, per_plane, READY), o...  11.8 us
    ppermute x8, starting transfers between devices, exchange(): return lax.ppermute(array, ('node', 'shard'), perm)  10.4 us
    pallas_call x2, Pallas kernels, load_rows(): pl.pallas_call(functools.partial(load_kernel, first, rows), out_shape=(pl...  9.41 us
    pallas_call x1, Pallas kernels, first_half(): pl.pallas_call(functools.partial(first_half_kernel, READY), out_shape=(ac...  6.62 us
    pallas_call x1, Pallas kernels, attend(): pl.pallas_call(attend_kernel, out_shape=(pltpu.VMEM((tok, width), F32), p...  3.56 us
    ppermute x2, waiting for transfers between devices, to_core(): return lax.ppermute(array, 'shard', [(0, 1), (1, 0)])  1.63 us
  transfers between devices with their start and end apart: 10, of which 7 were waited for; matrix products, arithmetic and copies ran while one was open for 0% of the time, Pallas kernels for 27%

profile of v7, /device:TPU:0, one launch (start us, length us, event | category | flops | bytes accessed | tf_op | source)
XLA Modules:
  0.0 60.5 jit_solution(17319329252976862055)
XLA Ops:
  0.0 3.6 %attend.1 = (f32[12,3072]{1,0:T(8,128)S(1)}, bf16[24,1664]{1,0:T(8,128)(2,1)S(1)}) custom-call(s32[12]{0:T(128)} %len_hbm.1, s32[2,12]{1,0:T(2,128)} %bitcast.5, bf16[12,3072]{1,0:T(8,128)(2,1)} %q_hbm.1, bf16[12,128,512]{2,1,0:T(8,128)(2,1)} %k_hbm.1, bf16[12,128,512]{2,1,0:T(8,128)(2,1)} %v_hbm.1, bf16[12,512]{1,0:T(8,128)(2,1)} %nk_hbm.1, ...), custom_call_target="tpu_custom_call" | custom-call | flops 100000000 | bytes 8000000 | tf_op jit(solution)/shard_map/attend/pallas_call | solution.py:289
  3.6 5.1 %collective-permute-start.2 = (bf16[24,1664]{1,0:T(8,128)(2,1)S(1)}, bf16[24,1664]{1,0:T(8,128)(2,1)S(1)}, u32[]{:S(2)}, u32[]{:S(2)}) collective-permute-start(bf16[24,1664]{1,0:T(8,128)(2,1)S(1)} %get-tuple-element.26.dep_ref.refs_0_), channel_id=1, source_target_pairs={{0,12},{1,11},{2,14},{3,9},{4,8},{5,15},{6,10},{7,13},{8,4},{9,3},... | collective-permute-start | bytes 239624 | tf_op jit(solution)/shard_map/ppermute | solution.py:608
  8.7 0.0 collective-permute-start.1
  8.7 0.6 %collective-permute-start = (bf16[24,1664]{1,0:T(8,128)(2,1)S(1)}, bf16[24,1664]{1,0:T(8,128)(2,1)S(1)}, u32[]{:S(2)}, u32[]{:S(2)}) collective-permute-start(bf16[24,1664]{1,0:T(8,128)(2,1)S(1)} %get-tuple-element.26.dep_ref.refs_0_), channel_id=1, source_target_pairs={{0,8},{1,9},{2,10},{3,11},{4,12},{5,13},{6,14},{7,15},{8,0},{9,1},... | collective-permute-start | bytes 239624 | tf_op jit(solution)/shard_map/ppermute | solution.py:608
  9.3 4.7 %load_weights.2 = (bf16[3072,2048]{1,0:T(8,128)(2,1)S(1)}, bf16[3072,2048]{1,0:T(8,128)(2,1)S(1)}, f32[8,128]{1,0:T(8,128)S(1)}) custom-call(bf16[24,1664]{1,0:T(8,128)(2,1)S(1)} %get-tuple-element.26.dep_ref.refs_0_, bf16[6144,2048]{1,0:T(8,128)(2,1)} %g_hbm.7, bf16[6144,2048]{1,0:T(8,128)(2,1)} %u_hbm.7), custom_call_target="tpu_custom_call" | custom-call | bytes 12582912 | tf_op jit(solution)/shard_map/load_weights/pallas_call | solution.py:86
  14.0 0.0 collective-permute-done.2.refs_3_
  14.1 0.0 collective-permute-done.1.refs_2_
  14.1 2.1 %collective-permute-done.refs_1_ = bf16[24,1664]{1,0:T(8,128)(2,1)S(1)} collective-permute-done((bf16[24,1664]{1,0:T(8,128)(2,1)S(1)}, bf16[24,1664]{1,0:T(8,128)(2,1)S(1)}, u32[]{:S(2)}, u32[]{:S(2)}) %collective-permute-start) | collective-permute-done | bytes 79904 | tf_op jit(solution)/shard_map/ppermute | solution.py:608
  16.2 0.1 unfold.1.dep_ref.array_ref
  16.2 0.1 collective-permute-start.3
  16.3 4.7 %load_weights.3 = (bf16[3072,2048]{1,0:T(8,128)(2,1)S(1)}, bf16[3072,2048]{1,0:T(8,128)(2,1)S(1)}, f32[8,128]{1,0:T(8,128)S(1)}) custom-call(bf16[48,3200]{1,0:T(8,128)(2,1)S(1)} %unfold.1.dep_ref.array_ref, bf16[6144,2048]{1,0:T(8,128)(2,1)} %g_hbm.7, bf16[6144,2048]{1,0:T(8,128)(2,1)} %u_hbm.7, ...), custom_call_target="tpu_custom_call", output_to_operand_aliasing={{0}: (3, {}), {1}: (4, {})} | custom-call | bytes 12582912 | tf_op jit(solution)/shard_map/load_weights/pallas_call | solution.py:86
  21.1 2.1 %collective-permute-done.3.array_ref = bf16[48,3200]{1,0:T(8,128)(2,1)S(1)} collective-permute-done((bf16[48,3200]{1,0:T(8,128)(2,1)S(1)}, bf16[48,3200]{1,0:T(8,128)(2,1)S(1)}, u32[]{:S(2)}, u32[]{:S(2)}) %collective-permute-start.3) | collective-permute-done | bytes 307232 | tf_op jit(solution)/shard_map/ppermute | solution.py:608
  23.2 0.1 collective-permute-start.4
  23.3 6.6 %first_half.1 = (f32[96,2048]{1,0:T(8,128)S(1)}, f32[96,2048]{1,0:T(8,128)S(1)}, bf16[3072,2048]{1,0:T(8,128)(2,1)S(1)}, bf16[3072,2048]{1,0:T(8,128)(2,1)S(1)}) custom-call(bf16[7,96,512]{2,1,0:T(8,128)(2,1)S(1)} %spread.3.x_ref, bf16[6144,2048]{1,0:T(8,128)(2,1)} %g_hbm.7, bf16[6144,2048]{1,0:T(8,128)(2,1)} %u_hbm.7, ...), custom_call_target="tpu_custom_call", output_to_operand_aliasing={{2}: (3, {}), {3}: (4, {})} | custom-call | flops 2415919104 | bytes 12582912 | tf_op jit(solution)/shard_map/first_half/pallas_call | solution.py:365
  29.9 0.0 collective-permute-done.4.ox_ref
  29.9 11.8 %second_half.1 = (f32[96,3072]{1,0:T(8,128)S(1)}, bf16[96,3072]{1,0:T(8,128)(2,1)S(1)}, bf16[3072,2048]{1,0:T(8,128)(2,1)S(1)}, bf16[3072,2048]{1,0:T(8,128)(2,1)S(1)}) custom-call(bf16[7,96,512]{2,1,0:T(8,128)(2,1)S(1)} %spread.3.x_ref, bf16[7,96,512]{2,1,0:T(8,128)(2,1)S(1)} %collective-permute-done.4.ox_ref, ...), custom_call_target="tpu_custom_call", output_to_operand_aliasing={{2}: (7, {}), {3}: (8, {})} | custom-call | flops 3623878656 | bytes 25165824 | tf_op jit(solution)/shard_map/second_half/pallas_call | solution.py:494
  41.8 0.6 collective-permute-start.5
  42.3 1.6 %collective-permute-done.5.got_ref = bf16[96,3072]{1,0:T(8,128)(2,1)S(1)} collective-permute-done((bf16[96,3072]{1,0:T(8,128)(2,1)S(1)}, bf16[96,3072]{1,0:T(8,128)(2,1)S(1)}, u32[]{:S(2)}, u32[]{:S(2)}) %collective-permute-start.5) | collective-permute-done | bytes 589856 | tf_op jit(solution)/shard_map/ppermute | solution.py:611
  44.0 0.1 split_rows.1
  44.1 0.1 collective-permute-start.6
  44.1 6.7 %collective-permute-done.6.got_ref = bf16[48,3072]{1,0:T(8,128)(2,1)S(1)} collective-permute-done((bf16[48,3072]{1,0:T(8,128)(2,1)S(1)}, bf16[48,3072]{1,0:T(8,128)(2,1)S(1)}, u32[]{:S(2)}, u32[]{:S(2)}) %collective-permute-start.6) | collective-permute-done | bytes 294944 | tf_op jit(solution)/shard_map/ppermute | solution.py:608
  50.9 0.1 split_last.1
  51.0 0.7 %collective-permute-start.7 = (bf16[24,1536]{1,0:T(8,128)(2,1)S(1)}, bf16[24,1536]{1,0:T(8,128)(2,1)S(1)}, u32[]{:S(2)}, u32[]{:S(2)}) collective-permute-start(bf16[24,1536]{1,0:T(8,128)(2,1)S(1)} %get-tuple-element.42), channel_id=1, source_target_pairs={{0,8},{1,9},{2,10},{3,11},{4,12},{5,13},{6,14},{7,15},{8,0},{9,1},... | collective-permute-start | bytes 221192 | tf_op jit(solution)/shard_map/ppermute | solution.py:608
  51.7 1.9 %collective-permute-start.8 = (bf16[24,1536]{1,0:T(8,128)(2,1)S(1)}, bf16[24,1536]{1,0:T(8,128)(2,1)S(1)}, u32[]{:S(2)}, u32[]{:S(2)}) collective-permute-start(bf16[24,1536]{1,0:T(8,128)(2,1)S(1)} %get-tuple-element.43), channel_id=1, source_target_pairs={{0,4},{1,3},{2,6},{3,1},{4,0},{5,7},{6,2},{7,5},{8,12},{9,11},{10,... | collective-permute-start | bytes 221192 | tf_op jit(solution)/shard_map/ppermute | solution.py:608
  53.6 1.8 %collective-permute-start.9 = (bf16[24,1536]{1,0:T(8,128)(2,1)S(1)}, bf16[24,1536]{1,0:T(8,128)(2,1)S(1)}, u32[]{:S(2)}, u32[]{:S(2)}) collective-permute-start(bf16[24,1536]{1,0:T(8,128)(2,1)S(1)} %get-tuple-element.44), channel_id=1, source_target_pairs={{0,12},{1,11},{2,14},{3,9},{4,8},{5,15},{6,10},{7,13},{8,4},{9,3},... | collective-permute-start | bytes 221192 | tf_op jit(solution)/shard_map/ppermute | solution.py:608
  55.4 1.9 %collective-permute-done.7.refs_0_ = bf16[24,1536]{1,0:T(8,128)(2,1)S(1)} collective-permute-done((bf16[24,1536]{1,0:T(8,128)(2,1)S(1)}, bf16[24,1536]{1,0:T(8,128)(2,1)S(1)}, u32[]{:S(2)}, u32[]{:S(2)}) %collective-permute-start.7) | collective-permute-done | bytes 73760 | tf_op jit(solution)/shard_map/ppermute | solution.py:608
  57.4 0.4 collective-permute-done.8.refs_1_
  57.7 2.1 %collective-permute-done.9.refs_2_ = bf16[24,1536]{1,0:T(8,128)(2,1)S(1)} collective-permute-done((bf16[24,1536]{1,0:T(8,128)(2,1)S(1)}, bf16[24,1536]{1,0:T(8,128)(2,1)S(1)}, u32[]{:S(2)}, u32[]{:S(2)}) %collective-permute-start.9) | collective-permute-done | bytes 73760 | tf_op jit(solution)/shard_map/ppermute | solution.py:608
  59.8 0.7 %finish.1 = bf16[12,3072]{1,0:T(8,128)(2,1)} custom-call(f32[12,3072]{1,0:T(8,128)S(1)} %get-tuple-element.25.carried_ref, f32[12,3072]{1,0:T(8,128)S(1)} %get-tuple-element.41.own_ref, bf16[24,1536]{1,0:T(8,128)(2,1)S(1)} %collective-permute-done.7.refs_0_, bf16[24,1536]{1,0:T(8,128)(2,1)S(1)} %collective-permute-done.8.refs_1_, ...), custom_call_target="tpu_custom_call" | custom-call | tf_op jit(solution)/shard_map/finish/pallas_call | solution.py:584
  (2 shorter events, 0.0 us)
Async XLA Ops:
  3.6 10.5 %collective-permute-start.2 = (bf16[24,1664]{1,0:T(8,128)(2,1)S(1)}, bf16[24,1664]{1,0:T(8,128)(2,1)S(1)}, u32[]{:S(2)}, u32[]{:S(2)}) collective-permute-start(bf16[24,1664]{1,0:T(8,128)(2,1)S(1)} %get-tuple-element.26.dep_ref.refs_0_), channel_id=1, source_target_pairs={{0,12},{1,11},{2,14},{3,9},{4,8},{5,15},{6,10},{7,13},{8,4},{9,3},... | collective-permute-start | bytes 239624 | tf_op jit(solution)/shard_map/ppermute | solution.py:608
  8.7 5.4 %collective-permute-start.1 = (bf16[24,1664]{1,0:T(8,128)(2,1)S(1)}, bf16[24,1664]{1,0:T(8,128)(2,1)S(1)}, u32[]{:S(2)}, u32[]{:S(2)}) collective-permute-start(bf16[24,1664]{1,0:T(8,128)(2,1)S(1)} %get-tuple-element.26.dep_ref.refs_0_), channel_id=1, source_target_pairs={{0,4},{1,3},{2,6},{3,1},{4,0},{5,7},{6,2},{7,5},{8,12},{9,11},{10,... | collective-permute-start | bytes 239624 | tf_op jit(solution)/shard_map/ppermute | solution.py:608
  8.7 7.5 %collective-permute-start = (bf16[24,1664]{1,0:T(8,128)(2,1)S(1)}, bf16[24,1664]{1,0:T(8,128)(2,1)S(1)}, u32[]{:S(2)}, u32[]{:S(2)}) collective-permute-start(bf16[24,1664]{1,0:T(8,128)(2,1)S(1)} %get-tuple-element.26.dep_ref.refs_0_), channel_id=1, source_target_pairs={{0,8},{1,9},{2,10},{3,11},{4,12},{5,13},{6,14},{7,15},{8,0},{9,1},... | collective-permute-start | bytes 239624 | tf_op jit(solution)/shard_map/ppermute | solution.py:608
  16.2 6.9 %collective-permute-start.3 = (bf16[48,3200]{1,0:T(8,128)(2,1)S(1)}, bf16[48,3200]{1,0:T(8,128)(2,1)S(1)}, u32[]{:S(2)}, u32[]{:S(2)}) collective-permute-start(bf16[48,3200]{1,0:T(8,128)(2,1)S(1)} %unfold.1.dep_ref.array_ref), channel_id=1, source_target_pairs={{0,2},{1,5},{2,0},{3,7},{4,6},{5,1},{6,4},{7,3},{8,10},{9,13},{10,... | collective-permute-start | bytes 921608 | tf_op jit(solution)/shard_map/ppermute | solution.py:608
  23.2 6.7 %collective-permute-start.4 = (bf16[7,96,512]{2,1,0:T(8,128)(2,1)S(1)}, bf16[7,96,512]{2,1,0:T(8,128)(2,1)S(1)}, u32[]{:S(2)}, u32[]{:S(2)}) collective-permute-start(bf16[7,96,512]{2,1,0:T(8,128)(2,1)S(1)} %spread.3.x_ref), channel_id=1, source_target_pairs={{0,1},{1,0},{2,3},{3,2},{4,5},{5,4},{6,7},{7,6},{8,9},{9,8},{10,11... | collective-permute-start | bytes 2064392 | tf_op jit(solution)/shard_map/ppermute | solution.py:611
  41.8 2.2 %collective-permute-start.5 = (bf16[96,3072]{1,0:T(8,128)(2,1)S(1)}, bf16[96,3072]{1,0:T(8,128)(2,1)S(1)}, u32[]{:S(2)}, u32[]{:S(2)}) collective-permute-start(bf16[96,3072]{1,0:T(8,128)(2,1)S(1)} %get-tuple-element.38), channel_id=1, source_target_pairs={{0,1},{1,0},{2,3},{3,2},{4,5},{5,4},{6,7},{7,6},{8,9},{9,8},{10,11... | collective-permute-start | bytes 1769480 | tf_op jit(solution)/shard_map/ppermute | solution.py:611
  44.1 6.8 %collective-permute-start.6 = (bf16[48,3072]{1,0:T(8,128)(2,1)S(1)}, bf16[48,3072]{1,0:T(8,128)(2,1)S(1)}, u32[]{:S(2)}, u32[]{:S(2)}) collective-permute-start(bf16[48,3072]{1,0:T(8,128)(2,1)S(1)} %get-tuple-element.40), channel_id=1, source_target_pairs={{0,2},{1,5},{2,0},{3,7},{4,6},{5,1},{6,4},{7,3},{8,10},{9,13},{10,... | collective-permute-start | bytes 884744 | tf_op jit(solution)/shard_map/ppermute | solution.py:608
  51.0 6.4 %collective-permute-start.7 = (bf16[24,1536]{1,0:T(8,128)(2,1)S(1)}, bf16[24,1536]{1,0:T(8,128)(2,1)S(1)}, u32[]{:S(2)}, u32[]{:S(2)}) collective-permute-start(bf16[24,1536]{1,0:T(8,128)(2,1)S(1)} %get-tuple-element.42), channel_id=1, source_target_pairs={{0,8},{1,9},{2,10},{3,11},{4,12},{5,13},{6,14},{7,15},{8,0},{9,1},... | collective-permute-start | bytes 221192 | tf_op jit(solution)/shard_map/ppermute | solution.py:608
  51.7 6.0 %collective-permute-start.8 = (bf16[24,1536]{1,0:T(8,128)(2,1)S(1)}, bf16[24,1536]{1,0:T(8,128)(2,1)S(1)}, u32[]{:S(2)}, u32[]{:S(2)}) collective-permute-start(bf16[24,1536]{1,0:T(8,128)(2,1)S(1)} %get-tuple-element.43), channel_id=1, source_target_pairs={{0,4},{1,3},{2,6},{3,1},{4,0},{5,7},{6,2},{7,5},{8,12},{9,11},{10,... | collective-permute-start | bytes 221192 | tf_op jit(solution)/shard_map/ppermute | solution.py:608
  53.6 6.2 %collective-permute-start.9 = (bf16[24,1536]{1,0:T(8,128)(2,1)S(1)}, bf16[24,1536]{1,0:T(8,128)(2,1)S(1)}, u32[]{:S(2)}, u32[]{:S(2)}) collective-permute-start(bf16[24,1536]{1,0:T(8,128)(2,1)S(1)} %get-tuple-element.44), channel_id=1, source_target_pairs={{0,12},{1,11},{2,14},{3,9},{4,8},{5,15},{6,10},{7,13},{8,4},{9,3},... | collective-permute-start | bytes 221192 | tf_op jit(solution)/shard_map/ppermute | solution.py:608

commit v8 on v7

v8 whole, which is shorter than its diff:
```python
import functools
import math

import jax
import jax.numpy as jnp
from jax import lax
from jax.experimental import pallas as pl
from jax.experimental.pallas import tpu as pltpu
from jax.sharding import PartitionSpec as P

MIB = 1 << 20
QUERY_HEADS = 48
KV_HEADS = 8
HEAD_DIM = 128
EXPERTS = 4
GROUP = QUERY_HEADS // KV_HEADS
LANES = 128
FOLD = 2
F32 = jnp.float32
BF16 = jnp.bfloat16


def small(shape, dtype):
    return math.prod(shape) * jnp.dtype(dtype).itemsize <= 17 * MIB // 4


def vmem_array(shape, dtype):
    return pltpu.VMEM(shape, dtype) if small(shape, dtype) else jax.ShapeDtypeStruct(shape, dtype)


def in_vmem(*arrays):
    return [
        pltpu.with_memory_space_constraint(a, pltpu.VMEM) if small(a.shape, a.dtype) else a
        for a in arrays
    ]


def in_vmem_always(arrays):
    return [pltpu.with_memory_space_constraint(a, pltpu.VMEM) for a in arrays]


def in_hbm(*arrays):
    return [pltpu.with_memory_space_constraint(a, pltpu.HBM) for a in arrays]


VMEM_SPEC = pl.BlockSpec(memory_space=pltpu.VMEM)
HBM_SPEC = pl.BlockSpec(memory_space=pltpu.HBM)
ROUTE_LANE = 3 + 3 * EXPERTS
HELD_BELOW = 10 * MIB


def own_side():
    return lax.axis_index("shard")


def chunk_of(units):
    return math.gcd(512, units)


def held_shape(gate_weight):
    width, units = gate_weight.shape
    return width // 2, units + chunk_of(units)


def row_copies(sources, targets, first, rows, sems):
    parts = sems.shape[1]
    part = rows // parts
    half, units = sources[0].shape[0] // 2, sources[0].shape[1]
    copies = []
    for p in range(parts):
        at = first + p * part
        for i, (source, target) in enumerate(zip(sources, targets)):
            copies.append(
                pltpu.make_async_copy(
                    source.at[pl.ds(pl.multiple_of(own_side() * half + at, 16), part), :],
                    target.at[pl.ds(at, part), pl.ds(0, units)], sems.at[i, p],
                )
            )
    return copies


def slot_at(q, chunk, slots):
    start = lax.rem(q, slots) * chunk
    return pl.ds(start if isinstance(q, int) else pl.multiple_of(start, LANES), chunk)


def other_copy(source, target, c, chunk, sem):
    half, units = target.shape[0], source.shape[1]
    chunks = units // chunk
    first = pl.multiple_of((1 - own_side()) * half, 16)
    column = c * chunk if isinstance(c, int) else pl.multiple_of(c * chunk, LANES)
    return pltpu.make_async_copy(
        source.at[pl.ds(first, half), pl.ds(column, chunk)],
        target.at[:, slot_at(chunks + c, chunk, chunks + 1)], sem,
    )


def load_kernel(first, rows, ahead, dep_ref, g_hbm, u_hbm, g_in, u_in, g_vmem, u_vmem, token_ref, sems, sem):
    del g_in, u_in
    copies = row_copies((g_hbm, u_hbm), (g_vmem, u_vmem), first, rows, sems)
    if ahead:
        copies.append(other_copy(g_hbm, g_vmem, 0, chunk_of(g_hbm.shape[1]), sem))
    for copy in copies:
        copy.start()
    token_ref[...] = jnp.zeros_like(token_ref)
    for copy in copies:
        copy.wait()


def load_rows(first, rows, ahead, after, gate_weight, up_weight, held):
    hidden = gate_weight.shape[1]
    return pl.pallas_call(
        functools.partial(load_kernel, first, rows, ahead),
        out_shape=tuple(pltpu.VMEM(h.shape, BF16) for h in held) + (pltpu.VMEM((8, LANES), F32),),
        in_specs=[pl.BlockSpec(memory_space=pl.ANY), HBM_SPEC, HBM_SPEC, VMEM_SPEC, VMEM_SPEC],
        out_specs=(VMEM_SPEC,) * 3,
        scratch_shapes=[pltpu.SemaphoreType.DMA((2, 4)), pltpu.SemaphoreType.DMA],
        input_output_aliases={3: 0, 4: 1},
        compiler_params=pltpu.CompilerParams(vmem_limit_bytes=HELD_BELOW),
        cost_estimate=pl.CostEstimate(flops=0, bytes_accessed=4 * rows * hidden, transcendentals=0),
        name="load_weights",
    )(*in_vmem(after), *in_hbm(gate_weight, up_weight), *in_vmem_always(held))


def unfold_kernel(tok, *refs):
    *arrays, _, out_ref, scr = refs
    fold_width = arrays[0].shape[1] - LANES
    for i, array in enumerate(arrays):
        rows = array[...].astype(F32)
        to = slice(i * tok, (i + 1) * tok)
        for f in range(FOLD):
            scr[to, f * fold_width:(f + 1) * fold_width] = rows[f * tok:(f + 1) * tok, :fold_width]
        scr[to, FOLD * fold_width:] = rows[:tok, fold_width:]
    out_ref[...] = scr[...].astype(BF16)


def unfold(tok, arrays, token):
    shape = (len(arrays) * tok, FOLD * (arrays[0].shape[1] - LANES) + LANES)
    return pl.pallas_call(
        functools.partial(unfold_kernel, tok),
        out_shape=pltpu.VMEM(shape, BF16),
        in_specs=[VMEM_SPEC] * (len(arrays) + 1),
        out_specs=VMEM_SPEC,
        scratch_shapes=[pltpu.VMEM(shape, F32)],
        compiler_params=pltpu.CompilerParams(vmem_limit_bytes=3 * MIB),
        name="unfold",
    )(*in_vmem_always([*arrays, token]))


def join_kernel(a_ref, b_ref, token_ref, out_ref):
    rows = a_ref.shape[0]
    out_ref[:rows, :] = a_ref[...]
    out_ref[rows:, :] = b_ref[...]


def join(a, b, token):
    return pl.pallas_call(
        join_kernel,
        out_shape=vmem_array((a.shape[0] + b.shape[0], a.shape[1]), BF16),
        in_specs=[VMEM_SPEC] * 3,
        out_specs=VMEM_SPEC,
        compiler_params=pltpu.CompilerParams(vmem_limit_bytes=HELD_BELOW),
        name="join",
    )(*in_vmem(a, b, token))


def split_three(value):
    first = value.astype(BF16).astype(F32)
    second = (value - first).astype(BF16).astype(F32)
    return first, second, value - first - second


def attend_kernel(
    ahead, len_hbm, routes_hbm, q_hbm, k_hbm, v_hbm, nk_hbm, nv_hbm, res_hbm, gain_hbm, rt_hbm,
    g_hbm, u_hbm, carried_ref, pay_ref, g_vmem, u_vmem,
    q_ref, k_ref, v_ref, nk_ref, nv_ref, res_ref, gain_ref, rt_ref,
    q_scr, o_scr, nk_scr, nv_scr, pay_scr, len_ref, routes_ref, sems, w_sems,
):
    tok, width = q_ref.shape
    cache_len, kv_width = k_ref.shape[1], k_ref.shape[2]
    heads = width // HEAD_DIM
    groups = kv_width // HEAD_DIM
    fold_width = width // FOLD
    scaling = 1.0 / math.sqrt(HEAD_DIM)
    columns = pl.ds(pl.multiple_of(own_side() * width, LANES), width)
    moves = [
        (q_hbm, q_ref), (k_hbm, k_ref), (nk_hbm, nk_ref), (len_hbm, len_ref), (v_hbm, v_ref),
        (nv_hbm, nv_ref), (res_hbm, res_ref),
        (gain_hbm.at[:, columns], gain_ref), (rt_hbm.at[:, columns], rt_ref),
        (routes_hbm, routes_ref),
    ]
    copies = [pltpu.make_async_copy(a, b, sems.at[i]) for i, (a, b) in enumerate(moves)]
    weights = row_copies((g_hbm, u_hbm), (g_vmem, u_vmem), 0, ahead, w_sems)
    for copy in copies:
        copy.start()
    copies[0].wait()
    for h in range(heads):
        q_scr[h * tok:(h + 1) * tok, :] = q_ref[:, h * HEAD_DIM:(h + 1) * HEAD_DIM].astype(F32)
    copies[2].wait()
    nk_scr[...] = nk_ref[...].astype(F32)
    row_group = lax.broadcasted_iota(jnp.int32, (heads, HEAD_DIM), 0) // GROUP
    position = lax.broadcasted_iota(jnp.int32, (heads, cache_len), 1)
    scores, fresh = [], []
    for t in range(tok):
        if t == 0:
            copies[1].wait()
            for copy in weights:
                copy.start()
        q_rows = q_scr[pl.ds(t, heads, stride=tok), :]
        q_wide = jnp.concatenate(
            [jnp.where(row_group == g, q_rows, 0.0) for g in range(groups)], axis=1
        )
        scores.append(
            lax.dot_general(
                q_wide.astype(BF16), k_ref[t], (((1,), (1,)), ((), ())),
                preferred_element_type=F32,
            ) * scaling
        )
        fresh.append(
            jnp.sum(q_wide * nk_scr[pl.ds(t, 1), :], axis=1, keepdims=True) * scaling
        )
    copies[3].wait()
    terms, fresh_terms, totals = [], [], []
    for t in range(tok):
        score = jnp.where(position < len_ref[t], scores[t], -1e30)
        largest = jnp.maximum(jnp.max(score, axis=1, keepdims=True), fresh[t])
        term = jnp.exp(score - largest)
        fresh_term = jnp.exp(fresh[t] - largest)
        totals.append(jnp.sum(term, axis=1, keepdims=True) + fresh_term)
        terms.append(term.astype(BF16))
        fresh_terms.append(fresh_term.astype(BF16).astype(F32))
    copies[5].wait()
    nv_scr[...] = nv_ref[...].astype(F32)
    for t in range(tok):
        if t == 0:
            copies[4].wait()
        wide = jnp.dot(terms[t], v_ref[t], preferred_element_type=F32)
        wide = wide + fresh_terms[t] * nv_scr[pl.ds(t, 1), :]
        picked = wide[:, :HEAD_DIM]
        for g in range(1, groups):
            picked = jnp.where(
                row_group == g, wide[:, g * HEAD_DIM:(g + 1) * HEAD_DIM], picked
            )
        o_scr[pl.ds(t, heads, stride=tok), :] = picked / totals[t]
    for copy in copies[6:]:
        copy.wait()
    for h in range(heads):
        cols = slice(h * HEAD_DIM, (h + 1) * HEAD_DIM)
        carried_ref[:, cols] = res_ref[:, cols].astype(F32) + o_scr[h * tok:(h + 1) * tok, :]
    carried = carried_ref[...]
    scaled = carried * gain_ref[...]
    rounded = scaled.astype(BF16).astype(F32)
    router = rt_ref[...].astype(F32)
    for f in range(FOLD):
        pay_scr[f * tok:(f + 1) * tok, :fold_width] = scaled[:, f * fold_width:(f + 1) * fold_width]
    lane = lax.broadcasted_iota(jnp.int32, (tok, LANES), 1)
    row = lax.broadcasted_iota(jnp.int32, (tok, LANES), 0)
    sums = [jnp.sum(carried * carried, axis=1, keepdims=True)]
    for e in range(EXPERTS):
        sums.append(jnp.sum(rounded * router[e:e + 1, :], axis=1, keepdims=True))
    extra = jnp.zeros((tok, LANES), F32)
    for i, total in enumerate(sums):
        for j, term in enumerate(split_three(total)):
            extra = jnp.where(lane == 3 * i + j, term, extra)
    for t in range(tok):
        for i in range(2):
            extra = jnp.where(
                jnp.logical_and(row == t, lane == ROUTE_LANE + i),
                routes_ref[i, t].astype(F32), extra,
            )
    for f in range(FOLD):
        pay_scr[f * tok:(f + 1) * tok, fold_width:] = extra
    pay_ref[...] = pay_scr[...].astype(BF16)
    for copy in weights:
        copy.wait()


def attend(
    ahead, lengths, routes_t, queries, key_cache, value_cache, new_key, new_value,
    residual, gain, router_t, gate_weight, up_weight,
):
    tok, width = queries.shape
    kv_width = new_key.shape[1]
    heads = width // HEAD_DIM
    wide = width // FOLD + LANES
    here = [
        pltpu.VMEM(a.shape, a.dtype)
        for a in (queries, key_cache, value_cache, new_key, new_value, residual)
    ]
    return pl.pallas_call(
        functools.partial(attend_kernel, ahead),
        out_shape=(
            pltpu.VMEM((tok, width), F32),
            pltpu.VMEM((FOLD * tok, wide), BF16),
            pltpu.VMEM(held_shape(gate_weight), BF16),
            pltpu.VMEM(held_shape(gate_weight), BF16),
        ),
        in_specs=[HBM_SPEC] * 12,
        out_specs=(VMEM_SPEC,) * 4,
        scratch_shapes=here + [
            pltpu.VMEM((1, width), F32),
            pltpu.VMEM((EXPERTS, width), BF16),
            pltpu.VMEM((heads * tok, HEAD_DIM), F32),
            pltpu.VMEM((heads * tok, HEAD_DIM), F32),
            pltpu.VMEM((tok, kv_width), F32),
            pltpu.VMEM((tok, kv_width), F32),
            pltpu.VMEM((FOLD * tok, wide), F32),
            pltpu.SMEM(lengths.shape, jnp.int32),
            pltpu.SMEM(routes_t.shape, jnp.int32),
            pltpu.SemaphoreType.DMA((10,)),
            pltpu.SemaphoreType.DMA((2, 1)),
        ],
        compiler_params=pltpu.CompilerParams(vmem_limit_bytes=HELD_BELOW),
        cost_estimate=pl.CostEstimate(flops=10**8, bytes_accessed=8 * 10**6, transcendentals=10**5),
        name="attend",
    )(
        *in_hbm(
            lengths, routes_t, queries, key_cache, value_cache, new_key, new_value, residual, gain, router_t,
            gate_weight, up_weight,
        ),
    )


def first_half_kernel(x_ref, g_hbm, u_hbm, g_in, u_in, gate_ref, up_ref, g_ref, u_ref, sems):
    del g_in, u_in
    half, units = g_ref.shape[0], gate_ref.shape[1]
    chunk = chunk_of(units)
    chunks = units // chunk
    ready = [(1, 0)] + [(0, 1), (1, 1), (0, 2)][:2 * (chunks - 1)]
    ready = [(i, c) for i, c in ready if c < chunks]

    def copy(i, c):
        return other_copy((g_hbm, u_hbm)[i], (g_ref, u_ref)[i], c, chunk, sems.at[i, c])

    copy(1, 0).start()

    def step(n, _):
        at = pl.ds(pl.multiple_of(n * chunk, LANES), chunk)
        rows = x_ref[:, :half]
        gate_ref[:, at] = jnp.dot(rows, g_ref[:, at], preferred_element_type=F32)
        up_ref[:, at] = jnp.dot(rows, u_ref[:, at], preferred_element_type=F32)
        for i, c in ready[1:]:
            @pl.when(n == c - 1)
            def _(i=i, c=c):
                copy(i, c).start()

        return 0

    lax.fori_loop(0, chunks, step, 0)
    for i, c in ready:
        copy(i, c).wait()


def first_half(mine, held, gate_weight, up_weight):
    rows = mine.shape[0]
    width, units = gate_weight.shape
    acc = pltpu.VMEM((rows, units), F32)
    return pl.pallas_call(
        first_half_kernel,
        out_shape=(acc, acc) + tuple(pltpu.VMEM(h.shape, BF16) for h in held),
        in_specs=[VMEM_SPEC] + [HBM_SPEC] * 2 + [VMEM_SPEC] * 2,
        out_specs=(VMEM_SPEC,) * 4,
        scratch_shapes=[pltpu.SemaphoreType.DMA((2, units // chunk_of(units)))],
        input_output_aliases={3: 2, 4: 3},
        compiler_params=pltpu.CompilerParams(vmem_limit_bytes=HELD_BELOW),
        cost_estimate=pl.CostEstimate(
            flops=2 * rows * width * units, bytes_accessed=width * units, transcendentals=0
        ),
        name="first_half",
    )(*in_vmem_always([mine]), *in_hbm(gate_weight, up_weight), *in_vmem_always(held))


def second_half_kernel(
    per_plane, x_ref, ox_ref, gate_ref, up_ref, g_hbm, u_hbm, d_hbm, g_in, u_in,
    staying_ref, leaving_ref, g_ref, u_ref, x_scr, h_scr, gu_sems, sems,
):
    del g_in, u_in
    rows, units = h_scr.shape
    width = staying_ref.shape[1]
    side = own_side()
    chunk = chunk_of(units)
    chunks = units // chunk
    slots = chunks + 1
    per_side = width // chunk
    pairs = per_side

    def gu_copy(i, c):
        return other_copy((g_hbm, u_hbm)[i], (g_ref, u_ref)[i], c, chunk, gu_sems.at[i, c])

    def down_copy(i, p):
        n = 2 * p + i
        column = jnp.where(n < per_side, 1 - side, side) * width + lax.rem(n, per_side) * chunk
        return pltpu.make_async_copy(
            d_hbm.at[:, pl.ds(pl.multiple_of(column, LANES), chunk)],
            (g_ref, u_ref)[i].at[pl.ds(0, units), slot_at(2 * chunks + p, chunk, slots)],
            sems.at[i, p],
        )

    def in_order(values):
        quarter = rows // 4
        return jnp.concatenate(
            [values[q * quarter:(q + 1) * quarter, :] for q in (0, 2, 1, 3)], axis=0
        )

    later = [(1, 2)] if chunks > 2 else []
    later += [(i, c) for c in range(3, chunks) for i in range(2)]
    for i, c in later:
        gu_copy(i, c).start()
    for i in range(2):
        down_copy(i, 0).start()
    x_scr[...] = in_order(ox_ref[:, :width].astype(F32)).astype(BF16)

    own = x_ref[:, width:].astype(F32)
    both = own + in_order(ox_ref[:, width:].astype(F32))
    lane = lax.broadcasted_iota(jnp.int32, (rows, LANES), 1)

    def pick(values, mask):
        return jnp.sum(jnp.where(mask, values, 0.0), axis=1, keepdims=True)

    scale = lax.rsqrt(pick(both, lane < 3) * (1.0 / (2 * width)) + 1e-05)
    first, second = pick(own, lane == ROUTE_LANE), pick(own, lane == ROUTE_LANE + 1)
    expert_of = (lane - 3) // 3
    logit_lane = jnp.logical_and(lane >= 3, lane < ROUTE_LANE)

    def logit_at(route):
        return pick(both, jnp.logical_and(logit_lane, expert_of == route.astype(jnp.int32))) * scale

    share = 1.0 / (1.0 + jnp.exp(logit_at(second) - logit_at(first)))
    here = (lax.axis_index("node") // per_plane).astype(F32)
    weight = jnp.where(first == here, share, 0.0) + jnp.where(second == here, 1.0 - share, 0.0)

    def hidden_step(c, _):
        for i, late in later:
            @pl.when(c == late)
            def _(i=i, late=late):
                gu_copy(i, late).wait()

        slot = slot_at(chunks + c, chunk, slots)
        at = pl.ds(pl.multiple_of(c * chunk, LANES), chunk)
        gate = gate_ref[:, at] + jnp.dot(x_scr[...], g_ref[:, slot], preferred_element_type=F32)
        up = up_ref[:, at] + jnp.dot(x_scr[...], u_ref[:, slot], preferred_element_type=F32)
        gate = gate * scale
        h_scr[:, at] = (gate / (1.0 + jnp.exp(-gate)) * (up * scale)).astype(BF16)

        @pl.when(c + 1 < pairs)
        def _():
            for i in range(2):
                down_copy(i, c + 1).start()

        return 0

    lax.fori_loop(0, chunks, hidden_step, 0)

    def down_step(p, _):
        slot = slot_at(2 * chunks + p, chunk, slots)
        for i, ref in enumerate((g_ref, u_ref)):
            n = 2 * p + i
            down_copy(i, p).wait()
            value = jnp.dot(h_scr[...], ref[:units, slot], preferred_element_type=F32) * weight
            to = pl.ds(pl.multiple_of(lax.rem(n, per_side) * chunk, LANES), chunk)

            @pl.when(n < per_side)
            def _(value=value, to=to):
                leaving_ref[:, to] = in_order(value).astype(BF16)

            @pl.when(n >= per_side)
            def _(value=value, to=to):
                staying_ref[:, to] = value

        @pl.when(p + slots < pairs)
        def _():
            for i in range(2):
                down_copy(i, p + slots).start()

        return 0

    lax.fori_loop(0, pairs, down_step, 0)


def second_half(per_plane, mine, other, sums, held, gate_weight, up_weight, down_weight):
    rows, units = sums[0].shape
    width = down_weight.shape[1] // 2
    chunk = chunk_of(units)
    return pl.pallas_call(
        functools.partial(second_half_kernel, per_plane),
        out_shape=(vmem_array((rows, width), F32), vmem_array((rows, width), BF16))
        + tuple(pltpu.VMEM(h.shape, BF16) for h in held),
        in_specs=[VMEM_SPEC] * 4 + [HBM_SPEC] * 3 + [VMEM_SPEC] * 2,
        out_specs=(VMEM_SPEC,) * 4,
        scratch_shapes=[
            pltpu.VMEM((rows, width), BF16),
            pltpu.VMEM((rows, units), BF16),
            pltpu.SemaphoreType.DMA((2, units // chunk)),
            pltpu.SemaphoreType.DMA((2, width // chunk)),
        ],
        input_output_aliases={7: 2, 8: 3},
        compiler_params=pltpu.CompilerParams(
            vmem_limit_bytes=HELD_BELOW if rows < 256 else 40 * MIB
        ),
        cost_estimate=pl.CostEstimate(
            flops=6 * rows * width * units, bytes_accessed=4 * width * units, transcendentals=0
        ),
        name="second_half",
    )(
        *in_vmem_always([mine, other]), *in_vmem(*sums),
        *in_hbm(gate_weight, up_weight, down_weight), *in_vmem_always(held),
    )[:2]


def split_kernel(own_ref, got_ref, keep_ref, send_ref):
    size = keep_ref.shape[0]
    keep_ref[...] = own_ref[:size, :] + got_ref[:size, :].astype(F32)
    send_ref[...] = (own_ref[size:, :] + got_ref[size:, :].astype(F32)).astype(BF16)


def split_rows(own, got):
    rows, width = own.shape
    size = rows // 2
    return pl.pallas_call(
        split_kernel,
        out_shape=(vmem_array((size, width), F32), vmem_array((size, width), BF16)),
        in_specs=[VMEM_SPEC] * 2,
        out_specs=(VMEM_SPEC,) * 2,
        compiler_params=pltpu.CompilerParams(vmem_limit_bytes=(8 if rows < 256 else 32) * MIB),
        name="split_rows",
    )(*in_vmem(own, got))


def split_last_kernel(own_ref, got_ref, keep_ref, *refs):
    *sends, total = refs
    total[...] = own_ref[...] + got_ref[...].astype(F32)
    tok, width = keep_ref.shape
    fold_width = width // FOLD
    keep_ref[...] = total[:tok, :]
    for i, send in enumerate(sends, 1):
        rows = total[i * tok:(i + 1) * tok, :]
        send[...] = jnp.concatenate(
            [rows[:, f * fold_width:(f + 1) * fold_width] for f in range(FOLD)], axis=0
        ).astype(BF16)


def split_last(own, got, parts):
    rows, width = own.shape
    tok = rows // parts
    return pl.pallas_call(
        split_last_kernel,
        out_shape=(pltpu.VMEM((tok, width), F32),)
        + (pltpu.VMEM((FOLD * tok, width // FOLD), BF16),) * (parts - 1),
        in_specs=[VMEM_SPEC] * 2,
        out_specs=(VMEM_SPEC,) * parts,
        scratch_shapes=[pltpu.VMEM((rows, width), F32)],
        compiler_params=pltpu.CompilerParams(vmem_limit_bytes=4 * MIB),
        name="split_last",
    )(*in_vmem(own, got))


def finish_kernel(carried_ref, own_ref, *refs):
    *got, out_ref, folded = refs
    tok, width = carried_ref.shape
    fold_width = width // FOLD
    total = got[0][...].astype(F32)
    for ref in got[1:]:
        total = total + ref[...].astype(F32)
    folded[...] = total
    for f in range(FOLD):
        at = slice(f * fold_width, (f + 1) * fold_width)
        value = carried_ref[:, at] + own_ref[:, at] + folded[f * tok:(f + 1) * tok, :]
        out_ref[:, at] = value.astype(BF16)


def finish(carried, own, got):
    tok, width = carried.shape
    return pl.pallas_call(
        finish_kernel,
        out_shape=jax.ShapeDtypeStruct((tok, width), BF16),
        in_specs=[VMEM_SPEC] * (2 + len(got)),
        out_specs=VMEM_SPEC,
        scratch_shapes=[pltpu.VMEM((FOLD * tok, width // FOLD), F32)],
        compiler_params=pltpu.CompilerParams(vmem_limit_bytes=8 * MIB),
        name="finish",
    )(*in_vmem(carried, own, *got))


def on_device(
    residual, queries, key_cache, value_cache, new_key, new_value, cache_lengths,
    norm_gain, router, routes, gate_weight, up_weight, down_weight,
):
    nodes = lax.axis_size("node")
    per_plane = nodes // EXPERTS
    stages = nodes.bit_length() - 1
    masks = [nodes >> (s + 1) for s in range(stages)]
    routes_of = (masks, masks[:-2] + masks[:-3:-1])

    def exchange(array, *flips):
        masks = [sum(side[s] for s in flips) for side in routes_of]
        perm = [(2 * n + c, 2 * (n ^ masks[c]) + c) for n in range(nodes) for c in range(2)]
        return lax.ppermute(array, ("node", "shard"), perm)

    def to_core(array):
        return lax.ppermute(array, "shard", [(0, 1), (1, 0)])

    tok = residual.shape[0]
    half = gate_weight.shape[0] // 2
    heights = [half // 6, half // 2, half // 3]
    carried, payload, *held = attend(
        heights[0], cache_lengths, routes.T, queries, key_cache, value_cache, new_key, new_value,
        residual, norm_gain.reshape(1, -1), router.T, gate_weight, up_weight,
    )
    near = ((0,), (1,), (0, 1))
    got = [exchange(payload, *flips) for flips in near]
    *held, token = load_rows(
        heights[0], heights[1], False, payload, gate_weight, up_weight, held
    )
    payload = unfold(tok, [payload, *got], token)
    for stage in range(2, stages):
        got = exchange(payload, stage)
        if stage == 2:
            *held, token = load_rows(
                heights[0] + heights[1], heights[2], True, payload, gate_weight, up_weight, held
            )
        payload = join(payload, got, token)
    mine = payload
    other = to_core(mine)
    gate, up, *held = first_half(mine, held, gate_weight, up_weight)
    staying, leaving = second_half(
        per_plane, mine, other, (gate, up), held, gate_weight, up_weight, down_weight
    )
    keep, got = staying, to_core(leaving)
    for stage in range(stages - 1, 1, -1):
        keep, send = split_rows(keep, got)
        got = exchange(send, stage)
    keep, *sends = split_last(keep, got, 1 + len(near))
    return finish(carried, keep, [exchange(send, *flips) for send, flips in zip(sends, near)])


def solution(mesh):
    rows = ("replica", "node")
    in_specs = (
        P(rows, "shard"),
        P(rows, "shard"),
        P(rows, None, "shard"),
        P(rows, None, "shard"),
        P(rows, "shard"),
        P(rows, "shard"),
        P(rows),
        P(),
        P(),
        P(rows, None),
        P(None, ("node", "shard")),
        P(None, ("node", "shard")),
        P(("node", "shard"), None),
    )
    return jax.shard_map(
        on_device,
        mesh=mesh,
        in_specs=in_specs,
        out_specs=P(rows, "shard"),
        check_vma=False,
    )
```

time: 60.6 us -> 70.2 us (1.16)
  local copies, waits for them, and re-layouts: 0 us -> 11 us
  waiting for transfers between devices: 16.9 us -> 14.6 us
  starting transfers between devices: 11 us -> 13.2 us
  Pallas kernels: 32.5 us -> 31.2 us
    unnamed x0 -> x4, local copies, waits for them, and re-layouts: none -> 11 us
    ppermute x8, waiting for transfers between devices: 15.3 us -> 13 us  [exchange(): return lax.ppermute(array, ('node', 'shard'), perm)]
    ppermute x8, starting transfers between devices: 10.4 us -> 12.5 us  [exchange(): return lax.ppermute(array, ('node', 'shard'), perm)]
    pallas_call x7 -> x6, Pallas kernels: 31.5 us -> 30.2 us  [the longest x1 12.1 us: second_half(): pl.pallas_call(functools.partial(second_half_kernel, per_plane), out_shap...]
  transfers between devices with their start and end apart: 10 -> 10, of which waited for: 7 -> 6; matrix products, arithmetic and copies ran while one was open for 0% -> 0% of each run, Pallas kernels for 27% -> 20%
where the time goes in v8:
time: 70.2 us; the launch traced here: 70.1 us
  Pallas kernels  31.2 us (44%)
  waiting for transfers between devices  14.6 us (21%)
  starting transfers between devices  13.2 us (19%)
  local copies, waits for them, and re-layouts  11 us (16%)
    ppermute x8, waiting for transfers between devices, exchange(): return lax.ppermute(array, ('node', 'shard'), perm)  13 us
    ppermute x8, starting transfers between devices, exchange(): return lax.ppermute(array, ('node', 'shard'), perm)  12.5 us
    pallas_call x1, Pallas kernels, second_half(): pl.pallas_call(functools.partial(second_half_kernel, per_plane), out_shap...  12.1 us
    unnamed x4, local copies, waits for them, and re-layouts  11 us
    pallas_call x2, Pallas kernels, load_rows(): pl.pallas_call(functools.partial(load_kernel, first, rows, ahead), out_sh...  9.18 us
    pallas_call x1, Pallas kernels, first_half(): pl.pallas_call(first_half_kernel, out_shape=(acc, acc) + tuple((pltpu.VME...  4.98 us
    pallas_call x1, Pallas kernels, attend(): pl.pallas_call(functools.partial(attend_kernel, ahead), out_shape=(pltpu....  3.93 us
    ppermute x2, waiting for transfers between devices, to_core(): return lax.ppermute(array, 'shard', [(0, 1), (1, 0)])  1.63 us
  transfers between devices with their start and end apart: 10, of which 6 were waited for; matrix products, arithmetic and copies ran while one was open for 0% of the time, Pallas kernels for 20%

profile of v8, /device:TPU:0, one launch (start us, length us, event | category | flops | bytes accessed | tf_op | source)
XLA Modules:
  0.0 70.1 jit_solution(2689293682983647847)
XLA Ops:
  0.0 3.9 %attend.1 = (f32[12,3072]{1,0:T(8,128)S(1)}, bf16[24,1664]{1,0:T(8,128)(2,1)S(1)}, bf16[3072,2560]{1,0:T(8,128)(2,1)S(1)}, bf16[3072,2560]{1,0:T(8,128)(2,1)S(1)}) custom-call(s32[12]{0:T(128)} %len_hbm.1, s32[2,12]{1,0:T(2,128)} %bitcast.5, bf16[12,3072]{1,0:T(8,128)(2,1)} %q_hbm.1, bf16[12,128,512]{2,1,0:T(8,128)(2,1)} %k_hbm.1, ...), custom_call_target="tpu_custom_call" | custom-call | flops 100000000 | bytes 8000000 | tf_op jit(solution)/shard_map/attend/pallas_call | solution.py:290
  3.9 5.1 %collective-permute-start.2 = (bf16[24,1664]{1,0:T(8,128)(2,1)S(1)}, bf16[24,1664]{1,0:T(8,128)(2,1)S(1)}, u32[]{:S(2)}, u32[]{:S(2)}) collective-permute-start(bf16[24,1664]{1,0:T(8,128)(2,1)S(1)} %get-tuple-element.28.dep_ref.refs_0_), channel_id=1, source_target_pairs={{0,12},{1,11},{2,14},{3,9},{4,8},{5,15},{6,10},{7,13},{8,4},{9,3},... | collective-permute-start | bytes 239624 | tf_op jit(solution)/shard_map/ppermute | solution.py:597
  9.1 0.0 collective-permute-start.1
  9.1 0.6 collective-permute-start
  9.7 4.7 %load_weights.2 = (bf16[3072,2560]{1,0:T(8,128)(2,1)S(1)}, bf16[3072,2560]{1,0:T(8,128)(2,1)S(1)}, f32[8,128]{1,0:T(8,128)S(1)}) custom-call(bf16[24,1664]{1,0:T(8,128)(2,1)S(1)} %get-tuple-element.28.dep_ref.refs_0_, bf16[6144,2048]{1,0:T(8,128)(2,1)} %g_hbm.9, bf16[6144,2048]{1,0:T(8,128)(2,1)} %u_hbm.9, ...), custom_call_target="tpu_custom_call", output_to_operand_aliasing={{0}: (3, {}), {1}: (4, {})} | custom-call | bytes 12582912 | tf_op jit(solution)/shard_map/load_weights/pallas_call | solution.py:112
  14.4 0.0 collective-permute-done.2.refs_3_
  14.4 0.0 collective-permute-done.1.refs_2_
  14.4 2.1 %collective-permute-done.refs_1_ = bf16[24,1664]{1,0:T(8,128)(2,1)S(1)} collective-permute-done((bf16[24,1664]{1,0:T(8,128)(2,1)S(1)}, bf16[24,1664]{1,0:T(8,128)(2,1)S(1)}, u32[]{:S(2)}, u32[]{:S(2)}) %collective-permute-start) | collective-permute-done | bytes 79904 | tf_op jit(solution)/shard_map/ppermute | solution.py:597
  16.6 0.1 unfold.1.dep_ref.a_ref
  16.6 0.1 collective-permute-start.3
  16.7 4.5 %load_weights.3 = (bf16[3072,2560]{1,0:T(8,128)(2,1)S(1)}, bf16[3072,2560]{1,0:T(8,128)(2,1)S(1)}, f32[8,128]{1,0:T(8,128)S(1)}) custom-call(bf16[48,3200]{1,0:T(8,128)(2,1)S(1)} %unfold.1.dep_ref.a_ref, bf16[6144,2048]{1,0:T(8,128)(2,1)} %g_hbm.9, bf16[6144,2048]{1,0:T(8,128)(2,1)} %u_hbm.9, ...), custom_call_target="tpu_custom_call", output_to_operand_aliasing={{0}: (3, {}), {1}: (4, {})} | custom-call | bytes 8388608 | tf_op jit(solution)/shard_map/load_weights/pallas_call | solution.py:112
  21.2 0.0 copy-start
  21.2 5.5 %copy-done = bf16[3072,2560]{1,0:T(8,128)(2,1)} copy-done((bf16[3072,2560]{1,0:T(8,128)(2,1)}, bf16[3072,2560]{1,0:T(8,128)(2,1)S(1)}, u32[]{:S(2)}) %copy-start) | copy-done | bytes 15728664
  26.7 0.0 collective-permute-done.3.b_ref
  26.7 0.1 collective-permute-start.4
  26.8 0.0 copy-start.1
  26.8 5.5 %copy-done.1 = bf16[3072,2560]{1,0:T(8,128)(2,1)S(1)} copy-done((bf16[3072,2560]{1,0:T(8,128)(2,1)S(1)}, bf16[3072,2560]{1,0:T(8,128)(2,1)}, u32[]{:S(2)}) %copy-start.1) | copy-done | bytes 15728664
  32.3 5.0 %first_half.1 = (f32[96,2048]{1,0:T(8,128)S(1)}, f32[96,2048]{1,0:T(8,128)S(1)}, bf16[3072,2560]{1,0:T(8,128)(2,1)S(1)}, bf16[3072,2560]{1,0:T(8,128)(2,1)S(1)}) custom-call(bf16[96,3200]{1,0:T(8,128)(2,1)S(1)} %join.1.x_ref, bf16[6144,2048]{1,0:T(8,128)(2,1)} %g_hbm.9, bf16[6144,2048]{1,0:T(8,128)(2,1)} %u_hbm.9, ...), custom_call_target="tpu_custom_call", output_to_operand_aliasing={{2}: (3, {}), {3}: (4, {})} | custom-call | flops 2415919104 | bytes 12582912 | tf_op jit(solution)/shard_map/first_half/pallas_call | solution.py:358
  37.3 0.0 collective-permute-done.4.ox_ref
  37.3 12.1 %second_half.1 = (f32[96,3072]{1,0:T(8,128)S(1)}, bf16[96,3072]{1,0:T(8,128)(2,1)S(1)}, bf16[3072,2560]{1,0:T(8,128)(2,1)S(1)}, bf16[3072,2560]{1,0:T(8,128)(2,1)S(1)}) custom-call(bf16[96,3200]{1,0:T(8,128)(2,1)S(1)} %join.1.x_ref, bf16[96,3200]{1,0:T(8,128)(2,1)S(1)} %collective-permute-done.4.ox_ref, ...), custom_call_target="tpu_custom_call", output_to_operand_aliasing={{2}: (7, {}), {3}: (8, {})} | custom-call | flops 3623878656 | bytes 25165824 | tf_op jit(solution)/shard_map/second_half/pallas_call | solution.py:484
  49.4 0.6 collective-permute-start.5
  50.0 1.6 %collective-permute-done.5.got_ref = bf16[96,3072]{1,0:T(8,128)(2,1)S(1)} collective-permute-done((bf16[96,3072]{1,0:T(8,128)(2,1)S(1)}, bf16[96,3072]{1,0:T(8,128)(2,1)S(1)}, u32[]{:S(2)}, u32[]{:S(2)}) %collective-permute-start.5) | collective-permute-done | bytes 589856 | tf_op jit(solution)/shard_map/ppermute | solution.py:600
  51.6 0.1 split_rows.1
  51.7 2.1 %collective-permute-start.6 = (bf16[48,3072]{1,0:T(8,128)(2,1)S(1)}, bf16[48,3072]{1,0:T(8,128)(2,1)S(1)}, u32[]{:S(2)}, u32[]{:S(2)}) collective-permute-start(bf16[48,3072]{1,0:T(8,128)(2,1)S(1)} %get-tuple-element.44), channel_id=1, source_target_pairs={{0,2},{1,5},{2,0},{3,7},{4,6},{5,1},{6,4},{7,3},{8,10},{9,13},{10,... | collective-permute-start | bytes 884744 | tf_op jit(solution)/shard_map/ppermute | solution.py:597
  53.8 4.7 %collective-permute-done.6.got_ref = bf16[48,3072]{1,0:T(8,128)(2,1)S(1)} collective-permute-done((bf16[48,3072]{1,0:T(8,128)(2,1)S(1)}, bf16[48,3072]{1,0:T(8,128)(2,1)S(1)}, u32[]{:S(2)}, u32[]{:S(2)}) %collective-permute-start.6) | collective-permute-done | bytes 294944 | tf_op jit(solution)/shard_map/ppermute | solution.py:597
  58.5 0.1 split_last.1
  58.6 2.8 %collective-permute-start.7 = (bf16[24,1536]{1,0:T(8,128)(2,1)S(1)}, bf16[24,1536]{1,0:T(8,128)(2,1)S(1)}, u32[]{:S(2)}, u32[]{:S(2)}) collective-permute-start(bf16[24,1536]{1,0:T(8,128)(2,1)S(1)} %get-tuple-element.46), channel_id=1, source_target_pairs={{0,8},{1,9},{2,10},{3,11},{4,12},{5,13},{6,14},{7,15},{8,0},{9,1},... | collective-permute-start | bytes 221192 | tf_op jit(solution)/shard_map/ppermute | solution.py:597
  61.4 1.8 %collective-permute-start.8 = (bf16[24,1536]{1,0:T(8,128)(2,1)S(1)}, bf16[24,1536]{1,0:T(8,128)(2,1)S(1)}, u32[]{:S(2)}, u32[]{:S(2)}) collective-permute-start(bf16[24,1536]{1,0:T(8,128)(2,1)S(1)} %get-tuple-element.47), channel_id=1, source_target_pairs={{0,4},{1,3},{2,6},{3,1},{4,0},{5,7},{6,2},{7,5},{8,12},{9,11},{10,... | collective-permute-start | bytes 221192 | tf_op jit(solution)/shard_map/ppermute | solution.py:597
  63.2 0.0 collective-permute-start.9
  63.2 2.3 %collective-permute-done.7.refs_0_ = bf16[24,1536]{1,0:T(8,128)(2,1)S(1)} collective-permute-done((bf16[24,1536]{1,0:T(8,128)(2,1)S(1)}, bf16[24,1536]{1,0:T(8,128)(2,1)S(1)}, u32[]{:S(2)}, u32[]{:S(2)}) %collective-permute-start.7) | collective-permute-done | bytes 73760 | tf_op jit(solution)/shard_map/ppermute | solution.py:597
  65.5 1.4 %collective-permute-done.8.refs_1_ = bf16[24,1536]{1,0:T(8,128)(2,1)S(1)} collective-permute-done((bf16[24,1536]{1,0:T(8,128)(2,1)S(1)}, bf16[24,1536]{1,0:T(8,128)(2,1)S(1)}, u32[]{:S(2)}, u32[]{:S(2)}) %collective-permute-start.8) | collective-permute-done | bytes 73760 | tf_op jit(solution)/shard_map/ppermute | solution.py:597
  66.9 2.4 %collective-permute-done.9.refs_2_ = bf16[24,1536]{1,0:T(8,128)(2,1)S(1)} collective-permute-done((bf16[24,1536]{1,0:T(8,128)(2,1)S(1)}, bf16[24,1536]{1,0:T(8,128)(2,1)S(1)}, u32[]{:S(2)}, u32[]{:S(2)}) %collective-permute-start.9) | collective-permute-done | bytes 73760 | tf_op jit(solution)/shard_map/ppermute | solution.py:597
  69.4 0.7 %finish.1 = bf16[12,3072]{1,0:T(8,128)(2,1)} custom-call(f32[12,3072]{1,0:T(8,128)S(1)} %get-tuple-element.27.carried_ref, f32[12,3072]{1,0:T(8,128)S(1)} %get-tuple-element.45.own_ref, bf16[24,1536]{1,0:T(8,128)(2,1)S(1)} %collective-permute-done.7.refs_0_, bf16[24,1536]{1,0:T(8,128)(2,1)S(1)} %collective-permute-done.8.refs_1_, ...), custom_call_target="tpu_custom_call" | custom-call | tf_op jit(solution)/shard_map/finish/pallas_call | solution.py:573
  (1 shorter events, 0.0 us)
Async XLA Ops:
  3.9 10.5 %collective-permute-start.2 = (bf16[24,1664]{1,0:T(8,128)(2,1)S(1)}, bf16[24,1664]{1,0:T(8,128)(2,1)S(1)}, u32[]{:S(2)}, u32[]{:S(2)}) collective-permute-start(bf16[24,1664]{1,0:T(8,128)(2,1)S(1)} %get-tuple-element.28.dep_ref.refs_0_), channel_id=1, source_target_pairs={{0,12},{1,11},{2,14},{3,9},{4,8},{5,15},{6,10},{7,13},{8,4},{9,3},... | collective-permute-start | bytes 239624 | tf_op jit(solution)/shard_map/ppermute | solution.py:597
  9.1 5.4 %collective-permute-start.1 = (bf16[24,1664]{1,0:T(8,128)(2,1)S(1)}, bf16[24,1664]{1,0:T(8,128)(2,1)S(1)}, u32[]{:S(2)}, u32[]{:S(2)}) collective-permute-start(bf16[24,1664]{1,0:T(8,128)(2,1)S(1)} %get-tuple-element.28.dep_ref.refs_0_), channel_id=1, source_target_pairs={{0,4},{1,3},{2,6},{3,1},{4,0},{5,7},{6,2},{7,5},{8,12},{9,11},{10,... | collective-permute-start | bytes 239624 | tf_op jit(solution)/shard_map/ppermute | solution.py:597
  9.1 7.5 %collective-permute-start = (bf16[24,1664]{1,0:T(8,128)(2,1)S(1)}, bf16[24,1664]{1,0:T(8,128)(2,1)S(1)}, u32[]{:S(2)}, u32[]{:S(2)}) collective-permute-start(bf16[24,1664]{1,0:T(8,128)(2,1)S(1)} %get-tuple-element.28.dep_ref.refs_0_), channel_id=1, source_target_pairs={{0,8},{1,9},{2,10},{3,11},{4,12},{5,13},{6,14},{7,15},{8,0},{9,1},... | collective-permute-start | bytes 239624 | tf_op jit(solution)/shard_map/ppermute | solution.py:597
  16.6 10.1 %collective-permute-start.3 = (bf16[48,3200]{1,0:T(8,128)(2,1)S(1)}, bf16[48,3200]{1,0:T(8,128)(2,1)S(1)}, u32[]{:S(2)}, u32[]{:S(2)}) collective-permute-start(bf16[48,3200]{1,0:T(8,128)(2,1)S(1)} %unfold.1.dep_ref.a_ref), channel_id=1, source_target_pairs={{0,2},{1,5},{2,0},{3,7},{4,6},{5,1},{6,4},{7,3},{8,10},{9,13},{10,... | collective-permute-start | bytes 921608 | tf_op jit(solution)/shard_map/ppermute | solution.py:597
  21.2 5.5 %copy-start = (bf16[3072,2560]{1,0:T(8,128)(2,1)}, bf16[3072,2560]{1,0:T(8,128)(2,1)S(1)}, u32[]{:S(2)}) copy-start(bf16[3072,2560]{1,0:T(8,128)(2,1)S(1)} %get-tuple-element.36.u_in) | copy-start | bytes 47185924
  26.7 10.5 %collective-permute-start.4 = (bf16[96,3200]{1,0:T(8,128)(2,1)S(1)}, bf16[96,3200]{1,0:T(8,128)(2,1)S(1)}, u32[]{:S(2)}, u32[]{:S(2)}) collective-permute-start(bf16[96,3200]{1,0:T(8,128)(2,1)S(1)} %join.1.x_ref), channel_id=1, source_target_pairs={{0,1},{1,0},{2,3},{3,2},{4,5},{5,4},{6,7},{7,6},{8,9},{9,8},{10,11... | collective-permute-start | bytes 1843208 | tf_op jit(solution)/shard_map/ppermute | solution.py:600
  26.8 5.5 %copy-start.1 = (bf16[3072,2560]{1,0:T(8,128)(2,1)S(1)}, bf16[3072,2560]{1,0:T(8,128)(2,1)}, u32[]{:S(2)}) copy-start(bf16[3072,2560]{1,0:T(8,128)(2,1)} %copy-done) | copy-start | bytes 47185924
  49.4 2.2 %collective-permute-start.5 = (bf16[96,3072]{1,0:T(8,128)(2,1)S(1)}, bf16[96,3072]{1,0:T(8,128)(2,1)S(1)}, u32[]{:S(2)}, u32[]{:S(2)}) collective-permute-start(bf16[96,3072]{1,0:T(8,128)(2,1)S(1)} %get-tuple-element.42), channel_id=1, source_target_pairs={{0,1},{1,0},{2,3},{3,2},{4,5},{5,4},{6,7},{7,6},{8,9},{9,8},{10,11... | collective-permute-start | bytes 1769480 | tf_op jit(solution)/shard_map/ppermute | solution.py:600
  51.7 6.8 %collective-permute-start.6 = (bf16[48,3072]{1,0:T(8,128)(2,1)S(1)}, bf16[48,3072]{1,0:T(8,128)(2,1)S(1)}, u32[]{:S(2)}, u32[]{:S(2)}) collective-permute-start(bf16[48,3072]{1,0:T(8,128)(2,1)S(1)} %get-tuple-element.44), channel_id=1, source_target_pairs={{0,2},{1,5},{2,0},{3,7},{4,6},{5,1},{6,4},{7,3},{8,10},{9,13},{10,... | collective-permute-start | bytes 884744 | tf_op jit(solution)/shard_map/ppermute | solution.py:597
  58.6 6.9 %collective-permute-start.7 = (bf16[24,1536]{1,0:T(8,128)(2,1)S(1)}, bf16[24,1536]{1,0:T(8,128)(2,1)S(1)}, u32[]{:S(2)}, u32[]{:S(2)}) collective-permute-start(bf16[24,1536]{1,0:T(8,128)(2,1)S(1)} %get-tuple-element.46), channel_id=1, source_target_pairs={{0,8},{1,9},{2,10},{3,11},{4,12},{5,13},{6,14},{7,15},{8,0},{9,1},... | collective-permute-start | bytes 221192 | tf_op jit(solution)/shard_map/ppermute | solution.py:597
  61.4 5.5 %collective-permute-start.8 = (bf16[24,1536]{1,0:T(8,128)(2,1)S(1)}, bf16[24,1536]{1,0:T(8,128)(2,1)S(1)}, u32[]{:S(2)}, u32[]{:S(2)}) collective-permute-start(bf16[24,1536]{1,0:T(8,128)(2,1)S(1)} %get-tuple-element.47), channel_id=1, source_target_pairs={{0,4},{1,3},{2,6},{3,1},{4,0},{5,7},{6,2},{7,5},{8,12},{9,11},{10,... | collective-permute-start | bytes 221192 | tf_op jit(solution)/shard_map/ppermute | solution.py:597
  63.2 6.2 %collective-permute-start.9 = (bf16[24,1536]{1,0:T(8,128)(2,1)S(1)}, bf16[24,1536]{1,0:T(8,128)(2,1)S(1)}, u32[]{:S(2)}, u32[]{:S(2)}) collective-permute-start(bf16[24,1536]{1,0:T(8,128)(2,1)S(1)} %get-tuple-element.48), channel_id=1, source_target_pairs={{0,12},{1,11},{2,14},{3,9},{4,8},{5,15},{6,10},{7,13},{8,4},{9,3},... | collective-permute-start | bytes 221192 | tf_op jit(solution)/shard_map/ppermute | solution.py:597

commit v9 on v8

--- a/solution.py
+++ b/solution.py
@@ -47,6 +47,7 @@
 HBM_SPEC = pl.BlockSpec(memory_space=pltpu.HBM)
 ROUTE_LANE = 3 + 3 * EXPERTS
 HELD_BELOW = 10 * MIB
+LOADED_BELOW = 12 * MIB
 
 
 def own_side():
@@ -59,7 +60,12 @@
 
 def held_shape(gate_weight):
     width, units = gate_weight.shape
-    return width // 2, units + chunk_of(units)
+    return width // 2, units
+
+
+def spare_shape(gate_weight):
+    width, units = gate_weight.shape
+    return 2, width // 2, chunk_of(units)
 
 
 def row_copies(sources, targets, first, rows, sems):
@@ -79,27 +85,23 @@
     return copies
 
 
-def slot_at(q, chunk, slots):
-    start = lax.rem(q, slots) * chunk
-    return pl.ds(start if isinstance(q, int) else pl.multiple_of(start, LANES), chunk)
-
-
-def other_copy(source, target, c, chunk, sem):
-    half, units = target.shape[0], source.shape[1]
-    chunks = units // chunk
+def chunk_at(n, chunk):
+    return pl.ds(n * chunk if isinstance(n, int) else pl.multiple_of(n * chunk, LANES), chunk)
+
+
+def other_copy(source, held, spare, c, chunk, sem):
+    half = source.shape[0] // 2
     first = pl.multiple_of((1 - own_side()) * half, 16)
-    column = c * chunk if isinstance(c, int) else pl.multiple_of(c * chunk, LANES)
-    return pltpu.make_async_copy(
-        source.at[pl.ds(first, half), pl.ds(column, chunk)],
-        target.at[:, slot_at(chunks + c, chunk, chunks + 1)], sem,
-    )
-
-
-def load_kernel(first, rows, ahead, dep_ref, g_hbm, u_hbm, g_in, u_in, g_vmem, u_vmem, token_ref, sems, sem):
-    del g_in, u_in
+    target = spare if isinstance(c, int) and c == 0 else held.at[:, chunk_at(c - 1, chunk)]
+    return pltpu.make_async_copy(source.at[pl.ds(first, half), chunk_at(c, chunk)], target, sem)
+
+
+def load_kernel(first, rows, ahead, dep_ref, g_hbm, u_hbm, g_in, u_in, g_vmem, u_vmem, *refs):
+    del dep_ref, g_in, u_in
+    *spare, token_ref, sems, sem = refs
     copies = row_copies((g_hbm, u_hbm), (g_vmem, u_vmem), first, rows, sems)
     if ahead:
-        copies.append(other_copy(g_hbm, g_vmem, 0, chunk_of(g_hbm.shape[1]), sem))
+        copies.append(other_copy(g_hbm, None, spare[0].at[0], 0, spare[0].shape[2], sem))
     for copy in copies:
         copy.start()
     token_ref[...] = jnp.zeros_like(token_ref)
@@ -109,14 +111,16 @@
 
 def load_rows(first, rows, ahead, after, gate_weight, up_weight, held):
     hidden = gate_weight.shape[1]
+    spare = (pltpu.VMEM(spare_shape(gate_weight), BF16),) if ahead else ()
     return pl.pallas_call(
         functools.partial(load_kernel, first, rows, ahead),
-        out_shape=tuple(pltpu.VMEM(h.shape, BF16) for h in held) + (pltpu.VMEM((8, LANES), F32),),
+        out_shape=tuple(pltpu.VMEM(h.shape, BF16) for h in held) + spare
+        + (pltpu.VMEM((8, LANES), F32),),
         in_specs=[pl.BlockSpec(memory_space=pl.ANY), HBM_SPEC, HBM_SPEC, VMEM_SPEC, VMEM_SPEC],
-        out_specs=(VMEM_SPEC,) * 3,
+        out_specs=(VMEM_SPEC,) * (3 + len(spare)),
         scratch_shapes=[pltpu.SemaphoreType.DMA((2, 4)), pltpu.SemaphoreType.DMA],
         input_output_aliases={3: 0, 4: 1},
-        compiler_params=pltpu.CompilerParams(vmem_limit_bytes=HELD_BELOW),
+        compiler_params=pltpu.CompilerParams(vmem_limit_bytes=LOADED_BELOW),
         cost_estimate=pl.CostEstimate(flops=0, bytes_accessed=4 * rows * hidden, transcendentals=0),
         name="load_weights",
     )(*in_vmem(after), *in_hbm(gate_weight, up_weight), *in_vmem_always(held))
@@ -191,7 +195,7 @@
     ]
     copies = [pltpu.make_async_copy(a, b, sems.at[i]) for i, (a, b) in enumerate(moves)]
     weights = row_copies((g_hbm, u_hbm), (g_vmem, u_vmem), 0, ahead, w_sems)
-    for copy in copies:
+    for copy in copies + weights:
         copy.start()
     copies[0].wait()
     for h in range(heads):
@@ -204,8 +208,6 @@
     for t in range(tok):
         if t == 0:
             copies[1].wait()
-            for copy in weights:
-                copy.start()
         q_rows = q_scr[pl.ds(t, heads, stride=tok), :]
         q_wide = jnp.concatenate(
             [jnp.where(row_group == g, q_rows, 0.0) for g in range(groups)], axis=1
@@ -310,7 +312,7 @@
             pltpu.SemaphoreType.DMA((10,)),
             pltpu.SemaphoreType.DMA((2, 1)),
         ],
-        compiler_params=pltpu.CompilerParams(vmem_limit_bytes=HELD_BELOW),
+        compiler_params=pltpu.CompilerParams(vmem_limit_bytes=LOADED_BELOW),
         cost_estimate=pl.CostEstimate(flops=10**8, bytes_accessed=8 * 10**6, transcendentals=10**5),
         name="attend",
     )(
@@ -321,8 +323,10 @@
     )
 
 
-def first_half_kernel(x_ref, g_hbm, u_hbm, g_in, u_in, gate_ref, up_ref, g_ref, u_ref, sems):
-    del g_in, u_in
+def first_half_kernel(
+    x_ref, g_hbm, u_hbm, g_in, u_in, spare_in, gate_ref, up_ref, g_ref, u_ref, spare_ref, sems
+):
+    del g_in, u_in, spare_in
     half, units = g_ref.shape[0], gate_ref.shape[1]
     chunk = chunk_of(units)
     chunks = units // chunk
@@ -330,12 +334,14 @@
     ready = [(i, c) for i, c in ready if c < chunks]
 
     def copy(i, c):
-        return other_copy((g_hbm, u_hbm)[i], (g_ref, u_ref)[i], c, chunk, sems.at[i, c])
+        return other_copy(
+            (g_hbm, u_hbm)[i], (g_ref, u_ref)[i], spare_ref.at[i], c, chunk, sems.at[i, c]
+        )
 
     copy(1, 0).start()
 
     def step(n, _):
-        at = pl.ds(pl.multiple_of(n * chunk, LANES), chunk)
+        at = chunk_at(n, chunk)
         rows = x_ref[:, :half]
         gate_ref[:, at] = jnp.dot(rows, g_ref[:, at], preferred_element_type=F32)
         up_ref[:, at] = jnp.dot(rows, u_ref[:, at], preferred_element_type=F32)
@@ -351,27 +357,27 @@
         copy(i, c).wait()
 
 
-def first_half(mine, held, gate_weight, up_weight):
+def first_half(mine, held, spare, gate_weight, up_weight):
     rows = mine.shape[0]
     width, units = gate_weight.shape
     acc = pltpu.VMEM((rows, units), F32)
     return pl.pallas_call(
         first_half_kernel,
-        out_shape=(acc, acc) + tuple(pltpu.VMEM(h.shape, BF16) for h in held),
-        in_specs=[VMEM_SPEC] + [HBM_SPEC] * 2 + [VMEM_SPEC] * 2,
-        out_specs=(VMEM_SPEC,) * 4,
+        out_shape=(acc, acc) + tuple(pltpu.VMEM(h.shape, BF16) for h in (*held, spare)),
+        in_specs=[VMEM_SPEC] + [HBM_SPEC] * 2 + [VMEM_SPEC] * 3,
+        out_specs=(VMEM_SPEC,) * 5,
         scratch_shapes=[pltpu.SemaphoreType.DMA((2, units // chunk_of(units)))],
-        input_output_aliases={3: 2, 4: 3},
+        input_output_aliases={3: 2, 4: 3, 5: 4},
         compiler_params=pltpu.CompilerParams(vmem_limit_bytes=HELD_BELOW),
         cost_estimate=pl.CostEstimate(
             flops=2 * rows * width * units, bytes_accessed=width * units, transcendentals=0
         ),
         name="first_half",
-    )(*in_vmem_always([mine]), *in_hbm(gate_weight, up_weight), *in_vmem_always(held))
+    )(*in_vmem_always([mine]), *in_hbm(gate_weight, up_weight), *in_vmem_always([*held, spare]))
 
 
 def second_half_kernel(
-    per_plane, x_ref, ox_ref, gate_ref, up_ref, g_hbm, u_hbm, d_hbm, g_in, u_in,
+    per_plane, x_ref, ox_ref, gate_ref, up_ref, spare_ref, g_hbm, u_hbm, d_hbm, g_in, u_in,
     staying_ref, leaving_ref, g_ref, u_ref, x_scr, h_scr, gu_sems, sems,
 ):
     del g_in, u_in
@@ -380,19 +386,21 @@
     side = own_side()
     chunk = chunk_of(units)
     chunks = units // chunk
-    slots = chunks + 1
     per_side = width // chunk
     pairs = per_side
 
     def gu_copy(i, c):
-        return other_copy((g_hbm, u_hbm)[i], (g_ref, u_ref)[i], c, chunk, gu_sems.at[i, c])
+        return other_copy((g_hbm, u_hbm)[i], (g_ref, u_ref)[i], None, c, chunk, gu_sems.at[i, c])
+
+    def down_slot(p):
+        return chunk_at(lax.rem(p + chunks - 1, chunks), chunk)
 
     def down_copy(i, p):
         n = 2 * p + i
         column = jnp.where(n < per_side, 1 - side, side) * width + lax.rem(n, per_side) * chunk
         return pltpu.make_async_copy(
             d_hbm.at[:, pl.ds(pl.multiple_of(column, LANES), chunk)],
-            (g_ref, u_ref)[i].at[pl.ds(0, units), slot_at(2 * chunks + p, chunk, slots)],
+            (g_ref, u_ref)[i].at[pl.ds(0, units), down_slot(p)],
             sems.at[i, p],
         )
 
@@ -429,30 +437,35 @@
     here = (lax.axis_index("node") // per_plane).astype(F32)
     weight = jnp.where(first == here, share, 0.0) + jnp.where(second == here, 1.0 - share, 0.0)
 
+    def hidden_chunk(c, g_part, u_part):
+        at = chunk_at(c, chunk)
+        gate = gate_ref[:, at] + jnp.dot(x_scr[...], g_part, preferred_element_type=F32)
+        up = up_ref[:, at] + jnp.dot(x_scr[...], u_part, preferred_element_type=F32)
+        gate = gate * scale
+        h_scr[:, at] = (gate / (1.0 + jnp.exp(-gate)) * (up * scale)).astype(BF16)
+
+    hidden_chunk(0, spare_ref[0], spare_ref[1])
+
     def hidden_step(c, _):
         for i, late in later:
             @pl.when(c == late)
             def _(i=i, late=late):
                 gu_copy(i, late).wait()
 
-        slot = slot_at(chunks + c, chunk, slots)
-        at = pl.ds(pl.multiple_of(c * chunk, LANES), chunk)
-        gate = gate_ref[:, at] + jnp.dot(x_scr[...], g_ref[:, slot], preferred_element_type=F32)
-        up = up_ref[:, at] + jnp.dot(x_scr[...], u_ref[:, slot], preferred_element_type=F32)
-        gate = gate * scale
-        h_scr[:, at] = (gate / (1.0 + jnp.exp(-gate)) * (up * scale)).astype(BF16)
-
-        @pl.when(c + 1 < pairs)
+        slot = chunk_at(c - 1, chunk)
+        hidden_chunk(c, g_ref[:, slot], u_ref[:, slot])
+
+        @pl.when(c < pairs)
         def _():
             for i in range(2):
-                down_copy(i, c + 1).start()
+                down_copy(i, c).start()
 
         return 0
 
-    lax.fori_loop(0, chunks, hidden_step, 0)
+    lax.fori_loop(1, chunks, hidden_step, 0)
 
     def down_step(p, _):
-        slot = slot_at(2 * chunks + p, chunk, slots)
+        slot = down_slot(p)
         for i, ref in enumerate((g_ref, u_ref)):
             n = 2 * p + i
             down_copy(i, p).wait()
@@ -467,17 +480,17 @@
             def _(value=value, to=to):
                 staying_ref[:, to] = value
 
-        @pl.when(p + slots < pairs)
+        @pl.when(p + chunks < pairs)
         def _():
             for i in range(2):
-                down_copy(i, p + slots).start()
+                down_copy(i, p + chunks).start()
 
         return 0
 
     lax.fori_loop(0, pairs, down_step, 0)
 
 
-def second_half(per_plane, mine, other, sums, held, gate_weight, up_weight, down_weight):
+def second_half(per_plane, mine, other, sums, held, spare, gate_weight, up_weight, down_weight):
     rows, units = sums[0].shape
     width = down_weight.shape[1] // 2
     chunk = chunk_of(units)
@@ -485,7 +498,7 @@
         functools.partial(second_half_kernel, per_plane),
         out_shape=(vmem_array((rows, width), F32), vmem_array((rows, width), BF16))
         + tuple(pltpu.VMEM(h.shape, BF16) for h in held),
-        in_specs=[VMEM_SPEC] * 4 + [HBM_SPEC] * 3 + [VMEM_SPEC] * 2,
+        in_specs=[VMEM_SPEC] * 5 + [HBM_SPEC] * 3 + [VMEM_SPEC] * 2,
         out_specs=(VMEM_SPEC,) * 4,
         scratch_shapes=[
             pltpu.VMEM((rows, width), BF16),
@@ -493,7 +506,7 @@
             pltpu.SemaphoreType.DMA((2, units // chunk)),
             pltpu.SemaphoreType.DMA((2, width // chunk)),
         ],
-        input_output_aliases={7: 2, 8: 3},
+        input_output_aliases={8: 2, 9: 3},
         compiler_params=pltpu.CompilerParams(
             vmem_limit_bytes=HELD_BELOW if rows < 256 else 40 * MIB
         ),
@@ -502,7 +515,7 @@
         ),
         name="second_half",
     )(
-        *in_vmem_always([mine, other]), *in_vmem(*sums),
+        *in_vmem_always([mine, other]), *in_vmem(*sums), *in_vmem_always([spare]),
         *in_hbm(gate_weight, up_weight, down_weight), *in_vmem_always(held),
     )[:2]
 
@@ -615,15 +628,15 @@
     for stage in range(2, stages):
         got = exchange(payload, stage)
         if stage == 2:
-            *held, token = load_rows(
+            *held, spare, token = load_rows(
                 heights[0] + heights[1], heights[2], True, payload, gate_weight, up_weight, held
             )
         payload = join(payload, got, token)
     mine = payload
     other = to_core(mine)
-    gate, up, *held = first_half(mine, held, gate_weight, up_weight)
+    gate, up, *held, spare = first_half(mine, held, spare, gate_weight, up_weight)
     staying, leaving = second_half(
-        per_plane, mine, other, (gate, up), held, gate_weight, up_weight, down_weight
+        per_plane, mine, other, (gate, up), held, spare, gate_weight, up_weight, down_weight
     )
     keep, got = staying, to_core(leaving)
     for stage in range(stages - 1, 1, -1):

time: 70.2 us -> 59.8 us (0.85)
  local copies, waits for them, and re-layouts: 11 us -> 0 us
    unnamed x4 -> x0, local copies, waits for them, and re-layouts: 11 us -> none
    pallas_call x1, Pallas kernels: 12.1 us -> 13 us  [second_half(): pl.pallas_call(functools.partial(second_half_kernel, per_plane), out_shap...]
    ppermute x8, starting transfers between devices: 12.5 us -> 13.2 us  [exchange(): return lax.ppermute(array, ('node', 'shard'), perm)]
  transfers between devices with their start and end apart: 10 -> 10, of which waited for: 6 -> 7; matrix products, arithmetic and copies ran while one was open for 0% -> 0% of each run, Pallas kernels for 20% -> 24%
where the time goes in v9:
time: 59.8 us; the launch traced here: 59.7 us
  Pallas kernels  31.6 us (53%)
  waiting for transfers between devices  14.1 us (24%)
  starting transfers between devices  13.9 us (23%)
    ppermute x8, starting transfers between devices, exchange(): return lax.ppermute(array, ('node', 'shard'), perm)  13.2 us
    pallas_call x1, Pallas kernels, second_half(): pl.pallas_call(functools.partial(second_half_kernel, per_plane), out_shap...  13 us
    ppermute x8, waiting for transfers between devices, exchange(): return lax.ppermute(array, ('node', 'shard'), perm)  12.5 us
    pallas_call x2, Pallas kernels, load_rows(): pl.pallas_call(functools.partial(load_kernel, first, rows, ahead), out_sh...  9.17 us
    pallas_call x1, Pallas kernels, first_half(): pl.pallas_call(first_half_kernel, out_shape=(acc, acc) + tuple((pltpu.VME...  4.99 us
    pallas_call x1, Pallas kernels, attend(): pl.pallas_call(functools.partial(attend_kernel, ahead), out_shape=(pltpu....  3.41 us
    ppermute x2, waiting for transfers between devices, to_core(): return lax.ppermute(array, 'shard', [(0, 1), (1, 0)])  1.63 us
  transfers between devices with their start and end apart: 10, of which 7 were waited for; matrix products, arithmetic and copies ran while one was open for 0% of the time, Pallas kernels for 24%

profile of v9, /device:TPU:0, one launch (start us, length us, event | category | flops | bytes accessed | tf_op | source)
XLA Modules:
  0.0 59.7 jit_solution(16336075692282292041)
XLA Ops:
  0.0 3.4 %attend.1 = (f32[12,3072]{1,0:T(8,128)S(1)}, bf16[24,1664]{1,0:T(8,128)(2,1)S(1)}, bf16[3072,2048]{1,0:T(8,128)(2,1)S(1)}, bf16[3072,2048]{1,0:T(8,128)(2,1)S(1)}) custom-call(s32[12]{0:T(128)} %len_hbm.1, s32[2,12]{1,0:T(2,128)} %bitcast.5, bf16[12,3072]{1,0:T(8,128)(2,1)} %q_hbm.1, bf16[12,128,512]{2,1,0:T(8,128)(2,1)} %k_hbm.1, ...), custom_call_target="tpu_custom_call" | custom-call | flops 100000000 | bytes 8000000 | tf_op jit(solution)/shard_map/attend/pallas_call | solution.py:292
  3.4 4.1 %collective-permute-start = (bf16[24,1664]{1,0:T(8,128)(2,1)S(1)}, bf16[24,1664]{1,0:T(8,128)(2,1)S(1)}, u32[]{:S(2)}, u32[]{:S(2)}) collective-permute-start(bf16[24,1664]{1,0:T(8,128)(2,1)S(1)} %get-tuple-element.30.dep_ref.refs_0_), channel_id=1, source_target_pairs={{0,8},{1,9},{2,10},{3,11},{4,12},{5,13},{6,14},{7,15},{8,0},{9,1},... | collective-permute-start | bytes 239624 | tf_op jit(solution)/shard_map/ppermute | solution.py:610
  7.5 1.6 %collective-permute-start.1 = (bf16[24,1664]{1,0:T(8,128)(2,1)S(1)}, bf16[24,1664]{1,0:T(8,128)(2,1)S(1)}, u32[]{:S(2)}, u32[]{:S(2)}) collective-permute-start(bf16[24,1664]{1,0:T(8,128)(2,1)S(1)} %get-tuple-element.30.dep_ref.refs_0_), channel_id=1, source_target_pairs={{0,4},{1,3},{2,6},{3,1},{4,0},{5,7},{6,2},{7,5},{8,12},{9,11},{10,... | collective-permute-start | bytes 239624 | tf_op jit(solution)/shard_map/ppermute | solution.py:610
  9.1 0.0 collective-permute-start.2
  9.1 4.7 %load_weights.2 = (bf16[3072,2048]{1,0:T(8,128)(2,1)S(1)}, bf16[3072,2048]{1,0:T(8,128)(2,1)S(1)}, f32[8,128]{1,0:T(8,128)S(1)}) custom-call(bf16[24,1664]{1,0:T(8,128)(2,1)S(1)} %get-tuple-element.30.dep_ref.refs_0_, bf16[6144,2048]{1,0:T(8,128)(2,1)} %g_hbm.9, bf16[6144,2048]{1,0:T(8,128)(2,1)} %u_hbm.9, ...), custom_call_target="tpu_custom_call", output_to_operand_aliasing={{0}: (3, {}), {1}: (4, {})} | custom-call | bytes 12582912 | tf_op jit(solution)/shard_map/load_weights/pallas_call | solution.py:115
  13.8 0.0 collective-permute-done.refs_1_
  13.8 0.0 collective-permute-done.1.refs_2_
  13.8 1.5 %collective-permute-done.2.refs_3_ = bf16[24,1664]{1,0:T(8,128)(2,1)S(1)} collective-permute-done((bf16[24,1664]{1,0:T(8,128)(2,1)S(1)}, bf16[24,1664]{1,0:T(8,128)(2,1)S(1)}, u32[]{:S(2)}, u32[]{:S(2)}) %collective-permute-start.2) | collective-permute-done | bytes 79904 | tf_op jit(solution)/shard_map/ppermute | solution.py:610
  15.3 0.1 unfold.1.dep_ref.a_ref
  15.4 1.6 %collective-permute-start.3 = (bf16[48,3200]{1,0:T(8,128)(2,1)S(1)}, bf16[48,3200]{1,0:T(8,128)(2,1)S(1)}, u32[]{:S(2)}, u32[]{:S(2)}) collective-permute-start(bf16[48,3200]{1,0:T(8,128)(2,1)S(1)} %unfold.1.dep_ref.a_ref), channel_id=1, source_target_pairs={{0,2},{1,5},{2,0},{3,7},{4,6},{5,1},{6,4},{7,3},{8,10},{9,13},{10,... | collective-permute-start | bytes 921608 | tf_op jit(solution)/shard_map/ppermute | solution.py:610
  16.9 4.5 %load_weights.3 = (bf16[3072,2048]{1,0:T(8,128)(2,1)S(1)}, bf16[3072,2048]{1,0:T(8,128)(2,1)S(1)}, bf16[2,3072,512]{2,1,0:T(8,128)(2,1)S(1)}, f32[8,128]{1,0:T(8,128)S(1)}) custom-call(bf16[48,3200]{1,0:T(8,128)(2,1)S(1)} %unfold.1.dep_ref.a_ref, bf16[6144,2048]{1,0:T(8,128)(2,1)} %g_hbm.9, ...), custom_call_target="tpu_custom_call", output_to_operand_aliasing={{0}: (3, {}), {1}: (4, {})} | custom-call | bytes 8388608 | tf_op jit(solution)/shard_map/load_weights/pallas_call | solution.py:115
  21.4 0.9 %collective-permute-done.3.b_ref = bf16[48,3200]{1,0:T(8,128)(2,1)S(1)} collective-permute-done((bf16[48,3200]{1,0:T(8,128)(2,1)S(1)}, bf16[48,3200]{1,0:T(8,128)(2,1)S(1)}, u32[]{:S(2)}, u32[]{:S(2)}) %collective-permute-start.3) | collective-permute-done | bytes 307232 | tf_op jit(solution)/shard_map/ppermute | solution.py:610
  22.4 0.1 collective-permute-start.4
  22.4 5.0 %first_half.1 = (f32[96,2048]{1,0:T(8,128)S(1)}, f32[96,2048]{1,0:T(8,128)S(1)}, bf16[3072,2048]{1,0:T(8,128)(2,1)S(1)}, bf16[3072,2048]{1,0:T(8,128)(2,1)S(1)}, bf16[2,3072,512]{2,1,0:T(8,128)(2,1)S(1)}) custom-call(bf16[96,3200]{1,0:T(8,128)(2,1)S(1)} %join.1.x_ref, ...), custom_call_target="tpu_custom_call", output_to_operand_aliasing={{2}: (3, {}), {3}: (4, {}), {4}: (5, {})} | custom-call | flops 2415919104 | bytes 12582912 | tf_op jit(solution)/shard_map/first_half/pallas_call | solution.py:364
  27.4 0.0 collective-permute-done.4.ox_ref
  27.4 13.0 %second_half.1 = (f32[96,3072]{1,0:T(8,128)S(1)}, bf16[96,3072]{1,0:T(8,128)(2,1)S(1)}, bf16[3072,2048]{1,0:T(8,128)(2,1)S(1)}, bf16[3072,2048]{1,0:T(8,128)(2,1)S(1)}) custom-call(bf16[96,3200]{1,0:T(8,128)(2,1)S(1)} %join.1.x_ref, bf16[96,3200]{1,0:T(8,128)(2,1)S(1)} %collective-permute-done.4.ox_ref, ...), custom_call_target="tpu_custom_call", output_to_operand_aliasing={{2}: (8, {}), {3}: (9, {})} | custom-call | flops 3623878656 | bytes 25165824 | tf_op jit(solution)/shard_map/second_half/pallas_call | solution.py:497
  40.5 0.6 collective-permute-start.5
  41.0 1.6 %collective-permute-done.5.got_ref = bf16[96,3072]{1,0:T(8,128)(2,1)S(1)} collective-permute-done((bf16[96,3072]{1,0:T(8,128)(2,1)S(1)}, bf16[96,3072]{1,0:T(8,128)(2,1)S(1)}, u32[]{:S(2)}, u32[]{:S(2)}) %collective-permute-start.5) | collective-permute-done | bytes 589856 | tf_op jit(solution)/shard_map/ppermute | solution.py:613
  42.7 0.1 split_rows.1
  42.8 1.5 %collective-permute-start.6 = (bf16[48,3072]{1,0:T(8,128)(2,1)S(1)}, bf16[48,3072]{1,0:T(8,128)(2,1)S(1)}, u32[]{:S(2)}, u32[]{:S(2)}) collective-permute-start(bf16[48,3072]{1,0:T(8,128)(2,1)S(1)} %get-tuple-element.48), channel_id=1, source_target_pairs={{0,2},{1,5},{2,0},{3,7},{4,6},{5,1},{6,4},{7,3},{8,10},{9,13},{10,... | collective-permute-start | bytes 884744 | tf_op jit(solution)/shard_map/ppermute | solution.py:610
  44.3 5.2 %collective-permute-done.6.got_ref = bf16[48,3072]{1,0:T(8,128)(2,1)S(1)} collective-permute-done((bf16[48,3072]{1,0:T(8,128)(2,1)S(1)}, bf16[48,3072]{1,0:T(8,128)(2,1)S(1)}, u32[]{:S(2)}, u32[]{:S(2)}) %collective-permute-start.6) | collective-permute-done | bytes 294944 | tf_op jit(solution)/shard_map/ppermute | solution.py:610
  49.6 0.1 split_last.1
  49.7 2.4 %collective-permute-start.7 = (bf16[24,1536]{1,0:T(8,128)(2,1)S(1)}, bf16[24,1536]{1,0:T(8,128)(2,1)S(1)}, u32[]{:S(2)}, u32[]{:S(2)}) collective-permute-start(bf16[24,1536]{1,0:T(8,128)(2,1)S(1)} %get-tuple-element.50), channel_id=1, source_target_pairs={{0,8},{1,9},{2,10},{3,11},{4,12},{5,13},{6,14},{7,15},{8,0},{9,1},... | collective-permute-start | bytes 221192 | tf_op jit(solution)/shard_map/ppermute | solution.py:610
  52.1 0.6 %collective-permute-start.8 = (bf16[24,1536]{1,0:T(8,128)(2,1)S(1)}, bf16[24,1536]{1,0:T(8,128)(2,1)S(1)}, u32[]{:S(2)}, u32[]{:S(2)}) collective-permute-start(bf16[24,1536]{1,0:T(8,128)(2,1)S(1)} %get-tuple-element.51), channel_id=1, source_target_pairs={{0,4},{1,3},{2,6},{3,1},{4,0},{5,7},{6,2},{7,5},{8,12},{9,11},{10,... | collective-permute-start | bytes 221192 | tf_op jit(solution)/shard_map/ppermute | solution.py:610
  52.7 1.4 %collective-permute-start.9 = (bf16[24,1536]{1,0:T(8,128)(2,1)S(1)}, bf16[24,1536]{1,0:T(8,128)(2,1)S(1)}, u32[]{:S(2)}, u32[]{:S(2)}) collective-permute-start(bf16[24,1536]{1,0:T(8,128)(2,1)S(1)} %get-tuple-element.52), channel_id=1, source_target_pairs={{0,12},{1,11},{2,14},{3,9},{4,8},{5,15},{6,10},{7,13},{8,4},{9,3},... | collective-permute-start | bytes 221192 | tf_op jit(solution)/shard_map/ppermute | solution.py:610
  54.1 1.7 %collective-permute-done.7.refs_0_ = bf16[24,1536]{1,0:T(8,128)(2,1)S(1)} collective-permute-done((bf16[24,1536]{1,0:T(8,128)(2,1)S(1)}, bf16[24,1536]{1,0:T(8,128)(2,1)S(1)}, u32[]{:S(2)}, u32[]{:S(2)}) %collective-permute-start.7) | collective-permute-done | bytes 73760 | tf_op jit(solution)/shard_map/ppermute | solution.py:610
  55.8 1.3 %collective-permute-done.8.refs_1_ = bf16[24,1536]{1,0:T(8,128)(2,1)S(1)} collective-permute-done((bf16[24,1536]{1,0:T(8,128)(2,1)S(1)}, bf16[24,1536]{1,0:T(8,128)(2,1)S(1)}, u32[]{:S(2)}, u32[]{:S(2)}) %collective-permute-start.8) | collective-permute-done | bytes 73760 | tf_op jit(solution)/shard_map/ppermute | solution.py:610
  57.1 1.9 %collective-permute-done.9.refs_2_ = bf16[24,1536]{1,0:T(8,128)(2,1)S(1)} collective-permute-done((bf16[24,1536]{1,0:T(8,128)(2,1)S(1)}, bf16[24,1536]{1,0:T(8,128)(2,1)S(1)}, u32[]{:S(2)}, u32[]{:S(2)}) %collective-permute-start.9) | collective-permute-done | bytes 73760 | tf_op jit(solution)/shard_map/ppermute | solution.py:610
  59.0 0.7 %finish.1 = bf16[12,3072]{1,0:T(8,128)(2,1)} custom-call(f32[12,3072]{1,0:T(8,128)S(1)} %get-tuple-element.29.carried_ref, f32[12,3072]{1,0:T(8,128)S(1)} %get-tuple-element.49.own_ref, bf16[24,1536]{1,0:T(8,128)(2,1)S(1)} %collective-permute-done.7.refs_0_, bf16[24,1536]{1,0:T(8,128)(2,1)S(1)} %collective-permute-done.8.refs_1_, ...), custom_call_target="tpu_custom_call" | custom-call | tf_op jit(solution)/shard_map/finish/pallas_call | solution.py:586
  (1 shorter events, 0.0 us)
Async XLA Ops:
  3.4 10.4 %collective-permute-start = (bf16[24,1664]{1,0:T(8,128)(2,1)S(1)}, bf16[24,1664]{1,0:T(8,128)(2,1)S(1)}, u32[]{:S(2)}, u32[]{:S(2)}) collective-permute-start(bf16[24,1664]{1,0:T(8,128)(2,1)S(1)} %get-tuple-element.30.dep_ref.refs_0_), channel_id=1, source_target_pairs={{0,8},{1,9},{2,10},{3,11},{4,12},{5,13},{6,14},{7,15},{8,0},{9,1},... | collective-permute-start | bytes 239624 | tf_op jit(solution)/shard_map/ppermute | solution.py:610
  7.5 6.3 %collective-permute-start.1 = (bf16[24,1664]{1,0:T(8,128)(2,1)S(1)}, bf16[24,1664]{1,0:T(8,128)(2,1)S(1)}, u32[]{:S(2)}, u32[]{:S(2)}) collective-permute-start(bf16[24,1664]{1,0:T(8,128)(2,1)S(1)} %get-tuple-element.30.dep_ref.refs_0_), channel_id=1, source_target_pairs={{0,4},{1,3},{2,6},{3,1},{4,0},{5,7},{6,2},{7,5},{8,12},{9,11},{10,... | collective-permute-start | bytes 239624 | tf_op jit(solution)/shard_map/ppermute | solution.py:610
  9.1 6.2 %collective-permute-start.2 = (bf16[24,1664]{1,0:T(8,128)(2,1)S(1)}, bf16[24,1664]{1,0:T(8,128)(2,1)S(1)}, u32[]{:S(2)}, u32[]{:S(2)}) collective-permute-start(bf16[24,1664]{1,0:T(8,128)(2,1)S(1)} %get-tuple-element.30.dep_ref.refs_0_), channel_id=1, source_target_pairs={{0,12},{1,11},{2,14},{3,9},{4,8},{5,15},{6,10},{7,13},{8,4},{9,3},... | collective-permute-start | bytes 239624 | tf_op jit(solution)/shard_map/ppermute | solution.py:610
  15.4 6.9 %collective-permute-start.3 = (bf16[48,3200]{1,0:T(8,128)(2,1)S(1)}, bf16[48,3200]{1,0:T(8,128)(2,1)S(1)}, u32[]{:S(2)}, u32[]{:S(2)}) collective-permute-start(bf16[48,3200]{1,0:T(8,128)(2,1)S(1)} %unfold.1.dep_ref.a_ref), channel_id=1, source_target_pairs={{0,2},{1,5},{2,0},{3,7},{4,6},{5,1},{6,4},{7,3},{8,10},{9,13},{10,... | collective-permute-start | bytes 921608 | tf_op jit(solution)/shard_map/ppermute | solution.py:610
  22.4 5.1 %collective-permute-start.4 = (bf16[96,3200]{1,0:T(8,128)(2,1)S(1)}, bf16[96,3200]{1,0:T(8,128)(2,1)S(1)}, u32[]{:S(2)}, u32[]{:S(2)}) collective-permute-start(bf16[96,3200]{1,0:T(8,128)(2,1)S(1)} %join.1.x_ref), channel_id=1, source_target_pairs={{0,1},{1,0},{2,3},{3,2},{4,5},{5,4},{6,7},{7,6},{8,9},{9,8},{10,11... | collective-permute-start | bytes 1843208 | tf_op jit(solution)/shard_map/ppermute | solution.py:613
  40.5 2.2 %collective-permute-start.5 = (bf16[96,3072]{1,0:T(8,128)(2,1)S(1)}, bf16[96,3072]{1,0:T(8,128)(2,1)S(1)}, u32[]{:S(2)}, u32[]{:S(2)}) collective-permute-start(bf16[96,3072]{1,0:T(8,128)(2,1)S(1)} %get-tuple-element.46), channel_id=1, source_target_pairs={{0,1},{1,0},{2,3},{3,2},{4,5},{5,4},{6,7},{7,6},{8,9},{9,8},{10,11... | collective-permute-start | bytes 1769480 | tf_op jit(solution)/shard_map/ppermute | solution.py:613
  42.8 6.8 %collective-permute-start.6 = (bf16[48,3072]{1,0:T(8,128)(2,1)S(1)}, bf16[48,3072]{1,0:T(8,128)(2,1)S(1)}, u32[]{:S(2)}, u32[]{:S(2)}) collective-permute-start(bf16[48,3072]{1,0:T(8,128)(2,1)S(1)} %get-tuple-element.48), channel_id=1, source_target_pairs={{0,2},{1,5},{2,0},{3,7},{4,6},{5,1},{6,4},{7,3},{8,10},{9,13},{10,... | collective-permute-start | bytes 884744 | tf_op jit(solution)/shard_map/ppermute | solution.py:610
  49.7 6.1 %collective-permute-start.7 = (bf16[24,1536]{1,0:T(8,128)(2,1)S(1)}, bf16[24,1536]{1,0:T(8,128)(2,1)S(1)}, u32[]{:S(2)}, u32[]{:S(2)}) collective-permute-start(bf16[24,1536]{1,0:T(8,128)(2,1)S(1)} %get-tuple-element.50), channel_id=1, source_target_pairs={{0,8},{1,9},{2,10},{3,11},{4,12},{5,13},{6,14},{7,15},{8,0},{9,1},... | collective-permute-start | bytes 221192 | tf_op jit(solution)/shard_map/ppermute | solution.py:610
  52.1 5.0 %collective-permute-start.8 = (bf16[24,1536]{1,0:T(8,128)(2,1)S(1)}, bf16[24,1536]{1,0:T(8,128)(2,1)S(1)}, u32[]{:S(2)}, u32[]{:S(2)}) collective-permute-start(bf16[24,1536]{1,0:T(8,128)(2,1)S(1)} %get-tuple-element.51), channel_id=1, source_target_pairs={{0,4},{1,3},{2,6},{3,1},{4,0},{5,7},{6,2},{7,5},{8,12},{9,11},{10,... | collective-permute-start | bytes 221192 | tf_op jit(solution)/shard_map/ppermute | solution.py:610
  52.7 6.3 %collective-permute-start.9 = (bf16[24,1536]{1,0:T(8,128)(2,1)S(1)}, bf16[24,1536]{1,0:T(8,128)(2,1)S(1)}, u32[]{:S(2)}, u32[]{:S(2)}) collective-permute-start(bf16[24,1536]{1,0:T(8,128)(2,1)S(1)} %get-tuple-element.52), channel_id=1, source_target_pairs={{0,12},{1,11},{2,14},{3,9},{4,8},{5,15},{6,10},{7,13},{8,4},{9,3},... | collective-permute-start | bytes 221192 | tf_op jit(solution)/shard_map/ppermute | solution.py:610

commit v10 on v9

--- a/solution.py
+++ b/solution.py
@@ -46,8 +46,8 @@
 VMEM_SPEC = pl.BlockSpec(memory_space=pltpu.VMEM)
 HBM_SPEC = pl.BlockSpec(memory_space=pltpu.HBM)
 ROUTE_LANE = 3 + 3 * EXPERTS
-HELD_BELOW = 10 * MIB
-LOADED_BELOW = 12 * MIB
+HELD_BELOW = 8 * MIB
+LOADED_BELOW = 10 * MIB
 
 
 def own_side():
@@ -65,7 +65,7 @@
 
 def spare_shape(gate_weight):
     width, units = gate_weight.shape
-    return 2, width // 2, chunk_of(units)
+    return min(2, units // chunk_of(units)), 2, width // 2, chunk_of(units)
 
 
 def row_copies(sources, targets, first, rows, sems):
@@ -89,19 +89,20 @@
     return pl.ds(n * chunk if isinstance(n, int) else pl.multiple_of(n * chunk, LANES), chunk)
 
 
-def other_copy(source, held, spare, c, chunk, sem):
+def other_copy(source, held, spare, i, c, chunk, sem):
     half = source.shape[0] // 2
     first = pl.multiple_of((1 - own_side()) * half, 16)
-    target = spare if isinstance(c, int) and c == 0 else held.at[:, chunk_at(c - 1, chunk)]
+    count = spare.shape[0]
+    target = spare.at[c, i] if c < count else held.at[:, chunk_at(c - count, chunk)]
     return pltpu.make_async_copy(source.at[pl.ds(first, half), chunk_at(c, chunk)], target, sem)
 
 
-def load_kernel(first, rows, ahead, dep_ref, g_hbm, u_hbm, g_in, u_in, g_vmem, u_vmem, *refs):
-    del dep_ref, g_in, u_in
-    *spare, token_ref, sems, sem = refs
+def load_kernel(first, rows, ahead, dep_ref, g_hbm, u_hbm, *refs):
+    g_vmem, u_vmem, spare, token_ref, sems, sem = refs[3:]
     copies = row_copies((g_hbm, u_hbm), (g_vmem, u_vmem), first, rows, sems)
     if ahead:
-        copies.append(other_copy(g_hbm, None, spare[0].at[0], 0, spare[0].shape[2], sem))
+        for i, source in enumerate((g_hbm, u_hbm)):
+            copies.append(other_copy(source, None, spare, i, 0, spare.shape[3], sem.at[i]))
     for copy in copies:
         copy.start()
     token_ref[...] = jnp.zeros_like(token_ref)
@@ -111,15 +112,13 @@
 
 def load_rows(first, rows, ahead, after, gate_weight, up_weight, held):
     hidden = gate_weight.shape[1]
-    spare = (pltpu.VMEM(spare_shape(gate_weight), BF16),) if ahead else ()
     return pl.pallas_call(
         functools.partial(load_kernel, first, rows, ahead),
-        out_shape=tuple(pltpu.VMEM(h.shape, BF16) for h in held) + spare
-        + (pltpu.VMEM((8, LANES), F32),),
-        in_specs=[pl.BlockSpec(memory_space=pl.ANY), HBM_SPEC, HBM_SPEC, VMEM_SPEC, VMEM_SPEC],
-        out_specs=(VMEM_SPEC,) * (3 + len(spare)),
-        scratch_shapes=[pltpu.SemaphoreType.DMA((2, 4)), pltpu.SemaphoreType.DMA],
-        input_output_aliases={3: 0, 4: 1},
+        out_shape=tuple(pltpu.VMEM(h.shape, BF16) for h in held) + (pltpu.VMEM((8, LANES), F32),),
+        in_specs=[pl.BlockSpec(memory_space=pl.ANY), HBM_SPEC, HBM_SPEC] + [VMEM_SPEC] * 3,
+        out_specs=(VMEM_SPEC,) * 4,
+        scratch_shapes=[pltpu.SemaphoreType.DMA((2, 4)), pltpu.SemaphoreType.DMA((2,))],
+        input_output_aliases={3: 0, 4: 1, 5: 2},
         compiler_params=pltpu.CompilerParams(vmem_limit_bytes=LOADED_BELOW),
         cost_estimate=pl.CostEstimate(flops=0, bytes_accessed=4 * rows * hidden, transcendentals=0),
         name="load_weights",
@@ -176,7 +175,7 @@
 
 def attend_kernel(
     ahead, len_hbm, routes_hbm, q_hbm, k_hbm, v_hbm, nk_hbm, nv_hbm, res_hbm, gain_hbm, rt_hbm,
-    g_hbm, u_hbm, carried_ref, pay_ref, g_vmem, u_vmem,
+    g_hbm, u_hbm, carried_ref, pay_ref, g_vmem, u_vmem, spare_ref,
     q_ref, k_ref, v_ref, nk_ref, nv_ref, res_ref, gain_ref, rt_ref,
     q_scr, o_scr, nk_scr, nv_scr, pay_scr, len_ref, routes_ref, sems, w_sems,
 ):
@@ -296,9 +295,10 @@
             pltpu.VMEM((FOLD * tok, wide), BF16),
             pltpu.VMEM(held_shape(gate_weight), BF16),
             pltpu.VMEM(held_shape(gate_weight), BF16),
+            pltpu.VMEM(spare_shape(gate_weight), BF16),
         ),
         in_specs=[HBM_SPEC] * 12,
-        out_specs=(VMEM_SPEC,) * 4,
+        out_specs=(VMEM_SPEC,) * 5,
         scratch_shapes=here + [
             pltpu.VMEM((1, width), F32),
             pltpu.VMEM((EXPERTS, width), BF16),
@@ -330,25 +330,28 @@
     half, units = g_ref.shape[0], gate_ref.shape[1]
     chunk = chunk_of(units)
     chunks = units // chunk
-    ready = [(1, 0)] + [(0, 1), (1, 1), (0, 2)][:2 * (chunks - 1)]
-    ready = [(i, c) for i, c in ready if c < chunks]
+    count = spare_ref.shape[0]
+    ready = [(i, c) for c in range(1, min(count + 1, chunks)) for i in range(2)]
 
     def copy(i, c):
         return other_copy(
-            (g_hbm, u_hbm)[i], (g_ref, u_ref)[i], spare_ref.at[i], c, chunk, sems.at[i, c]
+            (g_hbm, u_hbm)[i], (g_ref, u_ref)[i], spare_ref, i, c, chunk, sems.at[i, c]
         )
 
-    copy(1, 0).start()
+    for i, c in ready:
+        if c < count:
+            copy(i, c).start()
 
     def step(n, _):
         at = chunk_at(n, chunk)
         rows = x_ref[:, :half]
         gate_ref[:, at] = jnp.dot(rows, g_ref[:, at], preferred_element_type=F32)
         up_ref[:, at] = jnp.dot(rows, u_ref[:, at], preferred_element_type=F32)
-        for i, c in ready[1:]:
-            @pl.when(n == c - 1)
-            def _(i=i, c=c):
-                copy(i, c).start()
+        for i, c in ready:
+            if c >= count:
+                @pl.when(n == c - count)
+                def _(i=i, c=c):
+                    copy(i, c).start()
 
         return 0
 
@@ -357,13 +360,13 @@
         copy(i, c).wait()
 
 
-def first_half(mine, held, spare, gate_weight, up_weight):
+def first_half(mine, held, gate_weight, up_weight):
     rows = mine.shape[0]
     width, units = gate_weight.shape
     acc = pltpu.VMEM((rows, units), F32)
     return pl.pallas_call(
         first_half_kernel,
-        out_shape=(acc, acc) + tuple(pltpu.VMEM(h.shape, BF16) for h in (*held, spare)),
+        out_shape=(acc, acc) + tuple(pltpu.VMEM(h.shape, BF16) for h in held),
         in_specs=[VMEM_SPEC] + [HBM_SPEC] * 2 + [VMEM_SPEC] * 3,
         out_specs=(VMEM_SPEC,) * 5,
         scratch_shapes=[pltpu.SemaphoreType.DMA((2, units // chunk_of(units)))],
@@ -373,14 +376,14 @@
             flops=2 * rows * width * units, bytes_accessed=width * units, transcendentals=0
         ),
         name="first_half",
-    )(*in_vmem_always([mine]), *in_hbm(gate_weight, up_weight), *in_vmem_always([*held, spare]))
+    )(*in_vmem_always([mine]), *in_hbm(gate_weight, up_weight), *in_vmem_always(held))
 
 
 def second_half_kernel(
-    per_plane, x_ref, ox_ref, gate_ref, up_ref, spare_ref, g_hbm, u_hbm, d_hbm, g_in, u_in,
-    staying_ref, leaving_ref, g_ref, u_ref, x_scr, h_scr, gu_sems, sems,
+    per_plane, x_ref, ox_ref, gate_ref, up_ref, g_hbm, u_hbm, d_hbm, g_in, u_in, spare_in,
+    staying_ref, leaving_ref, g_ref, u_ref, spare_ref, h_scr, gu_sems, sems,
 ):
-    del g_in, u_in
+    del g_in, u_in, spare_in
     rows, units = h_scr.shape
     width = staying_ref.shape[1]
     side = own_side()
@@ -389,20 +392,34 @@
     per_side = width // chunk
     pairs = per_side
 
+    count = spare_ref.shape[0]
+    places = count + chunks
+
     def gu_copy(i, c):
-        return other_copy((g_hbm, u_hbm)[i], (g_ref, u_ref)[i], None, c, chunk, gu_sems.at[i, c])
-
-    def down_slot(p):
-        return chunk_at(lax.rem(p + chunks - 1, chunks), chunk)
-
-    def down_copy(i, p):
+        return other_copy(
+            (g_hbm, u_hbm)[i], (g_ref, u_ref)[i], spare_ref, i, c, chunk, gu_sems.at[i, c]
+        )
+
+    def down_place(i, part, r):
+        if part == 1:
+            return spare_ref.at[r - count, i, pl.ds(0, units)]
+        start = r + chunks - count if part == 0 else r - 2 * count
+        return (g_ref, u_ref)[i].at[pl.ds(0, units), chunk_at(start, chunk)]
+
+    def part_of(r):
+        return 0 if r < count else 1 if r < 2 * count else 2
+
+    def down_copy(i, p, part, r):
         n = 2 * p + i
         column = jnp.where(n < per_side, 1 - side, side) * width + lax.rem(n, per_side) * chunk
         return pltpu.make_async_copy(
-            d_hbm.at[:, pl.ds(pl.multiple_of(column, LANES), chunk)],
-            (g_ref, u_ref)[i].at[pl.ds(0, units), down_slot(p)],
+            d_hbm.at[:, pl.ds(pl.multiple_of(column, LANES), chunk)], down_place(i, part, r),
             sems.at[i, p],
         )
+
+    def start_down(p):
+        for i in range(2):
+            down_copy(i, p, part_of(p % places), p % places).start()
 
     def in_order(values):
         quarter = rows // 4
@@ -410,13 +427,11 @@
             [values[q * quarter:(q + 1) * quarter, :] for q in (0, 2, 1, 3)], axis=0
         )
 
-    later = [(1, 2)] if chunks > 2 else []
-    later += [(i, c) for c in range(3, chunks) for i in range(2)]
+    later = [(i, c) for c in range(count + 1, chunks) for i in range(2)]
     for i, c in later:
         gu_copy(i, c).start()
-    for i in range(2):
-        down_copy(i, 0).start()
-    x_scr[...] = in_order(ox_ref[:, :width].astype(F32)).astype(BF16)
+    for p in range(min(count, pairs)):
+        start_down(p)
 
     own = x_ref[:, width:].astype(F32)
     both = own + in_order(ox_ref[:, width:].astype(F32))
@@ -439,38 +454,43 @@
 
     def hidden_chunk(c, g_part, u_part):
         at = chunk_at(c, chunk)
-        gate = gate_ref[:, at] + jnp.dot(x_scr[...], g_part, preferred_element_type=F32)
-        up = up_ref[:, at] + jnp.dot(x_scr[...], u_part, preferred_element_type=F32)
+        rows_in = ox_ref[:, :width]
+        gate = gate_ref[:, at] + in_order(jnp.dot(rows_in, g_part, preferred_element_type=F32))
+        up = up_ref[:, at] + in_order(jnp.dot(rows_in, u_part, preferred_element_type=F32))
         gate = gate * scale
         h_scr[:, at] = (gate / (1.0 + jnp.exp(-gate)) * (up * scale)).astype(BF16)
-
-    hidden_chunk(0, spare_ref[0], spare_ref[1])
-
-    def hidden_step(c, _):
+        for late in range(chunks):
+            if count + late < pairs:
+                @pl.when(c == late)
+                def _(late=late):
+                    start_down(count + late)
+
+    def spare_step(c, _):
+        hidden_chunk(c, spare_ref[c, 0], spare_ref[c, 1])
+        return 0
+
+    def held_step(c, _):
         for i, late in later:
             @pl.when(c == late)
             def _(i=i, late=late):
                 gu_copy(i, late).wait()
 
-        slot = chunk_at(c - 1, chunk)
+        slot = chunk_at(c - count, chunk)
         hidden_chunk(c, g_ref[:, slot], u_ref[:, slot])
-
-        @pl.when(c < pairs)
-        def _():
-            for i in range(2):
-                down_copy(i, c).start()
-
         return 0
 
-    lax.fori_loop(1, chunks, hidden_step, 0)
-
-    def down_step(p, _):
-        slot = down_slot(p)
-        for i, ref in enumerate((g_ref, u_ref)):
+    lax.fori_loop(0, count, spare_step, 0)
+    lax.fori_loop(count, chunks, held_step, 0)
+
+    def down_step(turn, part, r, _):
+        p = turn * places + r
+        for i in range(2):
             n = 2 * p + i
-            down_copy(i, p).wait()
-            value = jnp.dot(h_scr[...], ref[:units, slot], preferred_element_type=F32) * weight
-            to = pl.ds(pl.multiple_of(lax.rem(n, per_side) * chunk, LANES), chunk)
+            down_copy(i, p, part, r).wait()
+            value = jnp.dot(
+                h_scr[...], down_place(i, part, r)[...], preferred_element_type=F32
+            ) * weight
+            to = chunk_at(lax.rem(n, per_side), chunk)
 
             @pl.when(n < per_side)
             def _(value=value, to=to):
@@ -480,17 +500,19 @@
             def _(value=value, to=to):
                 staying_ref[:, to] = value
 
-        @pl.when(p + chunks < pairs)
-        def _():
-            for i in range(2):
-                down_copy(i, p + chunks).start()
-
         return 0
 
-    lax.fori_loop(0, pairs, down_step, 0)
-
-
-def second_half(per_plane, mine, other, sums, held, spare, gate_weight, up_weight, down_weight):
+    for turn in range(-(-pairs // places)):
+        for part, (low, high) in enumerate(((0, count), (count, 2 * count), (2 * count, places))):
+            high = min(high, pairs - turn * places)
+            if low < high:
+                lax.fori_loop(low, high, functools.partial(down_step, turn, part), 0)
+            for r in range(low, high):
+                if (turn + 1) * places + r < pairs:
+                    start_down((turn + 1) * places + r)
+
+
+def second_half(per_plane, mine, other, sums, held, gate_weight, up_weight, down_weight):
     rows, units = sums[0].shape
     width = down_weight.shape[1] // 2
     chunk = chunk_of(units)
@@ -498,15 +520,14 @@
         functools.partial(second_half_kernel, per_plane),
         out_shape=(vmem_array((rows, width), F32), vmem_array((rows, width), BF16))
         + tuple(pltpu.VMEM(h.shape, BF16) for h in held),
-        in_specs=[VMEM_SPEC] * 5 + [HBM_SPEC] * 3 + [VMEM_SPEC] * 2,
-        out_specs=(VMEM_SPEC,) * 4,
+        in_specs=[VMEM_SPEC] * 4 + [HBM_SPEC] * 3 + [VMEM_SPEC] * 3,
+        out_specs=(VMEM_SPEC,) * 5,
         scratch_shapes=[
-            pltpu.VMEM((rows, width), BF16),
             pltpu.VMEM((rows, units), BF16),
             pltpu.SemaphoreType.DMA((2, units // chunk)),
             pltpu.SemaphoreType.DMA((2, width // chunk)),
         ],
-        input_output_aliases={8: 2, 9: 3},
+        input_output_aliases={7: 2, 8: 3, 9: 4},
         compiler_params=pltpu.CompilerParams(
             vmem_limit_bytes=HELD_BELOW if rows < 256 else 40 * MIB
         ),
@@ -515,7 +536,7 @@
         ),
         name="second_half",
     )(
-        *in_vmem_always([mine, other]), *in_vmem(*sums), *in_vmem_always([spare]),
+        *in_vmem_always([mine, other]), *in_vmem(*sums),
         *in_hbm(gate_weight, up_weight, down_weight), *in_vmem_always(held),
     )[:2]
 
@@ -628,15 +649,15 @@
     for stage in range(2, stages):
         got = exchange(payload, stage)
         if stage == 2:
-            *held, spare, token = load_rows(
+            *held, token = load_rows(
                 heights[0] + heights[1], heights[2], True, payload, gate_weight, up_weight, held
             )
         payload = join(payload, got, token)
     mine = payload
     other = to_core(mine)
-    gate, up, *held, spare = first_half(mine, held, spare, gate_weight, up_weight)
+    gate, up, *held = first_half(mine, held, gate_weight, up_weight)
     staying, leaving = second_half(
-        per_plane, mine, other, (gate, up), held, spare, gate_weight, up_weight, down_weight
+        per_plane, mine, other, (gate, up), held, gate_weight, up_weight, down_weight
     )
     keep, got = staying, to_core(leaving)
     for stage in range(stages - 1, 1, -1):

time: 59.8 us -> 58.6 us (0.980)
  starting transfers between devices: 13.9 us -> 11.5 us
  waiting for transfers between devices: 14.1 us -> 16.3 us
  Pallas kernels: 31.6 us -> 30.6 us
    ppermute x8, starting transfers between devices: 13.2 us -> 10.9 us  [exchange(): return lax.ppermute(array, ('node', 'shard'), perm)]
    ppermute x8, waiting for transfers between devices: 12.5 us -> 14.6 us  [exchange(): return lax.ppermute(array, ('node', 'shard'), perm)]
    pallas_call x1, Pallas kernels: 13 us -> 11.1 us  [second_half(): pl.pallas_call(functools.partial(second_half_kernel, per_plane), out_shap...]
    pallas_call x2, Pallas kernels: 9.17 us -> 10.1 us  [load_rows(): pl.pallas_call(functools.partial(load_kernel, first, rows, ahead), out_sh...]
  transfers between devices with their start and end apart: 10 -> 10, of which waited for: 7 -> 7; matrix products, arithmetic and copies ran while one was open for 0% -> 0% of each run, Pallas kernels for 24% -> 26%
where the time goes in v10:
time: 58.6 us; the launch traced here: 58.5 us
  Pallas kernels  30.6 us (52%)
  waiting for transfers between devices  16.3 us (28%)
  starting transfers between devices  11.5 us (20%)
    ppermute x8, waiting for transfers between devices, exchange(): return lax.ppermute(array, ('node', 'shard'), perm)  14.6 us
    pallas_call x1, Pallas kernels, second_half(): pl.pallas_call(functools.partial(second_half_kernel, per_plane), out_shap...  11.1 us
    ppermute x8, starting transfers between devices, exchange(): return lax.ppermute(array, ('node', 'shard'), perm)  10.9 us
    pallas_call x2, Pallas kernels, load_rows(): pl.pallas_call(functools.partial(load_kernel, first, rows, ahead), out_sh...  10.1 us
    pallas_call x1, Pallas kernels, first_half(): pl.pallas_call(first_half_kernel, out_shape=(acc, acc) + tuple((pltpu.VME...  5 us
    pallas_call x1, Pallas kernels, attend(): pl.pallas_call(functools.partial(attend_kernel, ahead), out_shape=(pltpu....  3.41 us
    ppermute x2, waiting for transfers between devices, to_core(): return lax.ppermute(array, 'shard', [(0, 1), (1, 0)])  1.63 us
  transfers between devices with their start and end apart: 10, of which 7 were waited for; matrix products, arithmetic and copies ran while one was open for 0% of the time, Pallas kernels for 26%

profile of v10, /device:TPU:0, one launch (start us, length us, event | category | flops | bytes accessed | tf_op | source)
XLA Modules:
  0.0 58.5 jit_solution(11017355615200477078)
XLA Ops:
  0.0 3.4 %attend.1 = (f32[12,3072]{1,0:T(8,128)S(1)}, bf16[24,1664]{1,0:T(8,128)(2,1)S(1)}, bf16[3072,2048]{1,0:T(8,128)(2,1)S(1)}, bf16[3072,2048]{1,0:T(8,128)(2,1)S(1)}, bf16[2,2,3072,512]{3,2,1,0:T(8,128)(2,1)S(1)}) custom-call(s32[12]{0:T(128)} %len_hbm.1, s32[2,12]{1,0:T(2,128)} %bitcast.5, bf16[12,3072]{1,0:T(8,128)(2,1)} %q_hbm.1, ...), custom_call_target="tpu_custom_call" | custom-call | flops 100000000 | bytes 8000000 | tf_op jit(solution)/shard_map/attend/pallas_call | solution.py:291
  3.4 5.1 %collective-permute-start.2 = (bf16[24,1664]{1,0:T(8,128)(2,1)S(1)}, bf16[24,1664]{1,0:T(8,128)(2,1)S(1)}, u32[]{:S(2)}, u32[]{:S(2)}) collective-permute-start(bf16[24,1664]{1,0:T(8,128)(2,1)S(1)} %get-tuple-element.32.dep_ref.refs_0_), channel_id=1, source_target_pairs={{0,12},{1,11},{2,14},{3,9},{4,8},{5,15},{6,10},{7,13},{8,4},{9,3},... | collective-permute-start | bytes 239624 | tf_op jit(solution)/shard_map/ppermute | solution.py:631
  8.5 0.0 collective-permute-start.1
  8.5 0.6 %collective-permute-start = (bf16[24,1664]{1,0:T(8,128)(2,1)S(1)}, bf16[24,1664]{1,0:T(8,128)(2,1)S(1)}, u32[]{:S(2)}, u32[]{:S(2)}) collective-permute-start(bf16[24,1664]{1,0:T(8,128)(2,1)S(1)} %get-tuple-element.32.dep_ref.refs_0_), channel_id=1, source_target_pairs={{0,8},{1,9},{2,10},{3,11},{4,12},{5,13},{6,14},{7,15},{8,0},{9,1},... | collective-permute-start | bytes 239624 | tf_op jit(solution)/shard_map/ppermute | solution.py:631
  9.2 4.7 %load_weights.2 = (bf16[3072,2048]{1,0:T(8,128)(2,1)S(1)}, bf16[3072,2048]{1,0:T(8,128)(2,1)S(1)}, bf16[2,2,3072,512]{3,2,1,0:T(8,128)(2,1)S(1)}, f32[8,128]{1,0:T(8,128)S(1)}) custom-call(bf16[24,1664]{1,0:T(8,128)(2,1)S(1)} %get-tuple-element.32.dep_ref.refs_0_, ...), custom_call_target="tpu_custom_call", output_to_operand_aliasing={{0}: (3, {}), {1}: (4, {}), {2}: (5, {})} | custom-call | bytes 12582912 | tf_op jit(solution)/shard_map/load_weights/pallas_call | solution.py:115
  13.9 0.0 collective-permute-done.2.refs_3_
  13.9 0.0 collective-permute-done.1.refs_2_
  13.9 2.1 %collective-permute-done.refs_1_ = bf16[24,1664]{1,0:T(8,128)(2,1)S(1)} collective-permute-done((bf16[24,1664]{1,0:T(8,128)(2,1)S(1)}, bf16[24,1664]{1,0:T(8,128)(2,1)S(1)}, u32[]{:S(2)}, u32[]{:S(2)}) %collective-permute-start) | collective-permute-done | bytes 79904 | tf_op jit(solution)/shard_map/ppermute | solution.py:631
  16.0 0.1 unfold.1.dep_ref.a_ref
  16.1 0.1 collective-permute-start.3
  16.2 5.4 %load_weights.3 = (bf16[3072,2048]{1,0:T(8,128)(2,1)S(1)}, bf16[3072,2048]{1,0:T(8,128)(2,1)S(1)}, bf16[2,2,3072,512]{3,2,1,0:T(8,128)(2,1)S(1)}, f32[8,128]{1,0:T(8,128)S(1)}) custom-call(bf16[48,3200]{1,0:T(8,128)(2,1)S(1)} %unfold.1.dep_ref.a_ref, bf16[6144,2048]{1,0:T(8,128)(2,1)} %g_hbm.9, ...), custom_call_target="tpu_custom_call", output_to_operand_aliasing={{0}: (3, {}), {1}: (4, {}), {2}: (5, {})} | custom-call | bytes 8388608 | tf_op jit(solution)/shard_map/load_weights/pallas_call | solution.py:115
  21.6 1.4 %collective-permute-done.3.b_ref = bf16[48,3200]{1,0:T(8,128)(2,1)S(1)} collective-permute-done((bf16[48,3200]{1,0:T(8,128)(2,1)S(1)}, bf16[48,3200]{1,0:T(8,128)(2,1)S(1)}, u32[]{:S(2)}, u32[]{:S(2)}) %collective-permute-start.3) | collective-permute-done | bytes 307232 | tf_op jit(solution)/shard_map/ppermute | solution.py:631
  23.1 0.1 collective-permute-start.4
  23.1 5.0 %first_half.1 = (f32[96,2048]{1,0:T(8,128)S(1)}, f32[96,2048]{1,0:T(8,128)S(1)}, bf16[3072,2048]{1,0:T(8,128)(2,1)S(1)}, bf16[3072,2048]{1,0:T(8,128)(2,1)S(1)}, bf16[2,2,3072,512]{3,2,1,0:T(8,128)(2,1)S(1)}) custom-call(bf16[96,3200]{1,0:T(8,128)(2,1)S(1)} %join.1.x_ref, ...), custom_call_target="tpu_custom_call", output_to_operand_aliasing={{2}: (3, {}), {3}: (4, {}), {4}: (5, {})} | custom-call | flops 2415919104 | bytes 12582912 | tf_op jit(solution)/shard_map/first_half/pallas_call | solution.py:367
  28.2 0.0 collective-permute-done.4.ox_ref
  28.2 11.1 %second_half.1 = (f32[96,3072]{1,0:T(8,128)S(1)}, bf16[96,3072]{1,0:T(8,128)(2,1)S(1)}, bf16[3072,2048]{1,0:T(8,128)(2,1)S(1)}, bf16[3072,2048]{1,0:T(8,128)(2,1)S(1)}, bf16[2,2,3072,512]{3,2,1,0:T(8,128)(2,1)S(1)}) custom-call(bf16[96,3200]{1,0:T(8,128)(2,1)S(1)} %join.1.x_ref, ...), custom_call_target="tpu_custom_call", output_to_operand_aliasing={{2}: (7, {}), {3}: (8, {}), {4}: (9, {})} | custom-call | flops 3623878656 | bytes 25165824 | tf_op jit(solution)/shard_map/second_half/pallas_call | solution.py:519
  39.3 0.6 collective-permute-start.5
  39.8 1.6 %collective-permute-done.5.got_ref = bf16[96,3072]{1,0:T(8,128)(2,1)S(1)} collective-permute-done((bf16[96,3072]{1,0:T(8,128)(2,1)S(1)}, bf16[96,3072]{1,0:T(8,128)(2,1)S(1)}, u32[]{:S(2)}, u32[]{:S(2)}) %collective-permute-start.5) | collective-permute-done | bytes 589856 | tf_op jit(solution)/shard_map/ppermute | solution.py:634
  41.4 0.1 split_rows.1
  41.5 0.6 %collective-permute-start.6 = (bf16[48,3072]{1,0:T(8,128)(2,1)S(1)}, bf16[48,3072]{1,0:T(8,128)(2,1)S(1)}, u32[]{:S(2)}, u32[]{:S(2)}) collective-permute-start(bf16[48,3072]{1,0:T(8,128)(2,1)S(1)} %get-tuple-element.52), channel_id=1, source_target_pairs={{0,2},{1,5},{2,0},{3,7},{4,6},{5,1},{6,4},{7,3},{8,10},{9,13},{10,... | collective-permute-start | bytes 884744 | tf_op jit(solution)/shard_map/ppermute | solution.py:631
  42.2 6.2 %collective-permute-done.6.got_ref = bf16[48,3072]{1,0:T(8,128)(2,1)S(1)} collective-permute-done((bf16[48,3072]{1,0:T(8,128)(2,1)S(1)}, bf16[48,3072]{1,0:T(8,128)(2,1)S(1)}, u32[]{:S(2)}, u32[]{:S(2)}) %collective-permute-start.6) | collective-permute-done | bytes 294944 | tf_op jit(solution)/shard_map/ppermute | solution.py:631
  48.3 0.1 split_last.1
  48.4 1.4 %collective-permute-start.7 = (bf16[24,1536]{1,0:T(8,128)(2,1)S(1)}, bf16[24,1536]{1,0:T(8,128)(2,1)S(1)}, u32[]{:S(2)}, u32[]{:S(2)}) collective-permute-start(bf16[24,1536]{1,0:T(8,128)(2,1)S(1)} %get-tuple-element.54), channel_id=1, source_target_pairs={{0,8},{1,9},{2,10},{3,11},{4,12},{5,13},{6,14},{7,15},{8,0},{9,1},... | collective-permute-start | bytes 221192 | tf_op jit(solution)/shard_map/ppermute | solution.py:631
  49.8 1.8 %collective-permute-start.8 = (bf16[24,1536]{1,0:T(8,128)(2,1)S(1)}, bf16[24,1536]{1,0:T(8,128)(2,1)S(1)}, u32[]{:S(2)}, u32[]{:S(2)}) collective-permute-start(bf16[24,1536]{1,0:T(8,128)(2,1)S(1)} %get-tuple-element.55), channel_id=1, source_target_pairs={{0,4},{1,3},{2,6},{3,1},{4,0},{5,7},{6,2},{7,5},{8,12},{9,11},{10,... | collective-permute-start | bytes 221192 | tf_op jit(solution)/shard_map/ppermute | solution.py:631
  51.6 1.3 %collective-permute-start.9 = (bf16[24,1536]{1,0:T(8,128)(2,1)S(1)}, bf16[24,1536]{1,0:T(8,128)(2,1)S(1)}, u32[]{:S(2)}, u32[]{:S(2)}) collective-permute-start(bf16[24,1536]{1,0:T(8,128)(2,1)S(1)} %get-tuple-element.56), channel_id=1, source_target_pairs={{0,12},{1,11},{2,14},{3,9},{4,8},{5,15},{6,10},{7,13},{8,4},{9,3},... | collective-permute-start | bytes 221192 | tf_op jit(solution)/shard_map/ppermute | solution.py:631
  52.9 2.3 %collective-permute-done.7.refs_0_ = bf16[24,1536]{1,0:T(8,128)(2,1)S(1)} collective-permute-done((bf16[24,1536]{1,0:T(8,128)(2,1)S(1)}, bf16[24,1536]{1,0:T(8,128)(2,1)S(1)}, u32[]{:S(2)}, u32[]{:S(2)}) %collective-permute-start.7) | collective-permute-done | bytes 73760 | tf_op jit(solution)/shard_map/ppermute | solution.py:631
  55.1 0.7 %collective-permute-done.8.refs_1_ = bf16[24,1536]{1,0:T(8,128)(2,1)S(1)} collective-permute-done((bf16[24,1536]{1,0:T(8,128)(2,1)S(1)}, bf16[24,1536]{1,0:T(8,128)(2,1)S(1)}, u32[]{:S(2)}, u32[]{:S(2)}) %collective-permute-start.8) | collective-permute-done | bytes 73760 | tf_op jit(solution)/shard_map/ppermute | solution.py:631
  55.9 1.9 %collective-permute-done.9.refs_2_ = bf16[24,1536]{1,0:T(8,128)(2,1)S(1)} collective-permute-done((bf16[24,1536]{1,0:T(8,128)(2,1)S(1)}, bf16[24,1536]{1,0:T(8,128)(2,1)S(1)}, u32[]{:S(2)}, u32[]{:S(2)}) %collective-permute-start.9) | collective-permute-done | bytes 73760 | tf_op jit(solution)/shard_map/ppermute | solution.py:631
  57.8 0.7 %finish.1 = bf16[12,3072]{1,0:T(8,128)(2,1)} custom-call(f32[12,3072]{1,0:T(8,128)S(1)} %get-tuple-element.31.carried_ref, f32[12,3072]{1,0:T(8,128)S(1)} %get-tuple-element.53.own_ref, bf16[24,1536]{1,0:T(8,128)(2,1)S(1)} %collective-permute-done.7.refs_0_, bf16[24,1536]{1,0:T(8,128)(2,1)S(1)} %collective-permute-done.8.refs_1_, ...), custom_call_target="tpu_custom_call" | custom-call | tf_op jit(solution)/shard_map/finish/pallas_call | solution.py:607
  (1 shorter events, 0.0 us)
Async XLA Ops:
  3.4 10.5 %collective-permute-start.2 = (bf16[24,1664]{1,0:T(8,128)(2,1)S(1)}, bf16[24,1664]{1,0:T(8,128)(2,1)S(1)}, u32[]{:S(2)}, u32[]{:S(2)}) collective-permute-start(bf16[24,1664]{1,0:T(8,128)(2,1)S(1)} %get-tuple-element.32.dep_ref.refs_0_), channel_id=1, source_target_pairs={{0,12},{1,11},{2,14},{3,9},{4,8},{5,15},{6,10},{7,13},{8,4},{9,3},... | collective-permute-start | bytes 239624 | tf_op jit(solution)/shard_map/ppermute | solution.py:631
  8.5 5.4 %collective-permute-start.1 = (bf16[24,1664]{1,0:T(8,128)(2,1)S(1)}, bf16[24,1664]{1,0:T(8,128)(2,1)S(1)}, u32[]{:S(2)}, u32[]{:S(2)}) collective-permute-start(bf16[24,1664]{1,0:T(8,128)(2,1)S(1)} %get-tuple-element.32.dep_ref.refs_0_), channel_id=1, source_target_pairs={{0,4},{1,3},{2,6},{3,1},{4,0},{5,7},{6,2},{7,5},{8,12},{9,11},{10,... | collective-permute-start | bytes 239624 | tf_op jit(solution)/shard_map/ppermute | solution.py:631
  8.5 7.5 %collective-permute-start = (bf16[24,1664]{1,0:T(8,128)(2,1)S(1)}, bf16[24,1664]{1,0:T(8,128)(2,1)S(1)}, u32[]{:S(2)}, u32[]{:S(2)}) collective-permute-start(bf16[24,1664]{1,0:T(8,128)(2,1)S(1)} %get-tuple-element.32.dep_ref.refs_0_), channel_id=1, source_target_pairs={{0,8},{1,9},{2,10},{3,11},{4,12},{5,13},{6,14},{7,15},{8,0},{9,1},... | collective-permute-start | bytes 239624 | tf_op jit(solution)/shard_map/ppermute | solution.py:631
  16.1 6.9 %collective-permute-start.3 = (bf16[48,3200]{1,0:T(8,128)(2,1)S(1)}, bf16[48,3200]{1,0:T(8,128)(2,1)S(1)}, u32[]{:S(2)}, u32[]{:S(2)}) collective-permute-start(bf16[48,3200]{1,0:T(8,128)(2,1)S(1)} %unfold.1.dep_ref.a_ref), channel_id=1, source_target_pairs={{0,2},{1,5},{2,0},{3,7},{4,6},{5,1},{6,4},{7,3},{8,10},{9,13},{10,... | collective-permute-start | bytes 921608 | tf_op jit(solution)/shard_map/ppermute | solution.py:631
  23.1 5.1 %collective-permute-start.4 = (bf16[96,3200]{1,0:T(8,128)(2,1)S(1)}, bf16[96,3200]{1,0:T(8,128)(2,1)S(1)}, u32[]{:S(2)}, u32[]{:S(2)}) collective-permute-start(bf16[96,3200]{1,0:T(8,128)(2,1)S(1)} %join.1.x_ref), channel_id=1, source_target_pairs={{0,1},{1,0},{2,3},{3,2},{4,5},{5,4},{6,7},{7,6},{8,9},{9,8},{10,11... | collective-permute-start | bytes 1843208 | tf_op jit(solution)/shard_map/ppermute | solution.py:634
  39.3 2.2 %collective-permute-start.5 = (bf16[96,3072]{1,0:T(8,128)(2,1)S(1)}, bf16[96,3072]{1,0:T(8,128)(2,1)S(1)}, u32[]{:S(2)}, u32[]{:S(2)}) collective-permute-start(bf16[96,3072]{1,0:T(8,128)(2,1)S(1)} %get-tuple-element.50), channel_id=1, source_target_pairs={{0,1},{1,0},{2,3},{3,2},{4,5},{5,4},{6,7},{7,6},{8,9},{9,8},{10,11... | collective-permute-start | bytes 1769480 | tf_op jit(solution)/shard_map/ppermute | solution.py:634
  41.5 6.8 %collective-permute-start.6 = (bf16[48,3072]{1,0:T(8,128)(2,1)S(1)}, bf16[48,3072]{1,0:T(8,128)(2,1)S(1)}, u32[]{:S(2)}, u32[]{:S(2)}) collective-permute-start(bf16[48,3072]{1,0:T(8,128)(2,1)S(1)} %get-tuple-element.52), channel_id=1, source_target_pairs={{0,2},{1,5},{2,0},{3,7},{4,6},{5,1},{6,4},{7,3},{8,10},{9,13},{10,... | collective-permute-start | bytes 884744 | tf_op jit(solution)/shard_map/ppermute | solution.py:631
  48.4 6.7 %collective-permute-start.7 = (bf16[24,1536]{1,0:T(8,128)(2,1)S(1)}, bf16[24,1536]{1,0:T(8,128)(2,1)S(1)}, u32[]{:S(2)}, u32[]{:S(2)}) collective-permute-start(bf16[24,1536]{1,0:T(8,128)(2,1)S(1)} %get-tuple-element.54), channel_id=1, source_target_pairs={{0,8},{1,9},{2,10},{3,11},{4,12},{5,13},{6,14},{7,15},{8,0},{9,1},... | collective-permute-start | bytes 221192 | tf_op jit(solution)/shard_map/ppermute | solution.py:631
  49.8 6.1 %collective-permute-start.8 = (bf16[24,1536]{1,0:T(8,128)(2,1)S(1)}, bf16[24,1536]{1,0:T(8,128)(2,1)S(1)}, u32[]{:S(2)}, u32[]{:S(2)}) collective-permute-start(bf16[24,1536]{1,0:T(8,128)(2,1)S(1)} %get-tuple-element.55), channel_id=1, source_target_pairs={{0,4},{1,3},{2,6},{3,1},{4,0},{5,7},{6,2},{7,5},{8,12},{9,11},{10,... | collective-permute-start | bytes 221192 | tf_op jit(solution)/shard_map/ppermute | solution.py:631
  51.6 6.2 %collective-permute-start.9 = (bf16[24,1536]{1,0:T(8,128)(2,1)S(1)}, bf16[24,1536]{1,0:T(8,128)(2,1)S(1)}, u32[]{:S(2)}, u32[]{:S(2)}) collective-permute-start(bf16[24,1536]{1,0:T(8,128)(2,1)S(1)} %get-tuple-element.56), channel_id=1, source_target_pairs={{0,12},{1,11},{2,14},{3,9},{4,8},{5,15},{6,10},{7,13},{8,4},{9,3},... | collective-permute-start | bytes 221192 | tf_op jit(solution)/shard_map/ppermute | solution.py:631

commit v11 on v10

--- a/solution.py
+++ b/solution.py
@@ -379,47 +379,84 @@
     )(*in_vmem_always([mine]), *in_hbm(gate_weight, up_weight), *in_vmem_always(held))
 
 
+def down_tools(d_hbm, g_ref, u_ref, spare_ref, h_ref, sems, width):
+    units = h_ref.shape[1]
+    chunk = chunk_of(units)
+    chunks, count = units // chunk, spare_ref.shape[0]
+    per_side = width // chunk
+    places = count + chunks
+    side = own_side()
+
+    def place(i, part, r):
+        if part == 1:
+            return spare_ref.at[r - count, i, pl.ds(0, units)]
+        start = r + chunks - count if part == 0 else r - 2 * count
+        return (g_ref, u_ref)[i].at[pl.ds(0, units), chunk_at(start, chunk)]
+
+    def copy(i, p, part, r):
+        n = 2 * p + i
+        column = jnp.where(n < per_side, 1 - side, side) * width + lax.rem(n, per_side) * chunk
+        return pltpu.make_async_copy(
+            d_hbm.at[:, pl.ds(pl.multiple_of(column, LANES), chunk)], place(i, part, r), sems.at[i, p]
+        )
+
+    def copies(p):
+        r = p % places
+        part = 0 if r < count else 1 if r < 2 * count else 2
+        return [copy(i, p, part, r) for i in range(2)]
+
+    def run(low, high, limit, put, ready=0):
+        def step(turn, part, r, _):
+            p = turn * places + r
+            for i in range(2):
+                @pl.when(p >= ready)
+                def _(i=i):
+                    copy(i, p, part, r).wait()
+
+                value = jnp.dot(h_ref[...], place(i, part, r)[...], preferred_element_type=F32)
+                put(chunk_at(lax.rem(2 * p + i, per_side), chunk), value)
+            return 0
+
+        for turn in range(low // places, -(-high // places)):
+            for part, (start, end) in enumerate(((0, count), (count, 2 * count), (2 * count, places))):
+                start = max(start, low - turn * places)
+                end = min(end, high - turn * places)
+                if start < end:
+                    lax.fori_loop(start, end, functools.partial(step, turn, part), 0)
+                for r in range(start, end):
+                    if (turn + 1) * places + r < limit:
+                        for item in copies((turn + 1) * places + r):
+                            item.start()
+
+    return copies, run, places
+
+
+def pairs_ahead(places, leaving):
+    return max(0, min(2, places - leaving))
+
+
 def second_half_kernel(
     per_plane, x_ref, ox_ref, gate_ref, up_ref, g_hbm, u_hbm, d_hbm, g_in, u_in, spare_in,
-    staying_ref, leaving_ref, g_ref, u_ref, spare_ref, h_scr, gu_sems, sems,
+    leaving_ref, h_scr, weight_ref, g_ref, u_ref, spare_ref, gu_sems, sems,
 ):
     del g_in, u_in, spare_in
     rows, units = h_scr.shape
-    width = staying_ref.shape[1]
-    side = own_side()
+    width = leaving_ref.shape[1]
     chunk = chunk_of(units)
     chunks = units // chunk
-    per_side = width // chunk
-    pairs = per_side
-
     count = spare_ref.shape[0]
-    places = count + chunks
+    leaving = width // chunk // 2
+    copies, run, places = down_tools(d_hbm, g_ref, u_ref, spare_ref, h_scr, sems, width)
+    ahead = pairs_ahead(places, leaving)
 
     def gu_copy(i, c):
         return other_copy(
             (g_hbm, u_hbm)[i], (g_ref, u_ref)[i], spare_ref, i, c, chunk, gu_sems.at[i, c]
         )
 
-    def down_place(i, part, r):
-        if part == 1:
-            return spare_ref.at[r - count, i, pl.ds(0, units)]
-        start = r + chunks - count if part == 0 else r - 2 * count
-        return (g_ref, u_ref)[i].at[pl.ds(0, units), chunk_at(start, chunk)]
-
-    def part_of(r):
-        return 0 if r < count else 1 if r < 2 * count else 2
-
-    def down_copy(i, p, part, r):
-        n = 2 * p + i
-        column = jnp.where(n < per_side, 1 - side, side) * width + lax.rem(n, per_side) * chunk
-        return pltpu.make_async_copy(
-            d_hbm.at[:, pl.ds(pl.multiple_of(column, LANES), chunk)], down_place(i, part, r),
-            sems.at[i, p],
-        )
-
     def start_down(p):
-        for i in range(2):
-            down_copy(i, p, part_of(p % places), p % places).start()
+        for item in copies(p):
+            item.start()
 
     def in_order(values):
         quarter = rows // 4
@@ -430,7 +467,7 @@
     later = [(i, c) for c in range(count + 1, chunks) for i in range(2)]
     for i, c in later:
         gu_copy(i, c).start()
-    for p in range(min(count, pairs)):
+    for p in range(min(count, leaving + ahead)):
         start_down(p)
 
     own = x_ref[:, width:].astype(F32)
@@ -460,7 +497,7 @@
         gate = gate * scale
         h_scr[:, at] = (gate / (1.0 + jnp.exp(-gate)) * (up * scale)).astype(BF16)
         for late in range(chunks):
-            if count + late < pairs:
+            if count + late < leaving + ahead:
                 @pl.when(c == late)
                 def _(late=late):
                     start_down(count + late)
@@ -482,34 +519,14 @@
     lax.fori_loop(0, count, spare_step, 0)
     lax.fori_loop(count, chunks, held_step, 0)
 
-    def down_step(turn, part, r, _):
-        p = turn * places + r
-        for i in range(2):
-            n = 2 * p + i
-            down_copy(i, p, part, r).wait()
-            value = jnp.dot(
-                h_scr[...], down_place(i, part, r)[...], preferred_element_type=F32
-            ) * weight
-            to = chunk_at(lax.rem(n, per_side), chunk)
-
-            @pl.when(n < per_side)
-            def _(value=value, to=to):
-                leaving_ref[:, to] = in_order(value).astype(BF16)
-
-            @pl.when(n >= per_side)
-            def _(value=value, to=to):
-                staying_ref[:, to] = value
-
-        return 0
-
-    for turn in range(-(-pairs // places)):
-        for part, (low, high) in enumerate(((0, count), (count, 2 * count), (2 * count, places))):
-            high = min(high, pairs - turn * places)
-            if low < high:
-                lax.fori_loop(low, high, functools.partial(down_step, turn, part), 0)
-            for r in range(low, high):
-                if (turn + 1) * places + r < pairs:
-                    start_down((turn + 1) * places + r)
+    def leave(to, value):
+        leaving_ref[:, to] = in_order(value * weight).astype(BF16)
+
+    run(0, leaving, leaving + ahead, leave)
+    weight_ref[...] = jnp.broadcast_to(weight, weight_ref.shape)
+    for p in range(leaving, leaving + ahead):
+        for item in copies(p):
+            item.wait()
 
 
 def second_half(per_plane, mine, other, sums, held, gate_weight, up_weight, down_weight):
@@ -518,16 +535,15 @@
     chunk = chunk_of(units)
     return pl.pallas_call(
         functools.partial(second_half_kernel, per_plane),
-        out_shape=(vmem_array((rows, width), F32), vmem_array((rows, width), BF16))
-        + tuple(pltpu.VMEM(h.shape, BF16) for h in held),
+        out_shape=(vmem_array((rows, width), BF16), pltpu.VMEM((rows, units), BF16))
+        + (pltpu.VMEM((rows, LANES), F32),) + tuple(pltpu.VMEM(h.shape, BF16) for h in held),
         in_specs=[VMEM_SPEC] * 4 + [HBM_SPEC] * 3 + [VMEM_SPEC] * 3,
-        out_specs=(VMEM_SPEC,) * 5,
+        out_specs=(VMEM_SPEC,) * 6,
         scratch_shapes=[
-            pltpu.VMEM((rows, units), BF16),
             pltpu.SemaphoreType.DMA((2, units // chunk)),
             pltpu.SemaphoreType.DMA((2, width // chunk)),
         ],
-        input_output_aliases={7: 2, 8: 3, 9: 4},
+        input_output_aliases={7: 3, 8: 4, 9: 5},
         compiler_params=pltpu.CompilerParams(
             vmem_limit_bytes=HELD_BELOW if rows < 256 else 40 * MIB
         ),
@@ -538,7 +554,48 @@
     )(
         *in_vmem_always([mine, other]), *in_vmem(*sums),
         *in_hbm(gate_weight, up_weight, down_weight), *in_vmem_always(held),
-    )[:2]
+    )
+
+
+def staying_kernel(
+    h_ref, weight_ref, d_hbm, g_in, u_in, spare_in, out_ref, g_ref, u_ref, spare_ref, sems
+):
+    del g_in, u_in, spare_in
+    width = out_ref.shape[1]
+    pairs = sems.shape[1]
+    leaving = pairs // 2
+    copies, run, places = down_tools(d_hbm, g_ref, u_ref, spare_ref, h_ref, sems, width)
+    ahead = pairs_ahead(places, leaving)
+    for p in range(leaving + ahead, min(leaving + places, pairs)):
+        for item in copies(p):
+            item.start()
+    weight = weight_ref[:, 0:1]
+
+    def stay(to, value):
+        out_ref[:, to] = value * weight
+
+    run(leaving, pairs, pairs, stay, leaving + ahead)
+
+
+def staying_half(hidden, weight, held, down_weight):
+    rows, units = hidden.shape
+    width = down_weight.shape[1] // 2
+    return pl.pallas_call(
+        staying_kernel,
+        out_shape=(vmem_array((rows, width), F32),)
+        + tuple(pltpu.VMEM(h.shape, BF16) for h in held),
+        in_specs=[VMEM_SPEC] * 2 + [HBM_SPEC] + [VMEM_SPEC] * 3,
+        out_specs=(VMEM_SPEC,) * 4,
+        scratch_shapes=[pltpu.SemaphoreType.DMA((2, width // chunk_of(units)))],
+        input_output_aliases={3: 1, 4: 2, 5: 3},
+        compiler_params=pltpu.CompilerParams(
+            vmem_limit_bytes=HELD_BELOW if rows < 256 else 40 * MIB
+        ),
+        cost_estimate=pl.CostEstimate(
+            flops=2 * rows * width * units, bytes_accessed=width * units, transcendentals=0
+        ),
+        name="staying_half",
+    )(*in_vmem_always([hidden, weight]), *in_hbm(down_weight), *in_vmem_always(held))[0]
 
 
 def split_kernel(own_ref, got_ref, keep_ref, send_ref):
@@ -656,10 +713,11 @@
     mine = payload
     other = to_core(mine)
     gate, up, *held = first_half(mine, held, gate_weight, up_weight)
-    staying, leaving = second_half(
+    leaving, hidden, weight, *held = second_half(
         per_plane, mine, other, (gate, up), held, gate_weight, up_weight, down_weight
     )
-    keep, got = staying, to_core(leaving)
+    got = to_core(leaving)
+    keep = staying_half(hidden, weight, held, down_weight)
     for stage in range(stages - 1, 1, -1):
         keep, send = split_rows(keep, got)
         got = exchange(send, stage)

time: 58.6 us -> 58.3 us (level)
  waiting for transfers between devices: 16.3 us -> 14.6 us
  Pallas kernels: 30.6 us -> 31.9 us
    pallas_call x0 -> x1, Pallas kernels: none -> 2.91 us  [staying_half(): pl.pallas_call(staying_kernel, out_shape=(vmem_array((rows, width), F32),...]
    pallas_call x1, Pallas kernels: 11.1 us -> 9.43 us  [second_half(): pl.pallas_call(functools.partial(second_half_kernel, per_plane), out_shap...]
    ppermute x2, waiting for transfers between devices: 1.63 us -> 0.01 us  [to_core(): return lax.ppermute(array, 'shard', [(0, 1), (1, 0)])]
  transfers between devices with their start and end apart: 10 -> 10, of which waited for: 7 -> 5; matrix products, arithmetic and copies ran while one was open for 0% -> 0% of each run, Pallas kernels for 26% -> 31%
where the time goes in v11:
time: 58.3 us; the launch traced here: 58.1 us
  Pallas kernels  31.9 us (55%)
  waiting for transfers between devices  14.6 us (25%)
  starting transfers between devices  11.5 us (20%)
    ppermute x8, waiting for transfers between devices, exchange(): return lax.ppermute(array, ('node', 'shard'), perm)  14.6 us
    ppermute x8, starting transfers between devices, exchange(): return lax.ppermute(array, ('node', 'shard'), perm)  10.9 us
    pallas_call x2, Pallas kernels, load_rows(): pl.pallas_call(functools.partial(load_kernel, first, rows, ahead), out_sh...  10.1 us
    pallas_call x1, Pallas kernels, second_half(): pl.pallas_call(functools.partial(second_half_kernel, per_plane), out_shap...  9.43 us
    pallas_call x1, Pallas kernels, first_half(): pl.pallas_call(first_half_kernel, out_shape=(acc, acc) + tuple((pltpu.VME...  5 us
    pallas_call x1, Pallas kernels, attend(): pl.pallas_call(functools.partial(attend_kernel, ahead), out_shape=(pltpu....  3.41 us
    pallas_call x1, Pallas kernels, staying_half(): pl.pallas_call(staying_kernel, out_shape=(vmem_array((rows, width), F32),...  2.91 us
  transfers between devices with their start and end apart: 10, of which 5 were waited for; matrix products, arithmetic and copies ran while one was open for 0% of the time, Pallas kernels for 31%

profile of v11, /device:TPU:0, one launch (start us, length us, event | category | flops | bytes accessed | tf_op | source)
XLA Modules:
  0.0 58.1 jit_solution(16888062361094719956)
XLA Ops:
  0.0 3.4 %attend.1 = (f32[12,3072]{1,0:T(8,128)S(1)}, bf16[24,1664]{1,0:T(8,128)(2,1)S(1)}, bf16[3072,2048]{1,0:T(8,128)(2,1)S(1)}, bf16[3072,2048]{1,0:T(8,128)(2,1)S(1)}, bf16[2,2,3072,512]{3,2,1,0:T(8,128)(2,1)S(1)}) custom-call(s32[12]{0:T(128)} %len_hbm.1, s32[2,12]{1,0:T(2,128)} %bitcast.5, bf16[12,3072]{1,0:T(8,128)(2,1)} %q_hbm.1, ...), custom_call_target="tpu_custom_call" | custom-call | flops 100000000 | bytes 8000000 | tf_op jit(solution)/shard_map/attend/pallas_call | solution.py:291
  3.4 5.1 %collective-permute-start.2 = (bf16[24,1664]{1,0:T(8,128)(2,1)S(1)}, bf16[24,1664]{1,0:T(8,128)(2,1)S(1)}, u32[]{:S(2)}, u32[]{:S(2)}) collective-permute-start(bf16[24,1664]{1,0:T(8,128)(2,1)S(1)} %get-tuple-element.37.dep_ref.refs_0_), channel_id=1, source_target_pairs={{0,12},{1,11},{2,14},{3,9},{4,8},{5,15},{6,10},{7,13},{8,4},{9,3},... | collective-permute-start | bytes 239624 | tf_op jit(solution)/shard_map/ppermute | solution.py:688
  8.5 0.0 collective-permute-start.1
  8.5 0.6 %collective-permute-start = (bf16[24,1664]{1,0:T(8,128)(2,1)S(1)}, bf16[24,1664]{1,0:T(8,128)(2,1)S(1)}, u32[]{:S(2)}, u32[]{:S(2)}) collective-permute-start(bf16[24,1664]{1,0:T(8,128)(2,1)S(1)} %get-tuple-element.37.dep_ref.refs_0_), channel_id=1, source_target_pairs={{0,8},{1,9},{2,10},{3,11},{4,12},{5,13},{6,14},{7,15},{8,0},{9,1},... | collective-permute-start | bytes 239624 | tf_op jit(solution)/shard_map/ppermute | solution.py:688
  9.2 4.7 %load_weights.2 = (bf16[3072,2048]{1,0:T(8,128)(2,1)S(1)}, bf16[3072,2048]{1,0:T(8,128)(2,1)S(1)}, bf16[2,2,3072,512]{3,2,1,0:T(8,128)(2,1)S(1)}, f32[8,128]{1,0:T(8,128)S(1)}) custom-call(bf16[24,1664]{1,0:T(8,128)(2,1)S(1)} %get-tuple-element.37.dep_ref.refs_0_, ...), custom_call_target="tpu_custom_call", output_to_operand_aliasing={{0}: (3, {}), {1}: (4, {}), {2}: (5, {})} | custom-call | bytes 12582912 | tf_op jit(solution)/shard_map/load_weights/pallas_call | solution.py:115
  13.9 0.0 collective-permute-done.2.refs_3_
  13.9 0.0 collective-permute-done.1.refs_2_
  13.9 2.1 %collective-permute-done.refs_1_ = bf16[24,1664]{1,0:T(8,128)(2,1)S(1)} collective-permute-done((bf16[24,1664]{1,0:T(8,128)(2,1)S(1)}, bf16[24,1664]{1,0:T(8,128)(2,1)S(1)}, u32[]{:S(2)}, u32[]{:S(2)}) %collective-permute-start) | collective-permute-done | bytes 79904 | tf_op jit(solution)/shard_map/ppermute | solution.py:688
  16.0 0.1 unfold.1.dep_ref.a_ref
  16.1 0.1 collective-permute-start.3
  16.2 5.4 %load_weights.3 = (bf16[3072,2048]{1,0:T(8,128)(2,1)S(1)}, bf16[3072,2048]{1,0:T(8,128)(2,1)S(1)}, bf16[2,2,3072,512]{3,2,1,0:T(8,128)(2,1)S(1)}, f32[8,128]{1,0:T(8,128)S(1)}) custom-call(bf16[48,3200]{1,0:T(8,128)(2,1)S(1)} %unfold.1.dep_ref.a_ref, bf16[6144,2048]{1,0:T(8,128)(2,1)} %g_hbm.9, ...), custom_call_target="tpu_custom_call", output_to_operand_aliasing={{0}: (3, {}), {1}: (4, {}), {2}: (5, {})} | custom-call | bytes 8388608 | tf_op jit(solution)/shard_map/load_weights/pallas_call | solution.py:115
  21.6 1.4 %collective-permute-done.3.b_ref = bf16[48,3200]{1,0:T(8,128)(2,1)S(1)} collective-permute-done((bf16[48,3200]{1,0:T(8,128)(2,1)S(1)}, bf16[48,3200]{1,0:T(8,128)(2,1)S(1)}, u32[]{:S(2)}, u32[]{:S(2)}) %collective-permute-start.3) | collective-permute-done | bytes 307232 | tf_op jit(solution)/shard_map/ppermute | solution.py:688
  23.1 0.1 collective-permute-start.4
  23.1 5.0 %first_half.1 = (f32[96,2048]{1,0:T(8,128)S(1)}, f32[96,2048]{1,0:T(8,128)S(1)}, bf16[3072,2048]{1,0:T(8,128)(2,1)S(1)}, bf16[3072,2048]{1,0:T(8,128)(2,1)S(1)}, bf16[2,2,3072,512]{3,2,1,0:T(8,128)(2,1)S(1)}) custom-call(bf16[96,3200]{1,0:T(8,128)(2,1)S(1)} %join.1.x_ref, ...), custom_call_target="tpu_custom_call", output_to_operand_aliasing={{2}: (3, {}), {3}: (4, {}), {4}: (5, {})} | custom-call | flops 2415919104 | bytes 12582912 | tf_op jit(solution)/shard_map/first_half/pallas_call | solution.py:367
  28.2 0.0 collective-permute-done.4.ox_ref
  28.2 9.4 %second_half.1 = (bf16[96,3072]{1,0:T(8,128)(2,1)S(1)}, bf16[96,2048]{1,0:T(8,128)(2,1)S(1)}, f32[96,128]{1,0:T(8,128)S(1)}, bf16[3072,2048]{1,0:T(8,128)(2,1)S(...) custom-call(bf16[96,3200]{1,0:T(8,128)(2,1)S(1)} %join.1.x_ref, ...), custom_call_target="tpu_custom_call", output_to_operand_aliasing={{3}: (7, {}), {4}: (8, {}), {5}: (9, {})} | custom-call | flops 3623878656 | bytes 25165824 | tf_op jit(solution)/shard_map/second_half/pallas_call | solution.py:536
  37.6 0.5 collective-permute-start.5
  38.1 2.9 %staying_half.1 = (f32[96,3072]{1,0:T(8,128)S(1)}, bf16[3072,2048]{1,0:T(8,128)(2,1)S(1)}, bf16[3072,2048]{1,0:T(8,128)(2,1)S(1)}, bf16[2,2,3072,512]{3,2,1,0:T(8,128)(2,1)S(1)}) custom-call(bf16[96,2048]{1,0:T(8,128)(2,1)S(1)} %get-tuple-element.54.h_ref, ...), custom_call_target="tpu_custom_call", output_to_operand_aliasing={{1}: (3, {}), {2}: (4, {}), {3}: (5, {})} | custom-call | flops 1207959552 | bytes 6291456 | tf_op jit(solution)/shard_map/staying_half/pallas_call | solution.py:583
  41.1 0.0 collective-permute-done.5.got_ref
  41.1 0.1 split_rows.1
  41.2 0.6 %collective-permute-start.6 = (bf16[48,3072]{1,0:T(8,128)(2,1)S(1)}, bf16[48,3072]{1,0:T(8,128)(2,1)S(1)}, u32[]{:S(2)}, u32[]{:S(2)}) collective-permute-start(bf16[48,3072]{1,0:T(8,128)(2,1)S(1)} %get-tuple-element.62), channel_id=1, source_target_pairs={{0,2},{1,5},{2,0},{3,7},{4,6},{5,1},{6,4},{7,3},{8,10},{9,13},{10,... | collective-permute-start | bytes 884744 | tf_op jit(solution)/shard_map/ppermute | solution.py:688
  41.8 6.2 %collective-permute-done.6.got_ref = bf16[48,3072]{1,0:T(8,128)(2,1)S(1)} collective-permute-done((bf16[48,3072]{1,0:T(8,128)(2,1)S(1)}, bf16[48,3072]{1,0:T(8,128)(2,1)S(1)}, u32[]{:S(2)}, u32[]{:S(2)}) %collective-permute-start.6) | collective-permute-done | bytes 294944 | tf_op jit(solution)/shard_map/ppermute | solution.py:688
  48.0 0.1 split_last.1
  48.1 1.0 %collective-permute-start.7 = (bf16[24,1536]{1,0:T(8,128)(2,1)S(1)}, bf16[24,1536]{1,0:T(8,128)(2,1)S(1)}, u32[]{:S(2)}, u32[]{:S(2)}) collective-permute-start(bf16[24,1536]{1,0:T(8,128)(2,1)S(1)} %get-tuple-element.64), channel_id=1, source_target_pairs={{0,8},{1,9},{2,10},{3,11},{4,12},{5,13},{6,14},{7,15},{8,0},{9,1},... | collective-permute-start | bytes 221192 | tf_op jit(solution)/shard_map/ppermute | solution.py:688
  49.1 2.2 %collective-permute-start.8 = (bf16[24,1536]{1,0:T(8,128)(2,1)S(1)}, bf16[24,1536]{1,0:T(8,128)(2,1)S(1)}, u32[]{:S(2)}, u32[]{:S(2)}) collective-permute-start(bf16[24,1536]{1,0:T(8,128)(2,1)S(1)} %get-tuple-element.65), channel_id=1, source_target_pairs={{0,4},{1,3},{2,6},{3,1},{4,0},{5,7},{6,2},{7,5},{8,12},{9,11},{10,... | collective-permute-start | bytes 221192 | tf_op jit(solution)/shard_map/ppermute | solution.py:688
  51.3 1.3 %collective-permute-start.9 = (bf16[24,1536]{1,0:T(8,128)(2,1)S(1)}, bf16[24,1536]{1,0:T(8,128)(2,1)S(1)}, u32[]{:S(2)}, u32[]{:S(2)}) collective-permute-start(bf16[24,1536]{1,0:T(8,128)(2,1)S(1)} %get-tuple-element.66), channel_id=1, source_target_pairs={{0,12},{1,11},{2,14},{3,9},{4,8},{5,15},{6,10},{7,13},{8,4},{9,3},... | collective-permute-start | bytes 221192 | tf_op jit(solution)/shard_map/ppermute | solution.py:688
  52.5 2.6 %collective-permute-done.7.refs_0_ = bf16[24,1536]{1,0:T(8,128)(2,1)S(1)} collective-permute-done((bf16[24,1536]{1,0:T(8,128)(2,1)S(1)}, bf16[24,1536]{1,0:T(8,128)(2,1)S(1)}, u32[]{:S(2)}, u32[]{:S(2)}) %collective-permute-start.7) | collective-permute-done | bytes 73760 | tf_op jit(solution)/shard_map/ppermute | solution.py:688
  55.1 0.0 collective-permute-done.8.refs_1_
  55.1 2.3 %collective-permute-done.9.refs_2_ = bf16[24,1536]{1,0:T(8,128)(2,1)S(1)} collective-permute-done((bf16[24,1536]{1,0:T(8,128)(2,1)S(1)}, bf16[24,1536]{1,0:T(8,128)(2,1)S(1)}, u32[]{:S(2)}, u32[]{:S(2)}) %collective-permute-start.9) | collective-permute-done | bytes 73760 | tf_op jit(solution)/shard_map/ppermute | solution.py:688
  57.4 0.7 %finish.1 = bf16[12,3072]{1,0:T(8,128)(2,1)} custom-call(f32[12,3072]{1,0:T(8,128)S(1)} %get-tuple-element.36.carried_ref, f32[12,3072]{1,0:T(8,128)S(1)} %get-tuple-element.63.own_ref, bf16[24,1536]{1,0:T(8,128)(2,1)S(1)} %collective-permute-done.7.refs_0_, bf16[24,1536]{1,0:T(8,128)(2,1)S(1)} %collective-permute-done.8.refs_1_, ...), custom_call_target="tpu_custom_call" | custom-call | tf_op jit(solution)/shard_map/finish/pallas_call | solution.py:664
  (1 shorter events, 0.0 us)
Async XLA Ops:
  3.4 10.5 %collective-permute-start.2 = (bf16[24,1664]{1,0:T(8,128)(2,1)S(1)}, bf16[24,1664]{1,0:T(8,128)(2,1)S(1)}, u32[]{:S(2)}, u32[]{:S(2)}) collective-permute-start(bf16[24,1664]{1,0:T(8,128)(2,1)S(1)} %get-tuple-element.37.dep_ref.refs_0_), channel_id=1, source_target_pairs={{0,12},{1,11},{2,14},{3,9},{4,8},{5,15},{6,10},{7,13},{8,4},{9,3},... | collective-permute-start | bytes 239624 | tf_op jit(solution)/shard_map/ppermute | solution.py:688
  8.5 5.4 %collective-permute-start.1 = (bf16[24,1664]{1,0:T(8,128)(2,1)S(1)}, bf16[24,1664]{1,0:T(8,128)(2,1)S(1)}, u32[]{:S(2)}, u32[]{:S(2)}) collective-permute-start(bf16[24,1664]{1,0:T(8,128)(2,1)S(1)} %get-tuple-element.37.dep_ref.refs_0_), channel_id=1, source_target_pairs={{0,4},{1,3},{2,6},{3,1},{4,0},{5,7},{6,2},{7,5},{8,12},{9,11},{10,... | collective-permute-start | bytes 239624 | tf_op jit(solution)/shard_map/ppermute | solution.py:688
  8.5 7.5 %collective-permute-start = (bf16[24,1664]{1,0:T(8,128)(2,1)S(1)}, bf16[24,1664]{1,0:T(8,128)(2,1)S(1)}, u32[]{:S(2)}, u32[]{:S(2)}) collective-permute-start(bf16[24,1664]{1,0:T(8,128)(2,1)S(1)} %get-tuple-element.37.dep_ref.refs_0_), channel_id=1, source_target_pairs={{0,8},{1,9},{2,10},{3,11},{4,12},{5,13},{6,14},{7,15},{8,0},{9,1},... | collective-permute-start | bytes 239624 | tf_op jit(solution)/shard_map/ppermute | solution.py:688
  16.1 6.9 %collective-permute-start.3 = (bf16[48,3200]{1,0:T(8,128)(2,1)S(1)}, bf16[48,3200]{1,0:T(8,128)(2,1)S(1)}, u32[]{:S(2)}, u32[]{:S(2)}) collective-permute-start(bf16[48,3200]{1,0:T(8,128)(2,1)S(1)} %unfold.1.dep_ref.a_ref), channel_id=1, source_target_pairs={{0,2},{1,5},{2,0},{3,7},{4,6},{5,1},{6,4},{7,3},{8,10},{9,13},{10,... | collective-permute-start | bytes 921608 | tf_op jit(solution)/shard_map/ppermute | solution.py:688
  23.1 5.1 %collective-permute-start.4 = (bf16[96,3200]{1,0:T(8,128)(2,1)S(1)}, bf16[96,3200]{1,0:T(8,128)(2,1)S(1)}, u32[]{:S(2)}, u32[]{:S(2)}) collective-permute-start(bf16[96,3200]{1,0:T(8,128)(2,1)S(1)} %join.1.x_ref), channel_id=1, source_target_pairs={{0,1},{1,0},{2,3},{3,2},{4,5},{5,4},{6,7},{7,6},{8,9},{9,8},{10,11... | collective-permute-start | bytes 1843208 | tf_op jit(solution)/shard_map/ppermute | solution.py:691
  37.6 3.5 %collective-permute-start.5 = (bf16[96,3072]{1,0:T(8,128)(2,1)S(1)}, bf16[96,3072]{1,0:T(8,128)(2,1)S(1)}, u32[]{:S(2)}, u32[]{:S(2)}) collective-permute-start(bf16[96,3072]{1,0:T(8,128)(2,1)S(1)} %get-tuple-element.60), channel_id=1, source_target_pairs={{0,1},{1,0},{2,3},{3,2},{4,5},{5,4},{6,7},{7,6},{8,9},{9,8},{10,11... | collective-permute-start | bytes 1769480 | tf_op jit(solution)/shard_map/ppermute | solution.py:691
  41.2 6.8 %collective-permute-start.6 = (bf16[48,3072]{1,0:T(8,128)(2,1)S(1)}, bf16[48,3072]{1,0:T(8,128)(2,1)S(1)}, u32[]{:S(2)}, u32[]{:S(2)}) collective-permute-start(bf16[48,3072]{1,0:T(8,128)(2,1)S(1)} %get-tuple-element.62), channel_id=1, source_target_pairs={{0,2},{1,5},{2,0},{3,7},{4,6},{5,1},{6,4},{7,3},{8,10},{9,13},{10,... | collective-permute-start | bytes 884744 | tf_op jit(solution)/shard_map/ppermute | solution.py:688
  48.1 7.0 %collective-permute-start.7 = (bf16[24,1536]{1,0:T(8,128)(2,1)S(1)}, bf16[24,1536]{1,0:T(8,128)(2,1)S(1)}, u32[]{:S(2)}, u32[]{:S(2)}) collective-permute-start(bf16[24,1536]{1,0:T(8,128)(2,1)S(1)} %get-tuple-element.64), channel_id=1, source_target_pairs={{0,8},{1,9},{2,10},{3,11},{4,12},{5,13},{6,14},{7,15},{8,0},{9,1},... | collective-permute-start | bytes 221192 | tf_op jit(solution)/shard_map/ppermute | solution.py:688
  49.1 6.0 %collective-permute-start.8 = (bf16[24,1536]{1,0:T(8,128)(2,1)S(1)}, bf16[24,1536]{1,0:T(8,128)(2,1)S(1)}, u32[]{:S(2)}, u32[]{:S(2)}) collective-permute-start(bf16[24,1536]{1,0:T(8,128)(2,1)S(1)} %get-tuple-element.65), channel_id=1, source_target_pairs={{0,4},{1,3},{2,6},{3,1},{4,0},{5,7},{6,2},{7,5},{8,12},{9,11},{10,... | collective-permute-start | bytes 221192 | tf_op jit(solution)/shard_map/ppermute | solution.py:688
  51.3 6.2 %collective-permute-start.9 = (bf16[24,1536]{1,0:T(8,128)(2,1)S(1)}, bf16[24,1536]{1,0:T(8,128)(2,1)S(1)}, u32[]{:S(2)}, u32[]{:S(2)}) collective-permute-start(bf16[24,1536]{1,0:T(8,128)(2,1)S(1)} %get-tuple-element.66), channel_id=1, source_target_pairs={{0,12},{1,11},{2,14},{3,9},{4,8},{5,15},{6,10},{7,13},{8,4},{9,3},... | collective-permute-start | bytes 221192 | tf_op jit(solution)/shard_map/ppermute | solution.py:688

commit v12 on v11

--- a/solution.py
+++ b/solution.py
@@ -128,7 +128,7 @@
 def unfold_kernel(tok, *refs):
     *arrays, _, out_ref, scr = refs
     fold_width = arrays[0].shape[1] - LANES
-    for i, array in enumerate(arrays):
+    for i, array in enumerate([arrays[0], *reversed(arrays[1:])]):
         rows = array[...].astype(F32)
         to = slice(i * tok, (i + 1) * tok)
         for f in range(FOLD):
@@ -323,6 +323,11 @@
     )
 
 
+def ready_parts(count, chunks):
+    parts = [(i, c) for c in range(1, chunks) for i in range(2)]
+    return parts[:2 * count + 1]
+
+
 def first_half_kernel(
     x_ref, g_hbm, u_hbm, g_in, u_in, spare_in, gate_ref, up_ref, g_ref, u_ref, spare_ref, sems
 ):
@@ -331,7 +336,7 @@
     chunk = chunk_of(units)
     chunks = units // chunk
     count = spare_ref.shape[0]
-    ready = [(i, c) for c in range(1, min(count + 1, chunks)) for i in range(2)]
+    ready = ready_parts(count, chunks)
 
     def copy(i, c):
         return other_copy(
@@ -464,7 +469,8 @@
             [values[q * quarter:(q + 1) * quarter, :] for q in (0, 2, 1, 3)], axis=0
         )
 
-    later = [(i, c) for c in range(count + 1, chunks) for i in range(2)]
+    there = ready_parts(count, chunks)
+    later = [(i, c) for c in range(1, chunks) for i in range(2) if (i, c) not in there]
     for i, c in later:
         gu_copy(i, c).start()
     for p in range(min(count, leaving + ahead)):
@@ -702,7 +708,7 @@
     *held, token = load_rows(
         heights[0], heights[1], False, payload, gate_weight, up_weight, held
     )
-    payload = unfold(tok, [payload, *got], token)
+    payload = unfold(tok, [payload, *reversed(got)], token)
     for stage in range(2, stages):
         got = exchange(payload, stage)
         if stage == 2:

time: 58.3 us -> 57.5 us (0.986)
  waiting for transfers between devices: 14.6 us -> 11.5 us
  starting transfers between devices: 11.5 us -> 13.8 us
    ppermute x8, waiting for transfers between devices: 14.6 us -> 11.5 us  [exchange(): return lax.ppermute(array, ('node', 'shard'), perm)]
    ppermute x8, starting transfers between devices: 10.9 us -> 13.2 us  [exchange(): return lax.ppermute(array, ('node', 'shard'), perm)]
    pallas_call x1, Pallas kernels: 9.43 us -> 8.53 us  [second_half(): pl.pallas_call(functools.partial(second_half_kernel, per_plane), out_shap...]
    pallas_call x1, Pallas kernels: 5 us -> 5.89 us  [first_half(): pl.pallas_call(first_half_kernel, out_shape=(acc, acc) + tuple((pltpu.VME...]
  transfers between devices with their start and end apart: 10 -> 10, of which waited for: 5 -> 5; matrix products, arithmetic and copies ran while one was open for 0% -> 0% of each run, Pallas kernels for 31% -> 33%
where the time goes in v12:
time: 57.5 us; the launch traced here: 57.3 us
  Pallas kernels  31.8 us (55%)
  starting transfers between devices  13.8 us (24%)
  waiting for transfers between devices  11.5 us (20%)
    ppermute x8, starting transfers between devices, exchange(): return lax.ppermute(array, ('node', 'shard'), perm)  13.2 us
    ppermute x8, waiting for transfers between devices, exchange(): return lax.ppermute(array, ('node', 'shard'), perm)  11.5 us
    pallas_call x2, Pallas kernels, load_rows(): pl.pallas_call(functools.partial(load_kernel, first, rows, ahead), out_sh...  10.1 us
    pallas_call x1, Pallas kernels, second_half(): pl.pallas_call(functools.partial(second_half_kernel, per_plane), out_shap...  8.53 us
    pallas_call x1, Pallas kernels, first_half(): pl.pallas_call(first_half_kernel, out_shape=(acc, acc) + tuple((pltpu.VME...  5.89 us
    pallas_call x1, Pallas kernels, attend(): pl.pallas_call(functools.partial(attend_kernel, ahead), out_shape=(pltpu....  3.41 us
    pallas_call x1, Pallas kernels, staying_half(): pl.pallas_call(staying_kernel, out_shape=(vmem_array((rows, width), F32),...  2.91 us
  transfers between devices with their start and end apart: 10, of which 5 were waited for; matrix products, arithmetic and copies ran while one was open for 0% of the time, Pallas kernels for 33%

profile of v12, /device:TPU:0, one launch (start us, length us, event | category | flops | bytes accessed | tf_op | source)
XLA Modules:
  0.0 57.3 jit_solution(15378721377990898065)
XLA Ops:
  0.0 3.4 %attend.1 = (f32[12,3072]{1,0:T(8,128)S(1)}, bf16[24,1664]{1,0:T(8,128)(2,1)S(1)}, bf16[3072,2048]{1,0:T(8,128)(2,1)S(1)}, bf16[3072,2048]{1,0:T(8,128)(2,1)S(1)}, bf16[2,2,3072,512]{3,2,1,0:T(8,128)(2,1)S(1)}) custom-call(s32[12]{0:T(128)} %len_hbm.1, s32[2,12]{1,0:T(2,128)} %bitcast.5, bf16[12,3072]{1,0:T(8,128)(2,1)} %q_hbm.1, ...), custom_call_target="tpu_custom_call" | custom-call | flops 100000000 | bytes 8000000 | tf_op jit(solution)/shard_map/attend/pallas_call | solution.py:291
  3.4 4.1 %collective-permute-start.2 = (bf16[24,1664]{1,0:T(8,128)(2,1)S(1)}, bf16[24,1664]{1,0:T(8,128)(2,1)S(1)}, u32[]{:S(2)}, u32[]{:S(2)}) collective-permute-start(bf16[24,1664]{1,0:T(8,128)(2,1)S(1)} %get-tuple-element.37.dep_ref.refs_0_), channel_id=1, source_target_pairs={{0,8},{1,9},{2,10},{3,11},{4,12},{5,13},{6,14},{7,15},{8,0},{9,1},... | collective-permute-start | bytes 239624 | tf_op jit(solution)/shard_map/ppermute | solution.py:694
  7.5 1.6 %collective-permute-start.1 = (bf16[24,1664]{1,0:T(8,128)(2,1)S(1)}, bf16[24,1664]{1,0:T(8,128)(2,1)S(1)}, u32[]{:S(2)}, u32[]{:S(2)}) collective-permute-start(bf16[24,1664]{1,0:T(8,128)(2,1)S(1)} %get-tuple-element.37.dep_ref.refs_0_), channel_id=1, source_target_pairs={{0,4},{1,3},{2,6},{3,1},{4,0},{5,7},{6,2},{7,5},{8,12},{9,11},{10,... | collective-permute-start | bytes 239624 | tf_op jit(solution)/shard_map/ppermute | solution.py:694
  9.1 0.0 collective-permute-start
  9.1 4.7 %load_weights.2 = (bf16[3072,2048]{1,0:T(8,128)(2,1)S(1)}, bf16[3072,2048]{1,0:T(8,128)(2,1)S(1)}, bf16[2,2,3072,512]{3,2,1,0:T(8,128)(2,1)S(1)}, f32[8,128]{1,0:T(8,128)S(1)}) custom-call(bf16[24,1664]{1,0:T(8,128)(2,1)S(1)} %get-tuple-element.37.dep_ref.refs_0_, ...), custom_call_target="tpu_custom_call", output_to_operand_aliasing={{0}: (3, {}), {1}: (4, {}), {2}: (5, {})} | custom-call | bytes 12582912 | tf_op jit(solution)/shard_map/load_weights/pallas_call | solution.py:115
  13.8 0.0 collective-permute-done.2.refs_3_
  13.8 0.0 collective-permute-done.1.refs_2_
  13.8 1.5 %collective-permute-done.refs_1_ = bf16[24,1664]{1,0:T(8,128)(2,1)S(1)} collective-permute-done((bf16[24,1664]{1,0:T(8,128)(2,1)S(1)}, bf16[24,1664]{1,0:T(8,128)(2,1)S(1)}, u32[]{:S(2)}, u32[]{:S(2)}) %collective-permute-start) | collective-permute-done | bytes 79904 | tf_op jit(solution)/shard_map/ppermute | solution.py:694
  15.3 0.1 unfold.1.dep_ref.a_ref
  15.4 1.6 %collective-permute-start.3 = (bf16[48,3200]{1,0:T(8,128)(2,1)S(1)}, bf16[48,3200]{1,0:T(8,128)(2,1)S(1)}, u32[]{:S(2)}, u32[]{:S(2)}) collective-permute-start(bf16[48,3200]{1,0:T(8,128)(2,1)S(1)} %unfold.1.dep_ref.a_ref), channel_id=1, source_target_pairs={{0,2},{1,5},{2,0},{3,7},{4,6},{5,1},{6,4},{7,3},{8,10},{9,13},{10,... | collective-permute-start | bytes 921608 | tf_op jit(solution)/shard_map/ppermute | solution.py:694
  16.9 5.4 %load_weights.3 = (bf16[3072,2048]{1,0:T(8,128)(2,1)S(1)}, bf16[3072,2048]{1,0:T(8,128)(2,1)S(1)}, bf16[2,2,3072,512]{3,2,1,0:T(8,128)(2,1)S(1)}, f32[8,128]{1,0:T(8,128)S(1)}) custom-call(bf16[48,3200]{1,0:T(8,128)(2,1)S(1)} %unfold.1.dep_ref.a_ref, bf16[6144,2048]{1,0:T(8,128)(2,1)} %g_hbm.9, ...), custom_call_target="tpu_custom_call", output_to_operand_aliasing={{0}: (3, {}), {1}: (4, {}), {2}: (5, {})} | custom-call | bytes 8388608 | tf_op jit(solution)/shard_map/load_weights/pallas_call | solution.py:115
  22.3 0.0 collective-permute-done.3.b_ref
  22.4 0.1 collective-permute-start.4
  22.5 5.9 %first_half.1 = (f32[96,2048]{1,0:T(8,128)S(1)}, f32[96,2048]{1,0:T(8,128)S(1)}, bf16[3072,2048]{1,0:T(8,128)(2,1)S(1)}, bf16[3072,2048]{1,0:T(8,128)(2,1)S(1)}, bf16[2,2,3072,512]{3,2,1,0:T(8,128)(2,1)S(1)}) custom-call(bf16[96,3200]{1,0:T(8,128)(2,1)S(1)} %join.1.x_ref, ...), custom_call_target="tpu_custom_call", output_to_operand_aliasing={{2}: (3, {}), {3}: (4, {}), {4}: (5, {})} | custom-call | flops 2415919104 | bytes 12582912 | tf_op jit(solution)/shard_map/first_half/pallas_call | solution.py:372
  28.4 0.0 collective-permute-done.4.ox_ref
  28.4 8.5 %second_half.1 = (bf16[96,3072]{1,0:T(8,128)(2,1)S(1)}, bf16[96,2048]{1,0:T(8,128)(2,1)S(1)}, f32[96,128]{1,0:T(8,128)S(1)}, bf16[3072,2048]{1,0:T(8,128)(2,1)S(...) custom-call(bf16[96,3200]{1,0:T(8,128)(2,1)S(1)} %join.1.x_ref, ...), custom_call_target="tpu_custom_call", output_to_operand_aliasing={{3}: (7, {}), {4}: (8, {}), {5}: (9, {})} | custom-call | flops 3623878656 | bytes 25165824 | tf_op jit(solution)/shard_map/second_half/pallas_call | solution.py:542
  36.9 0.5 collective-permute-start.5
  37.5 2.9 %staying_half.1 = (f32[96,3072]{1,0:T(8,128)S(1)}, bf16[3072,2048]{1,0:T(8,128)(2,1)S(1)}, bf16[3072,2048]{1,0:T(8,128)(2,1)S(1)}, bf16[2,2,3072,512]{3,2,1,0:T(8,128)(2,1)S(1)}) custom-call(bf16[96,2048]{1,0:T(8,128)(2,1)S(1)} %get-tuple-element.54.h_ref, ...), custom_call_target="tpu_custom_call", output_to_operand_aliasing={{1}: (3, {}), {2}: (4, {}), {3}: (5, {})} | custom-call | flops 1207959552 | bytes 6291456 | tf_op jit(solution)/shard_map/staying_half/pallas_call | solution.py:589
  40.4 0.0 collective-permute-done.5.got_ref
  40.4 0.1 split_rows.1
  40.5 1.5 %collective-permute-start.6 = (bf16[48,3072]{1,0:T(8,128)(2,1)S(1)}, bf16[48,3072]{1,0:T(8,128)(2,1)S(1)}, u32[]{:S(2)}, u32[]{:S(2)}) collective-permute-start(bf16[48,3072]{1,0:T(8,128)(2,1)S(1)} %get-tuple-element.62), channel_id=1, source_target_pairs={{0,2},{1,5},{2,0},{3,7},{4,6},{5,1},{6,4},{7,3},{8,10},{9,13},{10,... | collective-permute-start | bytes 884744 | tf_op jit(solution)/shard_map/ppermute | solution.py:694
  42.0 5.3 %collective-permute-done.6.got_ref = bf16[48,3072]{1,0:T(8,128)(2,1)S(1)} collective-permute-done((bf16[48,3072]{1,0:T(8,128)(2,1)S(1)}, bf16[48,3072]{1,0:T(8,128)(2,1)S(1)}, u32[]{:S(2)}, u32[]{:S(2)}) %collective-permute-start.6) | collective-permute-done | bytes 294944 | tf_op jit(solution)/shard_map/ppermute | solution.py:694
  47.3 0.1 split_last.1
  47.4 2.4 %collective-permute-start.7 = (bf16[24,1536]{1,0:T(8,128)(2,1)S(1)}, bf16[24,1536]{1,0:T(8,128)(2,1)S(1)}, u32[]{:S(2)}, u32[]{:S(2)}) collective-permute-start(bf16[24,1536]{1,0:T(8,128)(2,1)S(1)} %get-tuple-element.64), channel_id=1, source_target_pairs={{0,8},{1,9},{2,10},{3,11},{4,12},{5,13},{6,14},{7,15},{8,0},{9,1},... | collective-permute-start | bytes 221192 | tf_op jit(solution)/shard_map/ppermute | solution.py:694
  49.8 0.6 collective-permute-start.8
  50.4 1.5 %collective-permute-start.9 = (bf16[24,1536]{1,0:T(8,128)(2,1)S(1)}, bf16[24,1536]{1,0:T(8,128)(2,1)S(1)}, u32[]{:S(2)}, u32[]{:S(2)}) collective-permute-start(bf16[24,1536]{1,0:T(8,128)(2,1)S(1)} %get-tuple-element.66), channel_id=1, source_target_pairs={{0,12},{1,11},{2,14},{3,9},{4,8},{5,15},{6,10},{7,13},{8,4},{9,3},... | collective-permute-start | bytes 221192 | tf_op jit(solution)/shard_map/ppermute | solution.py:694
  51.8 1.6 %collective-permute-done.7.refs_0_ = bf16[24,1536]{1,0:T(8,128)(2,1)S(1)} collective-permute-done((bf16[24,1536]{1,0:T(8,128)(2,1)S(1)}, bf16[24,1536]{1,0:T(8,128)(2,1)S(1)}, u32[]{:S(2)}, u32[]{:S(2)}) %collective-permute-start.7) | collective-permute-done | bytes 73760 | tf_op jit(solution)/shard_map/ppermute | solution.py:694
  53.4 1.5 %collective-permute-done.8.refs_1_ = bf16[24,1536]{1,0:T(8,128)(2,1)S(1)} collective-permute-done((bf16[24,1536]{1,0:T(8,128)(2,1)S(1)}, bf16[24,1536]{1,0:T(8,128)(2,1)S(1)}, u32[]{:S(2)}, u32[]{:S(2)}) %collective-permute-start.8) | collective-permute-done | bytes 73760 | tf_op jit(solution)/shard_map/ppermute | solution.py:694
  54.9 1.7 %collective-permute-done.9.refs_2_ = bf16[24,1536]{1,0:T(8,128)(2,1)S(1)} collective-permute-done((bf16[24,1536]{1,0:T(8,128)(2,1)S(1)}, bf16[24,1536]{1,0:T(8,128)(2,1)S(1)}, u32[]{:S(2)}, u32[]{:S(2)}) %collective-permute-start.9) | collective-permute-done | bytes 73760 | tf_op jit(solution)/shard_map/ppermute | solution.py:694
  56.6 0.7 %finish.1 = bf16[12,3072]{1,0:T(8,128)(2,1)} custom-call(f32[12,3072]{1,0:T(8,128)S(1)} %get-tuple-element.36.carried_ref, f32[12,3072]{1,0:T(8,128)S(1)} %get-tuple-element.63.own_ref, bf16[24,1536]{1,0:T(8,128)(2,1)S(1)} %collective-permute-done.7.refs_0_, bf16[24,1536]{1,0:T(8,128)(2,1)S(1)} %collective-permute-done.8.refs_1_, ...), custom_call_target="tpu_custom_call" | custom-call | tf_op jit(solution)/shard_map/finish/pallas_call | solution.py:670
  (1 shorter events, 0.0 us)
Async XLA Ops:
  3.4 10.4 %collective-permute-start.2 = (bf16[24,1664]{1,0:T(8,128)(2,1)S(1)}, bf16[24,1664]{1,0:T(8,128)(2,1)S(1)}, u32[]{:S(2)}, u32[]{:S(2)}) collective-permute-start(bf16[24,1664]{1,0:T(8,128)(2,1)S(1)} %get-tuple-element.37.dep_ref.refs_0_), channel_id=1, source_target_pairs={{0,8},{1,9},{2,10},{3,11},{4,12},{5,13},{6,14},{7,15},{8,0},{9,1},... | collective-permute-start | bytes 239624 | tf_op jit(solution)/shard_map/ppermute | solution.py:694
  7.5 6.3 %collective-permute-start.1 = (bf16[24,1664]{1,0:T(8,128)(2,1)S(1)}, bf16[24,1664]{1,0:T(8,128)(2,1)S(1)}, u32[]{:S(2)}, u32[]{:S(2)}) collective-permute-start(bf16[24,1664]{1,0:T(8,128)(2,1)S(1)} %get-tuple-element.37.dep_ref.refs_0_), channel_id=1, source_target_pairs={{0,4},{1,3},{2,6},{3,1},{4,0},{5,7},{6,2},{7,5},{8,12},{9,11},{10,... | collective-permute-start | bytes 239624 | tf_op jit(solution)/shard_map/ppermute | solution.py:694
  9.1 6.2 %collective-permute-start = (bf16[24,1664]{1,0:T(8,128)(2,1)S(1)}, bf16[24,1664]{1,0:T(8,128)(2,1)S(1)}, u32[]{:S(2)}, u32[]{:S(2)}) collective-permute-start(bf16[24,1664]{1,0:T(8,128)(2,1)S(1)} %get-tuple-element.37.dep_ref.refs_0_), channel_id=1, source_target_pairs={{0,12},{1,11},{2,14},{3,9},{4,8},{5,15},{6,10},{7,13},{8,4},{9,3},... | collective-permute-start | bytes 239624 | tf_op jit(solution)/shard_map/ppermute | solution.py:694
  15.4 6.9 %collective-permute-start.3 = (bf16[48,3200]{1,0:T(8,128)(2,1)S(1)}, bf16[48,3200]{1,0:T(8,128)(2,1)S(1)}, u32[]{:S(2)}, u32[]{:S(2)}) collective-permute-start(bf16[48,3200]{1,0:T(8,128)(2,1)S(1)} %unfold.1.dep_ref.a_ref), channel_id=1, source_target_pairs={{0,2},{1,5},{2,0},{3,7},{4,6},{5,1},{6,4},{7,3},{8,10},{9,13},{10,... | collective-permute-start | bytes 921608 | tf_op jit(solution)/shard_map/ppermute | solution.py:694
  22.4 6.0 %collective-permute-start.4 = (bf16[96,3200]{1,0:T(8,128)(2,1)S(1)}, bf16[96,3200]{1,0:T(8,128)(2,1)S(1)}, u32[]{:S(2)}, u32[]{:S(2)}) collective-permute-start(bf16[96,3200]{1,0:T(8,128)(2,1)S(1)} %join.1.x_ref), channel_id=1, source_target_pairs={{0,1},{1,0},{2,3},{3,2},{4,5},{5,4},{6,7},{7,6},{8,9},{9,8},{10,11... | collective-permute-start | bytes 1843208 | tf_op jit(solution)/shard_map/ppermute | solution.py:697
  36.9 3.5 %collective-permute-start.5 = (bf16[96,3072]{1,0:T(8,128)(2,1)S(1)}, bf16[96,3072]{1,0:T(8,128)(2,1)S(1)}, u32[]{:S(2)}, u32[]{:S(2)}) collective-permute-start(bf16[96,3072]{1,0:T(8,128)(2,1)S(1)} %get-tuple-element.60), channel_id=1, source_target_pairs={{0,1},{1,0},{2,3},{3,2},{4,5},{5,4},{6,7},{7,6},{8,9},{9,8},{10,11... | collective-permute-start | bytes 1769480 | tf_op jit(solution)/shard_map/ppermute | solution.py:697
  40.5 6.8 %collective-permute-start.6 = (bf16[48,3072]{1,0:T(8,128)(2,1)S(1)}, bf16[48,3072]{1,0:T(8,128)(2,1)S(1)}, u32[]{:S(2)}, u32[]{:S(2)}) collective-permute-start(bf16[48,3072]{1,0:T(8,128)(2,1)S(1)} %get-tuple-element.62), channel_id=1, source_target_pairs={{0,2},{1,5},{2,0},{3,7},{4,6},{5,1},{6,4},{7,3},{8,10},{9,13},{10,... | collective-permute-start | bytes 884744 | tf_op jit(solution)/shard_map/ppermute | solution.py:694
  47.4 6.0 %collective-permute-start.7 = (bf16[24,1536]{1,0:T(8,128)(2,1)S(1)}, bf16[24,1536]{1,0:T(8,128)(2,1)S(1)}, u32[]{:S(2)}, u32[]{:S(2)}) collective-permute-start(bf16[24,1536]{1,0:T(8,128)(2,1)S(1)} %get-tuple-element.64), channel_id=1, source_target_pairs={{0,8},{1,9},{2,10},{3,11},{4,12},{5,13},{6,14},{7,15},{8,0},{9,1},... | collective-permute-start | bytes 221192 | tf_op jit(solution)/shard_map/ppermute | solution.py:694
  49.8 5.1 %collective-permute-start.8 = (bf16[24,1536]{1,0:T(8,128)(2,1)S(1)}, bf16[24,1536]{1,0:T(8,128)(2,1)S(1)}, u32[]{:S(2)}, u32[]{:S(2)}) collective-permute-start(bf16[24,1536]{1,0:T(8,128)(2,1)S(1)} %get-tuple-element.65), channel_id=1, source_target_pairs={{0,4},{1,3},{2,6},{3,1},{4,0},{5,7},{6,2},{7,5},{8,12},{9,11},{10,... | collective-permute-start | bytes 221192 | tf_op jit(solution)/shard_map/ppermute | solution.py:694
  50.4 6.3 %collective-permute-start.9 = (bf16[24,1536]{1,0:T(8,128)(2,1)S(1)}, bf16[24,1536]{1,0:T(8,128)(2,1)S(1)}, u32[]{:S(2)}, u32[]{:S(2)}) collective-permute-start(bf16[24,1536]{1,0:T(8,128)(2,1)S(1)} %get-tuple-element.66), channel_id=1, source_target_pairs={{0,12},{1,11},{2,14},{3,9},{4,8},{5,15},{6,10},{7,13},{8,4},{9,3},... | collective-permute-start | bytes 221192 | tf_op jit(solution)/shard_map/ppermute | solution.py:694

commit v13 on v12

--- a/solution.py
+++ b/solution.py
@@ -194,7 +194,7 @@
     ]
     copies = [pltpu.make_async_copy(a, b, sems.at[i]) for i, (a, b) in enumerate(moves)]
     weights = row_copies((g_hbm, u_hbm), (g_vmem, u_vmem), 0, ahead, w_sems)
-    for copy in copies + weights:
+    for copy in copies[:5] + weights + copies[5:]:
         copy.start()
     copies[0].wait()
     for h in range(heads):

time: 57.5 us -> 57.5 us (level)
  no operation moved by 1% of the time
where the time goes in v13:
time: 57.5 us; the launch traced here: 57.3 us
  Pallas kernels  31.8 us (55%)
  starting transfers between devices  13.8 us (24%)
  waiting for transfers between devices  11.5 us (20%)
    ppermute x8, starting transfers between devices, exchange(): return lax.ppermute(array, ('node', 'shard'), perm)  13.2 us
    ppermute x8, waiting for transfers between devices, exchange(): return lax.ppermute(array, ('node', 'shard'), perm)  11.5 us
    pallas_call x2, Pallas kernels, load_rows(): pl.pallas_call(functools.partial(load_kernel, first, rows, ahead), out_sh...  10.1 us
    pallas_call x1, Pallas kernels, second_half(): pl.pallas_call(functools.partial(second_half_kernel, per_plane), out_shap...  8.53 us
    pallas_call x1, Pallas kernels, first_half(): pl.pallas_call(first_half_kernel, out_shape=(acc, acc) + tuple((pltpu.VME...  5.89 us
    pallas_call x1, Pallas kernels, attend(): pl.pallas_call(functools.partial(attend_kernel, ahead), out_shape=(pltpu....  3.4 us
    pallas_call x1, Pallas kernels, staying_half(): pl.pallas_call(staying_kernel, out_shape=(vmem_array((rows, width), F32),...  2.91 us
  transfers between devices with their start and end apart: 10, of which 5 were waited for; matrix products, arithmetic and copies ran while one was open for 0% of the time, Pallas kernels for 33%

profile of v13, /device:TPU:0, one launch (start us, length us, event | category | flops | bytes accessed | tf_op | source)
XLA Modules:
  0.0 57.3 jit_solution(1295558526875050982)
XLA Ops:
  0.0 3.4 %attend.1 = (f32[12,3072]{1,0:T(8,128)S(1)}, bf16[24,1664]{1,0:T(8,128)(2,1)S(1)}, bf16[3072,2048]{1,0:T(8,128)(2,1)S(1)}, bf16[3072,2048]{1,0:T(8,128)(2,1)S(1)}, bf16[2,2,3072,512]{3,2,1,0:T(8,128)(2,1)S(1)}) custom-call(s32[12]{0:T(128)} %len_hbm.1, s32[2,12]{1,0:T(2,128)} %bitcast.5, bf16[12,3072]{1,0:T(8,128)(2,1)} %q_hbm.1, ...), custom_call_target="tpu_custom_call" | custom-call | flops 100000000 | bytes 8000000 | tf_op jit(solution)/shard_map/attend/pallas_call | solution.py:291
  3.4 4.1 %collective-permute-start.2 = (bf16[24,1664]{1,0:T(8,128)(2,1)S(1)}, bf16[24,1664]{1,0:T(8,128)(2,1)S(1)}, u32[]{:S(2)}, u32[]{:S(2)}) collective-permute-start(bf16[24,1664]{1,0:T(8,128)(2,1)S(1)} %get-tuple-element.37.dep_ref.refs_0_), channel_id=1, source_target_pairs={{0,8},{1,9},{2,10},{3,11},{4,12},{5,13},{6,14},{7,15},{8,0},{9,1},... | collective-permute-start | bytes 239624 | tf_op jit(solution)/shard_map/ppermute | solution.py:694
  7.5 1.6 %collective-permute-start.1 = (bf16[24,1664]{1,0:T(8,128)(2,1)S(1)}, bf16[24,1664]{1,0:T(8,128)(2,1)S(1)}, u32[]{:S(2)}, u32[]{:S(2)}) collective-permute-start(bf16[24,1664]{1,0:T(8,128)(2,1)S(1)} %get-tuple-element.37.dep_ref.refs_0_), channel_id=1, source_target_pairs={{0,4},{1,3},{2,6},{3,1},{4,0},{5,7},{6,2},{7,5},{8,12},{9,11},{10,... | collective-permute-start | bytes 239624 | tf_op jit(solution)/shard_map/ppermute | solution.py:694
  9.1 0.0 collective-permute-start
  9.1 4.7 %load_weights.2 = (bf16[3072,2048]{1,0:T(8,128)(2,1)S(1)}, bf16[3072,2048]{1,0:T(8,128)(2,1)S(1)}, bf16[2,2,3072,512]{3,2,1,0:T(8,128)(2,1)S(1)}, f32[8,128]{1,0:T(8,128)S(1)}) custom-call(bf16[24,1664]{1,0:T(8,128)(2,1)S(1)} %get-tuple-element.37.dep_ref.refs_0_, ...), custom_call_target="tpu_custom_call", output_to_operand_aliasing={{0}: (3, {}), {1}: (4, {}), {2}: (5, {})} | custom-call | bytes 12582912 | tf_op jit(solution)/shard_map/load_weights/pallas_call | solution.py:115
  13.8 0.0 collective-permute-done.2.refs_3_
  13.8 0.0 collective-permute-done.1.refs_2_
  13.8 1.5 %collective-permute-done.refs_1_ = bf16[24,1664]{1,0:T(8,128)(2,1)S(1)} collective-permute-done((bf16[24,1664]{1,0:T(8,128)(2,1)S(1)}, bf16[24,1664]{1,0:T(8,128)(2,1)S(1)}, u32[]{:S(2)}, u32[]{:S(2)}) %collective-permute-start) | collective-permute-done | bytes 79904 | tf_op jit(solution)/shard_map/ppermute | solution.py:694
  15.3 0.1 unfold.1.dep_ref.a_ref
  15.4 1.6 %collective-permute-start.3 = (bf16[48,3200]{1,0:T(8,128)(2,1)S(1)}, bf16[48,3200]{1,0:T(8,128)(2,1)S(1)}, u32[]{:S(2)}, u32[]{:S(2)}) collective-permute-start(bf16[48,3200]{1,0:T(8,128)(2,1)S(1)} %unfold.1.dep_ref.a_ref), channel_id=1, source_target_pairs={{0,2},{1,5},{2,0},{3,7},{4,6},{5,1},{6,4},{7,3},{8,10},{9,13},{10,... | collective-permute-start | bytes 921608 | tf_op jit(solution)/shard_map/ppermute | solution.py:694
  16.9 5.4 %load_weights.3 = (bf16[3072,2048]{1,0:T(8,128)(2,1)S(1)}, bf16[3072,2048]{1,0:T(8,128)(2,1)S(1)}, bf16[2,2,3072,512]{3,2,1,0:T(8,128)(2,1)S(1)}, f32[8,128]{1,0:T(8,128)S(1)}) custom-call(bf16[48,3200]{1,0:T(8,128)(2,1)S(1)} %unfold.1.dep_ref.a_ref, bf16[6144,2048]{1,0:T(8,128)(2,1)} %g_hbm.9, ...), custom_call_target="tpu_custom_call", output_to_operand_aliasing={{0}: (3, {}), {1}: (4, {}), {2}: (5, {})} | custom-call | bytes 8388608 | tf_op jit(solution)/shard_map/load_weights/pallas_call | solution.py:115
  22.3 0.0 collective-permute-done.3.b_ref
  22.4 0.1 collective-permute-start.4
  22.5 5.9 %first_half.1 = (f32[96,2048]{1,0:T(8,128)S(1)}, f32[96,2048]{1,0:T(8,128)S(1)}, bf16[3072,2048]{1,0:T(8,128)(2,1)S(1)}, bf16[3072,2048]{1,0:T(8,128)(2,1)S(1)}, bf16[2,2,3072,512]{3,2,1,0:T(8,128)(2,1)S(1)}) custom-call(bf16[96,3200]{1,0:T(8,128)(2,1)S(1)} %join.1.x_ref, ...), custom_call_target="tpu_custom_call", output_to_operand_aliasing={{2}: (3, {}), {3}: (4, {}), {4}: (5, {})} | custom-call | flops 2415919104 | bytes 12582912 | tf_op jit(solution)/shard_map/first_half/pallas_call | solution.py:372
  28.4 0.0 collective-permute-done.4.ox_ref
  28.4 8.5 %second_half.1 = (bf16[96,3072]{1,0:T(8,128)(2,1)S(1)}, bf16[96,2048]{1,0:T(8,128)(2,1)S(1)}, f32[96,128]{1,0:T(8,128)S(1)}, bf16[3072,2048]{1,0:T(8,128)(2,1)S(...) custom-call(bf16[96,3200]{1,0:T(8,128)(2,1)S(1)} %join.1.x_ref, ...), custom_call_target="tpu_custom_call", output_to_operand_aliasing={{3}: (7, {}), {4}: (8, {}), {5}: (9, {})} | custom-call | flops 3623878656 | bytes 25165824 | tf_op jit(solution)/shard_map/second_half/pallas_call | solution.py:542
  36.9 0.5 collective-permute-start.5
  37.5 2.9 %staying_half.1 = (f32[96,3072]{1,0:T(8,128)S(1)}, bf16[3072,2048]{1,0:T(8,128)(2,1)S(1)}, bf16[3072,2048]{1,0:T(8,128)(2,1)S(1)}, bf16[2,2,3072,512]{3,2,1,0:T(8,128)(2,1)S(1)}) custom-call(bf16[96,2048]{1,0:T(8,128)(2,1)S(1)} %get-tuple-element.54.h_ref, ...), custom_call_target="tpu_custom_call", output_to_operand_aliasing={{1}: (3, {}), {2}: (4, {}), {3}: (5, {})} | custom-call | flops 1207959552 | bytes 6291456 | tf_op jit(solution)/shard_map/staying_half/pallas_call | solution.py:589
  40.4 0.0 collective-permute-done.5.got_ref
  40.4 0.1 split_rows.1
  40.5 1.5 %collective-permute-start.6 = (bf16[48,3072]{1,0:T(8,128)(2,1)S(1)}, bf16[48,3072]{1,0:T(8,128)(2,1)S(1)}, u32[]{:S(2)}, u32[]{:S(2)}) collective-permute-start(bf16[48,3072]{1,0:T(8,128)(2,1)S(1)} %get-tuple-element.62), channel_id=1, source_target_pairs={{0,2},{1,5},{2,0},{3,7},{4,6},{5,1},{6,4},{7,3},{8,10},{9,13},{10,... | collective-permute-start | bytes 884744 | tf_op jit(solution)/shard_map/ppermute | solution.py:694
  42.0 5.3 %collective-permute-done.6.got_ref = bf16[48,3072]{1,0:T(8,128)(2,1)S(1)} collective-permute-done((bf16[48,3072]{1,0:T(8,128)(2,1)S(1)}, bf16[48,3072]{1,0:T(8,128)(2,1)S(1)}, u32[]{:S(2)}, u32[]{:S(2)}) %collective-permute-start.6) | collective-permute-done | bytes 294944 | tf_op jit(solution)/shard_map/ppermute | solution.py:694
  47.3 0.1 split_last.1
  47.4 2.4 %collective-permute-start.7 = (bf16[24,1536]{1,0:T(8,128)(2,1)S(1)}, bf16[24,1536]{1,0:T(8,128)(2,1)S(1)}, u32[]{:S(2)}, u32[]{:S(2)}) collective-permute-start(bf16[24,1536]{1,0:T(8,128)(2,1)S(1)} %get-tuple-element.64), channel_id=1, source_target_pairs={{0,8},{1,9},{2,10},{3,11},{4,12},{5,13},{6,14},{7,15},{8,0},{9,1},... | collective-permute-start | bytes 221192 | tf_op jit(solution)/shard_map/ppermute | solution.py:694
  49.8 0.6 collective-permute-start.8
  50.4 1.5 %collective-permute-start.9 = (bf16[24,1536]{1,0:T(8,128)(2,1)S(1)}, bf16[24,1536]{1,0:T(8,128)(2,1)S(1)}, u32[]{:S(2)}, u32[]{:S(2)}) collective-permute-start(bf16[24,1536]{1,0:T(8,128)(2,1)S(1)} %get-tuple-element.66), channel_id=1, source_target_pairs={{0,12},{1,11},{2,14},{3,9},{4,8},{5,15},{6,10},{7,13},{8,4},{9,3},... | collective-permute-start | bytes 221192 | tf_op jit(solution)/shard_map/ppermute | solution.py:694
  51.8 1.6 %collective-permute-done.7.refs_0_ = bf16[24,1536]{1,0:T(8,128)(2,1)S(1)} collective-permute-done((bf16[24,1536]{1,0:T(8,128)(2,1)S(1)}, bf16[24,1536]{1,0:T(8,128)(2,1)S(1)}, u32[]{:S(2)}, u32[]{:S(2)}) %collective-permute-start.7) | collective-permute-done | bytes 73760 | tf_op jit(solution)/shard_map/ppermute | solution.py:694
  53.4 1.5 %collective-permute-done.8.refs_1_ = bf16[24,1536]{1,0:T(8,128)(2,1)S(1)} collective-permute-done((bf16[24,1536]{1,0:T(8,128)(2,1)S(1)}, bf16[24,1536]{1,0:T(8,128)(2,1)S(1)}, u32[]{:S(2)}, u32[]{:S(2)}) %collective-permute-start.8) | collective-permute-done | bytes 73760 | tf_op jit(solution)/shard_map/ppermute | solution.py:694
  54.9 1.7 %collective-permute-done.9.refs_2_ = bf16[24,1536]{1,0:T(8,128)(2,1)S(1)} collective-permute-done((bf16[24,1536]{1,0:T(8,128)(2,1)S(1)}, bf16[24,1536]{1,0:T(8,128)(2,1)S(1)}, u32[]{:S(2)}, u32[]{:S(2)}) %collective-permute-start.9) | collective-permute-done | bytes 73760 | tf_op jit(solution)/shard_map/ppermute | solution.py:694
  56.6 0.7 %finish.1 = bf16[12,3072]{1,0:T(8,128)(2,1)} custom-call(f32[12,3072]{1,0:T(8,128)S(1)} %get-tuple-element.36.carried_ref, f32[12,3072]{1,0:T(8,128)S(1)} %get-tuple-element.63.own_ref, bf16[24,1536]{1,0:T(8,128)(2,1)S(1)} %collective-permute-done.7.refs_0_, bf16[24,1536]{1,0:T(8,128)(2,1)S(1)} %collective-permute-done.8.refs_1_, ...), custom_call_target="tpu_custom_call" | custom-call | tf_op jit(solution)/shard_map/finish/pallas_call | solution.py:670
  (1 shorter events, 0.0 us)
Async XLA Ops:
  3.4 10.4 %collective-permute-start.2 = (bf16[24,1664]{1,0:T(8,128)(2,1)S(1)}, bf16[24,1664]{1,0:T(8,128)(2,1)S(1)}, u32[]{:S(2)}, u32[]{:S(2)}) collective-permute-start(bf16[24,1664]{1,0:T(8,128)(2,1)S(1)} %get-tuple-element.37.dep_ref.refs_0_), channel_id=1, source_target_pairs={{0,8},{1,9},{2,10},{3,11},{4,12},{5,13},{6,14},{7,15},{8,0},{9,1},... | collective-permute-start | bytes 239624 | tf_op jit(solution)/shard_map/ppermute | solution.py:694
  7.5 6.3 %collective-permute-start.1 = (bf16[24,1664]{1,0:T(8,128)(2,1)S(1)}, bf16[24,1664]{1,0:T(8,128)(2,1)S(1)}, u32[]{:S(2)}, u32[]{:S(2)}) collective-permute-start(bf16[24,1664]{1,0:T(8,128)(2,1)S(1)} %get-tuple-element.37.dep_ref.refs_0_), channel_id=1, source_target_pairs={{0,4},{1,3},{2,6},{3,1},{4,0},{5,7},{6,2},{7,5},{8,12},{9,11},{10,... | collective-permute-start | bytes 239624 | tf_op jit(solution)/shard_map/ppermute | solution.py:694
  9.1 6.2 %collective-permute-start = (bf16[24,1664]{1,0:T(8,128)(2,1)S(1)}, bf16[24,1664]{1,0:T(8,128)(2,1)S(1)}, u32[]{:S(2)}, u32[]{:S(2)}) collective-permute-start(bf16[24,1664]{1,0:T(8,128)(2,1)S(1)} %get-tuple-element.37.dep_ref.refs_0_), channel_id=1, source_target_pairs={{0,12},{1,11},{2,14},{3,9},{4,8},{5,15},{6,10},{7,13},{8,4},{9,3},... | collective-permute-start | bytes 239624 | tf_op jit(solution)/shard_map/ppermute | solution.py:694
  15.4 6.9 %collective-permute-start.3 = (bf16[48,3200]{1,0:T(8,128)(2,1)S(1)}, bf16[48,3200]{1,0:T(8,128)(2,1)S(1)}, u32[]{:S(2)}, u32[]{:S(2)}) collective-permute-start(bf16[48,3200]{1,0:T(8,128)(2,1)S(1)} %unfold.1.dep_ref.a_ref), channel_id=1, source_target_pairs={{0,2},{1,5},{2,0},{3,7},{4,6},{5,1},{6,4},{7,3},{8,10},{9,13},{10,... | collective-permute-start | bytes 921608 | tf_op jit(solution)/shard_map/ppermute | solution.py:694
  22.4 6.0 %collective-permute-start.4 = (bf16[96,3200]{1,0:T(8,128)(2,1)S(1)}, bf16[96,3200]{1,0:T(8,128)(2,1)S(1)}, u32[]{:S(2)}, u32[]{:S(2)}) collective-permute-start(bf16[96,3200]{1,0:T(8,128)(2,1)S(1)} %join.1.x_ref), channel_id=1, source_target_pairs={{0,1},{1,0},{2,3},{3,2},{4,5},{5,4},{6,7},{7,6},{8,9},{9,8},{10,11... | collective-permute-start | bytes 1843208 | tf_op jit(solution)/shard_map/ppermute | solution.py:697
  36.9 3.5 %collective-permute-start.5 = (bf16[96,3072]{1,0:T(8,128)(2,1)S(1)}, bf16[96,3072]{1,0:T(8,128)(2,1)S(1)}, u32[]{:S(2)}, u32[]{:S(2)}) collective-permute-start(bf16[96,3072]{1,0:T(8,128)(2,1)S(1)} %get-tuple-element.60), channel_id=1, source_target_pairs={{0,1},{1,0},{2,3},{3,2},{4,5},{5,4},{6,7},{7,6},{8,9},{9,8},{10,11... | collective-permute-start | bytes 1769480 | tf_op jit(solution)/shard_map/ppermute | solution.py:697
  40.5 6.8 %collective-permute-start.6 = (bf16[48,3072]{1,0:T(8,128)(2,1)S(1)}, bf16[48,3072]{1,0:T(8,128)(2,1)S(1)}, u32[]{:S(2)}, u32[]{:S(2)}) collective-permute-start(bf16[48,3072]{1,0:T(8,128)(2,1)S(1)} %get-tuple-element.62), channel_id=1, source_target_pairs={{0,2},{1,5},{2,0},{3,7},{4,6},{5,1},{6,4},{7,3},{8,10},{9,13},{10,... | collective-permute-start | bytes 884744 | tf_op jit(solution)/shard_map/ppermute | solution.py:694
  47.4 6.0 %collective-permute-start.7 = (bf16[24,1536]{1,0:T(8,128)(2,1)S(1)}, bf16[24,1536]{1,0:T(8,128)(2,1)S(1)}, u32[]{:S(2)}, u32[]{:S(2)}) collective-permute-start(bf16[24,1536]{1,0:T(8,128)(2,1)S(1)} %get-tuple-element.64), channel_id=1, source_target_pairs={{0,8},{1,9},{2,10},{3,11},{4,12},{5,13},{6,14},{7,15},{8,0},{9,1},... | collective-permute-start | bytes 221192 | tf_op jit(solution)/shard_map/ppermute | solution.py:694
  49.8 5.1 %collective-permute-start.8 = (bf16[24,1536]{1,0:T(8,128)(2,1)S(1)}, bf16[24,1536]{1,0:T(8,128)(2,1)S(1)}, u32[]{:S(2)}, u32[]{:S(2)}) collective-permute-start(bf16[24,1536]{1,0:T(8,128)(2,1)S(1)} %get-tuple-element.65), channel_id=1, source_target_pairs={{0,4},{1,3},{2,6},{3,1},{4,0},{5,7},{6,2},{7,5},{8,12},{9,11},{10,... | collective-permute-start | bytes 221192 | tf_op jit(solution)/shard_map/ppermute | solution.py:694
  50.4 6.3 %collective-permute-start.9 = (bf16[24,1536]{1,0:T(8,128)(2,1)S(1)}, bf16[24,1536]{1,0:T(8,128)(2,1)S(1)}, u32[]{:S(2)}, u32[]{:S(2)}) collective-permute-start(bf16[24,1536]{1,0:T(8,128)(2,1)S(1)} %get-tuple-element.66), channel_id=1, source_target_pairs={{0,12},{1,11},{2,14},{3,9},{4,8},{5,15},{6,10},{7,13},{8,4},{9,3},... | collective-permute-start | bytes 221192 | tf_op jit(solution)/shard_map/ppermute | solution.py:694

commit v14 on v13

--- a/solution.py
+++ b/solution.py
@@ -128,7 +128,8 @@
 def unfold_kernel(tok, *refs):
     *arrays, _, out_ref, scr = refs
     fold_width = arrays[0].shape[1] - LANES
-    for i, array in enumerate([arrays[0], *reversed(arrays[1:])]):
+    first, near, both, far = arrays
+    for i, array in enumerate((first, far, near, both)):
         rows = array[...].astype(F32)
         to = slice(i * tok, (i + 1) * tok)
         for f in range(FOLD):
@@ -708,7 +709,7 @@
     *held, token = load_rows(
         heights[0], heights[1], False, payload, gate_weight, up_weight, held
     )
-    payload = unfold(tok, [payload, *reversed(got)], token)
+    payload = unfold(tok, [payload, got[1], got[2], got[0]], token)
     for stage in range(2, stages):
         got = exchange(payload, stage)
         if stage == 2:
@@ -728,7 +729,8 @@
         keep, send = split_rows(keep, got)
         got = exchange(send, stage)
     keep, *sends = split_last(keep, got, 1 + len(near))
-    return finish(carried, keep, [exchange(send, *flips) for send, flips in zip(sends, near)])
+    got = [exchange(send, *flips) for send, flips in zip(sends, near)]
+    return finish(carried, keep, [got[0], got[2], got[1]])
 
 
 def solution(mesh):

time: 57.5 us -> 57.4 us (level)
  waiting for transfers between devices: 11.5 us -> 10.6 us
    ppermute x8, waiting for transfers between devices: 11.5 us -> 10.6 us  [exchange(): return lax.ppermute(array, ('node', 'shard'), perm)]
  transfers between devices with their start and end apart: 10 -> 10, of which waited for: 5 -> 4; matrix products, arithmetic and copies ran while one was open for 0% -> 0% of each run, Pallas kernels for 33% -> 33%
where the time goes in v14:
time: 57.4 us; the launch traced here: 56.8 us
  Pallas kernels  31.8 us (55%)
  starting transfers between devices  14.3 us (25%)
  waiting for transfers between devices  10.6 us (18%)
    ppermute x8, starting transfers between devices, exchange(): return lax.ppermute(array, ('node', 'shard'), perm)  13.7 us
    ppermute x8, waiting for transfers between devices, exchange(): return lax.ppermute(array, ('node', 'shard'), perm)  10.6 us
    pallas_call x2, Pallas kernels, load_rows(): pl.pallas_call(functools.partial(load_kernel, first, rows, ahead), out_sh...  10.1 us
    pallas_call x1, Pallas kernels, second_half(): pl.pallas_call(functools.partial(second_half_kernel, per_plane), out_shap...  8.53 us
    pallas_call x1, Pallas kernels, first_half(): pl.pallas_call(first_half_kernel, out_shape=(acc, acc) + tuple((pltpu.VME...  5.89 us
    pallas_call x1, Pallas kernels, attend(): pl.pallas_call(functools.partial(attend_kernel, ahead), out_shape=(pltpu....  3.4 us
    pallas_call x1, Pallas kernels, staying_half(): pl.pallas_call(staying_kernel, out_shape=(vmem_array((rows, width), F32),...  2.91 us
  transfers between devices with their start and end apart: 10, of which 4 were waited for; matrix products, arithmetic and copies ran while one was open for 0% of the time, Pallas kernels for 33%

profile of v14, /device:TPU:0, one launch (start us, length us, event | category | flops | bytes accessed | tf_op | source)
XLA Modules:
  0.0 56.8 jit_solution(3249346989934562416)
XLA Ops:
  0.0 3.4 %attend.1 = (f32[12,3072]{1,0:T(8,128)S(1)}, bf16[24,1664]{1,0:T(8,128)(2,1)S(1)}, bf16[3072,2048]{1,0:T(8,128)(2,1)S(1)}, bf16[3072,2048]{1,0:T(8,128)(2,1)S(1)}, bf16[2,2,3072,512]{3,2,1,0:T(8,128)(2,1)S(1)}) custom-call(s32[12]{0:T(128)} %len_hbm.1, s32[2,12]{1,0:T(2,128)} %bitcast.5, bf16[12,3072]{1,0:T(8,128)(2,1)} %q_hbm.1, ...), custom_call_target="tpu_custom_call" | custom-call | flops 100000000 | bytes 8000000 | tf_op jit(solution)/shard_map/attend/pallas_call | solution.py:292
  3.4 4.1 %collective-permute-start.2 = (bf16[24,1664]{1,0:T(8,128)(2,1)S(1)}, bf16[24,1664]{1,0:T(8,128)(2,1)S(1)}, u32[]{:S(2)}, u32[]{:S(2)}) collective-permute-start(bf16[24,1664]{1,0:T(8,128)(2,1)S(1)} %get-tuple-element.37.dep_ref.refs_0_), channel_id=1, source_target_pairs={{0,8},{1,9},{2,10},{3,11},{4,12},{5,13},{6,14},{7,15},{8,0},{9,1},... | collective-permute-start | bytes 239624 | tf_op jit(solution)/shard_map/ppermute | solution.py:695
  7.5 1.3 %collective-permute-start.1 = (bf16[24,1664]{1,0:T(8,128)(2,1)S(1)}, bf16[24,1664]{1,0:T(8,128)(2,1)S(1)}, u32[]{:S(2)}, u32[]{:S(2)}) collective-permute-start(bf16[24,1664]{1,0:T(8,128)(2,1)S(1)} %get-tuple-element.37.dep_ref.refs_0_), channel_id=1, source_target_pairs={{0,12},{1,11},{2,14},{3,9},{4,8},{5,15},{6,10},{7,13},{8,4},{9,3},... | collective-permute-start | bytes 239624 | tf_op jit(solution)/shard_map/ppermute | solution.py:695
  8.9 0.2 collective-permute-start
  9.1 4.7 %load_weights.2 = (bf16[3072,2048]{1,0:T(8,128)(2,1)S(1)}, bf16[3072,2048]{1,0:T(8,128)(2,1)S(1)}, bf16[2,2,3072,512]{3,2,1,0:T(8,128)(2,1)S(1)}, f32[8,128]{1,0:T(8,128)S(1)}) custom-call(bf16[24,1664]{1,0:T(8,128)(2,1)S(1)} %get-tuple-element.37.dep_ref.refs_0_, ...), custom_call_target="tpu_custom_call", output_to_operand_aliasing={{0}: (3, {}), {1}: (4, {}), {2}: (5, {})} | custom-call | bytes 12582912 | tf_op jit(solution)/shard_map/load_weights/pallas_call | solution.py:115
  13.8 0.0 collective-permute-done.2.refs_3_
  13.8 0.5 collective-permute-done.1.refs_2_
  14.3 0.0 collective-permute-done.refs_1_
  14.3 0.1 unfold.1.dep_ref.a_ref
  14.4 2.5 %collective-permute-start.3 = (bf16[48,3200]{1,0:T(8,128)(2,1)S(1)}, bf16[48,3200]{1,0:T(8,128)(2,1)S(1)}, u32[]{:S(2)}, u32[]{:S(2)}) collective-permute-start(bf16[48,3200]{1,0:T(8,128)(2,1)S(1)} %unfold.1.dep_ref.a_ref), channel_id=1, source_target_pairs={{0,2},{1,5},{2,0},{3,7},{4,6},{5,1},{6,4},{7,3},{8,10},{9,13},{10,... | collective-permute-start | bytes 921608 | tf_op jit(solution)/shard_map/ppermute | solution.py:695
  16.9 5.4 %load_weights.3 = (bf16[3072,2048]{1,0:T(8,128)(2,1)S(1)}, bf16[3072,2048]{1,0:T(8,128)(2,1)S(1)}, bf16[2,2,3072,512]{3,2,1,0:T(8,128)(2,1)S(1)}, f32[8,128]{1,0:T(8,128)S(1)}) custom-call(bf16[48,3200]{1,0:T(8,128)(2,1)S(1)} %unfold.1.dep_ref.a_ref, bf16[6144,2048]{1,0:T(8,128)(2,1)} %g_hbm.9, ...), custom_call_target="tpu_custom_call", output_to_operand_aliasing={{0}: (3, {}), {1}: (4, {}), {2}: (5, {})} | custom-call | bytes 8388608 | tf_op jit(solution)/shard_map/load_weights/pallas_call | solution.py:115
  22.3 0.0 collective-permute-done.3.b_ref
  22.3 0.1 collective-permute-start.4
  22.4 5.9 %first_half.1 = (f32[96,2048]{1,0:T(8,128)S(1)}, f32[96,2048]{1,0:T(8,128)S(1)}, bf16[3072,2048]{1,0:T(8,128)(2,1)S(1)}, bf16[3072,2048]{1,0:T(8,128)(2,1)S(1)}, bf16[2,2,3072,512]{3,2,1,0:T(8,128)(2,1)S(1)}) custom-call(bf16[96,3200]{1,0:T(8,128)(2,1)S(1)} %join.1.x_ref, ...), custom_call_target="tpu_custom_call", output_to_operand_aliasing={{2}: (3, {}), {3}: (4, {}), {4}: (5, {})} | custom-call | flops 2415919104 | bytes 12582912 | tf_op jit(solution)/shard_map/first_half/pallas_call | solution.py:373
  28.3 0.0 collective-permute-done.4.ox_ref
  28.3 8.5 %second_half.1 = (bf16[96,3072]{1,0:T(8,128)(2,1)S(1)}, bf16[96,2048]{1,0:T(8,128)(2,1)S(1)}, f32[96,128]{1,0:T(8,128)S(1)}, bf16[3072,2048]{1,0:T(8,128)(2,1)S(...) custom-call(bf16[96,3200]{1,0:T(8,128)(2,1)S(1)} %join.1.x_ref, ...), custom_call_target="tpu_custom_call", output_to_operand_aliasing={{3}: (7, {}), {4}: (8, {}), {5}: (9, {})} | custom-call | flops 3623878656 | bytes 25165824 | tf_op jit(solution)/shard_map/second_half/pallas_call | solution.py:543
  36.9 0.5 collective-permute-start.5
  37.4 2.9 %staying_half.1 = (f32[96,3072]{1,0:T(8,128)S(1)}, bf16[3072,2048]{1,0:T(8,128)(2,1)S(1)}, bf16[3072,2048]{1,0:T(8,128)(2,1)S(1)}, bf16[2,2,3072,512]{3,2,1,0:T(8,128)(2,1)S(1)}) custom-call(bf16[96,2048]{1,0:T(8,128)(2,1)S(1)} %get-tuple-element.54.h_ref, ...), custom_call_target="tpu_custom_call", output_to_operand_aliasing={{1}: (3, {}), {2}: (4, {}), {3}: (5, {})} | custom-call | flops 1207959552 | bytes 6291456 | tf_op jit(solution)/shard_map/staying_half/pallas_call | solution.py:590
  40.3 0.0 collective-permute-done.5.got_ref
  40.3 0.1 split_rows.1
  40.4 1.5 %collective-permute-start.6 = (bf16[48,3072]{1,0:T(8,128)(2,1)S(1)}, bf16[48,3072]{1,0:T(8,128)(2,1)S(1)}, u32[]{:S(2)}, u32[]{:S(2)}) collective-permute-start(bf16[48,3072]{1,0:T(8,128)(2,1)S(1)} %get-tuple-element.62), channel_id=1, source_target_pairs={{0,2},{1,5},{2,0},{3,7},{4,6},{5,1},{6,4},{7,3},{8,10},{9,13},{10,... | collective-permute-start | bytes 884744 | tf_op jit(solution)/shard_map/ppermute | solution.py:695
  42.0 5.3 %collective-permute-done.6.got_ref = bf16[48,3072]{1,0:T(8,128)(2,1)S(1)} collective-permute-done((bf16[48,3072]{1,0:T(8,128)(2,1)S(1)}, bf16[48,3072]{1,0:T(8,128)(2,1)S(1)}, u32[]{:S(2)}, u32[]{:S(2)}) %collective-permute-start.6) | collective-permute-done | bytes 294944 | tf_op jit(solution)/shard_map/ppermute | solution.py:695
  47.2 0.1 split_last.1
  47.3 2.5 %collective-permute-start.7 = (bf16[24,1536]{1,0:T(8,128)(2,1)S(1)}, bf16[24,1536]{1,0:T(8,128)(2,1)S(1)}, u32[]{:S(2)}, u32[]{:S(2)}) collective-permute-start(bf16[24,1536]{1,0:T(8,128)(2,1)S(1)} %get-tuple-element.64), channel_id=1, source_target_pairs={{0,8},{1,9},{2,10},{3,11},{4,12},{5,13},{6,14},{7,15},{8,0},{9,1},... | collective-permute-start | bytes 221192 | tf_op jit(solution)/shard_map/ppermute | solution.py:695
  49.9 0.9 %collective-permute-start.8 = (bf16[24,1536]{1,0:T(8,128)(2,1)S(1)}, bf16[24,1536]{1,0:T(8,128)(2,1)S(1)}, u32[]{:S(2)}, u32[]{:S(2)}) collective-permute-start(bf16[24,1536]{1,0:T(8,128)(2,1)S(1)} %get-tuple-element.65), channel_id=1, source_target_pairs={{0,12},{1,11},{2,14},{3,9},{4,8},{5,15},{6,10},{7,13},{8,4},{9,3},... | collective-permute-start | bytes 221192 | tf_op jit(solution)/shard_map/ppermute | solution.py:695
  50.8 0.5 collective-permute-start.9
  51.3 2.4 %collective-permute-done.7.refs_0_ = bf16[24,1536]{1,0:T(8,128)(2,1)S(1)} collective-permute-done((bf16[24,1536]{1,0:T(8,128)(2,1)S(1)}, bf16[24,1536]{1,0:T(8,128)(2,1)S(1)}, u32[]{:S(2)}, u32[]{:S(2)}) %collective-permute-start.7) | collective-permute-done | bytes 73760 | tf_op jit(solution)/shard_map/ppermute | solution.py:695
  53.7 2.4 %collective-permute-done.8.refs_1_ = bf16[24,1536]{1,0:T(8,128)(2,1)S(1)} collective-permute-done((bf16[24,1536]{1,0:T(8,128)(2,1)S(1)}, bf16[24,1536]{1,0:T(8,128)(2,1)S(1)}, u32[]{:S(2)}, u32[]{:S(2)}) %collective-permute-start.8) | collective-permute-done | bytes 73760 | tf_op jit(solution)/shard_map/ppermute | solution.py:695
  56.1 0.0 collective-permute-done.9.refs_2_
  56.1 0.7 %finish.1 = bf16[12,3072]{1,0:T(8,128)(2,1)} custom-call(f32[12,3072]{1,0:T(8,128)S(1)} %get-tuple-element.36.carried_ref, f32[12,3072]{1,0:T(8,128)S(1)} %get-tuple-element.63.own_ref, bf16[24,1536]{1,0:T(8,128)(2,1)S(1)} %collective-permute-done.7.refs_0_, bf16[24,1536]{1,0:T(8,128)(2,1)S(1)} %collective-permute-done.8.refs_1_, ...), custom_call_target="tpu_custom_call" | custom-call | tf_op jit(solution)/shard_map/finish/pallas_call | solution.py:671
  (1 shorter events, 0.0 us)
Async XLA Ops:
  3.4 10.4 %collective-permute-start.2 = (bf16[24,1664]{1,0:T(8,128)(2,1)S(1)}, bf16[24,1664]{1,0:T(8,128)(2,1)S(1)}, u32[]{:S(2)}, u32[]{:S(2)}) collective-permute-start(bf16[24,1664]{1,0:T(8,128)(2,1)S(1)} %get-tuple-element.37.dep_ref.refs_0_), channel_id=1, source_target_pairs={{0,8},{1,9},{2,10},{3,11},{4,12},{5,13},{6,14},{7,15},{8,0},{9,1},... | collective-permute-start | bytes 239624 | tf_op jit(solution)/shard_map/ppermute | solution.py:695
  7.5 6.8 %collective-permute-start.1 = (bf16[24,1664]{1,0:T(8,128)(2,1)S(1)}, bf16[24,1664]{1,0:T(8,128)(2,1)S(1)}, u32[]{:S(2)}, u32[]{:S(2)}) collective-permute-start(bf16[24,1664]{1,0:T(8,128)(2,1)S(1)} %get-tuple-element.37.dep_ref.refs_0_), channel_id=1, source_target_pairs={{0,12},{1,11},{2,14},{3,9},{4,8},{5,15},{6,10},{7,13},{8,4},{9,3},... | collective-permute-start | bytes 239624 | tf_op jit(solution)/shard_map/ppermute | solution.py:695
  8.9 5.5 %collective-permute-start = (bf16[24,1664]{1,0:T(8,128)(2,1)S(1)}, bf16[24,1664]{1,0:T(8,128)(2,1)S(1)}, u32[]{:S(2)}, u32[]{:S(2)}) collective-permute-start(bf16[24,1664]{1,0:T(8,128)(2,1)S(1)} %get-tuple-element.37.dep_ref.refs_0_), channel_id=1, source_target_pairs={{0,4},{1,3},{2,6},{3,1},{4,0},{5,7},{6,2},{7,5},{8,12},{9,11},{10,... | collective-permute-start | bytes 239624 | tf_op jit(solution)/shard_map/ppermute | solution.py:695
  14.4 7.9 %collective-permute-start.3 = (bf16[48,3200]{1,0:T(8,128)(2,1)S(1)}, bf16[48,3200]{1,0:T(8,128)(2,1)S(1)}, u32[]{:S(2)}, u32[]{:S(2)}) collective-permute-start(bf16[48,3200]{1,0:T(8,128)(2,1)S(1)} %unfold.1.dep_ref.a_ref), channel_id=1, source_target_pairs={{0,2},{1,5},{2,0},{3,7},{4,6},{5,1},{6,4},{7,3},{8,10},{9,13},{10,... | collective-permute-start | bytes 921608 | tf_op jit(solution)/shard_map/ppermute | solution.py:695
  22.3 6.0 %collective-permute-start.4 = (bf16[96,3200]{1,0:T(8,128)(2,1)S(1)}, bf16[96,3200]{1,0:T(8,128)(2,1)S(1)}, u32[]{:S(2)}, u32[]{:S(2)}) collective-permute-start(bf16[96,3200]{1,0:T(8,128)(2,1)S(1)} %join.1.x_ref), channel_id=1, source_target_pairs={{0,1},{1,0},{2,3},{3,2},{4,5},{5,4},{6,7},{7,6},{8,9},{9,8},{10,11... | collective-permute-start | bytes 1843208 | tf_op jit(solution)/shard_map/ppermute | solution.py:698
  36.9 3.5 %collective-permute-start.5 = (bf16[96,3072]{1,0:T(8,128)(2,1)S(1)}, bf16[96,3072]{1,0:T(8,128)(2,1)S(1)}, u32[]{:S(2)}, u32[]{:S(2)}) collective-permute-start(bf16[96,3072]{1,0:T(8,128)(2,1)S(1)} %get-tuple-element.60), channel_id=1, source_target_pairs={{0,1},{1,0},{2,3},{3,2},{4,5},{5,4},{6,7},{7,6},{8,9},{9,8},{10,11... | collective-permute-start | bytes 1769480 | tf_op jit(solution)/shard_map/ppermute | solution.py:698
  40.4 6.8 %collective-permute-start.6 = (bf16[48,3072]{1,0:T(8,128)(2,1)S(1)}, bf16[48,3072]{1,0:T(8,128)(2,1)S(1)}, u32[]{:S(2)}, u32[]{:S(2)}) collective-permute-start(bf16[48,3072]{1,0:T(8,128)(2,1)S(1)} %get-tuple-element.62), channel_id=1, source_target_pairs={{0,2},{1,5},{2,0},{3,7},{4,6},{5,1},{6,4},{7,3},{8,10},{9,13},{10,... | collective-permute-start | bytes 884744 | tf_op jit(solution)/shard_map/ppermute | solution.py:695
  47.3 6.3 %collective-permute-start.7 = (bf16[24,1536]{1,0:T(8,128)(2,1)S(1)}, bf16[24,1536]{1,0:T(8,128)(2,1)S(1)}, u32[]{:S(2)}, u32[]{:S(2)}) collective-permute-start(bf16[24,1536]{1,0:T(8,128)(2,1)S(1)} %get-tuple-element.64), channel_id=1, source_target_pairs={{0,8},{1,9},{2,10},{3,11},{4,12},{5,13},{6,14},{7,15},{8,0},{9,1},... | collective-permute-start | bytes 221192 | tf_op jit(solution)/shard_map/ppermute | solution.py:695
  49.9 6.2 %collective-permute-start.8 = (bf16[24,1536]{1,0:T(8,128)(2,1)S(1)}, bf16[24,1536]{1,0:T(8,128)(2,1)S(1)}, u32[]{:S(2)}, u32[]{:S(2)}) collective-permute-start(bf16[24,1536]{1,0:T(8,128)(2,1)S(1)} %get-tuple-element.65), channel_id=1, source_target_pairs={{0,12},{1,11},{2,14},{3,9},{4,8},{5,15},{6,10},{7,13},{8,4},{9,3},... | collective-permute-start | bytes 221192 | tf_op jit(solution)/shard_map/ppermute | solution.py:695
  50.8 5.3 %collective-permute-start.9 = (bf16[24,1536]{1,0:T(8,128)(2,1)S(1)}, bf16[24,1536]{1,0:T(8,128)(2,1)S(1)}, u32[]{:S(2)}, u32[]{:S(2)}) collective-permute-start(bf16[24,1536]{1,0:T(8,128)(2,1)S(1)} %get-tuple-element.66), channel_id=1, source_target_pairs={{0,4},{1,3},{2,6},{3,1},{4,0},{5,7},{6,2},{7,5},{8,12},{9,11},{10,... | collective-permute-start | bytes 221192 | tf_op jit(solution)/shard_map/ppermute | solution.py:695

commit v15 on v13

--- a/solution.py
+++ b/solution.py
@@ -302,8 +302,8 @@
         scratch_shapes=here + [
             pltpu.VMEM((1, width), F32),
             pltpu.VMEM((EXPERTS, width), BF16),
-            pltpu.VMEM((heads * tok, HEAD_DIM), F32),
-            pltpu.VMEM((heads * tok, HEAD_DIM), F32),
+            pltpu.VMEM((heads * tok + 16, HEAD_DIM), F32),
+            pltpu.VMEM((heads * tok + 16, HEAD_DIM), F32),
             pltpu.VMEM((tok, kv_width), F32),
             pltpu.VMEM((tok, kv_width), F32),
             pltpu.VMEM((FOLD * tok, wide), F32),

time: 57.5 us -> 57.5 us (level)
  no operation moved by 1% of the time
where the time goes in v15:
time: 57.5 us; the launch traced here: 57.3 us
  Pallas kernels  31.8 us (55%)
  starting transfers between devices  13.8 us (24%)
  waiting for transfers between devices  11.5 us (20%)
    ppermute x8, starting transfers between devices, exchange(): return lax.ppermute(array, ('node', 'shard'), perm)  13.2 us
    ppermute x8, waiting for transfers between devices, exchange(): return lax.ppermute(array, ('node', 'shard'), perm)  11.5 us
    pallas_call x2, Pallas kernels, load_rows(): pl.pallas_call(functools.partial(load_kernel, first, rows, ahead), out_sh...  10.1 us
    pallas_call x1, Pallas kernels, second_half(): pl.pallas_call(functools.partial(second_half_kernel, per_plane), out_shap...  8.53 us
    pallas_call x1, Pallas kernels, first_half(): pl.pallas_call(first_half_kernel, out_shape=(acc, acc) + tuple((pltpu.VME...  5.89 us
    pallas_call x1, Pallas kernels, attend(): pl.pallas_call(functools.partial(attend_kernel, ahead), out_shape=(pltpu....  3.4 us
    pallas_call x1, Pallas kernels, staying_half(): pl.pallas_call(staying_kernel, out_shape=(vmem_array((rows, width), F32),...  2.91 us
  transfers between devices with their start and end apart: 10, of which 5 were waited for; matrix products, arithmetic and copies ran while one was open for 0% of the time, Pallas kernels for 33%

profile of v15, /device:TPU:0, one launch (start us, length us, event | category | flops | bytes accessed | tf_op | source)
XLA Modules:
  0.0 57.3 jit_solution(14258244945144813061)
XLA Ops:
  0.0 3.4 %attend.1 = (f32[12,3072]{1,0:T(8,128)S(1)}, bf16[24,1664]{1,0:T(8,128)(2,1)S(1)}, bf16[3072,2048]{1,0:T(8,128)(2,1)S(1)}, bf16[3072,2048]{1,0:T(8,128)(2,1)S(1)}, bf16[2,2,3072,512]{3,2,1,0:T(8,128)(2,1)S(1)}) custom-call(s32[12]{0:T(128)} %len_hbm.1, s32[2,12]{1,0:T(2,128)} %bitcast.5, bf16[12,3072]{1,0:T(8,128)(2,1)} %q_hbm.1, ...), custom_call_target="tpu_custom_call" | custom-call | flops 100000000 | bytes 8000000 | tf_op jit(solution)/shard_map/attend/pallas_call | solution.py:291
  3.4 4.1 %collective-permute-start.2 = (bf16[24,1664]{1,0:T(8,128)(2,1)S(1)}, bf16[24,1664]{1,0:T(8,128)(2,1)S(1)}, u32[]{:S(2)}, u32[]{:S(2)}) collective-permute-start(bf16[24,1664]{1,0:T(8,128)(2,1)S(1)} %get-tuple-element.37.dep_ref.refs_0_), channel_id=1, source_target_pairs={{0,8},{1,9},{2,10},{3,11},{4,12},{5,13},{6,14},{7,15},{8,0},{9,1},... | collective-permute-start | bytes 239624 | tf_op jit(solution)/shard_map/ppermute | solution.py:694
  7.5 1.6 %collective-permute-start.1 = (bf16[24,1664]{1,0:T(8,128)(2,1)S(1)}, bf16[24,1664]{1,0:T(8,128)(2,1)S(1)}, u32[]{:S(2)}, u32[]{:S(2)}) collective-permute-start(bf16[24,1664]{1,0:T(8,128)(2,1)S(1)} %get-tuple-element.37.dep_ref.refs_0_), channel_id=1, source_target_pairs={{0,4},{1,3},{2,6},{3,1},{4,0},{5,7},{6,2},{7,5},{8,12},{9,11},{10,... | collective-permute-start | bytes 239624 | tf_op jit(solution)/shard_map/ppermute | solution.py:694
  9.1 0.0 collective-permute-start
  9.1 4.7 %load_weights.2 = (bf16[3072,2048]{1,0:T(8,128)(2,1)S(1)}, bf16[3072,2048]{1,0:T(8,128)(2,1)S(1)}, bf16[2,2,3072,512]{3,2,1,0:T(8,128)(2,1)S(1)}, f32[8,128]{1,0:T(8,128)S(1)}) custom-call(bf16[24,1664]{1,0:T(8,128)(2,1)S(1)} %get-tuple-element.37.dep_ref.refs_0_, ...), custom_call_target="tpu_custom_call", output_to_operand_aliasing={{0}: (3, {}), {1}: (4, {}), {2}: (5, {})} | custom-call | bytes 12582912 | tf_op jit(solution)/shard_map/load_weights/pallas_call | solution.py:115
  13.8 0.0 collective-permute-done.2.refs_3_
  13.8 0.0 collective-permute-done.1.refs_2_
  13.8 1.5 %collective-permute-done.refs_1_ = bf16[24,1664]{1,0:T(8,128)(2,1)S(1)} collective-permute-done((bf16[24,1664]{1,0:T(8,128)(2,1)S(1)}, bf16[24,1664]{1,0:T(8,128)(2,1)S(1)}, u32[]{:S(2)}, u32[]{:S(2)}) %collective-permute-start) | collective-permute-done | bytes 79904 | tf_op jit(solution)/shard_map/ppermute | solution.py:694
  15.3 0.1 unfold.1.dep_ref.a_ref
  15.4 1.6 %collective-permute-start.3 = (bf16[48,3200]{1,0:T(8,128)(2,1)S(1)}, bf16[48,3200]{1,0:T(8,128)(2,1)S(1)}, u32[]{:S(2)}, u32[]{:S(2)}) collective-permute-start(bf16[48,3200]{1,0:T(8,128)(2,1)S(1)} %unfold.1.dep_ref.a_ref), channel_id=1, source_target_pairs={{0,2},{1,5},{2,0},{3,7},{4,6},{5,1},{6,4},{7,3},{8,10},{9,13},{10,... | collective-permute-start | bytes 921608 | tf_op jit(solution)/shard_map/ppermute | solution.py:694
  16.9 5.4 %load_weights.3 = (bf16[3072,2048]{1,0:T(8,128)(2,1)S(1)}, bf16[3072,2048]{1,0:T(8,128)(2,1)S(1)}, bf16[2,2,3072,512]{3,2,1,0:T(8,128)(2,1)S(1)}, f32[8,128]{1,0:T(8,128)S(1)}) custom-call(bf16[48,3200]{1,0:T(8,128)(2,1)S(1)} %unfold.1.dep_ref.a_ref, bf16[6144,2048]{1,0:T(8,128)(2,1)} %g_hbm.9, ...), custom_call_target="tpu_custom_call", output_to_operand_aliasing={{0}: (3, {}), {1}: (4, {}), {2}: (5, {})} | custom-call | bytes 8388608 | tf_op jit(solution)/shard_map/load_weights/pallas_call | solution.py:115
  22.3 0.0 collective-permute-done.3.b_ref
  22.4 0.1 collective-permute-start.4
  22.5 5.9 %first_half.1 = (f32[96,2048]{1,0:T(8,128)S(1)}, f32[96,2048]{1,0:T(8,128)S(1)}, bf16[3072,2048]{1,0:T(8,128)(2,1)S(1)}, bf16[3072,2048]{1,0:T(8,128)(2,1)S(1)}, bf16[2,2,3072,512]{3,2,1,0:T(8,128)(2,1)S(1)}) custom-call(bf16[96,3200]{1,0:T(8,128)(2,1)S(1)} %join.1.x_ref, ...), custom_call_target="tpu_custom_call", output_to_operand_aliasing={{2}: (3, {}), {3}: (4, {}), {4}: (5, {})} | custom-call | flops 2415919104 | bytes 12582912 | tf_op jit(solution)/shard_map/first_half/pallas_call | solution.py:372
  28.4 0.0 collective-permute-done.4.ox_ref
  28.4 8.5 %second_half.1 = (bf16[96,3072]{1,0:T(8,128)(2,1)S(1)}, bf16[96,2048]{1,0:T(8,128)(2,1)S(1)}, f32[96,128]{1,0:T(8,128)S(1)}, bf16[3072,2048]{1,0:T(8,128)(2,1)S(...) custom-call(bf16[96,3200]{1,0:T(8,128)(2,1)S(1)} %join.1.x_ref, ...), custom_call_target="tpu_custom_call", output_to_operand_aliasing={{3}: (7, {}), {4}: (8, {}), {5}: (9, {})} | custom-call | flops 3623878656 | bytes 25165824 | tf_op jit(solution)/shard_map/second_half/pallas_call | solution.py:542
  36.9 0.5 collective-permute-start.5
  37.5 2.9 %staying_half.1 = (f32[96,3072]{1,0:T(8,128)S(1)}, bf16[3072,2048]{1,0:T(8,128)(2,1)S(1)}, bf16[3072,2048]{1,0:T(8,128)(2,1)S(1)}, bf16[2,2,3072,512]{3,2,1,0:T(8,128)(2,1)S(1)}) custom-call(bf16[96,2048]{1,0:T(8,128)(2,1)S(1)} %get-tuple-element.54.h_ref, ...), custom_call_target="tpu_custom_call", output_to_operand_aliasing={{1}: (3, {}), {2}: (4, {}), {3}: (5, {})} | custom-call | flops 1207959552 | bytes 6291456 | tf_op jit(solution)/shard_map/staying_half/pallas_call | solution.py:589
  40.4 0.0 collective-permute-done.5.got_ref
  40.4 0.1 split_rows.1
  40.5 1.5 %collective-permute-start.6 = (bf16[48,3072]{1,0:T(8,128)(2,1)S(1)}, bf16[48,3072]{1,0:T(8,128)(2,1)S(1)}, u32[]{:S(2)}, u32[]{:S(2)}) collective-permute-start(bf16[48,3072]{1,0:T(8,128)(2,1)S(1)} %get-tuple-element.62), channel_id=1, source_target_pairs={{0,2},{1,5},{2,0},{3,7},{4,6},{5,1},{6,4},{7,3},{8,10},{9,13},{10,... | collective-permute-start | bytes 884744 | tf_op jit(solution)/shard_map/ppermute | solution.py:694
  42.0 5.3 %collective-permute-done.6.got_ref = bf16[48,3072]{1,0:T(8,128)(2,1)S(1)} collective-permute-done((bf16[48,3072]{1,0:T(8,128)(2,1)S(1)}, bf16[48,3072]{1,0:T(8,128)(2,1)S(1)}, u32[]{:S(2)}, u32[]{:S(2)}) %collective-permute-start.6) | collective-permute-done | bytes 294944 | tf_op jit(solution)/shard_map/ppermute | solution.py:694
  47.3 0.1 split_last.1
  47.4 2.4 %collective-permute-start.7 = (bf16[24,1536]{1,0:T(8,128)(2,1)S(1)}, bf16[24,1536]{1,0:T(8,128)(2,1)S(1)}, u32[]{:S(2)}, u32[]{:S(2)}) collective-permute-start(bf16[24,1536]{1,0:T(8,128)(2,1)S(1)} %get-tuple-element.64), channel_id=1, source_target_pairs={{0,8},{1,9},{2,10},{3,11},{4,12},{5,13},{6,14},{7,15},{8,0},{9,1},... | collective-permute-start | bytes 221192 | tf_op jit(solution)/shard_map/ppermute | solution.py:694
  49.8 0.6 collective-permute-start.8
  50.4 1.5 %collective-permute-start.9 = (bf16[24,1536]{1,0:T(8,128)(2,1)S(1)}, bf16[24,1536]{1,0:T(8,128)(2,1)S(1)}, u32[]{:S(2)}, u32[]{:S(2)}) collective-permute-start(bf16[24,1536]{1,0:T(8,128)(2,1)S(1)} %get-tuple-element.66), channel_id=1, source_target_pairs={{0,12},{1,11},{2,14},{3,9},{4,8},{5,15},{6,10},{7,13},{8,4},{9,3},... | collective-permute-start | bytes 221192 | tf_op jit(solution)/shard_map/ppermute | solution.py:694
  51.8 1.6 %collective-permute-done.7.refs_0_ = bf16[24,1536]{1,0:T(8,128)(2,1)S(1)} collective-permute-done((bf16[24,1536]{1,0:T(8,128)(2,1)S(1)}, bf16[24,1536]{1,0:T(8,128)(2,1)S(1)}, u32[]{:S(2)}, u32[]{:S(2)}) %collective-permute-start.7) | collective-permute-done | bytes 73760 | tf_op jit(solution)/shard_map/ppermute | solution.py:694
  53.4 1.5 %collective-permute-done.8.refs_1_ = bf16[24,1536]{1,0:T(8,128)(2,1)S(1)} collective-permute-done((bf16[24,1536]{1,0:T(8,128)(2,1)S(1)}, bf16[24,1536]{1,0:T(8,128)(2,1)S(1)}, u32[]{:S(2)}, u32[]{:S(2)}) %collective-permute-start.8) | collective-permute-done | bytes 73760 | tf_op jit(solution)/shard_map/ppermute | solution.py:694
  54.9 1.7 %collective-permute-done.9.refs_2_ = bf16[24,1536]{1,0:T(8,128)(2,1)S(1)} collective-permute-done((bf16[24,1536]{1,0:T(8,128)(2,1)S(1)}, bf16[24,1536]{1,0:T(8,128)(2,1)S(1)}, u32[]{:S(2)}, u32[]{:S(2)}) %collective-permute-start.9) | collective-permute-done | bytes 73760 | tf_op jit(solution)/shard_map/ppermute | solution.py:694
  56.6 0.7 %finish.1 = bf16[12,3072]{1,0:T(8,128)(2,1)} custom-call(f32[12,3072]{1,0:T(8,128)S(1)} %get-tuple-element.36.carried_ref, f32[12,3072]{1,0:T(8,128)S(1)} %get-tuple-element.63.own_ref, bf16[24,1536]{1,0:T(8,128)(2,1)S(1)} %collective-permute-done.7.refs_0_, bf16[24,1536]{1,0:T(8,128)(2,1)S(1)} %collective-permute-done.8.refs_1_, ...), custom_call_target="tpu_custom_call" | custom-call | tf_op jit(solution)/shard_map/finish/pallas_call | solution.py:670
  (1 shorter events, 0.0 us)
Async XLA Ops:
  3.4 10.4 %collective-permute-start.2 = (bf16[24,1664]{1,0:T(8,128)(2,1)S(1)}, bf16[24,1664]{1,0:T(8,128)(2,1)S(1)}, u32[]{:S(2)}, u32[]{:S(2)}) collective-permute-start(bf16[24,1664]{1,0:T(8,128)(2,1)S(1)} %get-tuple-element.37.dep_ref.refs_0_), channel_id=1, source_target_pairs={{0,8},{1,9},{2,10},{3,11},{4,12},{5,13},{6,14},{7,15},{8,0},{9,1},... | collective-permute-start | bytes 239624 | tf_op jit(solution)/shard_map/ppermute | solution.py:694
  7.5 6.3 %collective-permute-start.1 = (bf16[24,1664]{1,0:T(8,128)(2,1)S(1)}, bf16[24,1664]{1,0:T(8,128)(2,1)S(1)}, u32[]{:S(2)}, u32[]{:S(2)}) collective-permute-start(bf16[24,1664]{1,0:T(8,128)(2,1)S(1)} %get-tuple-element.37.dep_ref.refs_0_), channel_id=1, source_target_pairs={{0,4},{1,3},{2,6},{3,1},{4,0},{5,7},{6,2},{7,5},{8,12},{9,11},{10,... | collective-permute-start | bytes 239624 | tf_op jit(solution)/shard_map/ppermute | solution.py:694
  9.1 6.2 %collective-permute-start = (bf16[24,1664]{1,0:T(8,128)(2,1)S(1)}, bf16[24,1664]{1,0:T(8,128)(2,1)S(1)}, u32[]{:S(2)}, u32[]{:S(2)}) collective-permute-start(bf16[24,1664]{1,0:T(8,128)(2,1)S(1)} %get-tuple-element.37.dep_ref.refs_0_), channel_id=1, source_target_pairs={{0,12},{1,11},{2,14},{3,9},{4,8},{5,15},{6,10},{7,13},{8,4},{9,3},... | collective-permute-start | bytes 239624 | tf_op jit(solution)/shard_map/ppermute | solution.py:694
  15.4 6.9 %collective-permute-start.3 = (bf16[48,3200]{1,0:T(8,128)(2,1)S(1)}, bf16[48,3200]{1,0:T(8,128)(2,1)S(1)}, u32[]{:S(2)}, u32[]{:S(2)}) collective-permute-start(bf16[48,3200]{1,0:T(8,128)(2,1)S(1)} %unfold.1.dep_ref.a_ref), channel_id=1, source_target_pairs={{0,2},{1,5},{2,0},{3,7},{4,6},{5,1},{6,4},{7,3},{8,10},{9,13},{10,... | collective-permute-start | bytes 921608 | tf_op jit(solution)/shard_map/ppermute | solution.py:694
  22.4 6.0 %collective-permute-start.4 = (bf16[96,3200]{1,0:T(8,128)(2,1)S(1)}, bf16[96,3200]{1,0:T(8,128)(2,1)S(1)}, u32[]{:S(2)}, u32[]{:S(2)}) collective-permute-start(bf16[96,3200]{1,0:T(8,128)(2,1)S(1)} %join.1.x_ref), channel_id=1, source_target_pairs={{0,1},{1,0},{2,3},{3,2},{4,5},{5,4},{6,7},{7,6},{8,9},{9,8},{10,11... | collective-permute-start | bytes 1843208 | tf_op jit(solution)/shard_map/ppermute | solution.py:697
  36.9 3.5 %collective-permute-start.5 = (bf16[96,3072]{1,0:T(8,128)(2,1)S(1)}, bf16[96,3072]{1,0:T(8,128)(2,1)S(1)}, u32[]{:S(2)}, u32[]{:S(2)}) collective-permute-start(bf16[96,3072]{1,0:T(8,128)(2,1)S(1)} %get-tuple-element.60), channel_id=1, source_target_pairs={{0,1},{1,0},{2,3},{3,2},{4,5},{5,4},{6,7},{7,6},{8,9},{9,8},{10,11... | collective-permute-start | bytes 1769480 | tf_op jit(solution)/shard_map/ppermute | solution.py:697
  40.5 6.8 %collective-permute-start.6 = (bf16[48,3072]{1,0:T(8,128)(2,1)S(1)}, bf16[48,3072]{1,0:T(8,128)(2,1)S(1)}, u32[]{:S(2)}, u32[]{:S(2)}) collective-permute-start(bf16[48,3072]{1,0:T(8,128)(2,1)S(1)} %get-tuple-element.62), channel_id=1, source_target_pairs={{0,2},{1,5},{2,0},{3,7},{4,6},{5,1},{6,4},{7,3},{8,10},{9,13},{10,... | collective-permute-start | bytes 884744 | tf_op jit(solution)/shard_map/ppermute | solution.py:694
  47.4 6.0 %collective-permute-start.7 = (bf16[24,1536]{1,0:T(8,128)(2,1)S(1)}, bf16[24,1536]{1,0:T(8,128)(2,1)S(1)}, u32[]{:S(2)}, u32[]{:S(2)}) collective-permute-start(bf16[24,1536]{1,0:T(8,128)(2,1)S(1)} %get-tuple-element.64), channel_id=1, source_target_pairs={{0,8},{1,9},{2,10},{3,11},{4,12},{5,13},{6,14},{7,15},{8,0},{9,1},... | collective-permute-start | bytes 221192 | tf_op jit(solution)/shard_map/ppermute | solution.py:694
  49.8 5.1 %collective-permute-start.8 = (bf16[24,1536]{1,0:T(8,128)(2,1)S(1)}, bf16[24,1536]{1,0:T(8,128)(2,1)S(1)}, u32[]{:S(2)}, u32[]{:S(2)}) collective-permute-start(bf16[24,1536]{1,0:T(8,128)(2,1)S(1)} %get-tuple-element.65), channel_id=1, source_target_pairs={{0,4},{1,3},{2,6},{3,1},{4,0},{5,7},{6,2},{7,5},{8,12},{9,11},{10,... | collective-permute-start | bytes 221192 | tf_op jit(solution)/shard_map/ppermute | solution.py:694
  50.4 6.3 %collective-permute-start.9 = (bf16[24,1536]{1,0:T(8,128)(2,1)S(1)}, bf16[24,1536]{1,0:T(8,128)(2,1)S(1)}, u32[]{:S(2)}, u32[]{:S(2)}) collective-permute-start(bf16[24,1536]{1,0:T(8,128)(2,1)S(1)} %get-tuple-element.66), channel_id=1, source_target_pairs={{0,12},{1,11},{2,14},{3,9},{4,8},{5,15},{6,10},{7,13},{8,4},{9,3},... | collective-permute-start | bytes 221192 | tf_op jit(solution)/shard_map/ppermute | solution.py:694

commit v16 on v15

--- a/solution.py
+++ b/solution.py
@@ -89,12 +89,14 @@
     return pl.ds(n * chunk if isinstance(n, int) else pl.multiple_of(n * chunk, LANES), chunk)
 
 
-def other_copy(source, held, spare, i, c, chunk, sem):
+def other_copy(source, held, spare, i, c, chunk, sem, part=0, parts=1):
     half = source.shape[0] // 2
-    first = pl.multiple_of((1 - own_side()) * half, 16)
+    size = half // parts
+    first = pl.multiple_of((1 - own_side()) * half + part * size, 16)
+    rows = pl.ds(part * size, size)
     count = spare.shape[0]
-    target = spare.at[c, i] if c < count else held.at[:, chunk_at(c - count, chunk)]
-    return pltpu.make_async_copy(source.at[pl.ds(first, half), chunk_at(c, chunk)], target, sem)
+    target = spare.at[c, i, rows] if c < count else held.at[rows, chunk_at(c - count, chunk)]
+    return pltpu.make_async_copy(source.at[pl.ds(first, size), chunk_at(c, chunk)], target, sem)
 
 
 def load_kernel(first, rows, ahead, dep_ref, g_hbm, u_hbm, *refs):
@@ -102,7 +104,10 @@
     copies = row_copies((g_hbm, u_hbm), (g_vmem, u_vmem), first, rows, sems)
     if ahead:
         for i, source in enumerate((g_hbm, u_hbm)):
-            copies.append(other_copy(source, None, spare, i, 0, spare.shape[3], sem.at[i]))
+            for p in range(sem.shape[1]):
+                copies.append(other_copy(
+                    source, None, spare, i, 0, spare.shape[3], sem.at[i, p], p, sem.shape[1]
+                ))
     for copy in copies:
         copy.start()
     token_ref[...] = jnp.zeros_like(token_ref)
@@ -117,7 +122,7 @@
         out_shape=tuple(pltpu.VMEM(h.shape, BF16) for h in held) + (pltpu.VMEM((8, LANES), F32),),
         in_specs=[pl.BlockSpec(memory_space=pl.ANY), HBM_SPEC, HBM_SPEC] + [VMEM_SPEC] * 3,
         out_specs=(VMEM_SPEC,) * 4,
-        scratch_shapes=[pltpu.SemaphoreType.DMA((2, 4)), pltpu.SemaphoreType.DMA((2,))],
+        scratch_shapes=[pltpu.SemaphoreType.DMA((2, 4)), pltpu.SemaphoreType.DMA((2, 4))],
         input_output_aliases={3: 0, 4: 1, 5: 2},
         compiler_params=pltpu.CompilerParams(vmem_limit_bytes=LOADED_BELOW),
         cost_estimate=pl.CostEstimate(flops=0, bytes_accessed=4 * rows * hidden, transcendentals=0),
@@ -339,13 +344,18 @@
     ready = ready_parts(count, chunks)
 
     def copy(i, c):
-        return other_copy(
-            (g_hbm, u_hbm)[i], (g_ref, u_ref)[i], spare_ref, i, c, chunk, sems.at[i, c]
-        )
+        return [
+            other_copy(
+                (g_hbm, u_hbm)[i], (g_ref, u_ref)[i], spare_ref, i, c, chunk, sems.at[i, c, p], p,
+                sems.shape[2],
+            )
+            for p in range(sems.shape[2])
+        ]
 
     for i, c in ready:
         if c < count:
-            copy(i, c).start()
+            for item in copy(i, c):
+                item.start()
 
     def step(n, _):
         at = chunk_at(n, chunk)
@@ -356,13 +366,15 @@
             if c >= count:
                 @pl.when(n == c - count)
                 def _(i=i, c=c):
-                    copy(i, c).start()
+                    for item in copy(i, c):
+                        item.start()
 
         return 0
 
     lax.fori_loop(0, chunks, step, 0)
     for i, c in ready:
-        copy(i, c).wait()
+        for item in copy(i, c):
+            item.wait()
 
 
 def first_half(mine, held, gate_weight, up_weight):
@@ -374,7 +386,7 @@
         out_shape=(acc, acc) + tuple(pltpu.VMEM(h.shape, BF16) for h in held),
         in_specs=[VMEM_SPEC] + [HBM_SPEC] * 2 + [VMEM_SPEC] * 3,
         out_specs=(VMEM_SPEC,) * 5,
-        scratch_shapes=[pltpu.SemaphoreType.DMA((2, units // chunk_of(units)))],
+        scratch_shapes=[pltpu.SemaphoreType.DMA((2, units // chunk_of(units), 2))],
         input_output_aliases={3: 2, 4: 3, 5: 4},
         compiler_params=pltpu.CompilerParams(vmem_limit_bytes=HELD_BELOW),
         cost_estimate=pl.CostEstimate(

time: 57.5 us -> 57.6 us (level)
  no operation moved by 1% of the time
where the time goes in v16:
time: 57.6 us; the launch traced here: 57.4 us
  Pallas kernels  31.9 us (55%)
  starting transfers between devices  13.8 us (24%)
  waiting for transfers between devices  11.5 us (20%)
    ppermute x8, starting transfers between devices, exchange(): return lax.ppermute(array, ('node', 'shard'), perm)  13.2 us
    ppermute x8, waiting for transfers between devices, exchange(): return lax.ppermute(array, ('node', 'shard'), perm)  11.5 us
    pallas_call x2, Pallas kernels, load_rows(): pl.pallas_call(functools.partial(load_kernel, first, rows, ahead), out_sh...  10.1 us
    pallas_call x1, Pallas kernels, second_half(): pl.pallas_call(functools.partial(second_half_kernel, per_plane), out_shap...  8.53 us
    pallas_call x1, Pallas kernels, first_half(): pl.pallas_call(first_half_kernel, out_shape=(acc, acc) + tuple((pltpu.VME...  5.96 us
    pallas_call x1, Pallas kernels, attend(): pl.pallas_call(functools.partial(attend_kernel, ahead), out_shape=(pltpu....  3.4 us
    pallas_call x1, Pallas kernels, staying_half(): pl.pallas_call(staying_kernel, out_shape=(vmem_array((rows, width), F32),...  2.91 us
  transfers between devices with their start and end apart: 10, of which 5 were waited for; matrix products, arithmetic and copies ran while one was open for 0% of the time, Pallas kernels for 33%

profile of v16, /device:TPU:0, one launch (start us, length us, event | category | flops | bytes accessed | tf_op | source)
XLA Modules:
  0.0 57.4 jit_solution(1447560130654545520)
XLA Ops:
  0.0 3.4 %attend.1 = (f32[12,3072]{1,0:T(8,128)S(1)}, bf16[24,1664]{1,0:T(8,128)(2,1)S(1)}, bf16[3072,2048]{1,0:T(8,128)(2,1)S(1)}, bf16[3072,2048]{1,0:T(8,128)(2,1)S(1)}, bf16[2,2,3072,512]{3,2,1,0:T(8,128)(2,1)S(1)}) custom-call(s32[12]{0:T(128)} %len_hbm.1, s32[2,12]{1,0:T(2,128)} %bitcast.5, bf16[12,3072]{1,0:T(8,128)(2,1)} %q_hbm.1, ...), custom_call_target="tpu_custom_call" | custom-call | flops 100000000 | bytes 8000000 | tf_op jit(solution)/shard_map/attend/pallas_call | solution.py:296
  3.4 4.1 %collective-permute-start.2 = (bf16[24,1664]{1,0:T(8,128)(2,1)S(1)}, bf16[24,1664]{1,0:T(8,128)(2,1)S(1)}, u32[]{:S(2)}, u32[]{:S(2)}) collective-permute-start(bf16[24,1664]{1,0:T(8,128)(2,1)S(1)} %get-tuple-element.37.dep_ref.refs_0_), channel_id=1, source_target_pairs={{0,8},{1,9},{2,10},{3,11},{4,12},{5,13},{6,14},{7,15},{8,0},{9,1},... | collective-permute-start | bytes 239624 | tf_op jit(solution)/shard_map/ppermute | solution.py:706
  7.5 1.6 %collective-permute-start.1 = (bf16[24,1664]{1,0:T(8,128)(2,1)S(1)}, bf16[24,1664]{1,0:T(8,128)(2,1)S(1)}, u32[]{:S(2)}, u32[]{:S(2)}) collective-permute-start(bf16[24,1664]{1,0:T(8,128)(2,1)S(1)} %get-tuple-element.37.dep_ref.refs_0_), channel_id=1, source_target_pairs={{0,4},{1,3},{2,6},{3,1},{4,0},{5,7},{6,2},{7,5},{8,12},{9,11},{10,... | collective-permute-start | bytes 239624 | tf_op jit(solution)/shard_map/ppermute | solution.py:706
  9.1 0.0 collective-permute-start
  9.1 4.8 %load_weights.2 = (bf16[3072,2048]{1,0:T(8,128)(2,1)S(1)}, bf16[3072,2048]{1,0:T(8,128)(2,1)S(1)}, bf16[2,2,3072,512]{3,2,1,0:T(8,128)(2,1)S(1)}, f32[8,128]{1,0:T(8,128)S(1)}) custom-call(bf16[24,1664]{1,0:T(8,128)(2,1)S(1)} %get-tuple-element.37.dep_ref.refs_0_, ...), custom_call_target="tpu_custom_call", output_to_operand_aliasing={{0}: (3, {}), {1}: (4, {}), {2}: (5, {})} | custom-call | bytes 12582912 | tf_op jit(solution)/shard_map/load_weights/pallas_call | solution.py:120
  13.9 0.0 collective-permute-done.2.refs_3_
  13.9 0.0 collective-permute-done.1.refs_2_
  13.9 1.4 %collective-permute-done.refs_1_ = bf16[24,1664]{1,0:T(8,128)(2,1)S(1)} collective-permute-done((bf16[24,1664]{1,0:T(8,128)(2,1)S(1)}, bf16[24,1664]{1,0:T(8,128)(2,1)S(1)}, u32[]{:S(2)}, u32[]{:S(2)}) %collective-permute-start) | collective-permute-done | bytes 79904 | tf_op jit(solution)/shard_map/ppermute | solution.py:706
  15.3 0.1 unfold.1.dep_ref.a_ref
  15.4 1.6 %collective-permute-start.3 = (bf16[48,3200]{1,0:T(8,128)(2,1)S(1)}, bf16[48,3200]{1,0:T(8,128)(2,1)S(1)}, u32[]{:S(2)}, u32[]{:S(2)}) collective-permute-start(bf16[48,3200]{1,0:T(8,128)(2,1)S(1)} %unfold.1.dep_ref.a_ref), channel_id=1, source_target_pairs={{0,2},{1,5},{2,0},{3,7},{4,6},{5,1},{6,4},{7,3},{8,10},{9,13},{10,... | collective-permute-start | bytes 921608 | tf_op jit(solution)/shard_map/ppermute | solution.py:706
  16.9 5.4 %load_weights.3 = (bf16[3072,2048]{1,0:T(8,128)(2,1)S(1)}, bf16[3072,2048]{1,0:T(8,128)(2,1)S(1)}, bf16[2,2,3072,512]{3,2,1,0:T(8,128)(2,1)S(1)}, f32[8,128]{1,0:T(8,128)S(1)}) custom-call(bf16[48,3200]{1,0:T(8,128)(2,1)S(1)} %unfold.1.dep_ref.a_ref, bf16[6144,2048]{1,0:T(8,128)(2,1)} %g_hbm.9, ...), custom_call_target="tpu_custom_call", output_to_operand_aliasing={{0}: (3, {}), {1}: (4, {}), {2}: (5, {})} | custom-call | bytes 8388608 | tf_op jit(solution)/shard_map/load_weights/pallas_call | solution.py:120
  22.3 0.0 collective-permute-done.3.b_ref
  22.4 0.1 collective-permute-start.4
  22.4 6.0 %first_half.1 = (f32[96,2048]{1,0:T(8,128)S(1)}, f32[96,2048]{1,0:T(8,128)S(1)}, bf16[3072,2048]{1,0:T(8,128)(2,1)S(1)}, bf16[3072,2048]{1,0:T(8,128)(2,1)S(1)}, bf16[2,2,3072,512]{3,2,1,0:T(8,128)(2,1)S(1)}) custom-call(bf16[96,3200]{1,0:T(8,128)(2,1)S(1)} %join.1.x_ref, ...), custom_call_target="tpu_custom_call", output_to_operand_aliasing={{2}: (3, {}), {3}: (4, {}), {4}: (5, {})} | custom-call | flops 2415919104 | bytes 12582912 | tf_op jit(solution)/shard_map/first_half/pallas_call | solution.py:384
  28.4 0.0 collective-permute-done.4.ox_ref
  28.4 8.5 %second_half.1 = (bf16[96,3072]{1,0:T(8,128)(2,1)S(1)}, bf16[96,2048]{1,0:T(8,128)(2,1)S(1)}, f32[96,128]{1,0:T(8,128)S(1)}, bf16[3072,2048]{1,0:T(8,128)(2,1)S(...) custom-call(bf16[96,3200]{1,0:T(8,128)(2,1)S(1)} %join.1.x_ref, ...), custom_call_target="tpu_custom_call", output_to_operand_aliasing={{3}: (7, {}), {4}: (8, {}), {5}: (9, {})} | custom-call | flops 3623878656 | bytes 25165824 | tf_op jit(solution)/shard_map/second_half/pallas_call | solution.py:554
  37.0 0.5 collective-permute-start.5
  37.5 2.9 %staying_half.1 = (f32[96,3072]{1,0:T(8,128)S(1)}, bf16[3072,2048]{1,0:T(8,128)(2,1)S(1)}, bf16[3072,2048]{1,0:T(8,128)(2,1)S(1)}, bf16[2,2,3072,512]{3,2,1,0:T(8,128)(2,1)S(1)}) custom-call(bf16[96,2048]{1,0:T(8,128)(2,1)S(1)} %get-tuple-element.54.h_ref, ...), custom_call_target="tpu_custom_call", output_to_operand_aliasing={{1}: (3, {}), {2}: (4, {}), {3}: (5, {})} | custom-call | flops 1207959552 | bytes 6291456 | tf_op jit(solution)/shard_map/staying_half/pallas_call | solution.py:601
  40.4 0.0 collective-permute-done.5.got_ref
  40.4 0.1 split_rows.1
  40.5 1.5 %collective-permute-start.6 = (bf16[48,3072]{1,0:T(8,128)(2,1)S(1)}, bf16[48,3072]{1,0:T(8,128)(2,1)S(1)}, u32[]{:S(2)}, u32[]{:S(2)}) collective-permute-start(bf16[48,3072]{1,0:T(8,128)(2,1)S(1)} %get-tuple-element.62), channel_id=1, source_target_pairs={{0,2},{1,5},{2,0},{3,7},{4,6},{5,1},{6,4},{7,3},{8,10},{9,13},{10,... | collective-permute-start | bytes 884744 | tf_op jit(solution)/shard_map/ppermute | solution.py:706
  42.1 5.3 %collective-permute-done.6.got_ref = bf16[48,3072]{1,0:T(8,128)(2,1)S(1)} collective-permute-done((bf16[48,3072]{1,0:T(8,128)(2,1)S(1)}, bf16[48,3072]{1,0:T(8,128)(2,1)S(1)}, u32[]{:S(2)}, u32[]{:S(2)}) %collective-permute-start.6) | collective-permute-done | bytes 294944 | tf_op jit(solution)/shard_map/ppermute | solution.py:706
  47.3 0.1 split_last.1
  47.4 2.4 %collective-permute-start.7 = (bf16[24,1536]{1,0:T(8,128)(2,1)S(1)}, bf16[24,1536]{1,0:T(8,128)(2,1)S(1)}, u32[]{:S(2)}, u32[]{:S(2)}) collective-permute-start(bf16[24,1536]{1,0:T(8,128)(2,1)S(1)} %get-tuple-element.64), channel_id=1, source_target_pairs={{0,8},{1,9},{2,10},{3,11},{4,12},{5,13},{6,14},{7,15},{8,0},{9,1},... | collective-permute-start | bytes 221192 | tf_op jit(solution)/shard_map/ppermute | solution.py:706
  49.9 0.6 %collective-permute-start.8 = (bf16[24,1536]{1,0:T(8,128)(2,1)S(1)}, bf16[24,1536]{1,0:T(8,128)(2,1)S(1)}, u32[]{:S(2)}, u32[]{:S(2)}) collective-permute-start(bf16[24,1536]{1,0:T(8,128)(2,1)S(1)} %get-tuple-element.65), channel_id=1, source_target_pairs={{0,4},{1,3},{2,6},{3,1},{4,0},{5,7},{6,2},{7,5},{8,12},{9,11},{10,... | collective-permute-start | bytes 221192 | tf_op jit(solution)/shard_map/ppermute | solution.py:706
  50.5 1.4 %collective-permute-start.9 = (bf16[24,1536]{1,0:T(8,128)(2,1)S(1)}, bf16[24,1536]{1,0:T(8,128)(2,1)S(1)}, u32[]{:S(2)}, u32[]{:S(2)}) collective-permute-start(bf16[24,1536]{1,0:T(8,128)(2,1)S(1)} %get-tuple-element.66), channel_id=1, source_target_pairs={{0,12},{1,11},{2,14},{3,9},{4,8},{5,15},{6,10},{7,13},{8,4},{9,3},... | collective-permute-start | bytes 221192 | tf_op jit(solution)/shard_map/ppermute | solution.py:706
  51.9 1.5 %collective-permute-done.7.refs_0_ = bf16[24,1536]{1,0:T(8,128)(2,1)S(1)} collective-permute-done((bf16[24,1536]{1,0:T(8,128)(2,1)S(1)}, bf16[24,1536]{1,0:T(8,128)(2,1)S(1)}, u32[]{:S(2)}, u32[]{:S(2)}) %collective-permute-start.7) | collective-permute-done | bytes 73760 | tf_op jit(solution)/shard_map/ppermute | solution.py:706
  53.4 1.5 %collective-permute-done.8.refs_1_ = bf16[24,1536]{1,0:T(8,128)(2,1)S(1)} collective-permute-done((bf16[24,1536]{1,0:T(8,128)(2,1)S(1)}, bf16[24,1536]{1,0:T(8,128)(2,1)S(1)}, u32[]{:S(2)}, u32[]{:S(2)}) %collective-permute-start.8) | collective-permute-done | bytes 73760 | tf_op jit(solution)/shard_map/ppermute | solution.py:706
  55.0 1.8 %collective-permute-done.9.refs_2_ = bf16[24,1536]{1,0:T(8,128)(2,1)S(1)} collective-permute-done((bf16[24,1536]{1,0:T(8,128)(2,1)S(1)}, bf16[24,1536]{1,0:T(8,128)(2,1)S(1)}, u32[]{:S(2)}, u32[]{:S(2)}) %collective-permute-start.9) | collective-permute-done | bytes 73760 | tf_op jit(solution)/shard_map/ppermute | solution.py:706
  56.7 0.7 %finish.1 = bf16[12,3072]{1,0:T(8,128)(2,1)} custom-call(f32[12,3072]{1,0:T(8,128)S(1)} %get-tuple-element.36.carried_ref, f32[12,3072]{1,0:T(8,128)S(1)} %get-tuple-element.63.own_ref, bf16[24,1536]{1,0:T(8,128)(2,1)S(1)} %collective-permute-done.7.refs_0_, bf16[24,1536]{1,0:T(8,128)(2,1)S(1)} %collective-permute-done.8.refs_1_, ...), custom_call_target="tpu_custom_call" | custom-call | tf_op jit(solution)/shard_map/finish/pallas_call | solution.py:682
  (1 shorter events, 0.0 us)
Async XLA Ops:
  3.4 10.5 %collective-permute-start.2 = (bf16[24,1664]{1,0:T(8,128)(2,1)S(1)}, bf16[24,1664]{1,0:T(8,128)(2,1)S(1)}, u32[]{:S(2)}, u32[]{:S(2)}) collective-permute-start(bf16[24,1664]{1,0:T(8,128)(2,1)S(1)} %get-tuple-element.37.dep_ref.refs_0_), channel_id=1, source_target_pairs={{0,8},{1,9},{2,10},{3,11},{4,12},{5,13},{6,14},{7,15},{8,0},{9,1},... | collective-permute-start | bytes 239624 | tf_op jit(solution)/shard_map/ppermute | solution.py:706
  7.5 6.4 %collective-permute-start.1 = (bf16[24,1664]{1,0:T(8,128)(2,1)S(1)}, bf16[24,1664]{1,0:T(8,128)(2,1)S(1)}, u32[]{:S(2)}, u32[]{:S(2)}) collective-permute-start(bf16[24,1664]{1,0:T(8,128)(2,1)S(1)} %get-tuple-element.37.dep_ref.refs_0_), channel_id=1, source_target_pairs={{0,4},{1,3},{2,6},{3,1},{4,0},{5,7},{6,2},{7,5},{8,12},{9,11},{10,... | collective-permute-start | bytes 239624 | tf_op jit(solution)/shard_map/ppermute | solution.py:706
  9.1 6.2 %collective-permute-start = (bf16[24,1664]{1,0:T(8,128)(2,1)S(1)}, bf16[24,1664]{1,0:T(8,128)(2,1)S(1)}, u32[]{:S(2)}, u32[]{:S(2)}) collective-permute-start(bf16[24,1664]{1,0:T(8,128)(2,1)S(1)} %get-tuple-element.37.dep_ref.refs_0_), channel_id=1, source_target_pairs={{0,12},{1,11},{2,14},{3,9},{4,8},{5,15},{6,10},{7,13},{8,4},{9,3},... | collective-permute-start | bytes 239624 | tf_op jit(solution)/shard_map/ppermute | solution.py:706
  15.4 6.9 %collective-permute-start.3 = (bf16[48,3200]{1,0:T(8,128)(2,1)S(1)}, bf16[48,3200]{1,0:T(8,128)(2,1)S(1)}, u32[]{:S(2)}, u32[]{:S(2)}) collective-permute-start(bf16[48,3200]{1,0:T(8,128)(2,1)S(1)} %unfold.1.dep_ref.a_ref), channel_id=1, source_target_pairs={{0,2},{1,5},{2,0},{3,7},{4,6},{5,1},{6,4},{7,3},{8,10},{9,13},{10,... | collective-permute-start | bytes 921608 | tf_op jit(solution)/shard_map/ppermute | solution.py:706
  22.4 6.1 %collective-permute-start.4 = (bf16[96,3200]{1,0:T(8,128)(2,1)S(1)}, bf16[96,3200]{1,0:T(8,128)(2,1)S(1)}, u32[]{:S(2)}, u32[]{:S(2)}) collective-permute-start(bf16[96,3200]{1,0:T(8,128)(2,1)S(1)} %join.1.x_ref), channel_id=1, source_target_pairs={{0,1},{1,0},{2,3},{3,2},{4,5},{5,4},{6,7},{7,6},{8,9},{9,8},{10,11... | collective-permute-start | bytes 1843208 | tf_op jit(solution)/shard_map/ppermute | solution.py:709
  37.0 3.5 %collective-permute-start.5 = (bf16[96,3072]{1,0:T(8,128)(2,1)S(1)}, bf16[96,3072]{1,0:T(8,128)(2,1)S(1)}, u32[]{:S(2)}, u32[]{:S(2)}) collective-permute-start(bf16[96,3072]{1,0:T(8,128)(2,1)S(1)} %get-tuple-element.60), channel_id=1, source_target_pairs={{0,1},{1,0},{2,3},{3,2},{4,5},{5,4},{6,7},{7,6},{8,9},{9,8},{10,11... | collective-permute-start | bytes 1769480 | tf_op jit(solution)/shard_map/ppermute | solution.py:709
  40.5 6.8 %collective-permute-start.6 = (bf16[48,3072]{1,0:T(8,128)(2,1)S(1)}, bf16[48,3072]{1,0:T(8,128)(2,1)S(1)}, u32[]{:S(2)}, u32[]{:S(2)}) collective-permute-start(bf16[48,3072]{1,0:T(8,128)(2,1)S(1)} %get-tuple-element.62), channel_id=1, source_target_pairs={{0,2},{1,5},{2,0},{3,7},{4,6},{5,1},{6,4},{7,3},{8,10},{9,13},{10,... | collective-permute-start | bytes 884744 | tf_op jit(solution)/shard_map/ppermute | solution.py:706
  47.4 6.0 %collective-permute-start.7 = (bf16[24,1536]{1,0:T(8,128)(2,1)S(1)}, bf16[24,1536]{1,0:T(8,128)(2,1)S(1)}, u32[]{:S(2)}, u32[]{:S(2)}) collective-permute-start(bf16[24,1536]{1,0:T(8,128)(2,1)S(1)} %get-tuple-element.64), channel_id=1, source_target_pairs={{0,8},{1,9},{2,10},{3,11},{4,12},{5,13},{6,14},{7,15},{8,0},{9,1},... | collective-permute-start | bytes 221192 | tf_op jit(solution)/shard_map/ppermute | solution.py:706
  49.9 5.1 %collective-permute-start.8 = (bf16[24,1536]{1,0:T(8,128)(2,1)S(1)}, bf16[24,1536]{1,0:T(8,128)(2,1)S(1)}, u32[]{:S(2)}, u32[]{:S(2)}) collective-permute-start(bf16[24,1536]{1,0:T(8,128)(2,1)S(1)} %get-tuple-element.65), channel_id=1, source_target_pairs={{0,4},{1,3},{2,6},{3,1},{4,0},{5,7},{6,2},{7,5},{8,12},{9,11},{10,... | collective-permute-start | bytes 221192 | tf_op jit(solution)/shard_map/ppermute | solution.py:706
  50.5 6.2 %collective-permute-start.9 = (bf16[24,1536]{1,0:T(8,128)(2,1)S(1)}, bf16[24,1536]{1,0:T(8,128)(2,1)S(1)}, u32[]{:S(2)}, u32[]{:S(2)}) collective-permute-start(bf16[24,1536]{1,0:T(8,128)(2,1)S(1)} %get-tuple-element.66), channel_id=1, source_target_pairs={{0,12},{1,11},{2,14},{3,9},{4,8},{5,15},{6,10},{7,13},{8,4},{9,3},... | collective-permute-start | bytes 221192 | tf_op jit(solution)/shard_map/ppermute | solution.py:706
